TPU v7x, 32 devices: a whole 2x2x4 slice. The times are simulated.
32 devices in a mesh: dp: 16 (over z, x, core), ctx: 2 (over y).
Axes of the slice: x: 2, y: 2, z: 4, core: 2. Of those that a mesh axis runs over, the one named last changes fastest.
Arguments:
- hidden_in: bfloat16 [16, 256, 2688], P('dp', 'ctx'), may hold values from -0.08984375 to 0.08984375
- queries: bfloat16 [16, 256, 2048], P('dp', 'ctx'), may hold values from -60 to 60
- key_states: bfloat16 [16, 256, 1024], P('dp', 'ctx'), may hold values from -4 to 4
- value_states: bfloat16 [16, 256, 1024], P('dp', 'ctx'), may hold values from -6 to 6
- out_grad: bfloat16 [16, 256, 2048], P('dp', 'ctx'), may hold values from -48 to 48
- segment_ids: int32 [16, 256], P('dp', 'ctx'), may hold values from 0 to 3, never falling along the last dimension, each value on 1 to 128 neighbouring positions
Outputs:
- query_grad: bfloat16 [16, 256, 2048], P('dp', 'ctx')
- key_grad: bfloat16 [16, 256, 1024], P('dp', 'ctx')
- value_grad: bfloat16 [16, 256, 1024], P('dp', 'ctx')
- weight_grad: float32 [2688, 2048], P('dp', 'ctx')
Inputs may be any that keep to these rules, and one draw needn't show every extreme that they name: `segment_ids`: documents of a trace are numbered in order of position.
All inputs are finite; a program needn't handle non-finite values.
Results may differ from a plain program's by a relative error of at most 0.0096.
Values may be sent and summed in bfloat16 or wider, within the bound.
No kernel may reach another device: no remote copies, remote signals or barrier semaphores. Data moves between devices by JAX's collectives and lax.ppermute only.
A program may use at most 128 MiB of HBM per device.

v0:
```python
from functools import partial

import jax
import jax.numpy as jnp
from jax import lax
from jax.sharding import PartitionSpec as P

HD = 128
WIN = 1024


SCORE_FLOOR = -1e30


def shifted(value, axis, steps):
    count = lax.axis_size(axis)
    leading, last = (max(0, -steps), min(count, count - steps))
    return lax.ppermute(value, axis, [(source, source + steps) for source in range(leading, last)])


def head_grads(allowed, score_scale, operands):
    query_head, key_head, value_head, grad_head = operands
    scores = (
        jnp.einsum("igd,jd->gij", query_head, key_head, preferred_element_type=jnp.float32)
        * score_scale
    )
    scores = jnp.where(allowed[None], scores, SCORE_FLOOR)
    row_peak = jnp.max(scores, axis=2, keepdims=True)
    weights = jnp.where(allowed[None], jnp.exp(scores - row_peak), 0.0)
    probs_full = weights / jnp.sum(weights, axis=2, keepdims=True)
    probs_low = probs_full.astype(jnp.bfloat16)
    attn_out = jnp.einsum("gij,jd->gid", probs_low, value_head, preferred_element_type=jnp.float32)
    row_delta = jnp.einsum("igd,gid->gi", grad_head.astype(jnp.float32), attn_out)
    dprobs = jnp.einsum("igd,jd->gij", grad_head, value_head, preferred_element_type=jnp.float32)
    dscores = (probs_full * (dprobs - row_delta[:, :, None])).astype(jnp.bfloat16)
    query_part = (
        jnp.einsum("gij,jd->igd", dscores, key_head, preferred_element_type=jnp.float32)
        * score_scale
    ).astype(jnp.bfloat16)
    key_part = (
        jnp.einsum("gij,igd->jd", dscores, query_head, preferred_element_type=jnp.float32)
        * score_scale
    ).astype(jnp.bfloat16)
    value_part = jnp.einsum(
        "gij,igd->jd", probs_low, grad_head, preferred_element_type=jnp.float32
    ).astype(jnp.bfloat16)
    return (query_part, key_part, value_part)


def attend(allowed, score_scale, heads_in):
    query_heads, key_heads, value_heads, grad_heads = heads_in
    results = lax.map(
        partial(head_grads, allowed, score_scale), (query_heads, key_heads, value_heads, grad_heads)
    )
    return (results[0], results[1], results[2])


def local(hidden_in, queries, key_states, value_states, out_grad, segment_ids):
    tok_rows = queries.shape[1]
    key_width = key_states.shape[2]
    query_width = queries.shape[2]
    kv_heads = key_width // HD
    group_size = query_width // key_width
    score_scale = HD ** (-0.5)
    ctx_count = lax.axis_size("ctx")
    hop_count = min(WIN // tok_rows, ctx_count - 1)
    rim_span = hop_count * tok_rows
    ctx_place = lax.axis_index("ctx")
    own_keys = key_states[0]
    own_values = value_states[0]
    own_segs = segment_ids[0].astype(jnp.bfloat16)
    fetched = [
        shifted((own_keys, own_values, own_segs), "ctx", hop_index)
        for hop_index in range(hop_count, 0, -1)
    ]
    key_window = jnp.concatenate([fetched_item[0] for fetched_item in fetched] + [own_keys], axis=0)
    value_window = jnp.concatenate(
        [fetched_item[1] for fetched_item in fetched] + [own_values], axis=0
    )
    seg_window = jnp.concatenate([fetched_item[2] for fetched_item in fetched] + [own_segs], axis=0)
    seg_float = seg_window.astype(jnp.float32)
    query_segs = own_segs.astype(jnp.float32)
    query_pos = ctx_place * tok_rows + jnp.arange(tok_rows, dtype=jnp.int32)
    key_pos = ctx_place * tok_rows - rim_span + jnp.arange(tok_rows + rim_span, dtype=jnp.int32)
    distance = query_pos[:, None] - key_pos[None, :]
    allowed = (
        (key_pos[None, :] >= 0)
        & (distance >= 0)
        & (distance < WIN)
        & (query_segs[:, None] == seg_float[None, :])
    )
    query_heads = queries[0].reshape(tok_rows, kv_heads, group_size, HD).transpose(1, 0, 2, 3)
    grad_heads = out_grad[0].reshape(tok_rows, kv_heads, group_size, HD).transpose(1, 0, 2, 3)
    key_heads = key_window.reshape(-1, kv_heads, HD).transpose(1, 0, 2)
    value_heads = value_window.reshape(-1, kv_heads, HD).transpose(1, 0, 2)
    heads_in = (query_heads, key_heads, value_heads, grad_heads)
    query_part, key_part, value_part = attend(allowed, score_scale, heads_in)
    query_grad = query_part.transpose(1, 0, 2, 3).reshape(tok_rows, query_width)
    key_rows = key_part.transpose(1, 0, 2).reshape(-1, key_width)
    value_rows = value_part.transpose(1, 0, 2).reshape(-1, key_width)
    key_total = key_rows[rim_span:].astype(jnp.float32)
    value_total = value_rows[rim_span:].astype(jnp.float32)
    for hop_index in range(1, hop_count + 1):
        lower_row = rim_span - hop_index * tok_rows
        returned = shifted(
            (
                key_rows[lower_row : lower_row + tok_rows],
                value_rows[lower_row : lower_row + tok_rows],
            ),
            "ctx",
            -hop_index,
        )
        key_total = key_total + returned[0].astype(jnp.float32)
        value_total = value_total + returned[1].astype(jnp.float32)
    key_grad = key_total.astype(jnp.bfloat16)
    value_grad = value_total.astype(jnp.bfloat16)
    features = hidden_in[0]
    both_grads = jnp.concatenate([key_grad, value_grad], axis=1)
    contract_rows = (((0,), (0,)), ((), ()))
    column_block = lax.all_to_all(both_grads, "ctx", split_axis=1, concat_axis=0, tiled=True)
    trace_term = lax.dot_general(
        lax.all_gather(features, "ctx", axis=0, tiled=True),
        column_block,
        contract_rows,
        preferred_element_type=jnp.float32,
    )
    weight_grad = lax.psum_scatter(trace_term, "dp", scatter_dimension=0, tiled=True)
    return (query_grad[None], key_grad[None], value_grad[None], weight_grad)


def solution(mesh):
    placed = (
        P("dp", "ctx", None),
        P("dp", "ctx", None),
        P("dp", "ctx", None),
        P("dp", "ctx", None),
        P("dp", "ctx", None),
        P("dp", "ctx"),
    )
    return jax.shard_map(
        local,
        mesh=mesh,
        in_specs=placed,
        out_specs=(
            P("dp", "ctx", None),
            P("dp", "ctx", None),
            P("dp", "ctx", None),
            P("dp", "ctx"),
        ),
        check_vma=False,
    )
```

profile of v0, /device:TPU:0, one launch (start us, length us, event | category | flops | bytes accessed | tf_op | source)
XLA Modules:
  0.0 245.3 jit_solution(2708121774500196724)
XLA Ops:
  8.6 4.9 %collective-permute-start.1 = (bf16[128]{0:T(256)(128)(2,1)S(1)}, bf16[128]{0:T(256)(128)(2,1)S(1)}, u32[]{:S(2)}, u32[]{:S(2)}) collective-permute-start(bf16[128]{0:T(256)(128)(2,1)S(1)} %get-tuple-element.177), channel_id=1, source_target_pairs={{0,1},{2,3},{4,5},{6,7},{8,9},{10,11},{12,13},{14,15},{16,17},{18,... | collective-permute-start | bytes 776 | tf_op jit(solution)/shard_map/ppermute | solution.py:18
  13.5 1.1 copy.64
  14.6 2.0 collective-permute-start.2
  16.8 1.3 collective-permute-start
  18.8 6.2 %collective-permute-done.2 = bf16[128,1024]{0,1:T(8,128)(2,1)} collective-permute-done((bf16[128,1024]{0,1:T(8,128)(2,1)S(1)}, bf16[128,1024]{0,1:T(8,128)(2,1)}, u32[]{:S(2)}, u32[]{:S(2)}) %collective-permute-start.2) | collective-permute-done | bytes 262176 | tf_op jit(solution)/shard_map/ppermute | solution.py:18
  25.0 1.0 maximum_bitcast_fusion.1
  26.0 9.1 %collective-permute-done = bf16[128,1024]{0,1:T(8,128)(2,1)S(1)} collective-permute-done((bf16[128,1024]{0,1:T(8,128)(2,1)S(1)}, bf16[128,1024]{0,1:T(8,128)(2,1)S(1)}, u32[]{:S(2)}, u32[]{:S(2)}) %collective-permute-start) | collective-permute-done | bytes 262176 | tf_op jit(solution)/shard_map/ppermute | solution.py:18
  35.8 1.0 maximum_bitcast_fusion
  36.8 36.8 %while.15 = (s32[]{:T(128)}, bf16[8,128,2,128]{1,3,2,0:T(8,128)(2,1)}, bf16[8,256,128]{2,1,0:T(8,128)(2,1)S(1)}, bf16[8,256,128]{2,1,0:T(8,128)(2,1)S(1)}, bf16[...) while((s32[]{:T(128)}, ...), condition=%wide.region_3.4_spmd.clone, body=%wide.region_0.3_spmd.clone.sunk | while | flops 136086528 | bytes 2474897 | solution.py:52
  37.2 1.0 fusion.130
  38.8 1.2 fusion.132
  41.8 1.0 fusion.130
  43.3 1.2 fusion.132
  47.9 1.2 fusion.132
  51.0 1.0 fusion.130
  52.5 1.2 fusion.132
  55.6 1.0 fusion.130
  57.1 1.2 fusion.132
  60.2 1.0 fusion.130
  61.7 1.2 fusion.132
  66.3 1.2 fusion.132
  70.9 1.2 fusion.132
  73.9 1.3 collective-permute-start.4
  75.4 1.3 collective-permute-start.3
  77.1 6.6 %collective-permute-done.4 = bf16[128,1024]{0,1:T(8,128)(2,1)S(1)} collective-permute-done((bf16[128,1024]{0,1:T(8,128)(2,1)S(1)}, bf16[128,1024]{0,1:T(8,128)(2,1)S(1)}, u32[]{:S(2)}, u32[]{:S(2)}) %collective-permute-start.4) | collective-permute-done | bytes 262176 | tf_op jit(solution)/shard_map/ppermute | solution.py:18
  83.8 2.8 %collective-permute-done.3 = bf16[128,1024]{0,1:T(8,128)(2,1)S(1)} collective-permute-done((bf16[128,1024]{0,1:T(8,128)(2,1)S(1)}, bf16[128,1024]{0,1:T(8,128)(2,1)S(1)}, u32[]{:S(2)}, u32[]{:S(2)}) %collective-permute-start.3) | collective-permute-done | bytes 262176 | tf_op jit(solution)/shard_map/ppermute | solution.py:18
  86.6 9.0 %all_to_all.19 = bf16[128,2,1024]{0,2,1:T(8,128)(2,1)S(1)} all-to-all(bf16[128,2,1024]{0,2,1:T(8,128)(2,1)S(1)} %bitcast.222), channel_id=1, replica_groups=mesh['dp'=16,'ctx'=2] {'ctx'}, dimensions={1} | all-to-all | bytes 1048576 | tf_op jit(solution)/shard_map/all_to_all | solution.py:120
  95.8 7.2 %convolution_bitcast_fusion.3 = f32[2688,1024]{0,1:T(8,128)} fusion(bf16[256,1024]{1,0:T(8,128)(2,1)S(1)} %bitcast.220, bf16[1,256,2688]{2,1,0:T(8,128)(2,1)} %all-gather.3.cloned.1.call-done), kind=kOutput, calls=%fused_computation.58 | convolution fusion | flops 1409286144 | bytes 12910592 | tf_op jit(solution)/shard_map/dot_general | solution.py:121
  103.1 12.1 %copy.91 = f32[2688,1024]{1,0:T(8,128)} copy(f32[2688,1024]{0,1:T(8,128)} %convolution_bitcast_fusion.3) | data formatting | bytes 22020096
  115.2 1.0 copy-done.2
  116.2 1.0 copy.88
  118.9 119.5 %reduce-scatter.4.cloned.1.call-done = f32[168,1024]{1,0:T(8,128)} async-done(((f32[2688,1024]{1,0:T(8,128)}), f32[168,1024]{1,0:T(8,128)}) %reduce-scatter.4.cloned.1.call-update) | async-done | bytes 688144
  (97 shorter events, 27.9 us)
Async XLA Ops:
  7.2 9.5 %copy-start.3 = (bf16[1,128,1024]{2,1,0:T(8,128)(2,1)S(1)}, bf16[1,128,1024]{2,1,0:T(8,128)(2,1)}, u32[]{:S(2)}) copy-start(bf16[1,128,1024]{2,1,0:T(8,128)(2,1)} %param.10) | copy-start | bytes 786436
  7.2 11.0 %copy-start = (bf16[1,128,2048]{2,1,0:T(8,128)(2,1)S(1)}, bf16[1,128,2048]{2,1,0:T(8,128)(2,1)}, u32[]{:S(2)}) copy-start(bf16[1,128,2048]{2,1,0:T(8,128)(2,1)} %param.9) | copy-start | bytes 1572868
  7.2 11.3 %copy-start.1 = (bf16[1,128,2048]{2,1,0:T(8,128)(2,1)S(1)}, bf16[1,128,2048]{2,1,0:T(8,128)(2,1)}, u32[]{:S(2)}) copy-start(bf16[1,128,2048]{2,1,0:T(8,128)(2,1)} %param.12) | copy-start | bytes 1572868
  7.2 88.6 %all-gather.3.cloned.1.call-start = ((), (), s32[]{:S(2)}) async-start(), calls=%async_computation.2 | async-start | bytes 2064384 | tf_op jit(solution)/shard_map/all_gather | solution.py:122
  7.9 230.5 %reduce-scatter.4.cloned.1.call-start = ((), (), s32[]{:S(2)}) async-start(), calls=%async_computation.3 | async-start | bytes 11698176
  8.6 10.2 %collective-permute-start.1 = (bf16[128]{0:T(256)(128)(2,1)S(1)}, bf16[128]{0:T(256)(128)(2,1)S(1)}, u32[]{:S(2)}, u32[]{:S(2)}) collective-permute-start(bf16[128]{0:T(256)(128)(2,1)S(1)} %get-tuple-element.177), channel_id=1, source_target_pairs={{0,1},{2,3},{4,5},{6,7},{8,9},{10,11},{12,13},{14,15},{16,17},{18,... | collective-permute-start | bytes 776 | tf_op jit(solution)/shard_map/ppermute | solution.py:18
  14.6 10.4 %collective-permute-start.2 = (bf16[128,1024]{0,1:T(8,128)(2,1)S(1)}, bf16[128,1024]{0,1:T(8,128)(2,1)}, u32[]{:S(2)}, u32[]{:S(2)}) collective-permute-start(bf16[128,1024]{0,1:T(8,128)(2,1)S(1)} %bitcast.227), channel_id=1, source_target_pairs={{0,1},{2,3},{4,5},{6,7},{8,9},{10,11},{12,13},{14,15},{16,17},{18,... | collective-permute-start | bytes 786440 | tf_op jit(solution)/shard_map/ppermute | solution.py:18
  16.8 18.3 %collective-permute-start = (bf16[128,1024]{0,1:T(8,128)(2,1)S(1)}, bf16[128,1024]{0,1:T(8,128)(2,1)S(1)}, u32[]{:S(2)}, u32[]{:S(2)}) collective-permute-start(bf16[128,1024]{0,1:T(8,128)(2,1)S(1)} %bitcast.225), channel_id=1, source_target_pairs={{0,1},{2,3},{4,5},{6,7},{8,9},{10,11},{12,13},{14,15},{16,17},{18,... | collective-permute-start | bytes 786440 | tf_op jit(solution)/shard_map/ppermute | solution.py:18
  35.1 0.7 copy-start.4
  73.9 9.8 %collective-permute-start.4 = (bf16[128,1024]{0,1:T(8,128)(2,1)S(1)}, bf16[128,1024]{0,1:T(8,128)(2,1)S(1)}, u32[]{:S(2)}, u32[]{:S(2)}) collective-permute-start(bf16[128,1024]{0,1:T(8,128)(2,1)S(1)} %bitcast.232), channel_id=1, source_target_pairs={{1,0},{3,2},{5,4},{7,6},{9,8},{11,10},{13,12},{15,14},{17,16},{19,... | collective-permute-start | bytes 786440 | tf_op jit(solution)/shard_map/ppermute | solution.py:18
  75.4 11.1 %collective-permute-start.3 = (bf16[128,1024]{0,1:T(8,128)(2,1)S(1)}, bf16[128,1024]{0,1:T(8,128)(2,1)S(1)}, u32[]{:S(2)}, u32[]{:S(2)}) collective-permute-start(bf16[128,1024]{0,1:T(8,128)(2,1)S(1)} %bitcast.233), channel_id=1, source_target_pairs={{1,0},{3,2},{5,4},{7,6},{9,8},{11,10},{13,12},{15,14},{17,16},{19,... | collective-permute-start | bytes 786440 | tf_op jit(solution)/shard_map/ppermute | solution.py:18
  115.2 1.0 copy-start.2
Sparse Core Ops, SparseCore 0:
  9.6 32.4 all-gather.2
  115.3 123.0 reduce-scatter.3
where the time goes:
time: 246 us; the launch traced here: 245 us
  waiting for transfers between devices  145 us (59%)
  matrix products  41.3 us (17%)
  local copies, waits for them, and re-layouts  20.4 us (8%)
  between operations  14.3 us (6%)
  starting transfers between devices  10.8 us (4%)
  blocking collectives  8.99 us (4%)
  other arithmetic  4.34 us (2%)
    unnamed x3, waiting for transfers between devices  120 us
    ppermute x5, waiting for transfers between devices, shifted(): lax.ppermute(value, axis, [(source, source + steps) for source in range(l...  24.6 us
    unnamed x17, local copies, waits for them, and re-layouts  17.4 us
    ppermute x5, starting transfers between devices, shifted(): lax.ppermute(value, axis, [(source, source + steps) for source in range(l...  10.7 us
    dot_general x8, matrix products, head_grads(): jnp.einsum('igd,jd->gij', grad_head, value_head, preferred_element_type=j...  9.39 us
    all_to_all x1, blocking collectives, local(): lax.all_to_all(both_grads, 'ctx', split_axis=1, concat_axis=0, tiled=True)  8.99 us
    sub x8, matrix products, head_grads(): weights = jnp.where(allowed[None], jnp.exp(scores - row_peak), 0.0)  8 us
    dot_general x1, matrix products, local(): lax.dot_general(lax.all_gather(features, 'ctx', axis=0, tiled=True), colu...  7.22 us
  transfers between devices with their start and end apart: 7, of which 5 were waited for; matrix products, arithmetic and copies ran while one was open for 18% of the time, Pallas kernels for 0%

commit v1 on v0

v1 whole, which is shorter than its diff:
```python
from functools import partial

import jax
import jax.numpy as jnp
from jax import lax
from jax.experimental import pallas as pl
from jax.experimental.pallas import tpu as pltpu
from jax.sharding import PartitionSpec as P

HD = 128
WIN = 1024
CHUNKS = 2
SCORE_FLOOR = -1e30
MIB = 1024 * 1024

NT = (((1,), (1,)), ((), ()))
TN = (((0,), (0,)), ((), ()))


def dot_f32(left, right, dims=(((1,), (0,)), ((), ()))):
    return lax.dot_general(left, right, dims, preferred_element_type=jnp.float32)


def shifted(value, axis, steps):
    count = lax.axis_size(axis)
    leading, last = (max(0, -steps), min(count, count - steps))
    return lax.ppermute(value, axis, [(source, source + steps) for source in range(leading, last)])


def attention_kernel(hops, group, place_ref, *refs):
    segs_ref, query_ref, grad_ref, key_ref, value_ref = refs[:5]
    rim_refs = refs[5 : 5 + 2 * hops]
    rim_segs = rim_refs[hops:]
    rim_pairs = rim_refs[:hops]
    outs = refs[5 + 2 * hops :]
    tok = query_ref.shape[0]
    heads = key_ref.shape[1] // HD
    rim = hops * tok
    span = rim + tok
    place = place_ref[0]
    scale = HD**-0.5

    query_segs = segs_ref[...].astype(jnp.float32)
    key_cols = [
        jnp.transpose(jnp.broadcast_to(ref[...].astype(jnp.float32), (tok, tok)))
        for ref in (*rim_segs, segs_ref)
    ]
    key_segs = jnp.concatenate(key_cols, axis=0)
    key_at = lax.broadcasted_iota(jnp.int32, (span, tok), 0)
    distance = rim + lax.broadcasted_iota(jnp.int32, (span, tok), 1) - key_at
    allowed = (
        (key_at >= rim - place * tok)
        & (distance >= 0)
        & (distance < WIN)
        & (key_segs == query_segs)
    )
    floor = jnp.where(allowed, 0.0, SCORE_FLOOR)
    floor = jnp.concatenate([floor] * group, axis=1)
    keep = floor == 0.0

    for head in range(heads):
        cols = slice(head * HD, (head + 1) * HD)
        value_cols = slice((heads + head) * HD, (heads + head + 1) * HD)
        q_cols = [slice((head * group + g) * HD, (head * group + g + 1) * HD) for g in range(group)]
        query = jnp.concatenate([query_ref[:, c] for c in q_cols], axis=0)
        grad = jnp.concatenate([grad_ref[:, c] for c in q_cols], axis=0)
        keys = jnp.concatenate([ref[:, cols] for ref in rim_pairs] + [key_ref[:, cols]], axis=0)
        values = jnp.concatenate(
            [ref[:, value_cols] for ref in rim_pairs] + [value_ref[:, cols]], axis=0
        )
        scores = jnp.where(keep, dot_f32(keys, query, NT) * scale, SCORE_FLOOR)
        weights = jnp.exp(scores - jnp.max(scores, axis=0, keepdims=True))
        probs = weights * (1.0 / jnp.sum(weights, axis=0, keepdims=True))
        probs_low = probs.astype(jnp.bfloat16)
        dprobs = dot_f32(values, grad, NT)
        delta = jnp.sum(probs_low.astype(jnp.float32) * dprobs, axis=0, keepdims=True)
        dscores = (probs * (dprobs - delta)).astype(jnp.bfloat16)
        query_part = (dot_f32(dscores, keys, TN) * scale).astype(jnp.bfloat16)
        for g, c in enumerate(q_cols):
            outs[0][:, c] = query_part[g * tok : (g + 1) * tok]
        key_part = dot_f32(dscores, query) * scale
        value_part = dot_f32(probs_low, grad)
        if hops == 1:
            first = place == 0
            key_rim, key_own = key_part[:tok], key_part[tok:]
            value_rim, value_own = value_part[:tok], value_part[tok:]
            outs[1][:, cols] = jnp.where(first, value_own, key_rim).astype(jnp.bfloat16)
            outs[2][:, cols] = jnp.where(first, key_own, value_rim).astype(jnp.bfloat16)
            outs[3][:, cols] = key_own.astype(jnp.bfloat16)
            outs[4][:, cols] = value_own.astype(jnp.bfloat16)
            outs[5][:, cols] = value_rim.astype(jnp.bfloat16)
        else:
            outs[1][:, cols] = key_part.astype(jnp.bfloat16)
            outs[2][:, cols] = value_part.astype(jnp.bfloat16)


def attend(chunk, place, segs, queries, out_grad, keys, values, rim_pairs, rim_segs):
    hops = len(rim_pairs)
    tok = queries.shape[0]
    group = queries.shape[1] // keys.shape[1]
    width = keys.shape[1] // CHUNKS
    heads = width // HD
    span = (hops + 1) * tok
    whole = lambda *shape: pl.BlockSpec(shape, lambda i, *_: (0,) * len(shape))
    part = lambda *shape: pl.BlockSpec(shape, lambda i, *_: (0, chunk))
    shape_of = lambda *shape: jax.ShapeDtypeStruct(shape, jnp.bfloat16)
    if hops == 1:
        out_shapes = [(tok, width)] * 5
    else:
        out_shapes = [(span, width)] * 2
    out_shapes = [(tok, group * width)] + out_shapes
    return pl.pallas_call(
        partial(attention_kernel, hops, group),
        grid_spec=pltpu.PrefetchScalarGridSpec(
            num_scalar_prefetch=1,
            grid=(1,),
            in_specs=[
                whole(1, tok),
                part(tok, group * width),
                part(tok, group * width),
                part(tok, width),
                part(tok, width),
            ]
            + [whole(tok, 2 * width)] * hops
            + [whole(1, tok)] * hops,
            out_specs=[whole(*shape) for shape in out_shapes],
        ),
        out_shape=[shape_of(*shape) for shape in out_shapes],
        compiler_params=pltpu.CompilerParams(vmem_limit_bytes=48 * MIB),
        cost_estimate=pl.CostEstimate(
            flops=heads * group * tok * span * HD * 10,
            bytes_accessed=16 * tok * width,
            transcendentals=heads * group * tok * span,
        ),
    )(place, segs, queries, out_grad, keys, values, *rim_pairs, *rim_segs)


def product_kernel(traces, *refs):
    own_ref, other_ref = refs[:2]
    grad_refs = refs[2 : 2 + traces]
    send_ref, keep_ref = refs[2 + traces :]
    features = jnp.concatenate(
        [ref[t] for t in range(traces) for ref in (own_ref, other_ref)], axis=1
    )
    grads = jnp.concatenate([ref[...] for ref in grad_refs], axis=0)
    half = features.shape[0] // 2
    send_ref[...] = dot_f32(features[:half], grads).astype(jnp.bfloat16)
    keep_ref[...] = dot_f32(features[half:], grads)


def product(own_features, other_features, grads):
    traces, rows, tok = own_features.shape
    width = grads[0].shape[1]
    return pl.pallas_call(
        partial(product_kernel, traces),
        out_shape=[
            jax.ShapeDtypeStruct((rows // 2, width), jnp.bfloat16),
            jax.ShapeDtypeStruct((rows // 2, width), jnp.float32),
        ],
        compiler_params=pltpu.CompilerParams(vmem_limit_bytes=48 * MIB),
        cost_estimate=pl.CostEstimate(
            flops=4 * traces * tok * rows * width,
            bytes_accessed=4 * traces * tok * (rows + width) + 3 * rows * width,
            transcendentals=0,
        ),
    )(own_features, other_features, *grads)


def local(hidden_in, queries, key_states, value_states, out_grad, segment_ids):
    tok = queries.shape[1]
    key_width = key_states.shape[2]
    width = key_width // CHUNKS
    ctx_count = lax.axis_size("ctx")
    hops = min(WIN // tok, ctx_count - 1)
    place = lax.axis_index("ctx")
    first = place == 0
    place_arg = place.astype(jnp.int32).reshape(1)

    dp_count = lax.axis_size("dp")
    slow_count, core_count = 4, 2
    mid_count = dp_count // (slow_count * core_count)
    dp_place = lax.axis_index("dp")
    core_at = dp_place % core_count
    mid_at = dp_place // core_count % mid_count
    slow_at = dp_place // (core_count * mid_count)

    def dp_send(value, move):
        pairs = []
        for source in range(dp_count):
            core = source % core_count
            mid = source // core_count % mid_count
            slow = source // (core_count * mid_count)
            slow, mid, core = move(slow, mid, core)
            pairs.append((source, (slow * mid_count + mid) * core_count + core))
        return lax.ppermute(value, "dp", pairs)

    swap_core = lambda slow, mid, core: (slow, mid, core ^ 1)
    mid_by = lambda step: lambda slow, mid, core: (slow, (mid + step) % mid_count, core)
    flip_slow = lambda bit: lambda slow, mid, core: (slow ^ bit, mid, core)
    swap_ctx = [(c, c ^ 1) for c in range(ctx_count)]

    own_keys, own_values = key_states[0], value_states[0]

    steps = range(hops, 0, -1)
    rim_pairs = []
    for chunk in range(CHUNKS):
        cols = slice(chunk * width, (chunk + 1) * width)
        pair = jnp.concatenate([own_keys[:, cols], own_values[:, cols]], axis=1)
        rim_pairs.append([shifted(pair, "ctx", step) for step in steps])
    rim_segs = [shifted(segment_ids, "ctx", step) for step in steps]

    rows = hidden_in.shape[2] // dp_count
    by_feature = hidden_in[0].T.reshape(slow_count, mid_count, core_count, rows, tok)
    order = (3, 1, 2, 0)
    by_feature = jnp.stack(
        [lax.dynamic_index_in_dim(by_feature, slow_at ^ flip, 0, False) for flip in order], axis=2
    )
    core_block = lambda at: lax.dynamic_index_in_dim(by_feature, at, 1, False)
    features = jnp.stack([core_block(core_at), dp_send(core_block(1 - core_at), swap_core)], axis=1)
    mid_block = lambda at: lax.dynamic_index_in_dim(features, at % mid_count, 0, False)
    features = jnp.concatenate(
        [mid_block(mid_at)]
        + [dp_send(mid_block(mid_at + step), mid_by(step)) for step in range(1, mid_count)],
        axis=0,
    )
    features = features.reshape(core_count * mid_count, slow_count * rows, tok)

    attended = [
        attend(
            chunk,
            place_arg,
            segment_ids,
            queries[0],
            out_grad[0],
            own_keys,
            own_values,
            rim_pairs[chunk],
            rim_segs,
        )
        for chunk in range(CHUNKS)
    ]
    query_grad = jnp.concatenate([outs[0] for outs in attended], axis=1)

    if ctx_count == 2:
        other_features = lax.ppermute(features, "ctx", swap_ctx)
        key_grads, value_grads, columns = [], [], []
        for _, sent, addend, key_own, value_own, value_rim in attended:
            late_keys = lax.ppermute(key_own, "ctx", [(1, 0)])
            arrived = lax.ppermute(sent, "ctx", swap_ctx)
            total = (addend.astype(jnp.float32) + arrived.astype(jnp.float32)).astype(jnp.bfloat16)
            columns.append(
                jnp.concatenate(
                    [jnp.where(first, total, value_own), jnp.where(first, late_keys, total)], axis=0
                )
            )
            key_grads.append(jnp.where(first, total, key_own))
            returned = lax.ppermute(value_rim, "ctx", [(1, 0)])
            value_grads.append(
                (value_own.astype(jnp.float32) + returned.astype(jnp.float32)).astype(jnp.bfloat16)
            )
        key_grad = jnp.concatenate(key_grads, axis=1)
        value_grad = jnp.concatenate(value_grads, axis=1)
    else:
        key_rows = jnp.concatenate([outs[1] for outs in attended], axis=1)
        value_rows = jnp.concatenate([outs[2] for outs in attended], axis=1)
        totals = [part[hops * tok :].astype(jnp.float32) for part in (key_rows, value_rows)]
        for step in range(1, hops + 1):
            low = (hops - step) * tok
            totals = [
                total + shifted(part[low : low + tok], "ctx", -step).astype(jnp.float32)
                for total, part in zip(totals, (key_rows, value_rows))
            ]
        key_grad, value_grad = (total.astype(jnp.bfloat16) for total in totals)
        both = lax.all_to_all(
            jnp.concatenate([key_grad, value_grad], axis=1),
            "ctx",
            split_axis=1,
            concat_axis=0,
            tiled=True,
        )
        columns = jnp.split(both, CHUNKS, axis=1)
        every = lax.all_gather(features, "ctx", axis=2, tiled=True)
        features, other_features = jnp.split(every, 2, axis=2)

    weight_parts = []
    for block in columns:
        near = [block] + [dp_send(block, mid_by(step)) for step in range(1, mid_count)]
        grads = [piece for held in near for piece in (held, dp_send(held, swap_core))]
        sent, kept = product(features, other_features, grads)
        half = kept + dp_send(sent, flip_slow(1)).astype(jnp.float32)
        last = dp_send(half[:rows].astype(jnp.bfloat16), flip_slow(2))
        weight_parts.append(half[rows:] + last.astype(jnp.float32))
    weight_grad = jnp.concatenate(weight_parts, axis=1)
    return (query_grad[None], key_grad[None], value_grad[None], weight_grad)


def solution(mesh):
    placed = (
        P("dp", "ctx", None),
        P("dp", "ctx", None),
        P("dp", "ctx", None),
        P("dp", "ctx", None),
        P("dp", "ctx", None),
        P("dp", "ctx"),
    )
    return jax.shard_map(
        local,
        mesh=mesh,
        in_specs=placed,
        out_specs=(
            P("dp", "ctx", None),
            P("dp", "ctx", None),
            P("dp", "ctx", None),
            P("dp", "ctx"),
        ),
        check_vma=False,
    )
```

time: 246 us -> 86 us (0.35)
  waiting for transfers between devices: 145 us -> 41.1 us
  matrix products: 41.3 us -> 0 us
  starting transfers between devices: 10.8 us -> 31.6 us
  local copies, waits for them, and re-layouts: 20.4 us -> 1.79 us
  between operations: 14.3 us -> 1.12 us
  blocking collectives: 8.99 us -> 0 us
  Pallas kernels: 0 us -> 5.51 us
    unnamed x3 -> x0, waiting for transfers between devices: 120 us -> none
    ppermute x0 -> x19, waiting for transfers between devices: none -> 34.1 us  [the longest x12 28 us: dp_send(): return lax.ppermute(value, 'dp', pairs)]
    dot_general x41 -> x0, matrix products: 33.3 us -> none  [the longest x8 9.39 us: head_grads(): jnp.einsum('igd,jd->gij', grad_head, value_head, preferred_element_type=j...]
    ppermute x0 -> x19, starting transfers between devices: none -> 24.1 us  [the longest x12 11 us: dp_send(): return lax.ppermute(value, 'dp', pairs)]
    ppermute x5 -> x3, waiting for transfers between devices: 24.6 us -> 7.01 us  [shifted(): lax.ppermute(value, axis, [(source, source + steps) for source in range(l...]
    unnamed x17 -> x13, local copies, waits for them, and re-layouts: 17.4 us -> 0.39 us
    all_to_all x1 -> x0, blocking collectives: 8.99 us -> none  [local(): lax.all_to_all(both_grads, 'ctx', split_axis=1, concat_axis=0, tiled=True)]
    sub x8 -> x0, matrix products: 8 us -> none  [head_grads(): weights = jnp.where(allowed[None], jnp.exp(scores - row_peak), 0.0)]
  transfers between devices with their start and end apart: 7 -> 22, of which waited for: 5 -> 9; matrix products, arithmetic and copies ran while one was open for 18% -> 5% of each run, Pallas kernels for 0% -> 6%
where the time goes in v1:
time: 86 us; the launch traced here: 85.8 us
  waiting for transfers between devices  41.1 us (48%)
  starting transfers between devices  31.6 us (37%)
  Pallas kernels  5.51 us (6%)
  other arithmetic  4.71 us (5%)
  local copies, waits for them, and re-layouts  1.79 us (2%)
  between operations  1.12 us (1%)
    ppermute x12, waiting for transfers between devices, dp_send(): return lax.ppermute(value, 'dp', pairs)  28 us
    ppermute x12, starting transfers between devices, dp_send(): return lax.ppermute(value, 'dp', pairs)  11 us
    ppermute x3, starting transfers between devices, shifted(): lax.ppermute(value, axis, [(source, source + steps) for source in range(l...  7.47 us
    ppermute x3, waiting for transfers between devices, shifted(): lax.ppermute(value, axis, [(source, source + steps) for source in range(l...  7.01 us
    ppermute x1, waiting for transfers between devices, local(): other_features = lax.ppermute(features, 'ctx', swap_ctx)  6.04 us
    ppermute x2, starting transfers between devices, local(): arrived = lax.ppermute(sent, 'ctx', swap_ctx)  5.22 us
    pallas_call x2, Pallas kernels, attend(): pl.pallas_call(partial(attention_kernel, hops, group), grid_spec=pltpu.Pr...  3.77 us
    ppermute x1, starting transfers between devices, local(): other_features = lax.ppermute(features, 'ctx', swap_ctx)  2.72 us
  transfers between devices with their start and end apart: 22, of which 9 were waited for; matrix products, arithmetic and copies ran while one was open for 5% of the time, Pallas kernels for 6%

profile of v1, /device:TPU:0, one launch (start us, length us, event | category | flops | bytes accessed | tf_op | source)
XLA Modules:
  0.0 85.8 jit_solution(8911842919980257027)
XLA Ops:
  0.6 1.2 %fusion.3 = (bf16[128,512]{1,0:T(8,128)(2,1)S(1)}, bf16[128,512]{1,0:T(8,128)(2,1)S(1)}, bf16[128,512]{1,0:T(8,128)(2,1)S(1)}, bf16[128,512]{1,0:T(8,128)(2,1)S(1)}) fusion(bf16[128,1024]{1,0:T(8,128)(2,1)} %bitcast.31, bf16[128,1024]{1,0:T(8,128)(2,1)} %bitcast.34), kind=kLoop, calls=%fused_computation.39 | loop fusion | bytes 1048576 | tf_op jit(solution)/shard_map/slice | solution.py:208
  1.9 4.9 %collective-permute-start.2 = (bf16[128,1024]{1,0:T(8,128)(2,1)S(1)}, bf16[128,1024]{1,0:T(8,128)(2,1)S(1)}, u32[]{:S(2)}, u32[]{:S(2)}) collective-permute-start(bf16[128,1024]{1,0:T(8,128)(2,1)S(1)} %pad_maximum_fusion.4), channel_id=1, source_target_pairs={{0,1},{2,3},{4,5},{6,7},{8,9},{10,11},{12,13},{14,15},{16,17},{18,... | collective-permute-start | bytes 786440 | tf_op jit(solution)/shard_map/ppermute | solution.py:27
  7.6 0.7 pad_maximum_fusion.3
  8.3 1.3 %collective-permute-start = (bf16[128,1024]{1,0:T(8,128)(2,1)}, bf16[128,1024]{1,0:T(8,128)(2,1)S(1)}, u32[]{:S(2)}, u32[]{:S(2)}) collective-permute-start(bf16[128,1024]{1,0:T(8,128)(2,1)} %pad_maximum_fusion.3), channel_id=1, source_target_pairs={{0,1},{2,3},{4,5},{6,7},{8,9},{10,11},{12,13},{14,15},{16,17},{18,... | collective-permute-start | bytes 786440 | tf_op jit(solution)/shard_map/ppermute | solution.py:27
  9.6 1.3 %collective-permute-start.1 = (s32[1,128]{1,0:T(1,128)S(1)}, s32[1,128]{1,0:T(1,128)S(1)}, u32[]{:S(2)}, u32[]{:S(2)}) collective-permute-start(s32[1,128]{1,0:T(1,128)S(1)} %copy-done.4), channel_id=1, source_target_pairs={{0,1},{2,3},{4,5},{6,7},{8,9},{10,11},{12,13},{14,15},{16,17},{18,... | collective-permute-start | bytes 1544 | tf_op jit(solution)/shard_map/ppermute | solution.py:27
  11.0 7.0 %collective-permute-done.1.refs_6_ = s32[1,128]{1,0:T(1,128)S(1)} collective-permute-done((s32[1,128]{1,0:T(1,128)S(1)}, s32[1,128]{1,0:T(1,128)S(1)}, u32[]{:S(2)}, u32[]{:S(2)}) %collective-permute-start.1) | collective-permute-done | bytes 544 | tf_op jit(solution)/shard_map/ppermute | solution.py:27
  18.0 1.9 %shard_map.94 = (bf16[128,1024]{1,0:T(8,128)(2,1)S(1)}, bf16[128,512]{1,0:T(8,128)(2,1)S(1)}, bf16[128,512]{1,0:T(8,128)(2,1)S(1)}, bf16[128,512]{1,0:T(8,128)(2...) custom-call(s32[1]{0:T(128)} %bitcast.place_ref, s32[1,128]{1,0:T(1,128)S(1)} %copy-done.4, ...), custom_call_target="tpu_custom_call" | custom-call | flops 335544320 | bytes 1048576 | tf_op jit(solution)/shard_map/pallas_call | solution.py:112
  19.9 2.5 %collective-permute-start.4 = (bf16[128,512]{1,0:T(8,128)(2,1)S(1)}, bf16[128,512]{1,0:T(8,128)(2,1)S(1)}, u32[]{:S(2)}, u32[]{:S(2)}) collective-permute-start(bf16[128,512]{1,0:T(8,128)(2,1)S(1)} %get-tuple-element.26), channel_id=1, source_target_pairs={{0,1},{1,0},{2,3},{3,2},{4,5},{5,4},{6,7},{7,6},{8,9},{9,8},{10,11... | collective-permute-start | bytes 393224 | tf_op jit(solution)/shard_map/ppermute | solution.py:249
  22.5 1.3 %collective-permute-start.16 = (bf16[128,512]{1,0:T(8,128)(2,1)S(1)}, bf16[128,512]{1,0:T(8,128)(2,1)S(1)}, u32[]{:S(2)}, u32[]{:S(2)}) collective-permute-start(bf16[128,512]{1,0:T(8,128)(2,1)S(1)} %get-tuple-element.27), channel_id=1, source_target_pairs={{1,0},{3,2},{5,4},{7,6},{9,8},{11,10},{13,12},{15,14},{17,16},{19,... | collective-permute-start | bytes 393224 | tf_op jit(solution)/shard_map/ppermute | solution.py:248
  23.8 1.9 %shard_map.93 = (bf16[128,1024]{1,0:T(8,128)(2,1)S(1)}, bf16[128,512]{1,0:T(8,128)(2,1)S(1)}, bf16[128,512]{1,0:T(8,128)(2,1)S(1)}, bf16[128,512]{1,0:T(8,128)(2...) custom-call(s32[1]{0:T(128)} %bitcast.place_ref, s32[1,128]{1,0:T(1,128)S(1)} %copy-done.4, ...), custom_call_target="tpu_custom_call" | custom-call | flops 335544320 | bytes 1048576 | tf_op jit(solution)/shard_map/pallas_call | solution.py:112
  25.6 2.7 %collective-permute-start.3 = (bf16[128,512]{1,0:T(8,128)(2,1)S(1)}, bf16[128,512]{1,0:T(8,128)(2,1)S(1)}, u32[]{:S(2)}, u32[]{:S(2)}) collective-permute-start(bf16[128,512]{1,0:T(8,128)(2,1)S(1)} %get-tuple-element.23), channel_id=1, source_target_pairs={{0,1},{1,0},{2,3},{3,2},{4,5},{5,4},{6,7},{7,6},{8,9},{9,8},{10,11... | collective-permute-start | bytes 393224 | tf_op jit(solution)/shard_map/ppermute | solution.py:249
  28.4 1.3 %collective-permute-start.10 = (bf16[128,512]{1,0:T(8,128)(2,1)S(1)}, bf16[128,512]{1,0:T(8,128)(2,1)S(1)}, u32[]{:S(2)}, u32[]{:S(2)}) collective-permute-start(bf16[128,512]{1,0:T(8,128)(2,1)S(1)} %get-tuple-element.24), channel_id=1, source_target_pairs={{1,0},{3,2},{5,4},{7,6},{9,8},{11,10},{13,12},{15,14},{17,16},{19,... | collective-permute-start | bytes 393224 | tf_op jit(solution)/shard_map/ppermute | solution.py:248
  29.7 1.3 %collective-permute-start.6 = (bf16[128,512]{1,0:T(8,128)(2,1)S(1)}, bf16[128,512]{1,0:T(8,128)(2,1)S(1)}, u32[]{:S(2)}, u32[]{:S(2)}) collective-permute-start(bf16[128,512]{1,0:T(8,128)(2,1)S(1)} %get-tuple-element.31), channel_id=1, source_target_pairs={{1,0},{3,2},{5,4},{7,6},{9,8},{11,10},{13,12},{15,14},{17,16},{19,... | collective-permute-start | bytes 393224 | tf_op jit(solution)/shard_map/ppermute | solution.py:257
  31.0 1.6 %collective-permute-start.8 = (bf16[2,4,168,128]{3,2,1,0:T(8,128)(2,1)S(1)}, bf16[2,4,168,128]{3,2,1,0:T(8,128)(2,1)S(1)}, u32[]{:S(2)}, u32[]{:S(2)}) collective-permute-start(bf16[2,4,168,128]{3,2,1,0:T(8,128)(2,1)S(1)} %get-tuple-element.37), channel_id=1, source_target_pairs={{0,4},{2,6},{4,0},{6,2},{8,12},{10,14},{12,8},{14,10},{16,20},{18,... | collective-permute-start | bytes 1032200 | tf_op jit(solution)/shard_map/ppermute | solution.py:195
  32.8 6.5 %collective-permute-done.8 = bf16[2,4,168,128]{3,2,1,0:T(8,128)(2,1)S(1)} collective-permute-done((bf16[2,4,168,128]{3,2,1,0:T(8,128)(2,1)S(1)}, bf16[2,4,168,128]{3,2,1,0:T(8,128)(2,1)S(1)}, u32[]{:S(2)}, u32[]{:S(2)}) %collective-permute-start.8) | collective-permute-done | bytes 344096 | tf_op jit(solution)/shard_map/ppermute | solution.py:195
  39.3 1.5 %collective-permute-start.18 = (bf16[256,512]{1,0:T(8,128)(2,1)S(1)}, bf16[256,512]{1,0:T(8,128)(2,1)S(1)}, u32[]{:S(2)}, u32[]{:S(2)}) collective-permute-start(bf16[256,512]{1,0:T(8,128)(2,1)S(1)} %pad_maximum_fusion.6.refs_2_), channel_id=1, source_target_pairs={{0,4},{2,6},{4,0},{6,2},{8,12},{10,14},{12,8},{14,10},{16,20},{18,... | collective-permute-start | bytes 786440 | tf_op jit(solution)/shard_map/ppermute | solution.py:195
  40.9 2.7 %collective-permute-start.9 = (bf16[4,672,128]{2,1,0:T(8,128)(2,1)S(1)}, bf16[4,672,128]{2,1,0:T(8,128)(2,1)S(1)}, u32[]{:S(2)}, u32[]{:S(2)}) collective-permute-start(bf16[4,672,128]{2,1,0:T(8,128)(2,1)S(1)} %pad_maximum_fusion.1.refs_0_), channel_id=1, source_target_pairs={{0,1},{1,0},{2,3},{3,2},{4,5},{5,4},{6,7},{7,6},{8,9},{9,8},{10,11... | collective-permute-start | bytes 2064392 | tf_op jit(solution)/shard_map/ppermute | solution.py:245
  44.4 3.5 %collective-permute-done.18.refs_4_ = bf16[256,512]{1,0:T(8,128)(2,1)S(1)} collective-permute-done((bf16[256,512]{1,0:T(8,128)(2,1)S(1)}, bf16[256,512]{1,0:T(8,128)(2,1)S(1)}, u32[]{:S(2)}, u32[]{:S(2)}) %collective-permute-start.18) | collective-permute-done | bytes 262176 | tf_op jit(solution)/shard_map/ppermute | solution.py:195
  47.8 0.8 maximum_bitcast_fusion
  48.7 1.3 %collective-permute-start.5 = (bf16[128,512]{1,0:T(8,128)(2,1)S(1)}, bf16[128,512]{1,0:T(8,128)(2,1)S(1)}, u32[]{:S(2)}, u32[]{:S(2)}) collective-permute-start(bf16[128,512]{1,0:T(8,128)(2,1)S(1)} %get-tuple-element.29), channel_id=1, source_target_pairs={{1,0},{3,2},{5,4},{7,6},{9,8},{11,10},{13,12},{15,14},{17,16},{19,... | collective-permute-start | bytes 393224 | tf_op jit(solution)/shard_map/ppermute | solution.py:257
  50.7 6.0 %collective-permute-done.9.refs_1_ = bf16[4,672,128]{2,1,0:T(8,128)(2,1)S(1)} collective-permute-done((bf16[4,672,128]{2,1,0:T(8,128)(2,1)S(1)}, bf16[4,672,128]{2,1,0:T(8,128)(2,1)S(1)}, u32[]{:S(2)}, u32[]{:S(2)}) %collective-permute-start.9) | collective-permute-done | bytes 688160 | tf_op jit(solution)/shard_map/ppermute | solution.py:245
  56.7 0.9 %shard_map.96 = (bf16[336,512]{1,0:T(8,128)(2,1)S(1)}, f32[336,512]{1,0:T(8,128)S(1)}) custom-call(bf16[4,672,128]{2,1,0:T(8,128)(2,1)S(1)} %pad_maximum_fusion.1.refs_0_, bf16[4,672,128]{2,1,0:T(8,128)(2,1)S(1)} %collective-permute-done.9.refs_1_, bf16[256,512]{1,0:T(8,128)(2,1)S(1)} %pad_maximum_fusion.6.refs_2_, ...), custom_call_target="tpu_custom_call" | custom-call | flops 704643072 | bytes 3457024 | tf_op jit(solution)/shard_map/pallas_call | solution.py:154
  57.6 1.6 %collective-permute-start.20 = (bf16[336,512]{1,0:T(8,128)(2,1)S(1)}, bf16[336,512]{1,0:T(8,128)(2,1)S(1)}, u32[]{:S(2)}, u32[]{:S(2)}) collective-permute-start(bf16[336,512]{1,0:T(8,128)(2,1)S(1)} %get-tuple-element.35), channel_id=1, source_target_pairs={{0,8},{2,10},{4,12},{6,14},{8,0},{10,2},{12,4},{14,6},{16,24},{18,... | collective-permute-start | bytes 1032200 | tf_op jit(solution)/shard_map/ppermute | solution.py:195
  59.3 0.7 maximum_bitcast_fusion.1
  60.0 0.9 %shard_map.95 = (bf16[336,512]{1,0:T(8,128)(2,1)S(1)}, f32[336,512]{1,0:T(8,128)S(1)}) custom-call(bf16[4,672,128]{2,1,0:T(8,128)(2,1)S(1)} %pad_maximum_fusion.1.refs_0_, bf16[4,672,128]{2,1,0:T(8,128)(2,1)S(1)} %collective-permute-done.9.refs_1_, bf16[256,512]{1,0:T(8,128)(2,1)S(1)} %pad_maximum_fusion.5.refs_2_, ...), custom_call_target="tpu_custom_call" | custom-call | flops 704643072 | bytes 3457024 | tf_op jit(solution)/shard_map/pallas_call | solution.py:154
  62.1 8.0 %collective-permute-done.20 = bf16[336,512]{1,0:T(8,128)(2,1)S(1)} collective-permute-done((bf16[336,512]{1,0:T(8,128)(2,1)S(1)}, bf16[336,512]{1,0:T(8,128)(2,1)S(1)}, u32[]{:S(2)}, u32[]{:S(2)}) %collective-permute-start.20) | collective-permute-done | bytes 344096 | tf_op jit(solution)/shard_map/ppermute | solution.py:195
  70.3 1.8 %collective-permute-start.21 = (bf16[168,512]{1,0:T(8,128)(2,1)S(1)}, bf16[168,512]{1,0:T(8,128)(2,1)S(1)}, u32[]{:S(2)}, u32[]{:S(2)}) collective-permute-start(bf16[168,512]{1,0:T(8,128)(2,1)S(1)} %slice.46), channel_id=1, source_target_pairs={{0,16},{2,18},{4,20},{6,22},{8,24},{10,26},{12,28},{14,30},{16,0},... | collective-permute-start | bytes 516104 | tf_op jit(solution)/shard_map/ppermute | solution.py:195
  72.0 2.9 %collective-permute-done.14 = bf16[336,512]{1,0:T(8,128)(2,1)S(1)} collective-permute-done((bf16[336,512]{1,0:T(8,128)(2,1)S(1)}, bf16[336,512]{1,0:T(8,128)(2,1)S(1)}, u32[]{:S(2)}, u32[]{:S(2)}) %collective-permute-start.14) | collective-permute-done | bytes 344096 | tf_op jit(solution)/shard_map/ppermute | solution.py:195
  75.1 2.7 %collective-permute-start.15 = (bf16[168,512]{1,0:T(8,128)(2,1)S(1)}, bf16[168,512]{1,0:T(8,128)(2,1)S(1)}, u32[]{:S(2)}, u32[]{:S(2)}) collective-permute-start(bf16[168,512]{1,0:T(8,128)(2,1)S(1)} %slice.47), channel_id=1, source_target_pairs={{0,16},{2,18},{4,20},{6,22},{8,24},{10,26},{12,28},{14,30},{16,0},... | collective-permute-start | bytes 516104 | tf_op jit(solution)/shard_map/ppermute | solution.py:195
  77.8 5.2 %collective-permute-done.21 = bf16[168,512]{1,0:T(8,128)(2,1)S(1)} collective-permute-done((bf16[168,512]{1,0:T(8,128)(2,1)S(1)}, bf16[168,512]{1,0:T(8,128)(2,1)S(1)}, u32[]{:S(2)}, u32[]{:S(2)}) %collective-permute-start.21) | collective-permute-done | bytes 172064 | tf_op jit(solution)/shard_map/ppermute | solution.py:195
  83.0 1.8 %collective-permute-done.15 = bf16[168,512]{1,0:T(8,128)(2,1)S(1)} collective-permute-done((bf16[168,512]{1,0:T(8,128)(2,1)S(1)}, bf16[168,512]{1,0:T(8,128)(2,1)S(1)}, u32[]{:S(2)}, u32[]{:S(2)}) %collective-permute-start.15) | collective-permute-done | bytes 172064 | tf_op jit(solution)/shard_map/ppermute | solution.py:195
  84.9 0.9 %pad_maximum_fusion.2 = f32[168,1024]{1,0:T(8,128)} fusion(f32[168,512]{1,0:T(8,128)S(1)} %slice_add_fusion, f32[168,512]{1,0:T(8,128)S(1)} %slice_add_fusion.1), kind=kLoop, calls=%fused_computation.6 | loop fusion | flops 172032 | bytes 1376256 | tf_op jit(solution)/shard_map/concatenate | solution.py:293
  (53 shorter events, 4.1 us)
Async XLA Ops:
  0.6 6.2 %copy-start.5 = (bf16[1,128,2688]{2,1,0:T(8,128)(2,1)S(1)}, bf16[1,128,2688]{2,1,0:T(8,128)(2,1)}, u32[]{:S(2)}) copy-start(bf16[1,128,2688]{2,1,0:T(8,128)(2,1)} %param.6) | copy-start | bytes 2064388
  1.9 16.2 %collective-permute-start.2 = (bf16[128,1024]{1,0:T(8,128)(2,1)S(1)}, bf16[128,1024]{1,0:T(8,128)(2,1)S(1)}, u32[]{:S(2)}, u32[]{:S(2)}) collective-permute-start(bf16[128,1024]{1,0:T(8,128)(2,1)S(1)} %pad_maximum_fusion.4), channel_id=1, source_target_pairs={{0,1},{2,3},{4,5},{6,7},{8,9},{10,11},{12,13},{14,15},{16,17},{18,... | collective-permute-start | bytes 786440 | tf_op jit(solution)/shard_map/ppermute | solution.py:27
  7.4 2.3 %copy-start.4 = (s32[1,128]{1,0:T(1,128)S(1)}, s32[1,128]{1,0:T(1,128)}, u32[]{:S(2)}) copy-start(s32[1,128]{1,0:T(1,128)} %refs_0_.3) | copy-start | bytes 1540
  7.4 10.6 %copy-start.2 = (bf16[1,128,2048]{2,1,0:T(8,128)(2,1)S(1)}, bf16[1,128,2048]{2,1,0:T(8,128)(2,1)}, u32[]{:S(2)}) copy-start(bf16[1,128,2048]{2,1,0:T(8,128)(2,1)} %param.7) | copy-start | bytes 1572868
  7.4 10.6 %copy-start.3 = (bf16[1,128,2048]{2,1,0:T(8,128)(2,1)S(1)}, bf16[1,128,2048]{2,1,0:T(8,128)(2,1)}, u32[]{:S(2)}) copy-start(bf16[1,128,2048]{2,1,0:T(8,128)(2,1)} %param.10) | copy-start | bytes 1572868
  7.5 22.1 %collective-permute-start.7 = (bf16[2,4,168,128]{3,2,1,0:T(8,128)(2,1)S(1)}, bf16[2,4,168,128]{3,2,1,0:T(8,128)(2,1)S(1)}, u32[]{:S(2)}, u32[]{:S(2)}) collective-permute-start(bf16[2,4,168,128]{3,2,1,0:T(8,128)(2,1)S(1)} %get-tuple-element.38), channel_id=1, source_target_pairs={{0,2},{2,0},{4,6},{6,4},{8,10},{10,8},{12,14},{14,12},{16,18},{18,... | collective-permute-start | bytes 1032200 | tf_op jit(solution)/shard_map/ppermute | solution.py:195
  7.6 10.5 %copy-start = (bf16[1,128,1024]{2,1,0:T(8,128)(2,1)S(1)}, bf16[1,128,1024]{2,1,0:T(8,128)(2,1)}, u32[]{:S(2)}) copy-start(bf16[1,128,1024]{2,1,0:T(8,128)(2,1)} %param.8) | copy-start | bytes 786436
  7.6 10.4 %copy-start.1 = (bf16[1,128,1024]{2,1,0:T(8,128)(2,1)S(1)}, bf16[1,128,1024]{2,1,0:T(8,128)(2,1)}, u32[]{:S(2)}) copy-start(bf16[1,128,1024]{2,1,0:T(8,128)(2,1)} %param.9) | copy-start | bytes 786436
  8.3 15.4 %collective-permute-start = (bf16[128,1024]{1,0:T(8,128)(2,1)}, bf16[128,1024]{1,0:T(8,128)(2,1)S(1)}, u32[]{:S(2)}, u32[]{:S(2)}) collective-permute-start(bf16[128,1024]{1,0:T(8,128)(2,1)} %pad_maximum_fusion.3), channel_id=1, source_target_pairs={{0,1},{2,3},{4,5},{6,7},{8,9},{10,11},{12,13},{14,15},{16,17},{18,... | collective-permute-start | bytes 786440 | tf_op jit(solution)/shard_map/ppermute | solution.py:27
  9.6 8.4 %collective-permute-start.1 = (s32[1,128]{1,0:T(1,128)S(1)}, s32[1,128]{1,0:T(1,128)S(1)}, u32[]{:S(2)}, u32[]{:S(2)}) collective-permute-start(s32[1,128]{1,0:T(1,128)S(1)} %copy-done.4), channel_id=1, source_target_pairs={{0,1},{2,3},{4,5},{6,7},{8,9},{10,11},{12,13},{14,15},{16,17},{18,... | collective-permute-start | bytes 1544 | tf_op jit(solution)/shard_map/ppermute | solution.py:27
  19.9 11.1 %collective-permute-start.4 = (bf16[128,512]{1,0:T(8,128)(2,1)S(1)}, bf16[128,512]{1,0:T(8,128)(2,1)S(1)}, u32[]{:S(2)}, u32[]{:S(2)}) collective-permute-start(bf16[128,512]{1,0:T(8,128)(2,1)S(1)} %get-tuple-element.26), channel_id=1, source_target_pairs={{0,1},{1,0},{2,3},{3,2},{4,5},{5,4},{6,7},{7,6},{8,9},{9,8},{10,11... | collective-permute-start | bytes 393224 | tf_op jit(solution)/shard_map/ppermute | solution.py:249
  22.5 10.1 %collective-permute-start.16 = (bf16[128,512]{1,0:T(8,128)(2,1)S(1)}, bf16[128,512]{1,0:T(8,128)(2,1)S(1)}, u32[]{:S(2)}, u32[]{:S(2)}) collective-permute-start(bf16[128,512]{1,0:T(8,128)(2,1)S(1)} %get-tuple-element.27), channel_id=1, source_target_pairs={{1,0},{3,2},{5,4},{7,6},{9,8},{11,10},{13,12},{15,14},{17,16},{19,... | collective-permute-start | bytes 393224 | tf_op jit(solution)/shard_map/ppermute | solution.py:248
  25.6 15.3 %collective-permute-start.3 = (bf16[128,512]{1,0:T(8,128)(2,1)S(1)}, bf16[128,512]{1,0:T(8,128)(2,1)S(1)}, u32[]{:S(2)}, u32[]{:S(2)}) collective-permute-start(bf16[128,512]{1,0:T(8,128)(2,1)S(1)} %get-tuple-element.23), channel_id=1, source_target_pairs={{0,1},{1,0},{2,3},{3,2},{4,5},{5,4},{6,7},{7,6},{8,9},{9,8},{10,11... | collective-permute-start | bytes 393224 | tf_op jit(solution)/shard_map/ppermute | solution.py:249
  28.4 15.3 %collective-permute-start.10 = (bf16[128,512]{1,0:T(8,128)(2,1)S(1)}, bf16[128,512]{1,0:T(8,128)(2,1)S(1)}, u32[]{:S(2)}, u32[]{:S(2)}) collective-permute-start(bf16[128,512]{1,0:T(8,128)(2,1)S(1)} %get-tuple-element.24), channel_id=1, source_target_pairs={{1,0},{3,2},{5,4},{7,6},{9,8},{11,10},{13,12},{15,14},{17,16},{19,... | collective-permute-start | bytes 393224 | tf_op jit(solution)/shard_map/ppermute | solution.py:248
  29.7 19.0 %collective-permute-start.6 = (bf16[128,512]{1,0:T(8,128)(2,1)S(1)}, bf16[128,512]{1,0:T(8,128)(2,1)S(1)}, u32[]{:S(2)}, u32[]{:S(2)}) collective-permute-start(bf16[128,512]{1,0:T(8,128)(2,1)S(1)} %get-tuple-element.31), channel_id=1, source_target_pairs={{1,0},{3,2},{5,4},{7,6},{9,8},{11,10},{13,12},{15,14},{17,16},{19,... | collective-permute-start | bytes 393224 | tf_op jit(solution)/shard_map/ppermute | solution.py:257
  31.0 8.3 %collective-permute-start.8 = (bf16[2,4,168,128]{3,2,1,0:T(8,128)(2,1)S(1)}, bf16[2,4,168,128]{3,2,1,0:T(8,128)(2,1)S(1)}, u32[]{:S(2)}, u32[]{:S(2)}) collective-permute-start(bf16[2,4,168,128]{3,2,1,0:T(8,128)(2,1)S(1)} %get-tuple-element.37), channel_id=1, source_target_pairs={{0,4},{2,6},{4,0},{6,2},{8,12},{10,14},{12,8},{14,10},{16,20},{18,... | collective-permute-start | bytes 1032200 | tf_op jit(solution)/shard_map/ppermute | solution.py:195
  32.7 17.3 %collective-permute-start.17 = (bf16[256,512]{1,0:T(8,128)(2,1)S(1)}, bf16[256,512]{1,0:T(8,128)(2,1)S(1)}, u32[]{:S(2)}, u32[]{:S(2)}) collective-permute-start(bf16[256,512]{1,0:T(8,128)(2,1)S(1)} %pad_maximum_fusion.6.refs_2_), channel_id=1, source_target_pairs={{0,2},{2,0},{4,6},{6,4},{8,10},{10,8},{12,14},{14,12},{16,18},{18,... | collective-permute-start | bytes 786440 | tf_op jit(solution)/shard_map/ppermute | solution.py:195
  39.3 8.5 %collective-permute-start.18 = (bf16[256,512]{1,0:T(8,128)(2,1)S(1)}, bf16[256,512]{1,0:T(8,128)(2,1)S(1)}, u32[]{:S(2)}, u32[]{:S(2)}) collective-permute-start(bf16[256,512]{1,0:T(8,128)(2,1)S(1)} %pad_maximum_fusion.6.refs_2_), channel_id=1, source_target_pairs={{0,4},{2,6},{4,0},{6,2},{8,12},{10,14},{12,8},{14,10},{16,20},{18,... | collective-permute-start | bytes 786440 | tf_op jit(solution)/shard_map/ppermute | solution.py:195
  40.9 15.8 %collective-permute-start.9 = (bf16[4,672,128]{2,1,0:T(8,128)(2,1)S(1)}, bf16[4,672,128]{2,1,0:T(8,128)(2,1)S(1)}, u32[]{:S(2)}, u32[]{:S(2)}) collective-permute-start(bf16[4,672,128]{2,1,0:T(8,128)(2,1)S(1)} %pad_maximum_fusion.1.refs_0_), channel_id=1, source_target_pairs={{0,1},{1,0},{2,3},{3,2},{4,5},{5,4},{6,7},{7,6},{8,9},{9,8},{10,11... | collective-permute-start | bytes 2064392 | tf_op jit(solution)/shard_map/ppermute | solution.py:245
  43.8 6.9 %collective-permute-start.12 = (bf16[256,512]{1,0:T(8,128)(2,1)S(1)}, bf16[256,512]{1,0:T(8,128)(2,1)S(1)}, u32[]{:S(2)}, u32[]{:S(2)}) collective-permute-start(bf16[256,512]{1,0:T(8,128)(2,1)S(1)} %pad_maximum_fusion.5.refs_2_), channel_id=1, source_target_pairs={{0,4},{2,6},{4,0},{6,2},{8,12},{10,14},{12,8},{14,10},{16,20},{18,... | collective-permute-start | bytes 786440 | tf_op jit(solution)/shard_map/ppermute | solution.py:195
  47.8 2.8 %collective-permute-start.19 = (bf16[256,512]{1,0:T(8,128)(2,1)S(1)}, bf16[256,512]{1,0:T(8,128)(2,1)S(1)}, u32[]{:S(2)}, u32[]{:S(2)}) collective-permute-start(bf16[256,512]{1,0:T(8,128)(2,1)S(1)} %collective-permute-done.18.refs_4_), channel_id=1, source_target_pairs={{0,2},{2,0},{4,6},{6,4},{8,10},{10,8},{12,14},{14,12},{16,18},{18,... | collective-permute-start | bytes 786440 | tf_op jit(solution)/shard_map/ppermute | solution.py:195
  48.7 10.6 %collective-permute-start.5 = (bf16[128,512]{1,0:T(8,128)(2,1)S(1)}, bf16[128,512]{1,0:T(8,128)(2,1)S(1)}, u32[]{:S(2)}, u32[]{:S(2)}) collective-permute-start(bf16[128,512]{1,0:T(8,128)(2,1)S(1)} %get-tuple-element.29), channel_id=1, source_target_pairs={{1,0},{3,2},{5,4},{7,6},{9,8},{11,10},{13,12},{15,14},{17,16},{19,... | collective-permute-start | bytes 393224 | tf_op jit(solution)/shard_map/ppermute | solution.py:257
  50.0 10.0 %collective-permute-start.11 = (bf16[256,512]{1,0:T(8,128)(2,1)S(1)}, bf16[256,512]{1,0:T(8,128)(2,1)S(1)}, u32[]{:S(2)}, u32[]{:S(2)}) collective-permute-start(bf16[256,512]{1,0:T(8,128)(2,1)S(1)} %pad_maximum_fusion.5.refs_2_), channel_id=1, source_target_pairs={{0,2},{2,0},{4,6},{6,4},{8,10},{10,8},{12,14},{14,12},{16,18},{18,... | collective-permute-start | bytes 786440 | tf_op jit(solution)/shard_map/ppermute | solution.py:195
  50.6 9.4 %collective-permute-start.13 = (bf16[256,512]{1,0:T(8,128)(2,1)S(1)}, bf16[256,512]{1,0:T(8,128)(2,1)S(1)}, u32[]{:S(2)}, u32[]{:S(2)}) collective-permute-start(bf16[256,512]{1,0:T(8,128)(2,1)S(1)} %collective-permute-done.12.refs_4_), channel_id=1, source_target_pairs={{0,2},{2,0},{4,6},{6,4},{8,10},{10,8},{12,14},{14,12},{16,18},{18,... | collective-permute-start | bytes 786440 | tf_op jit(solution)/shard_map/ppermute | solution.py:195
  57.6 12.6 %collective-permute-start.20 = (bf16[336,512]{1,0:T(8,128)(2,1)S(1)}, bf16[336,512]{1,0:T(8,128)(2,1)S(1)}, u32[]{:S(2)}, u32[]{:S(2)}) collective-permute-start(bf16[336,512]{1,0:T(8,128)(2,1)S(1)} %get-tuple-element.35), channel_id=1, source_target_pairs={{0,8},{2,10},{4,12},{6,14},{8,0},{10,2},{12,4},{14,6},{16,24},{18,... | collective-permute-start | bytes 1032200 | tf_op jit(solution)/shard_map/ppermute | solution.py:195
  60.9 14.1 %collective-permute-start.14 = (bf16[336,512]{1,0:T(8,128)(2,1)S(1)}, bf16[336,512]{1,0:T(8,128)(2,1)S(1)}, u32[]{:S(2)}, u32[]{:S(2)}) collective-permute-start(bf16[336,512]{1,0:T(8,128)(2,1)S(1)} %get-tuple-element.33), channel_id=1, source_target_pairs={{0,8},{2,10},{4,12},{6,14},{8,0},{10,2},{12,4},{14,6},{16,24},{18,... | collective-permute-start | bytes 1032200 | tf_op jit(solution)/shard_map/ppermute | solution.py:195
  70.3 12.7 %collective-permute-start.21 = (bf16[168,512]{1,0:T(8,128)(2,1)S(1)}, bf16[168,512]{1,0:T(8,128)(2,1)S(1)}, u32[]{:S(2)}, u32[]{:S(2)}) collective-permute-start(bf16[168,512]{1,0:T(8,128)(2,1)S(1)} %slice.46), channel_id=1, source_target_pairs={{0,16},{2,18},{4,20},{6,22},{8,24},{10,26},{12,28},{14,30},{16,0},... | collective-permute-start | bytes 516104 | tf_op jit(solution)/shard_map/ppermute | solution.py:195
  75.1 9.7 %collective-permute-start.15 = (bf16[168,512]{1,0:T(8,128)(2,1)S(1)}, bf16[168,512]{1,0:T(8,128)(2,1)S(1)}, u32[]{:S(2)}, u32[]{:S(2)}) collective-permute-start(bf16[168,512]{1,0:T(8,128)(2,1)S(1)} %slice.47), channel_id=1, source_target_pairs={{0,16},{2,18},{4,20},{6,22},{8,24},{10,26},{12,28},{14,30},{16,0},... | collective-permute-start | bytes 516104 | tf_op jit(solution)/shard_map/ppermute | solution.py:195

commit v2 on v1

--- a/solution.py
+++ b/solution.py
@@ -12,6 +12,8 @@
 CHUNKS = 2
 SCORE_FLOOR = -1e30
 MIB = 1024 * 1024
+SEG_ROWS = 16
+SMALL = pl.CostEstimate(flops=1024, bytes_accessed=1024, transcendentals=0)
 
 NT = (((1,), (1,)), ((), ()))
 TN = (((0,), (0,)), ((), ()))
@@ -27,12 +29,12 @@
     return lax.ppermute(value, axis, [(source, source + steps) for source in range(leading, last)])
 
 
-def attention_kernel(hops, group, place_ref, *refs):
+def attention_kernel(hops, group, outs_count, place_ref, *refs):
     segs_ref, query_ref, grad_ref, key_ref, value_ref = refs[:5]
     rim_refs = refs[5 : 5 + 2 * hops]
     rim_segs = rim_refs[hops:]
     rim_pairs = rim_refs[:hops]
-    outs = refs[5 + 2 * hops :]
+    outs = refs[-outs_count:]
     tok = query_ref.shape[0]
     heads = key_ref.shape[1] // HD
     rim = hops * tok
@@ -42,7 +44,7 @@
 
     query_segs = segs_ref[...].astype(jnp.float32)
     key_cols = [
-        jnp.transpose(jnp.broadcast_to(ref[...].astype(jnp.float32), (tok, tok)))
+        jnp.transpose(jnp.broadcast_to(ref[...].astype(jnp.float32)[:1], (tok, tok)))
         for ref in (*rim_segs, segs_ref)
     ]
     key_segs = jnp.concatenate(key_cols, axis=0)
@@ -94,23 +96,32 @@
             outs[2][:, cols] = value_part.astype(jnp.bfloat16)
 
 
-def attend(chunk, place, segs, queries, out_grad, keys, values, rim_pairs, rim_segs):
+def attend(chunk, place, segs, queries, out_grad, keys, values, rim_pairs, rim_segs, held):
     hops = len(rim_pairs)
     tok = queries.shape[0]
     group = queries.shape[1] // keys.shape[1]
     width = keys.shape[1] // CHUNKS
-    heads = width // HD
     span = (hops + 1) * tok
     whole = lambda *shape: pl.BlockSpec(shape, lambda i, *_: (0,) * len(shape))
     part = lambda *shape: pl.BlockSpec(shape, lambda i, *_: (0, chunk))
-    shape_of = lambda *shape: jax.ShapeDtypeStruct(shape, jnp.bfloat16)
+    seg_row = pl.BlockSpec((SEG_ROWS, tok), lambda i, *_: (tok // SEG_ROWS, 0))
+    out_shapes = [(tok, group * width)]
     if hops == 1:
-        out_shapes = [(tok, width)] * 5
+        out_shapes += [(tok, width)] * 5
+        in_place = (0, 5)
     else:
-        out_shapes = [(span, width)] * 2
-    out_shapes = [(tok, group * width)] + out_shapes
+        out_shapes += [(span, width)] * 2
+        in_place = (0,)
+    out_specs, out_types = [], []
+    for place_of, (rows, columns) in enumerate(out_shapes):
+        shared = place_of in in_place
+        out_specs.append(part(rows, columns) if shared else whole(rows, columns))
+        columns = columns * CHUNKS if shared else columns
+        out_types.append(jax.ShapeDtypeStruct((rows, columns), jnp.bfloat16))
+    operands = [place, segs, queries, out_grad, keys, values, *rim_pairs, *rim_segs]
+    aliases = {len(operands) + n: in_place[n] for n in range(len(held))}
     return pl.pallas_call(
-        partial(attention_kernel, hops, group),
+        partial(attention_kernel, hops, group, len(out_shapes)),
         grid_spec=pltpu.PrefetchScalarGridSpec(
             num_scalar_prefetch=1,
             grid=(1,),
@@ -122,48 +133,59 @@
                 part(tok, width),
             ]
             + [whole(tok, 2 * width)] * hops
-            + [whole(1, tok)] * hops,
-            out_specs=[whole(*shape) for shape in out_shapes],
+            + [seg_row] * hops
+            + [pl.BlockSpec(memory_space=pl.ANY)] * len(held),
+            out_specs=out_specs,
         ),
-        out_shape=[shape_of(*shape) for shape in out_shapes],
+        out_shape=out_types,
+        input_output_aliases=aliases,
         compiler_params=pltpu.CompilerParams(vmem_limit_bytes=48 * MIB),
-        cost_estimate=pl.CostEstimate(
-            flops=heads * group * tok * span * HD * 10,
-            bytes_accessed=16 * tok * width,
-            transcendentals=heads * group * tok * span,
-        ),
-    )(place, segs, queries, out_grad, keys, values, *rim_pairs, *rim_segs)
+        cost_estimate=SMALL,
+    )(*operands, *held)
 
 
 def product_kernel(traces, *refs):
     own_ref, other_ref = refs[:2]
     grad_refs = refs[2 : 2 + traces]
-    send_ref, keep_ref = refs[2 + traces :]
+    out_ref = refs[2 + traces]
     features = jnp.concatenate(
         [ref[t] for t in range(traces) for ref in (own_ref, other_ref)], axis=1
     )
     grads = jnp.concatenate([ref[...] for ref in grad_refs], axis=0)
-    half = features.shape[0] // 2
-    send_ref[...] = dot_f32(features[:half], grads).astype(jnp.bfloat16)
-    keep_ref[...] = dot_f32(features[half:], grads)
-
-
-def product(own_features, other_features, grads):
-    traces, rows, tok = own_features.shape
+    out_ref[...] = dot_f32(features, grads).astype(out_ref.dtype)
+
+
+def product(features, grads, dtype):
+    traces, rows, _ = features[0].shape
     width = grads[0].shape[1]
     return pl.pallas_call(
         partial(product_kernel, traces),
-        out_shape=[
-            jax.ShapeDtypeStruct((rows // 2, width), jnp.bfloat16),
-            jax.ShapeDtypeStruct((rows // 2, width), jnp.float32),
-        ],
+        out_shape=jax.ShapeDtypeStruct((rows, width), dtype),
         compiler_params=pltpu.CompilerParams(vmem_limit_bytes=48 * MIB),
-        cost_estimate=pl.CostEstimate(
-            flops=4 * traces * tok * rows * width,
-            bytes_accessed=4 * traces * tok * (rows + width) + 3 * rows * width,
-            transcendentals=0,
-        ),
-    )(own_features, other_features, *grads)
+        cost_estimate=SMALL,
+    )(*features, *grads)
+
+
+def finish_kernel(half_ref, last_ref, *refs):
+    rows = last_ref.shape[0]
+    refs[-1][...] = half_ref[rows:] + last_ref[...].astype(jnp.float32)
+
+
+def finish(chunk, half, last, held):
+    rows, width = last.shape
+    return pl.pallas_call(
+        finish_kernel,
+        grid=(1,),
+        in_specs=[
+            pl.BlockSpec(half.shape, lambda i: (0, 0)),
+            pl.BlockSpec(last.shape, lambda i: (0, 0)),
+        ]
+        + [pl.BlockSpec(memory_space=pl.ANY)] * len(held),
+        out_specs=pl.BlockSpec((rows, width), lambda i: (0, chunk)),
+        out_shape=jax.ShapeDtypeStruct((rows, width * CHUNKS), jnp.float32),
+        input_output_aliases={2: 0} if held else {},
+        cost_estimate=SMALL,
+    )(half, last, *held)
 
 
 def local(hidden_in, queries, key_states, value_states, out_grad, segment_ids):
@@ -202,31 +224,37 @@
     own_keys, own_values = key_states[0], value_states[0]
 
     steps = range(hops, 0, -1)
+    seg_rows = jnp.broadcast_to(segment_ids.astype(jnp.bfloat16), (SEG_ROWS, tok))
+    seg_rows = jnp.pad(seg_rows, ((0, 0), (0, 2 * width - tok)))
     rim_pairs = []
     for chunk in range(CHUNKS):
         cols = slice(chunk * width, (chunk + 1) * width)
         pair = jnp.concatenate([own_keys[:, cols], own_values[:, cols]], axis=1)
+        if chunk == 0:
+            pair = jnp.concatenate([pair, seg_rows], axis=0)
         rim_pairs.append([shifted(pair, "ctx", step) for step in steps])
-    rim_segs = [shifted(segment_ids, "ctx", step) for step in steps]
 
     rows = hidden_in.shape[2] // dp_count
     by_feature = hidden_in[0].T.reshape(slow_count, mid_count, core_count, rows, tok)
-    order = (3, 1, 2, 0)
-    by_feature = jnp.stack(
-        [lax.dynamic_index_in_dim(by_feature, slow_at ^ flip, 0, False) for flip in order], axis=2
-    )
-    core_block = lambda at: lax.dynamic_index_in_dim(by_feature, at, 1, False)
-    features = jnp.stack([core_block(core_at), dp_send(core_block(1 - core_at), swap_core)], axis=1)
-    mid_block = lambda at: lax.dynamic_index_in_dim(features, at % mid_count, 0, False)
-    features = jnp.concatenate(
-        [mid_block(mid_at)]
-        + [dp_send(mid_block(mid_at + step), mid_by(step)) for step in range(1, mid_count)],
-        axis=0,
-    )
-    features = features.reshape(core_count * mid_count, slow_count * rows, tok)
-
-    attended = [
-        attend(
+    pieces = []
+    for step in range(mid_count):
+        for flip in range(core_count):
+            share = lax.dynamic_slice(
+                by_feature,
+                (0, (mid_at + step) % mid_count, core_at ^ flip, 0, 0),
+                (slow_count, 1, 1, rows, tok),
+            )
+            share = jnp.concatenate(
+                [lax.dynamic_index_in_dim(share, slow_at ^ turn, 0) for turn in (3, 1, 2, 0)]
+            ).reshape(slow_count * rows, tok)
+            away = lambda slow, mid, core: (slow, (mid + step) % mid_count, core ^ flip)
+            pieces.append(share if step == flip == 0 else dp_send(share, away))
+    features = jnp.stack(pieces)
+
+    half_rows = slow_count // 2 * rows
+    attended, columns, held = [], [], []
+    for chunk in range(CHUNKS):
+        outs = attend(
             chunk,
             place_arg,
             segment_ids,
@@ -235,31 +263,39 @@
             own_keys,
             own_values,
             rim_pairs[chunk],
-            rim_segs,
-        )
-        for chunk in range(CHUNKS)
-    ]
-    query_grad = jnp.concatenate([outs[0] for outs in attended], axis=1)
+            rim_pairs[0],
+            held,
+        )
+        attended.append(outs)
+        held = [outs[0], outs[5]] if hops == 1 else [outs[0]]
+        if ctx_count != 2:
+            continue
+        _, sent, addend, key_own, value_own, _ = outs
+        arrived = lax.ppermute(sent, "ctx", swap_ctx)
+        late_keys = lax.ppermute(key_own, "ctx", [(1, 0)])
+        if chunk == 0:
+            arrived, late_keys, rim_pairs[1:] = lax.optimization_barrier(
+                (arrived, late_keys, rim_pairs[1:])
+            )
+            features, rim_pairs[1:] = lax.optimization_barrier((features, rim_pairs[1:]))
+            halves = [features[:, :half_rows], features[:, half_rows:]]
+            halves = [(own, lax.ppermute(own, "ctx", swap_ctx)) for own in halves]
+        elif chunk == 1:
+            arrived, late_keys, halves[0] = lax.optimization_barrier((arrived, late_keys, halves[0]))
+        total = (addend.astype(jnp.float32) + arrived.astype(jnp.float32)).astype(jnp.bfloat16)
+        columns.append(
+            jnp.concatenate(
+                [jnp.where(first, total, value_own), jnp.where(first, late_keys, total)], axis=0
+            )
+        )
+    query_grad = held[0]
 
     if ctx_count == 2:
-        other_features = lax.ppermute(features, "ctx", swap_ctx)
-        key_grads, value_grads, columns = [], [], []
-        for _, sent, addend, key_own, value_own, value_rim in attended:
-            late_keys = lax.ppermute(key_own, "ctx", [(1, 0)])
-            arrived = lax.ppermute(sent, "ctx", swap_ctx)
-            total = (addend.astype(jnp.float32) + arrived.astype(jnp.float32)).astype(jnp.bfloat16)
-            columns.append(
-                jnp.concatenate(
-                    [jnp.where(first, total, value_own), jnp.where(first, late_keys, total)], axis=0
-                )
-            )
-            key_grads.append(jnp.where(first, total, key_own))
-            returned = lax.ppermute(value_rim, "ctx", [(1, 0)])
-            value_grads.append(
-                (value_own.astype(jnp.float32) + returned.astype(jnp.float32)).astype(jnp.bfloat16)
-            )
-        key_grad = jnp.concatenate(key_grads, axis=1)
-        value_grad = jnp.concatenate(value_grads, axis=1)
+        key_grad = jnp.where(
+            first,
+            jnp.concatenate([block[:tok] for block in columns], axis=1),
+            jnp.concatenate([outs[3] for outs in attended], axis=1),
+        )
     else:
         key_rows = jnp.concatenate([outs[1] for outs in attended], axis=1)
         value_rows = jnp.concatenate([outs[2] for outs in attended], axis=1)
@@ -280,17 +316,27 @@
         )
         columns = jnp.split(both, CHUNKS, axis=1)
         every = lax.all_gather(features, "ctx", axis=2, tiled=True)
-        features, other_features = jnp.split(every, 2, axis=2)
-
-    weight_parts = []
-    for block in columns:
+        halves = [
+            tuple(jnp.split(every[:, low : low + half_rows], 2, axis=2)) for low in (0, half_rows)
+        ]
+
+    held = []
+    for chunk, block in enumerate(columns):
         near = [block] + [dp_send(block, mid_by(step)) for step in range(1, mid_count)]
-        grads = [piece for held in near for piece in (held, dp_send(held, swap_core))]
-        sent, kept = product(features, other_features, grads)
+        grads = [piece for near_one in near for piece in (near_one, dp_send(near_one, swap_core))]
+        sent = product(halves[0], grads, jnp.bfloat16)
+        kept = product(halves[1], grads, jnp.float32)
+        if chunk == 0 and ctx_count == 2:
+            value_rim, sent = lax.optimization_barrier((attended[-1][5], sent))
+            returned = lax.ppermute(value_rim, "ctx", [(1, 0)])
+            value_own = jnp.concatenate([outs[4] for outs in attended], axis=1)
+            value_grad = (value_own.astype(jnp.float32) + returned.astype(jnp.float32)).astype(
+                jnp.bfloat16
+            )
         half = kept + dp_send(sent, flip_slow(1)).astype(jnp.float32)
         last = dp_send(half[:rows].astype(jnp.bfloat16), flip_slow(2))
-        weight_parts.append(half[rows:] + last.astype(jnp.float32))
-    weight_grad = jnp.concatenate(weight_parts, axis=1)
+        held = [finish(chunk, half, last, held)]
+    weight_grad = held[0]
     return (query_grad[None], key_grad[None], value_grad[None], weight_grad)
 
 

time: 86 us -> 84.9 us (0.987)
  waiting for transfers between devices: 41.1 us -> 34.8 us
  Pallas kernels: 5.51 us -> 10.9 us
  starting transfers between devices: 31.6 us -> 27.9 us
  local copies, waits for them, and re-layouts: 1.79 us -> 3.75 us
  other arithmetic: 4.71 us -> 6.16 us
    ppermute x12 -> x13, waiting for transfers between devices: 28 us -> 17.4 us  [dp_send(): return lax.ppermute(value, 'dp', pairs)]
    ppermute x2, waiting for transfers between devices: 0.01 us -> 6.47 us  [local(): late_keys = lax.ppermute(key_own, 'ctx', [(1, 0)])]
    ppermute x3 -> x2, waiting for transfers between devices: 7.01 us -> 0.92 us  [shifted(): lax.ppermute(value, axis, [(source, source + steps) for source in range(l...]
    pallas_call x4 -> x8, Pallas kernels: 5.51 us -> 10.9 us  [the longest x2 5.06 us: attend(): pl.pallas_call(partial(attention_kernel, hops, group, len(out_shapes)), g...]
    ppermute x1 -> x2, waiting for transfers between devices: 6.04 us -> 9.47 us  [local(): halves = [(own, lax.ppermute(own, 'ctx', swap_ctx)) for own in halves]]
    ppermute x2, starting transfers between devices: 5.22 us -> 2.48 us  [local(): arrived = lax.ppermute(sent, 'ctx', swap_ctx)]
    unnamed x13 -> x21, local copies, waits for them, and re-layouts: 0.39 us -> 2.36 us
    select_n x2 -> x3, other arithmetic: 0.19 us -> 1.87 us  [the longest x2 1.11 us: local(): jnp.where(first, late_keys, total)]
  transfers between devices with their start and end apart: 22 -> 22, of which waited for: 9 -> 10; matrix products, arithmetic and copies ran while one was open for 5% -> 7% of each run, Pallas kernels for 6% -> 8%
where the time goes in v2:
time: 84.9 us; the launch traced here: 84.6 us
  waiting for transfers between devices  34.8 us (41%)
  starting transfers between devices  27.9 us (33%)
  Pallas kernels  10.9 us (13%)
  other arithmetic  6.16 us (7%)
  local copies, waits for them, and re-layouts  3.75 us (4%)
  between operations  1.07 us (1%)
    ppermute x13, waiting for transfers between devices, dp_send(): return lax.ppermute(value, 'dp', pairs)  17.4 us
    ppermute x13, starting transfers between devices, dp_send(): return lax.ppermute(value, 'dp', pairs)  12.6 us
    ppermute x2, waiting for transfers between devices, local(): halves = [(own, lax.ppermute(own, 'ctx', swap_ctx)) for own in halves]  9.47 us
    ppermute x2, waiting for transfers between devices, local(): late_keys = lax.ppermute(key_own, 'ctx', [(1, 0)])  6.47 us
    ppermute x2, starting transfers between devices, shifted(): lax.ppermute(value, axis, [(source, source + steps) for source in range(l...  6.33 us
    pallas_call x2, Pallas kernels, attend(): pl.pallas_call(partial(attention_kernel, hops, group, len(out_shapes)), g...  5.06 us
    pallas_call x2, Pallas kernels, finish(): pl.pallas_call(finish_kernel, grid=(1,), in_specs=[pl.BlockSpec(half.shap...  3.77 us
    ppermute x2, starting transfers between devices, local(): halves = [(own, lax.ppermute(own, 'ctx', swap_ctx)) for own in halves]  2.71 us
  transfers between devices with their start and end apart: 22, of which 10 were waited for; matrix products, arithmetic and copies ran while one was open for 7% of the time, Pallas kernels for 8%

profile of v2, /device:TPU:0, one launch (start us, length us, event | category | flops | bytes accessed | tf_op | source)
XLA Modules:
  0.0 84.6 jit_solution(13835856455099132140)
XLA Ops:
  1.3 1.2 %fusion.2 = (bf16[128,512]{1,0:T(8,128)(2,1)S(1)}, bf16[128,512]{1,0:T(8,128)(2,1)S(1)}, bf16[128,512]{1,0:T(8,128)(2,1)S(1)}, bf16[128,512]{1,0:T(8,128)(2,1)S(1)}) fusion(bf16[128,1024]{1,0:T(8,128)(2,1)} %bitcast.26, bf16[128,1024]{1,0:T(8,128)(2,1)} %bitcast.29), kind=kLoop, calls=%fused_computation.40 | loop fusion | bytes 1048576 | tf_op jit(solution)/shard_map/slice | solution.py:232
  2.5 4.9 %collective-permute-start.3 = (bf16[144,1024]{1,0:T(8,128)(2,1)S(1)}, bf16[144,1024]{1,0:T(8,128)(2,1)S(1)}, u32[]{:S(2)}, u32[]{:S(2)}) collective-permute-start(bf16[144,1024]{1,0:T(8,128)(2,1)S(1)} %pad_maximum_fusion.1), channel_id=1, source_target_pairs={{0,1},{2,3},{4,5},{6,7},{8,9},{10,11},{12,13},{14,15},{16,17},{18,... | collective-permute-start | bytes 884744 | tf_op jit(solution)/shard_map/ppermute | solution.py:29
  8.1 0.7 pad_maximum_fusion.7
  8.8 1.5 %collective-permute-start.1 = (bf16[672,128]{1,0:T(8,128)(2,1)}, bf16[672,128]{1,0:T(8,128)(2,1)}, u32[]{:S(2)}, u32[]{:S(2)}) collective-permute-start(bf16[672,128]{1,0:T(8,128)(2,1)} %bitcast.13), channel_id=1, source_target_pairs={{0,4},{2,6},{4,0},{6,2},{8,12},{10,14},{12,8},{14,10},{16,20},{18,... | collective-permute-start | bytes 516104 | tf_op jit(solution)/shard_map/ppermute | solution.py:217
  11.4 1.4 %collective-permute-start.6 = (bf16[128,1024]{1,0:T(8,128)(2,1)S(1)}, bf16[128,1024]{1,0:T(8,128)(2,1)S(1)}, u32[]{:S(2)}, u32[]{:S(2)}) collective-permute-start(bf16[128,1024]{1,0:T(8,128)(2,1)S(1)} %pad_maximum_fusion.2), channel_id=1, source_target_pairs={{0,1},{2,3},{4,5},{6,7},{8,9},{10,11},{12,13},{14,15},{16,17},{18,... | collective-permute-start | bytes 786440 | tf_op jit(solution)/shard_map/ppermute | solution.py:29
  12.8 0.9 %collective-permute-done.3.refs_5_.refs_6_ = bf16[144,1024]{1,0:T(8,128)(2,1)S(1)} collective-permute-done((bf16[144,1024]{1,0:T(8,128)(2,1)S(1)}, bf16[144,1024]{1,0:T(8,128)(2,1)S(1)}, u32[]{:S(2)}, u32[]{:S(2)}) %collective-permute-start.3) | collective-permute-done | bytes 294944 | tf_op jit(solution)/shard_map/ppermute | solution.py:29
  14.4 2.5 %shard_map.93 = (bf16[128,2048]{1,0:T(8,128)(2,1)}, bf16[128,512]{1,0:T(8,128)(2,1)S(1)}, bf16[128,512]{1,0:T(8,128)(2,1)S(1)}, bf16[128,512]{1,0:T(8,128)(2,1)S...) custom-call(s32[1]{0:T(128)} %bitcast.place_ref, s32[1,128]{1,0:T(1,128)S(1)} %copy-done.4, ...), custom_call_target="tpu_custom_call" | custom-call | flops 1024 | bytes 1024 | tf_op jit(solution)/shard_map/pallas_call | solution.py:123
  17.0 2.5 %collective-permute-start.4 = (bf16[128,512]{1,0:T(8,128)(2,1)S(1)}, bf16[128,512]{1,0:T(8,128)(2,1)}, u32[]{:S(2)}, u32[]{:S(2)}) collective-permute-start(bf16[128,512]{1,0:T(8,128)(2,1)S(1)} %get-tuple-element.27), channel_id=1, source_target_pairs={{0,1},{1,0},{2,3},{3,2},{4,5},{5,4},{6,7},{7,6},{8,9},{9,8},{10,11... | collective-permute-start | bytes 393224 | tf_op jit(solution)/shard_map/ppermute | solution.py:274
  19.4 1.3 %collective-permute-start.5 = (bf16[128,512]{1,0:T(8,128)(2,1)S(1)}, bf16[128,512]{1,0:T(8,128)(2,1)}, u32[]{:S(2)}, u32[]{:S(2)}) collective-permute-start(bf16[128,512]{1,0:T(8,128)(2,1)S(1)} %get-tuple-element.28), channel_id=1, source_target_pairs={{1,0},{3,2},{5,4},{7,6},{9,8},{11,10},{13,12},{15,14},{17,16},{19,... | collective-permute-start | bytes 393224 | tf_op jit(solution)/shard_map/ppermute | solution.py:275
  20.8 1.2 %pad_maximum_fusion = bf16[4,672,128]{2,1,0:T(8,128)(2,1)S(1)} fusion(bf16[1,672,128]{2,1,0:T(8,128)(2,1)} %bitcast.16, bf16[1,672,128]{2,1,0:T(8,128)(2,1)} %bitcast.14, bf16[1,672,128]{2,1,0:T(8,128)(2,1)} %bitcast.12, bf16[1,672,128]{2,1,0:T(8,128)(2,1)S(1)} %bitcast.41), kind=kLoop, calls=%fused_computation | loop fusion | flops 1032192 | bytes 1376256 | tf_op jit(solution)/shard_map/stack | solution.py:252
  22.5 3.9 %collective-permute-done.5 = bf16[128,512]{1,0:T(8,128)(2,1)} collective-permute-done((bf16[128,512]{1,0:T(8,128)(2,1)S(1)}, bf16[128,512]{1,0:T(8,128)(2,1)}, u32[]{:S(2)}, u32[]{:S(2)}) %collective-permute-start.5) | collective-permute-done | bytes 131104 | tf_op jit(solution)/shard_map/ppermute | solution.py:275
  26.4 2.5 %shard_map.94 = (bf16[128,2048]{1,0:T(8,128)(2,1)}, bf16[128,512]{1,0:T(8,128)(2,1)S(1)}, bf16[128,512]{1,0:T(8,128)(2,1)S(1)}, bf16[128,512]{1,0:T(8,128)(2,1)S...) custom-call(s32[1]{0:T(128)} %bitcast.place_ref, ...), custom_call_target="tpu_custom_call", output_to_operand_aliasing={{0}: (8, {}), {5}: (9, {})} | custom-call | flops 1024 | bytes 1024 | tf_op jit(solution)/shard_map/pallas_call | solution.py:123
  28.9 1.3 %collective-permute-start.8 = (bf16[128,512]{1,0:T(8,128)(2,1)S(1)}, bf16[128,512]{1,0:T(8,128)(2,1)S(1)}, u32[]{:S(2)}, u32[]{:S(2)}) collective-permute-start(bf16[128,512]{1,0:T(8,128)(2,1)S(1)} %get-tuple-element.39), channel_id=1, source_target_pairs={{1,0},{3,2},{5,4},{7,6},{9,8},{11,10},{13,12},{15,14},{17,16},{19,... | collective-permute-start | bytes 393224 | tf_op jit(solution)/shard_map/ppermute | solution.py:275
  30.3 2.7 %collective-permute-start.9 = (bf16[4,336,128]{2,1,0:T(8,128)(2,1)S(1)}, bf16[4,336,128]{2,1,0:T(8,128)(2,1)S(1)}, u32[]{:S(2)}, u32[]{:S(2)}) collective-permute-start(bf16[4,336,128]{2,1,0:T(8,128)(2,1)S(1)} %get-tuple-element.44.refs_0_), channel_id=1, source_target_pairs={{0,1},{1,0},{2,3},{3,2},{4,5},{5,4},{6,7},{7,6},{8,9},{9,8},{10,11... | collective-permute-start | bytes 1032200 | tf_op jit(solution)/shard_map/ppermute | solution.py:282
  33.0 1.0 %broadcast_select_fusion.1 = (bf16[128,512]{1,0:T(8,128)(2,1)S(1)}, bf16[128,512]{1,0:T(8,128)(2,1)S(1)}) fusion(bf16[128,512]{1,0:T(8,128)(2,1)} %collective-permute-done.5, pred[]{:T(512)S(6)} %eq.10, bf16[128,512]{1,0:T(8,128)(2,1)} %collective-permute-done.4, bf16[128,512]{1,0:T(8,128)(2,1)S(1)} %get-tuple-element.34, ...), kind=kLoop, calls=%fused_computation.19 | loop fusion | flops 393216 | bytes 786433 | tf_op jit(solution)/shard_map/jit(_where)/select_n | solution.py:288
  34.0 1.6 %collective-permute-start.11 = (bf16[256,512]{1,0:T(8,128)(2,1)S(1)}, bf16[256,512]{1,0:T(8,128)(2,1)S(1)}, u32[]{:S(2)}, u32[]{:S(2)}) collective-permute-start(bf16[256,512]{1,0:T(8,128)(2,1)S(1)} %pad_maximum_fusion.3.refs_2_), channel_id=1, source_target_pairs={{0,4},{2,6},{4,0},{6,2},{8,12},{10,14},{12,8},{14,10},{16,20},{18,... | collective-permute-start | bytes 786440 | tf_op jit(solution)/shard_map/ppermute | solution.py:217
  35.6 2.6 %collective-permute-done.8 = bf16[128,512]{1,0:T(8,128)(2,1)S(1)} collective-permute-done((bf16[128,512]{1,0:T(8,128)(2,1)S(1)}, bf16[128,512]{1,0:T(8,128)(2,1)S(1)}, u32[]{:S(2)}, u32[]{:S(2)}) %collective-permute-start.8) | collective-permute-done | bytes 131104 | tf_op jit(solution)/shard_map/ppermute | solution.py:275
  38.2 4.4 %collective-permute-done.9.refs_1_ = bf16[4,336,128]{2,1,0:T(8,128)(2,1)S(1)} collective-permute-done((bf16[4,336,128]{2,1,0:T(8,128)(2,1)S(1)}, bf16[4,336,128]{2,1,0:T(8,128)(2,1)S(1)}, u32[]{:S(2)}, u32[]{:S(2)}) %collective-permute-start.9) | collective-permute-done | bytes 344096 | tf_op jit(solution)/shard_map/ppermute | solution.py:282
  42.6 1.6 %collective-permute-start.16 = (bf16[256,512]{1,0:T(8,128)(2,1)S(1)}, bf16[256,512]{1,0:T(8,128)(2,1)S(1)}, u32[]{:S(2)}, u32[]{:S(2)}) collective-permute-start(bf16[256,512]{1,0:T(8,128)(2,1)S(1)} %pad_maximum_fusion.4.refs_2_), channel_id=1, source_target_pairs={{0,4},{2,6},{4,0},{6,2},{8,12},{10,14},{12,8},{14,10},{16,20},{18,... | collective-permute-start | bytes 786440 | tf_op jit(solution)/shard_map/ppermute | solution.py:217
  44.7 4.4 %collective-permute-done.16.refs_4_ = bf16[256,512]{1,0:T(8,128)(2,1)S(1)} collective-permute-done((bf16[256,512]{1,0:T(8,128)(2,1)S(1)}, bf16[256,512]{1,0:T(8,128)(2,1)S(1)}, u32[]{:S(2)}, u32[]{:S(2)}) %collective-permute-start.16) | collective-permute-done | bytes 262176 | tf_op jit(solution)/shard_map/ppermute | solution.py:217
  49.6 1.6 %collective-permute-start.20 = (bf16[336,512]{1,0:T(8,128)(2,1)S(1)}, bf16[336,512]{1,0:T(8,128)(2,1)S(1)}, u32[]{:S(2)}, u32[]{:S(2)}) collective-permute-start(bf16[336,512]{1,0:T(8,128)(2,1)S(1)} %shard_map.95), channel_id=1, source_target_pairs={{0,8},{2,10},{4,12},{6,14},{8,0},{10,2},{12,4},{14,6},{16,24},{18,... | collective-permute-start | bytes 1032200 | tf_op jit(solution)/shard_map/ppermute | solution.py:217
  51.8 1.0 %collective-permute-start.18 = (bf16[336,512]{1,0:T(8,128)(2,1)S(1)}, bf16[336,512]{1,0:T(8,128)(2,1)S(1)}, u32[]{:S(2)}, u32[]{:S(2)}) collective-permute-start(bf16[336,512]{1,0:T(8,128)(2,1)S(1)} %shard_map.97), channel_id=1, source_target_pairs={{0,8},{2,10},{4,12},{6,14},{8,0},{10,2},{12,4},{14,6},{16,24},{18,... | collective-permute-start | bytes 1032200 | tf_op jit(solution)/shard_map/ppermute | solution.py:217
  52.8 0.8 maximum_select_fusion
  53.5 1.3 %collective-permute-start.13 = (bf16[128,1024]{1,0:T(8,128)(2,1)S(1)}, bf16[128,1024]{1,0:T(8,128)(2,1)S(1)}, u32[]{:S(2)}, u32[]{:S(2)}) collective-permute-start(bf16[128,1024]{1,0:T(8,128)(2,1)S(1)} %get-tuple-element.47), channel_id=1, source_target_pairs={{1,0},{3,2},{5,4},{7,6},{9,8},{11,10},{13,12},{15,14},{17,16},{19,... | collective-permute-start | bytes 786440 | tf_op jit(solution)/shard_map/ppermute | solution.py:331
  54.8 5.1 %collective-permute-done.14.refs_1_ = bf16[4,336,128]{2,1,0:T(8,128)(2,1)S(1)} collective-permute-done((bf16[4,336,128]{2,1,0:T(8,128)(2,1)S(1)}, bf16[4,336,128]{2,1,0:T(8,128)(2,1)S(1)}, u32[]{:S(2)}, u32[]{:S(2)}) %collective-permute-start.14) | collective-permute-done | bytes 344096 | tf_op jit(solution)/shard_map/ppermute | solution.py:282
  60.7 2.7 %collective-permute-start.21 = (bf16[168,512]{1,0:T(8,128)(2,1)S(1)}, bf16[168,512]{1,0:T(8,128)(2,1)S(1)}, u32[]{:S(2)}, u32[]{:S(2)}) collective-permute-start(bf16[168,512]{1,0:T(8,128)(2,1)S(1)} %slice.42), channel_id=1, source_target_pairs={{0,16},{2,18},{4,20},{6,22},{8,24},{10,26},{12,28},{14,30},{16,0},... | collective-permute-start | bytes 516104 | tf_op jit(solution)/shard_map/ppermute | solution.py:217
  63.9 7.4 %collective-permute-done.18 = bf16[336,512]{1,0:T(8,128)(2,1)S(1)} collective-permute-done((bf16[336,512]{1,0:T(8,128)(2,1)S(1)}, bf16[336,512]{1,0:T(8,128)(2,1)S(1)}, u32[]{:S(2)}, u32[]{:S(2)}) %collective-permute-start.18) | collective-permute-done | bytes 344096 | tf_op jit(solution)/shard_map/ppermute | solution.py:217
  71.3 1.8 %collective-permute-start.19 = (bf16[168,512]{1,0:T(8,128)(2,1)S(1)}, bf16[168,512]{1,0:T(8,128)(2,1)S(1)}, u32[]{:S(2)}, u32[]{:S(2)}) collective-permute-start(bf16[168,512]{1,0:T(8,128)(2,1)S(1)} %slice.43), channel_id=1, source_target_pairs={{0,16},{2,18},{4,20},{6,22},{8,24},{10,26},{12,28},{14,30},{16,0},... | collective-permute-start | bytes 516104 | tf_op jit(solution)/shard_map/ppermute | solution.py:217
  73.1 0.8 fusion
  74.5 1.9 %shard_map.99.refs_0_ = f32[168,1024]{1,0:T(8,128)} custom-call(f32[336,512]{1,0:T(8,128)} %copy-done.5, bf16[168,512]{1,0:T(8,128)(2,1)} %copy-done.8), custom_call_target="tpu_custom_call" | custom-call | flops 1024 | bytes 1024 | tf_op jit(solution)/shard_map/pallas_call | solution.py:176
  76.4 5.6 %collective-permute-done.19.last_ref = bf16[168,512]{1,0:T(8,128)(2,1)S(1)} collective-permute-done((bf16[168,512]{1,0:T(8,128)(2,1)S(1)}, bf16[168,512]{1,0:T(8,128)(2,1)S(1)}, u32[]{:S(2)}, u32[]{:S(2)}) %collective-permute-start.19) | collective-permute-done | bytes 172064 | tf_op jit(solution)/shard_map/ppermute | solution.py:217
  82.7 1.9 %shard_map.100 = f32[168,1024]{1,0:T(8,128)} custom-call(f32[336,512]{1,0:T(8,128)} %copy-done.6, bf16[168,512]{1,0:T(8,128)(2,1)} %copy-done.9, f32[168,1024]{1,0:T(8,128)} %shard_map.99.refs_0_), custom_call_target="tpu_custom_call", output_to_operand_aliasing={{}: (2, {})} | custom-call | flops 1024 | bytes 1024 | tf_op jit(solution)/shard_map/pallas_call | solution.py:176
  (64 shorter events, 7.9 us)
Async XLA Ops:
  1.3 6.3 %copy-start.7 = (bf16[1,128,2688]{2,1,0:T(8,128)(2,1)S(1)}, bf16[1,128,2688]{2,1,0:T(8,128)(2,1)}, u32[]{:S(2)}) copy-start(bf16[1,128,2688]{2,1,0:T(8,128)(2,1)} %param.6) | copy-start | bytes 2064388
  2.5 11.2 %collective-permute-start.3 = (bf16[144,1024]{1,0:T(8,128)(2,1)S(1)}, bf16[144,1024]{1,0:T(8,128)(2,1)S(1)}, u32[]{:S(2)}, u32[]{:S(2)}) collective-permute-start(bf16[144,1024]{1,0:T(8,128)(2,1)S(1)} %pad_maximum_fusion.1), channel_id=1, source_target_pairs={{0,1},{2,3},{4,5},{6,7},{8,9},{10,11},{12,13},{14,15},{16,17},{18,... | collective-permute-start | bytes 884744 | tf_op jit(solution)/shard_map/ppermute | solution.py:29
  8.0 5.8 %copy-start.3 = (bf16[1,128,2048]{2,1,0:T(8,128)(2,1)S(1)}, bf16[1,128,2048]{2,1,0:T(8,128)(2,1)}, u32[]{:S(2)}) copy-start(bf16[1,128,2048]{2,1,0:T(8,128)(2,1)} %param.10) | copy-start | bytes 1572868
  8.1 11.4 %collective-permute-start = (bf16[672,128]{1,0:T(8,128)(2,1)S(1)}, bf16[672,128]{1,0:T(8,128)(2,1)}, u32[]{:S(2)}, u32[]{:S(2)}) collective-permute-start(bf16[672,128]{1,0:T(8,128)(2,1)S(1)} %bitcast.43), channel_id=1, source_target_pairs={{0,2},{2,0},{4,6},{6,4},{8,10},{10,8},{12,14},{14,12},{16,18},{18,... | collective-permute-start | bytes 516104 | tf_op jit(solution)/shard_map/ppermute | solution.py:217
  8.1 5.6 %copy-start.2 = (bf16[1,128,2048]{2,1,0:T(8,128)(2,1)S(1)}, bf16[1,128,2048]{2,1,0:T(8,128)(2,1)}, u32[]{:S(2)}) copy-start(bf16[1,128,2048]{2,1,0:T(8,128)(2,1)} %param.7) | copy-start | bytes 1572868
  8.8 11.9 %collective-permute-start.1 = (bf16[672,128]{1,0:T(8,128)(2,1)}, bf16[672,128]{1,0:T(8,128)(2,1)}, u32[]{:S(2)}, u32[]{:S(2)}) collective-permute-start(bf16[672,128]{1,0:T(8,128)(2,1)} %bitcast.13), channel_id=1, source_target_pairs={{0,4},{2,6},{4,0},{6,2},{8,12},{10,14},{12,8},{14,10},{16,20},{18,... | collective-permute-start | bytes 516104 | tf_op jit(solution)/shard_map/ppermute | solution.py:217
  11.0 9.7 %collective-permute-start.2 = (bf16[672,128]{1,0:T(8,128)(2,1)}, bf16[672,128]{1,0:T(8,128)(2,1)}, u32[]{:S(2)}, u32[]{:S(2)}) collective-permute-start(bf16[672,128]{1,0:T(8,128)(2,1)} %bitcast.15), channel_id=1, source_target_pairs={{0,6},{2,4},{4,2},{6,0},{8,14},{10,12},{12,10},{14,8},{16,22},{18,... | collective-permute-start | bytes 516104 | tf_op jit(solution)/shard_map/ppermute | solution.py:217
  11.4 2.4 %copy-start = (bf16[1,128,1024]{2,1,0:T(8,128)(2,1)S(1)}, bf16[1,128,1024]{2,1,0:T(8,128)(2,1)}, u32[]{:S(2)}) copy-start(bf16[1,128,1024]{2,1,0:T(8,128)(2,1)} %param.8) | copy-start | bytes 786436
  11.4 2.4 %copy-start.1 = (bf16[1,128,1024]{2,1,0:T(8,128)(2,1)S(1)}, bf16[1,128,1024]{2,1,0:T(8,128)(2,1)}, u32[]{:S(2)}) copy-start(bf16[1,128,1024]{2,1,0:T(8,128)(2,1)} %param.9) | copy-start | bytes 786436
  11.4 10.6 %collective-permute-start.6 = (bf16[128,1024]{1,0:T(8,128)(2,1)S(1)}, bf16[128,1024]{1,0:T(8,128)(2,1)S(1)}, u32[]{:S(2)}, u32[]{:S(2)}) collective-permute-start(bf16[128,1024]{1,0:T(8,128)(2,1)S(1)} %pad_maximum_fusion.2), channel_id=1, source_target_pairs={{0,1},{2,3},{4,5},{6,7},{8,9},{10,11},{12,13},{14,15},{16,17},{18,... | collective-permute-start | bytes 786440 | tf_op jit(solution)/shard_map/ppermute | solution.py:29
  13.8 0.7 copy-start.4
  17.0 5.5 %collective-permute-start.4 = (bf16[128,512]{1,0:T(8,128)(2,1)S(1)}, bf16[128,512]{1,0:T(8,128)(2,1)}, u32[]{:S(2)}, u32[]{:S(2)}) collective-permute-start(bf16[128,512]{1,0:T(8,128)(2,1)S(1)} %get-tuple-element.27), channel_id=1, source_target_pairs={{0,1},{1,0},{2,3},{3,2},{4,5},{5,4},{6,7},{7,6},{8,9},{9,8},{10,11... | collective-permute-start | bytes 393224 | tf_op jit(solution)/shard_map/ppermute | solution.py:274
  19.4 7.0 %collective-permute-start.5 = (bf16[128,512]{1,0:T(8,128)(2,1)S(1)}, bf16[128,512]{1,0:T(8,128)(2,1)}, u32[]{:S(2)}, u32[]{:S(2)}) collective-permute-start(bf16[128,512]{1,0:T(8,128)(2,1)S(1)} %get-tuple-element.28), channel_id=1, source_target_pairs={{1,0},{3,2},{5,4},{7,6},{9,8},{11,10},{13,12},{15,14},{17,16},{19,... | collective-permute-start | bytes 393224 | tf_op jit(solution)/shard_map/ppermute | solution.py:275
  28.9 6.7 %collective-permute-start.7 = (bf16[128,512]{1,0:T(8,128)(2,1)S(1)}, bf16[128,512]{1,0:T(8,128)(2,1)S(1)}, u32[]{:S(2)}, u32[]{:S(2)}) collective-permute-start(bf16[128,512]{1,0:T(8,128)(2,1)S(1)} %get-tuple-element.38), channel_id=1, source_target_pairs={{0,1},{1,0},{2,3},{3,2},{4,5},{5,4},{6,7},{7,6},{8,9},{9,8},{10,11... | collective-permute-start | bytes 393224 | tf_op jit(solution)/shard_map/ppermute | solution.py:274
  28.9 9.2 %collective-permute-start.8 = (bf16[128,512]{1,0:T(8,128)(2,1)S(1)}, bf16[128,512]{1,0:T(8,128)(2,1)S(1)}, u32[]{:S(2)}, u32[]{:S(2)}) collective-permute-start(bf16[128,512]{1,0:T(8,128)(2,1)S(1)} %get-tuple-element.39), channel_id=1, source_target_pairs={{1,0},{3,2},{5,4},{7,6},{9,8},{11,10},{13,12},{15,14},{17,16},{19,... | collective-permute-start | bytes 393224 | tf_op jit(solution)/shard_map/ppermute | solution.py:275
  30.3 12.3 %collective-permute-start.9 = (bf16[4,336,128]{2,1,0:T(8,128)(2,1)S(1)}, bf16[4,336,128]{2,1,0:T(8,128)(2,1)S(1)}, u32[]{:S(2)}, u32[]{:S(2)}) collective-permute-start(bf16[4,336,128]{2,1,0:T(8,128)(2,1)S(1)} %get-tuple-element.44.refs_0_), channel_id=1, source_target_pairs={{0,1},{1,0},{2,3},{3,2},{4,5},{5,4},{6,7},{7,6},{8,9},{9,8},{10,11... | collective-permute-start | bytes 1032200 | tf_op jit(solution)/shard_map/ppermute | solution.py:282
  34.0 10.2 %collective-permute-start.11 = (bf16[256,512]{1,0:T(8,128)(2,1)S(1)}, bf16[256,512]{1,0:T(8,128)(2,1)S(1)}, u32[]{:S(2)}, u32[]{:S(2)}) collective-permute-start(bf16[256,512]{1,0:T(8,128)(2,1)S(1)} %pad_maximum_fusion.3.refs_2_), channel_id=1, source_target_pairs={{0,4},{2,6},{4,0},{6,2},{8,12},{10,14},{12,8},{14,10},{16,20},{18,... | collective-permute-start | bytes 786440 | tf_op jit(solution)/shard_map/ppermute | solution.py:217
  42.6 6.4 %collective-permute-start.16 = (bf16[256,512]{1,0:T(8,128)(2,1)S(1)}, bf16[256,512]{1,0:T(8,128)(2,1)S(1)}, u32[]{:S(2)}, u32[]{:S(2)}) collective-permute-start(bf16[256,512]{1,0:T(8,128)(2,1)S(1)} %pad_maximum_fusion.4.refs_2_), channel_id=1, source_target_pairs={{0,4},{2,6},{4,0},{6,2},{8,12},{10,14},{12,8},{14,10},{16,20},{18,... | collective-permute-start | bytes 786440 | tf_op jit(solution)/shard_map/ppermute | solution.py:217
  44.2 4.9 %collective-permute-start.10 = (bf16[256,512]{1,0:T(8,128)(2,1)S(1)}, bf16[256,512]{1,0:T(8,128)(2,1)S(1)}, u32[]{:S(2)}, u32[]{:S(2)}) collective-permute-start(bf16[256,512]{1,0:T(8,128)(2,1)S(1)} %pad_maximum_fusion.3.refs_2_), channel_id=1, source_target_pairs={{0,2},{2,0},{4,6},{6,4},{8,10},{10,8},{12,14},{14,12},{16,18},{18,... | collective-permute-start | bytes 786440 | tf_op jit(solution)/shard_map/ppermute | solution.py:217
  44.2 4.9 %collective-permute-start.12 = (bf16[256,512]{1,0:T(8,128)(2,1)S(1)}, bf16[256,512]{1,0:T(8,128)(2,1)S(1)}, u32[]{:S(2)}, u32[]{:S(2)}) collective-permute-start(bf16[256,512]{1,0:T(8,128)(2,1)S(1)} %collective-permute-done.11.refs_4_), channel_id=1, source_target_pairs={{0,2},{2,0},{4,6},{6,4},{8,10},{10,8},{12,14},{14,12},{16,18},{18,... | collective-permute-start | bytes 786440 | tf_op jit(solution)/shard_map/ppermute | solution.py:217
  44.7 6.6 %collective-permute-start.15 = (bf16[256,512]{1,0:T(8,128)(2,1)S(1)}, bf16[256,512]{1,0:T(8,128)(2,1)S(1)}, u32[]{:S(2)}, u32[]{:S(2)}) collective-permute-start(bf16[256,512]{1,0:T(8,128)(2,1)S(1)} %pad_maximum_fusion.4.refs_2_), channel_id=1, source_target_pairs={{0,2},{2,0},{4,6},{6,4},{8,10},{10,8},{12,14},{14,12},{16,18},{18,... | collective-permute-start | bytes 786440 | tf_op jit(solution)/shard_map/ppermute | solution.py:217
  49.1 2.2 %collective-permute-start.17 = (bf16[256,512]{1,0:T(8,128)(2,1)S(1)}, bf16[256,512]{1,0:T(8,128)(2,1)S(1)}, u32[]{:S(2)}, u32[]{:S(2)}) collective-permute-start(bf16[256,512]{1,0:T(8,128)(2,1)S(1)} %collective-permute-done.16.refs_4_), channel_id=1, source_target_pairs={{0,2},{2,0},{4,6},{6,4},{8,10},{10,8},{12,14},{14,12},{16,18},{18,... | collective-permute-start | bytes 786440 | tf_op jit(solution)/shard_map/ppermute | solution.py:217
  49.1 10.9 %collective-permute-start.14 = (bf16[4,336,128]{2,1,0:T(8,128)(2,1)S(1)}, bf16[4,336,128]{2,1,0:T(8,128)(2,1)S(1)}, u32[]{:S(2)}, u32[]{:S(2)}) collective-permute-start(bf16[4,336,128]{2,1,0:T(8,128)(2,1)S(1)} %get-tuple-element.50.refs_0_), channel_id=1, source_target_pairs={{0,1},{1,0},{2,3},{3,2},{4,5},{5,4},{6,7},{7,6},{8,9},{9,8},{10,11... | collective-permute-start | bytes 1032200 | tf_op jit(solution)/shard_map/ppermute | solution.py:282
  49.6 10.9 %collective-permute-start.20 = (bf16[336,512]{1,0:T(8,128)(2,1)S(1)}, bf16[336,512]{1,0:T(8,128)(2,1)S(1)}, u32[]{:S(2)}, u32[]{:S(2)}) collective-permute-start(bf16[336,512]{1,0:T(8,128)(2,1)S(1)} %shard_map.95), channel_id=1, source_target_pairs={{0,8},{2,10},{4,12},{6,14},{8,0},{10,2},{12,4},{14,6},{16,24},{18,... | collective-permute-start | bytes 1032200 | tf_op jit(solution)/shard_map/ppermute | solution.py:217
  51.8 19.4 %collective-permute-start.18 = (bf16[336,512]{1,0:T(8,128)(2,1)S(1)}, bf16[336,512]{1,0:T(8,128)(2,1)S(1)}, u32[]{:S(2)}, u32[]{:S(2)}) collective-permute-start(bf16[336,512]{1,0:T(8,128)(2,1)S(1)} %shard_map.97), channel_id=1, source_target_pairs={{0,8},{2,10},{4,12},{6,14},{8,0},{10,2},{12,4},{14,6},{16,24},{18,... | collective-permute-start | bytes 1032200 | tf_op jit(solution)/shard_map/ppermute | solution.py:217
  53.5 19.6 %collective-permute-start.13 = (bf16[128,1024]{1,0:T(8,128)(2,1)S(1)}, bf16[128,1024]{1,0:T(8,128)(2,1)S(1)}, u32[]{:S(2)}, u32[]{:S(2)}) collective-permute-start(bf16[128,1024]{1,0:T(8,128)(2,1)S(1)} %get-tuple-element.47), channel_id=1, source_target_pairs={{1,0},{3,2},{5,4},{7,6},{9,8},{11,10},{13,12},{15,14},{17,16},{19,... | collective-permute-start | bytes 786440 | tf_op jit(solution)/shard_map/ppermute | solution.py:331
  60.6 3.2 %copy-start.5 = (f32[336,512]{1,0:T(8,128)}, f32[336,512]{1,0:T(8,128)S(1)}, u32[]{:S(2)}) copy-start(f32[336,512]{1,0:T(8,128)S(1)} %convert_add_fusion.half_ref) | copy-start | bytes 2064388
  60.7 13.2 %collective-permute-start.21 = (bf16[168,512]{1,0:T(8,128)(2,1)S(1)}, bf16[168,512]{1,0:T(8,128)(2,1)S(1)}, u32[]{:S(2)}, u32[]{:S(2)}) collective-permute-start(bf16[168,512]{1,0:T(8,128)(2,1)S(1)} %slice.42), channel_id=1, source_target_pairs={{0,16},{2,18},{4,20},{6,22},{8,24},{10,26},{12,28},{14,30},{16,0},... | collective-permute-start | bytes 516104 | tf_op jit(solution)/shard_map/ppermute | solution.py:217
  71.3 5.1 %copy-start.6 = (f32[336,512]{1,0:T(8,128)}, f32[336,512]{1,0:T(8,128)S(1)}, u32[]{:S(2)}) copy-start(f32[336,512]{1,0:T(8,128)S(1)} %convert_add_fusion.1.half_ref) | copy-start | bytes 2064388
  71.3 10.7 %collective-permute-start.19 = (bf16[168,512]{1,0:T(8,128)(2,1)S(1)}, bf16[168,512]{1,0:T(8,128)(2,1)S(1)}, u32[]{:S(2)}, u32[]{:S(2)}) collective-permute-start(bf16[168,512]{1,0:T(8,128)(2,1)S(1)} %slice.43), channel_id=1, source_target_pairs={{0,16},{2,18},{4,20},{6,22},{8,24},{10,26},{12,28},{14,30},{16,0},... | collective-permute-start | bytes 516104 | tf_op jit(solution)/shard_map/ppermute | solution.py:217
  73.9 0.7 copy-start.8
  82.0 0.7 copy-start.9

commit v3 on v2

--- a/solution.py
+++ b/solution.py
@@ -10,6 +10,7 @@
 HD = 128
 WIN = 1024
 CHUNKS = 2
+SPLIT = 2
 SCORE_FLOOR = -1e30
 MIB = 1024 * 1024
 SEG_ROWS = 16
@@ -96,7 +97,7 @@
             outs[2][:, cols] = value_part.astype(jnp.bfloat16)
 
 
-def attend(chunk, place, segs, queries, out_grad, keys, values, rim_pairs, rim_segs, held):
+def attend(chunk, place, segs, queries, out_grad, keys, values, rim_pairs, rim_segs):
     hops = len(rim_pairs)
     tok = queries.shape[0]
     group = queries.shape[1] // keys.shape[1]
@@ -106,20 +107,8 @@
     part = lambda *shape: pl.BlockSpec(shape, lambda i, *_: (0, chunk))
     seg_row = pl.BlockSpec((SEG_ROWS, tok), lambda i, *_: (tok // SEG_ROWS, 0))
     out_shapes = [(tok, group * width)]
-    if hops == 1:
-        out_shapes += [(tok, width)] * 5
-        in_place = (0, 5)
-    else:
-        out_shapes += [(span, width)] * 2
-        in_place = (0,)
-    out_specs, out_types = [], []
-    for place_of, (rows, columns) in enumerate(out_shapes):
-        shared = place_of in in_place
-        out_specs.append(part(rows, columns) if shared else whole(rows, columns))
-        columns = columns * CHUNKS if shared else columns
-        out_types.append(jax.ShapeDtypeStruct((rows, columns), jnp.bfloat16))
+    out_shapes += [(tok, width)] * 5 if hops == 1 else [(span, width)] * 2
     operands = [place, segs, queries, out_grad, keys, values, *rim_pairs, *rim_segs]
-    aliases = {len(operands) + n: in_place[n] for n in range(len(held))}
     return pl.pallas_call(
         partial(attention_kernel, hops, group, len(out_shapes)),
         grid_spec=pltpu.PrefetchScalarGridSpec(
@@ -133,59 +122,45 @@
                 part(tok, width),
             ]
             + [whole(tok, 2 * width)] * hops
-            + [seg_row] * hops
-            + [pl.BlockSpec(memory_space=pl.ANY)] * len(held),
-            out_specs=out_specs,
+            + [seg_row] * hops,
+            out_specs=[whole(*shape) for shape in out_shapes],
         ),
-        out_shape=out_types,
-        input_output_aliases=aliases,
+        out_shape=[jax.ShapeDtypeStruct(shape, jnp.bfloat16) for shape in out_shapes],
         compiler_params=pltpu.CompilerParams(vmem_limit_bytes=48 * MIB),
         cost_estimate=SMALL,
-    )(*operands, *held)
+    )(*operands)
 
 
 def product_kernel(traces, *refs):
-    own_ref, other_ref = refs[:2]
-    grad_refs = refs[2 : 2 + traces]
-    out_ref = refs[2 + traces]
+    own_refs, first_ref, rest_ref = refs[:traces], refs[traces], refs[traces + 1]
+    grad_refs = refs[traces + 2 : 2 * traces + 2]
+    outs = refs[2 * traces + 2 :]
+    away = [first_ref[...]] + [rest_ref[t] for t in range(traces - 1)]
     features = jnp.concatenate(
-        [ref[t] for t in range(traces) for ref in (own_ref, other_ref)], axis=1
+        [piece for t in range(traces) for piece in (own_refs[t][...], away[t])], axis=1
     )
     grads = jnp.concatenate([ref[...] for ref in grad_refs], axis=0)
-    out_ref[...] = dot_f32(features, grads).astype(out_ref.dtype)
-
-
-def product(features, grads, dtype):
-    traces, rows, _ = features[0].shape
-    width = grads[0].shape[1]
+    width = outs[0].shape[1]
+    for n, out in enumerate(outs):
+        out[...] = dot_f32(features, grads[:, n * width : (n + 1) * width]).astype(out.dtype)
+
+
+def product(half, own, first_away, rest_away, grads, dtype):
+    traces, (rows, tok) = len(own), own[0].shape
+    rows //= 2
+    width = grads[0].shape[1] // SPLIT
+    half_of = lambda array: pl.BlockSpec((rows, array.shape[1]), lambda i: (half, 0))
+    whole = lambda array: pl.BlockSpec(array.shape, lambda i: (0,) * array.ndim)
     return pl.pallas_call(
         partial(product_kernel, traces),
-        out_shape=jax.ShapeDtypeStruct((rows, width), dtype),
+        grid=(1,),
+        in_specs=[half_of(piece) for piece in (*own, first_away)]
+        + [whole(piece) for piece in (rest_away, *grads)],
+        out_specs=[pl.BlockSpec((rows, width), lambda i: (0, 0))] * SPLIT,
+        out_shape=[jax.ShapeDtypeStruct((rows, width), dtype)] * SPLIT,
         compiler_params=pltpu.CompilerParams(vmem_limit_bytes=48 * MIB),
         cost_estimate=SMALL,
-    )(*features, *grads)
-
-
-def finish_kernel(half_ref, last_ref, *refs):
-    rows = last_ref.shape[0]
-    refs[-1][...] = half_ref[rows:] + last_ref[...].astype(jnp.float32)
-
-
-def finish(chunk, half, last, held):
-    rows, width = last.shape
-    return pl.pallas_call(
-        finish_kernel,
-        grid=(1,),
-        in_specs=[
-            pl.BlockSpec(half.shape, lambda i: (0, 0)),
-            pl.BlockSpec(last.shape, lambda i: (0, 0)),
-        ]
-        + [pl.BlockSpec(memory_space=pl.ANY)] * len(held),
-        out_specs=pl.BlockSpec((rows, width), lambda i: (0, chunk)),
-        out_shape=jax.ShapeDtypeStruct((rows, width * CHUNKS), jnp.float32),
-        input_output_aliases={2: 0} if held else {},
-        cost_estimate=SMALL,
-    )(half, last, *held)
+    )(*own, first_away, rest_away, *grads)
 
 
 def local(hidden_in, queries, key_states, value_states, out_grad, segment_ids):
@@ -249,48 +224,51 @@
             ).reshape(slow_count * rows, tok)
             away = lambda slow, mid, core: (slow, (mid + step) % mid_count, core ^ flip)
             pieces.append(share if step == flip == 0 else dp_send(share, away))
-    features = jnp.stack(pieces)
 
     half_rows = slow_count // 2 * rows
-    attended, columns, held = [], [], []
+    low_high = [(0, half_rows), (half_rows, 2 * half_rows)]
+
+    attended = []
     for chunk in range(CHUNKS):
-        outs = attend(
-            chunk,
-            place_arg,
-            segment_ids,
-            queries[0],
-            out_grad[0],
-            own_keys,
-            own_values,
-            rim_pairs[chunk],
-            rim_pairs[0],
-            held,
-        )
-        attended.append(outs)
-        held = [outs[0], outs[5]] if hops == 1 else [outs[0]]
-        if ctx_count != 2:
-            continue
-        _, sent, addend, key_own, value_own, _ = outs
-        arrived = lax.ppermute(sent, "ctx", swap_ctx)
-        late_keys = lax.ppermute(key_own, "ctx", [(1, 0)])
-        if chunk == 0:
-            arrived, late_keys, rim_pairs[1:] = lax.optimization_barrier(
-                (arrived, late_keys, rim_pairs[1:])
+        if chunk > 0:
+            rim_pairs[chunk], _ = lax.optimization_barrier((rim_pairs[chunk], attended[-1][1]))
+        attended.append(
+            attend(
+                chunk,
+                place_arg,
+                segment_ids,
+                queries[0],
+                out_grad[0],
+                own_keys,
+                own_values,
+                rim_pairs[chunk],
+                rim_pairs[0],
             )
-            features, rim_pairs[1:] = lax.optimization_barrier((features, rim_pairs[1:]))
-            halves = [features[:, :half_rows], features[:, half_rows:]]
-            halves = [(own, lax.ppermute(own, "ctx", swap_ctx)) for own in halves]
-        elif chunk == 1:
-            arrived, late_keys, halves[0] = lax.optimization_barrier((arrived, late_keys, halves[0]))
-        total = (addend.astype(jnp.float32) + arrived.astype(jnp.float32)).astype(jnp.bfloat16)
-        columns.append(
-            jnp.concatenate(
+        )
+    query_grad = jnp.concatenate([outs[0] for outs in attended], axis=1)
+
+    if ctx_count == 2:
+        first_away = lax.ppermute(pieces[0], "ctx", swap_ctx)
+        columns, rest_away = [], []
+        for chunk, (_, sent, addend, key_own, value_own, _) in enumerate(attended):
+            if chunk > 0:
+                sent, key_own, _ = lax.optimization_barrier((sent, key_own, arrived))
+            arrived = lax.ppermute(sent, "ctx", swap_ctx)
+            late_keys = lax.ppermute(key_own, "ctx", [(1, 0)])
+            if chunk == 0:
+                arrived, late_keys, first_away, *_ = lax.optimization_barrier(
+                    (arrived, late_keys, first_away, rim_pairs[1:])
+                )
+            total = (addend.astype(jnp.float32) + arrived.astype(jnp.float32)).astype(jnp.bfloat16)
+            block = jnp.concatenate(
                 [jnp.where(first, total, value_own), jnp.where(first, late_keys, total)], axis=0
             )
-        )
-    query_grad = held[0]
-
-    if ctx_count == 2:
+            if chunk == 0:
+                for low, high in low_high:
+                    rest = jnp.stack([piece[low:high] for piece in pieces[1:]])
+                    rest, block = lax.optimization_barrier((rest, block))
+                    rest_away.append(lax.ppermute(rest, "ctx", swap_ctx))
+            columns.append(block)
         key_grad = jnp.where(
             first,
             jnp.concatenate([block[:tok] for block in columns], axis=1),
@@ -315,28 +293,44 @@
             tiled=True,
         )
         columns = jnp.split(both, CHUNKS, axis=1)
-        every = lax.all_gather(features, "ctx", axis=2, tiled=True)
-        halves = [
-            tuple(jnp.split(every[:, low : low + half_rows], 2, axis=2)) for low in (0, half_rows)
+        every = lax.all_gather(jnp.stack(pieces), "ctx", axis=2, tiled=True)
+        near, away = jnp.split(every, 2, axis=2)
+        pieces, first_away = list(near), away[0]
+        rest_away = [away[1:, low:high] for low, high in low_high]
+
+    gathered = []
+    for block in columns:
+        near = [block] + [dp_send(block, mid_by(step)) for step in range(1, mid_count)]
+        gathered.append(
+            [piece for near_one in near for piece in (near_one, dp_send(near_one, swap_core))]
+        )
+    gathered[-1], rest_away[1] = lax.optimization_barrier((gathered[-1], rest_away[1]))
+    sent, kept = (
+        [
+            piece
+            for grads in gathered
+            for piece in product(half, pieces, first_away, rest_away[half], grads, dtype)
         ]
-
-    held = []
-    for chunk, block in enumerate(columns):
-        near = [block] + [dp_send(block, mid_by(step)) for step in range(1, mid_count)]
-        grads = [piece for near_one in near for piece in (near_one, dp_send(near_one, swap_core))]
-        sent = product(halves[0], grads, jnp.bfloat16)
-        kept = product(halves[1], grads, jnp.float32)
-        if chunk == 0 and ctx_count == 2:
-            value_rim, sent = lax.optimization_barrier((attended[-1][5], sent))
-            returned = lax.ppermute(value_rim, "ctx", [(1, 0)])
-            value_own = jnp.concatenate([outs[4] for outs in attended], axis=1)
-            value_grad = (value_own.astype(jnp.float32) + returned.astype(jnp.float32)).astype(
-                jnp.bfloat16
-            )
-        half = kept + dp_send(sent, flip_slow(1)).astype(jnp.float32)
-        last = dp_send(half[:rows].astype(jnp.bfloat16), flip_slow(2))
-        held = [finish(chunk, half, last, held)]
-    weight_grad = held[0]
+        for half, dtype in ((0, jnp.bfloat16), (1, jnp.float32))
+    )
+    if ctx_count == 2:
+        value_rim = jnp.concatenate([outs[5] for outs in attended], axis=1)
+        value_rim, sent[0] = lax.optimization_barrier((value_rim, sent[0]))
+        returned = lax.ppermute(value_rim, "ctx", [(1, 0)])
+        value_own = jnp.concatenate([outs[4] for outs in attended], axis=1)
+        value_grad = (value_own.astype(jnp.float32) + returned.astype(jnp.float32)).astype(
+            jnp.bfloat16
+        )
+    halves = [
+        near + dp_send(far, flip_slow(1)).astype(jnp.float32) for near, far in zip(kept, sent)
+    ]
+    last = [dp_send(half[:rows].astype(jnp.bfloat16), flip_slow(2)) for half in halves]
+    piece_width = halves[0].shape[1]
+    weight_grad = jnp.zeros((rows, piece_width * len(halves)), jnp.float32)
+    for n, (half, final) in enumerate(zip(halves, last)):
+        weight_grad = lax.dynamic_update_slice(
+            weight_grad, half[rows:] + final.astype(jnp.float32), (0, n * piece_width)
+        )
     return (query_grad[None], key_grad[None], value_grad[None], weight_grad)
 
 

time: 84.9 us -> 78.5 us (0.925)
  Pallas kernels: 10.9 us -> 5.86 us
  starting transfers between devices: 27.9 us -> 32.7 us
  other arithmetic: 6.16 us -> 3.04 us
  waiting for transfers between devices: 34.8 us -> 32.9 us
  local copies, waits for them, and re-layouts: 3.75 us -> 2.6 us
    ppermute x2 -> x3, waiting for transfers between devices: 9.47 us -> 3.34 us  [the longest x2 3.34 us: local(): rest_away.append(lax.ppermute(rest, 'ctx', swap_ctx))]
    ppermute x13 -> x17, waiting for transfers between devices: 17.4 us -> 23.5 us  [dp_send(): return lax.ppermute(value, 'dp', pairs)]
    ppermute x13 -> x17, starting transfers between devices: 12.6 us -> 17.4 us  [dp_send(): return lax.ppermute(value, 'dp', pairs)]
    pallas_call x6 -> x4, Pallas kernels: 5.82 us -> 2.08 us  [product(): pl.pallas_call(partial(product_kernel, traces), grid=(1,), in_specs=[half...]
    ppermute x2, waiting for transfers between devices: 6.47 us -> 3.91 us  [local(): late_keys = lax.ppermute(key_own, 'ctx', [(1, 0)])]
    ppermute x2, starting transfers between devices: 6.33 us -> 4.05 us  [shifted(): lax.ppermute(value, axis, [(source, source + steps) for source in range(l...]
    ppermute x2, starting transfers between devices: 2.48 us -> 4.34 us  [local(): arrived = lax.ppermute(sent, 'ctx', swap_ctx)]
    ppermute x2, waiting for transfers between devices: 0.51 us -> 2.18 us  [local(): arrived = lax.ppermute(sent, 'ctx', swap_ctx)]
  transfers between devices with their start and end apart: 22 -> 27, of which waited for: 10 -> 14; matrix products, arithmetic and copies ran while one was open for 7% -> 4% of each run, Pallas kernels for 8% -> 7%
where the time goes in v3:
time: 78.5 us; the launch traced here: 78.3 us
  waiting for transfers between devices  32.9 us (42%)
  starting transfers between devices  32.7 us (42%)
  Pallas kernels  5.86 us (7%)
  other arithmetic  3.04 us (4%)
  local copies, waits for them, and re-layouts  2.6 us (3%)
  between operations  1.19 us (2%)
    ppermute x17, waiting for transfers between devices, dp_send(): return lax.ppermute(value, 'dp', pairs)  23.5 us
    ppermute x17, starting transfers between devices, dp_send(): return lax.ppermute(value, 'dp', pairs)  17.4 us
    ppermute x2, starting transfers between devices, local(): arrived = lax.ppermute(sent, 'ctx', swap_ctx)  4.34 us
    ppermute x2, starting transfers between devices, shifted(): lax.ppermute(value, axis, [(source, source + steps) for source in range(l...  4.05 us
    ppermute x2, waiting for transfers between devices, local(): late_keys = lax.ppermute(key_own, 'ctx', [(1, 0)])  3.91 us
    pallas_call x2, Pallas kernels, attend(): pl.pallas_call(partial(attention_kernel, hops, group, len(out_shapes)), g...  3.79 us
    ppermute x2, waiting for transfers between devices, local(): rest_away.append(lax.ppermute(rest, 'ctx', swap_ctx))  3.34 us
    ppermute x1, starting transfers between devices, local(): first_away = lax.ppermute(pieces[0], 'ctx', swap_ctx)  3.03 us
  transfers between devices with their start and end apart: 27, of which 14 were waited for; matrix products, arithmetic and copies ran while one was open for 4% of the time, Pallas kernels for 7%

profile of v3, /device:TPU:0, one launch (start us, length us, event | category | flops | bytes accessed | tf_op | source)
XLA Modules:
  0.0 78.3 jit_solution(3802988221715078769)
XLA Ops:
  0.8 1.4 %copy.26 = bf16[1,128,2688]{1,2,0:T(8,128)(2,1)S(1)} copy(bf16[1,128,2688]{2,1,0:T(8,128)(2,1)} %param.6) | data formatting | bytes 1376256 | tf_op args[0]
  2.3 3.0 %collective-permute-start.7 = (bf16[672,128]{1,0:T(8,128)(2,1)S(1)}, bf16[672,128]{1,0:T(8,128)(2,1)S(1)}, u32[]{:S(2)}, u32[]{:S(2)}) collective-permute-start(bf16[672,128]{1,0:T(8,128)(2,1)S(1)} %bitcast.37), channel_id=1, source_target_pairs={{0,1},{1,0},{2,3},{3,2},{4,5},{5,4},{6,7},{7,6},{8,9},{9,8},{10,11... | collective-permute-start | bytes 516104 | tf_op jit(solution)/shard_map/ppermute | solution.py:251
  5.5 2.7 %collective-permute-start = (bf16[144,1024]{1,0:T(8,128)(2,1)S(1)}, bf16[144,1024]{1,0:T(8,128)(2,1)S(1)}, u32[]{:S(2)}, u32[]{:S(2)}) collective-permute-start(bf16[144,1024]{1,0:T(8,128)(2,1)S(1)} %pad_maximum_fusion), channel_id=1, source_target_pairs={{0,1},{2,3},{4,5},{6,7},{8,9},{10,11},{12,13},{14,15},{16,17},{18,... | collective-permute-start | bytes 884744 | tf_op jit(solution)/shard_map/ppermute | solution.py:30
  8.3 1.3 %collective-permute-start.1 = (bf16[128,1024]{1,0:T(8,128)(2,1)S(1)}, bf16[128,1024]{1,0:T(8,128)(2,1)S(1)}, u32[]{:S(2)}, u32[]{:S(2)}) collective-permute-start(bf16[128,1024]{1,0:T(8,128)(2,1)S(1)} %pad_maximum_fusion.1), channel_id=1, source_target_pairs={{0,1},{2,3},{4,5},{6,7},{8,9},{10,11},{12,13},{14,15},{16,17},{18,... | collective-permute-start | bytes 786440 | tf_op jit(solution)/shard_map/ppermute | solution.py:30
  9.7 1.6 %collective-permute-start.3 = (bf16[672,128]{1,0:T(8,128)(2,1)S(1)}, bf16[672,128]{1,0:T(8,128)(2,1)S(1)}, u32[]{:S(2)}, u32[]{:S(2)}) collective-permute-start(bf16[672,128]{1,0:T(8,128)(2,1)S(1)} %bitcast.57), channel_id=1, source_target_pairs={{0,4},{2,6},{4,0},{6,2},{8,12},{10,14},{12,8},{14,10},{16,20},{18,... | collective-permute-start | bytes 516104 | tf_op jit(solution)/shard_map/ppermute | solution.py:192
  11.4 1.0 %collective-permute-start.4 = (bf16[672,128]{1,0:T(8,128)(2,1)S(1)}, bf16[672,128]{1,0:T(8,128)(2,1)S(1)}, u32[]{:S(2)}, u32[]{:S(2)}) collective-permute-start(bf16[672,128]{1,0:T(8,128)(2,1)S(1)} %bitcast.56), channel_id=1, source_target_pairs={{0,6},{2,4},{4,2},{6,0},{8,14},{10,12},{12,10},{14,8},{16,22},{18,... | collective-permute-start | bytes 516104 | tf_op jit(solution)/shard_map/ppermute | solution.py:192
  12.4 4.6 %collective-permute-done.3.refs_2_ = bf16[672,128]{1,0:T(8,128)(2,1)S(1)} collective-permute-done((bf16[672,128]{1,0:T(8,128)(2,1)S(1)}, bf16[672,128]{1,0:T(8,128)(2,1)S(1)}, u32[]{:S(2)}, u32[]{:S(2)}) %collective-permute-start.3) | collective-permute-done | bytes 172064 | tf_op jit(solution)/shard_map/ppermute | solution.py:192
  17.0 1.9 %shard_map.93 = (bf16[128,1024]{1,0:T(8,128)(2,1)S(1)}, bf16[128,512]{1,0:T(8,128)(2,1)S(1)}, bf16[128,512]{1,0:T(8,128)(2,1)S(1)}, bf16[128,512]{1,0:T(8,128)(2...) custom-call(s32[1]{0:T(128)} %bitcast.place_ref, s32[1,128]{1,0:T(1,128)S(1)} %copy-done.4, ...), custom_call_target="tpu_custom_call" | custom-call | flops 1024 | bytes 1024 | tf_op jit(solution)/shard_map/pallas_call | solution.py:112
  18.9 1.6 %collective-permute-start.5 = (bf16[128,512]{1,0:T(8,128)(2,1)S(1)}, bf16[128,512]{1,0:T(8,128)(2,1)S(1)}, u32[]{:S(2)}, u32[]{:S(2)}) collective-permute-start(bf16[128,512]{1,0:T(8,128)(2,1)S(1)} %get-tuple-element.42), channel_id=1, source_target_pairs={{0,1},{1,0},{2,3},{3,2},{4,5},{5,4},{6,7},{7,6},{8,9},{9,8},{10,11... | collective-permute-start | bytes 393224 | tf_op jit(solution)/shard_map/ppermute | solution.py:256
  20.6 1.3 %collective-permute-start.6 = (bf16[128,512]{1,0:T(8,128)(2,1)S(1)}, bf16[128,512]{1,0:T(8,128)(2,1)S(1)}, u32[]{:S(2)}, u32[]{:S(2)}) collective-permute-start(bf16[128,512]{1,0:T(8,128)(2,1)S(1)} %get-tuple-element.46), channel_id=1, source_target_pairs={{1,0},{3,2},{5,4},{7,6},{9,8},{11,10},{13,12},{15,14},{17,16},{19,... | collective-permute-start | bytes 393224 | tf_op jit(solution)/shard_map/ppermute | solution.py:257
  21.9 1.9 %shard_map.94 = (bf16[128,1024]{1,0:T(8,128)(2,1)S(1)}, bf16[128,512]{1,0:T(8,128)(2,1)S(1)}, bf16[128,512]{1,0:T(8,128)(2,1)S(1)}, bf16[128,512]{1,0:T(8,128)(2...) custom-call(s32[1]{0:T(128)} %bitcast.place_ref, s32[1,128]{1,0:T(1,128)S(1)} %copy-done.4, ...), custom_call_target="tpu_custom_call" | custom-call | flops 1024 | bytes 1024 | tf_op jit(solution)/shard_map/pallas_call | solution.py:112
  24.6 2.8 %collective-permute-done.6 = bf16[128,512]{1,0:T(8,128)(2,1)S(1)} collective-permute-done((bf16[128,512]{1,0:T(8,128)(2,1)S(1)}, bf16[128,512]{1,0:T(8,128)(2,1)S(1)}, u32[]{:S(2)}, u32[]{:S(2)}) %collective-permute-start.6) | collective-permute-done | bytes 131104 | tf_op jit(solution)/shard_map/ppermute | solution.py:257
  27.4 1.3 %collective-permute-start.14 = (bf16[128,512]{1,0:T(8,128)(2,1)S(1)}, bf16[128,512]{1,0:T(8,128)(2,1)S(1)}, u32[]{:S(2)}, u32[]{:S(2)}) collective-permute-start(bf16[128,512]{1,0:T(8,128)(2,1)S(1)} %get-tuple-element.63), channel_id=1, source_target_pairs={{1,0},{3,2},{5,4},{7,6},{9,8},{11,10},{13,12},{15,14},{17,16},{19,... | collective-permute-start | bytes 393224 | tf_op jit(solution)/shard_map/ppermute | solution.py:257
  28.7 2.7 %collective-permute-start.8 = (bf16[128,512]{1,0:T(8,128)(2,1)S(1)}, bf16[128,512]{1,0:T(8,128)(2,1)S(1)}, u32[]{:S(2)}, u32[]{:S(2)}) collective-permute-start(bf16[128,512]{1,0:T(8,128)(2,1)S(1)} %get-tuple-element.55), channel_id=1, source_target_pairs={{0,1},{1,0},{2,3},{3,2},{4,5},{5,4},{6,7},{7,6},{8,9},{9,8},{10,11... | collective-permute-start | bytes 393224 | tf_op jit(solution)/shard_map/ppermute | solution.py:256
  31.5 1.6 %collective-permute-start.11 = (bf16[256,512]{1,0:T(8,128)(2,1)S(1)}, bf16[256,512]{1,0:T(8,128)(2,1)S(1)}, u32[]{:S(2)}, u32[]{:S(2)}) collective-permute-start(bf16[256,512]{1,0:T(8,128)(2,1)S(1)} %pad_maximum_fusion.2.refs_6_), channel_id=1, source_target_pairs={{0,4},{2,6},{4,0},{6,2},{8,12},{10,14},{12,8},{14,10},{16,20},{18,... | collective-permute-start | bytes 786440 | tf_op jit(solution)/shard_map/ppermute | solution.py:192
  33.1 1.2 %collective-permute-done.14 = bf16[128,512]{1,0:T(8,128)(2,1)S(1)} collective-permute-done((bf16[128,512]{1,0:T(8,128)(2,1)S(1)}, bf16[128,512]{1,0:T(8,128)(2,1)S(1)}, u32[]{:S(2)}, u32[]{:S(2)}) %collective-permute-start.14) | collective-permute-done | bytes 131104 | tf_op jit(solution)/shard_map/ppermute | solution.py:257
  34.3 1.4 %collective-permute-done.8 = bf16[128,512]{1,0:T(8,128)(2,1)S(1)} collective-permute-done((bf16[128,512]{1,0:T(8,128)(2,1)S(1)}, bf16[128,512]{1,0:T(8,128)(2,1)S(1)}, u32[]{:S(2)}, u32[]{:S(2)}) %collective-permute-start.8) | collective-permute-done | bytes 131104 | tf_op jit(solution)/shard_map/ppermute | solution.py:256
  35.8 1.9 %collective-permute-start.16 = (bf16[256,512]{1,0:T(8,128)(2,1)S(1)}, bf16[256,512]{1,0:T(8,128)(2,1)S(1)}, u32[]{:S(2)}, u32[]{:S(2)}) collective-permute-start(bf16[256,512]{1,0:T(8,128)(2,1)S(1)} %pad_maximum_fusion.4.refs_6_), channel_id=1, source_target_pairs={{0,4},{2,6},{4,0},{6,2},{8,12},{10,14},{12,8},{14,10},{16,20},{18,... | collective-permute-start | bytes 786440 | tf_op jit(solution)/shard_map/ppermute | solution.py:192
  37.7 1.8 %collective-permute-done.11.refs_8_ = bf16[256,512]{1,0:T(8,128)(2,1)S(1)} collective-permute-done((bf16[256,512]{1,0:T(8,128)(2,1)S(1)}, bf16[256,512]{1,0:T(8,128)(2,1)S(1)}, u32[]{:S(2)}, u32[]{:S(2)}) %collective-permute-start.11) | collective-permute-done | bytes 262176 | tf_op jit(solution)/shard_map/ppermute | solution.py:192
  40.4 1.3 %collective-permute-done.9.refs_5_ = bf16[3,336,128]{2,1,0:T(8,128)(2,1)S(1)} collective-permute-done((bf16[3,336,128]{2,1,0:T(8,128)(2,1)S(1)}, bf16[3,336,128]{2,1,0:T(8,128)(2,1)S(1)}, u32[]{:S(2)}, u32[]{:S(2)}) %collective-permute-start.9) | collective-permute-done | bytes 258080 | tf_op jit(solution)/shard_map/ppermute | solution.py:270
  41.7 1.9 %collective-permute-done.16.refs_8_ = bf16[256,512]{1,0:T(8,128)(2,1)S(1)} collective-permute-done((bf16[256,512]{1,0:T(8,128)(2,1)S(1)}, bf16[256,512]{1,0:T(8,128)(2,1)S(1)}, u32[]{:S(2)}, u32[]{:S(2)}) %collective-permute-start.16) | collective-permute-done | bytes 262176 | tf_op jit(solution)/shard_map/ppermute | solution.py:192
  44.1 1.6 %collective-permute-start.19 = (bf16[336,256]{1,0:T(8,128)(2,1)S(1)}, bf16[336,256]{1,0:T(8,128)(2,1)S(1)}, u32[]{:S(2)}, u32[]{:S(2)}) collective-permute-start(bf16[336,256]{1,0:T(8,128)(2,1)S(1)} %get-tuple-element.67), channel_id=1, source_target_pairs={{0,8},{2,10},{4,12},{6,14},{8,0},{10,2},{12,4},{14,6},{16,24},{18,... | collective-permute-start | bytes 516104 | tf_op jit(solution)/shard_map/ppermute | solution.py:192
  47.0 2.0 %collective-permute-done.18.refs_5_ = bf16[3,336,128]{2,1,0:T(8,128)(2,1)S(1)} collective-permute-done((bf16[3,336,128]{2,1,0:T(8,128)(2,1)S(1)}, bf16[3,336,128]{2,1,0:T(8,128)(2,1)S(1)}, u32[]{:S(2)}, u32[]{:S(2)}) %collective-permute-start.18) | collective-permute-done | bytes 258080 | tf_op jit(solution)/shard_map/ppermute | solution.py:270
  49.0 1.3 %collective-permute-start.13 = (bf16[128,1024]{1,0:T(8,128)(2,1)S(1)}, bf16[128,1024]{1,0:T(8,128)(2,1)S(1)}, u32[]{:S(2)}, u32[]{:S(2)}) collective-permute-start(bf16[128,1024]{1,0:T(8,128)(2,1)S(1)} %pad_maximum_fusion.3), channel_id=1, source_target_pairs={{1,0},{3,2},{5,4},{7,6},{9,8},{11,10},{13,12},{15,14},{17,16},{19,... | collective-permute-start | bytes 786440 | tf_op jit(solution)/shard_map/ppermute | solution.py:319
  50.8 1.6 %collective-permute-start.25 = (bf16[336,256]{1,0:T(8,128)(2,1)S(1)}, bf16[336,256]{1,0:T(8,128)(2,1)S(1)}, u32[]{:S(2)}, u32[]{:S(2)}) collective-permute-start(bf16[336,256]{1,0:T(8,128)(2,1)S(1)} %get-tuple-element.77), channel_id=1, source_target_pairs={{0,8},{2,10},{4,12},{6,14},{8,0},{10,2},{12,4},{14,6},{16,24},{18,... | collective-permute-start | bytes 516104 | tf_op jit(solution)/shard_map/ppermute | solution.py:192
  54.1 2.7 %collective-permute-start.20 = (bf16[168,256]{1,0:T(8,128)(2,1)S(1)}, bf16[168,256]{1,0:T(8,128)(2,1)S(1)}, u32[]{:S(2)}, u32[]{:S(2)}) collective-permute-start(bf16[168,256]{1,0:T(8,128)(2,1)S(1)} %slice.122), channel_id=1, source_target_pairs={{0,16},{2,18},{4,20},{6,22},{8,24},{10,26},{12,28},{14,30},{16,0},... | collective-permute-start | bytes 258056 | tf_op jit(solution)/shard_map/ppermute | solution.py:192
  56.8 1.0 %collective-permute-start.22 = (bf16[168,256]{1,0:T(8,128)(2,1)S(1)}, bf16[168,256]{1,0:T(8,128)(2,1)S(1)}, u32[]{:S(2)}, u32[]{:S(2)}) collective-permute-start(bf16[168,256]{1,0:T(8,128)(2,1)S(1)} %slice.121), channel_id=1, source_target_pairs={{0,16},{2,18},{4,20},{6,22},{8,24},{10,26},{12,28},{14,30},{16,0},... | collective-permute-start | bytes 258056 | tf_op jit(solution)/shard_map/ppermute | solution.py:192
  57.7 5.6 %collective-permute-done.20 = bf16[168,256]{1,0:T(8,128)(2,1)S(1)} collective-permute-done((bf16[168,256]{1,0:T(8,128)(2,1)S(1)}, bf16[168,256]{1,0:T(8,128)(2,1)S(1)}, u32[]{:S(2)}, u32[]{:S(2)}) %collective-permute-start.20) | collective-permute-done | bytes 86048 | tf_op jit(solution)/shard_map/ppermute | solution.py:192
  63.4 1.4 %collective-permute-done.22 = bf16[168,256]{1,0:T(8,128)(2,1)S(1)} collective-permute-done((bf16[168,256]{1,0:T(8,128)(2,1)S(1)}, bf16[168,256]{1,0:T(8,128)(2,1)S(1)}, u32[]{:S(2)}, u32[]{:S(2)}) %collective-permute-start.22) | collective-permute-done | bytes 86048 | tf_op jit(solution)/shard_map/ppermute | solution.py:192
  65.8 3.4 %collective-permute-start.24 = (bf16[168,256]{1,0:T(8,128)(2,1)S(1)}, bf16[168,256]{1,0:T(8,128)(2,1)S(1)}, u32[]{:S(2)}, u32[]{:S(2)}) collective-permute-start(bf16[168,256]{1,0:T(8,128)(2,1)S(1)} %slice.120), channel_id=1, source_target_pairs={{0,16},{2,18},{4,20},{6,22},{8,24},{10,26},{12,28},{14,30},{16,0},... | collective-permute-start | bytes 258056 | tf_op jit(solution)/shard_map/ppermute | solution.py:192
  69.3 2.5 %collective-permute-done.24 = bf16[168,256]{1,0:T(8,128)(2,1)S(1)} collective-permute-done((bf16[168,256]{1,0:T(8,128)(2,1)S(1)}, bf16[168,256]{1,0:T(8,128)(2,1)S(1)}, u32[]{:S(2)}, u32[]{:S(2)}) %collective-permute-start.24) | collective-permute-done | bytes 86048 | tf_op jit(solution)/shard_map/ppermute | solution.py:192
  71.8 5.6 %collective-permute-done.26 = bf16[168,256]{1,0:T(8,128)(2,1)S(1)} collective-permute-done((bf16[168,256]{1,0:T(8,128)(2,1)S(1)}, bf16[168,256]{1,0:T(8,128)(2,1)S(1)}, u32[]{:S(2)}, u32[]{:S(2)}) %collective-permute-start.26) | collective-permute-done | bytes 86048 | tf_op jit(solution)/shard_map/ppermute | solution.py:192
  (78 shorter events, 8.3 us)
Async XLA Ops:
  2.2 3.2 %copy-start.1 = (bf16[1,128,1024]{2,1,0:T(8,128)(2,1)S(1)}, bf16[1,128,1024]{2,1,0:T(8,128)(2,1)}, u32[]{:S(2)}) copy-start(bf16[1,128,1024]{2,1,0:T(8,128)(2,1)} %param.9) | copy-start | bytes 786436
  2.3 3.1 %copy-start = (bf16[1,128,1024]{2,1,0:T(8,128)(2,1)S(1)}, bf16[1,128,1024]{2,1,0:T(8,128)(2,1)}, u32[]{:S(2)}) copy-start(bf16[1,128,1024]{2,1,0:T(8,128)(2,1)} %param.8) | copy-start | bytes 786436
  2.3 3.0 %copy-start.4 = (s32[1,128]{1,0:T(1,128)S(1)}, s32[1,128]{1,0:T(1,128)}, u32[]{:S(2)}) copy-start(s32[1,128]{1,0:T(1,128)} %refs_0_.3) | copy-start | bytes 1540
  2.3 21.5 %collective-permute-start.7 = (bf16[672,128]{1,0:T(8,128)(2,1)S(1)}, bf16[672,128]{1,0:T(8,128)(2,1)S(1)}, u32[]{:S(2)}, u32[]{:S(2)}) collective-permute-start(bf16[672,128]{1,0:T(8,128)(2,1)S(1)} %bitcast.37), channel_id=1, source_target_pairs={{0,1},{1,0},{2,3},{3,2},{4,5},{5,4},{6,7},{7,6},{8,9},{9,8},{10,11... | collective-permute-start | bytes 516104 | tf_op jit(solution)/shard_map/ppermute | solution.py:251
  5.5 11.5 %collective-permute-start = (bf16[144,1024]{1,0:T(8,128)(2,1)S(1)}, bf16[144,1024]{1,0:T(8,128)(2,1)S(1)}, u32[]{:S(2)}, u32[]{:S(2)}) collective-permute-start(bf16[144,1024]{1,0:T(8,128)(2,1)S(1)} %pad_maximum_fusion), channel_id=1, source_target_pairs={{0,1},{2,3},{4,5},{6,7},{8,9},{10,11},{12,13},{14,15},{16,17},{18,... | collective-permute-start | bytes 884744 | tf_op jit(solution)/shard_map/ppermute | solution.py:30
  8.3 13.7 %collective-permute-start.1 = (bf16[128,1024]{1,0:T(8,128)(2,1)S(1)}, bf16[128,1024]{1,0:T(8,128)(2,1)S(1)}, u32[]{:S(2)}, u32[]{:S(2)}) collective-permute-start(bf16[128,1024]{1,0:T(8,128)(2,1)S(1)} %pad_maximum_fusion.1), channel_id=1, source_target_pairs={{0,1},{2,3},{4,5},{6,7},{8,9},{10,11},{12,13},{14,15},{16,17},{18,... | collective-permute-start | bytes 786440 | tf_op jit(solution)/shard_map/ppermute | solution.py:30
  9.6 1.7 %collective-permute-start.2 = (bf16[672,128]{1,0:T(8,128)(2,1)S(1)}, bf16[672,128]{1,0:T(8,128)(2,1)S(1)}, u32[]{:S(2)}, u32[]{:S(2)}) collective-permute-start(bf16[672,128]{1,0:T(8,128)(2,1)S(1)} %bitcast.58), channel_id=1, source_target_pairs={{0,2},{2,0},{4,6},{6,4},{8,10},{10,8},{12,14},{14,12},{16,18},{18,... | collective-permute-start | bytes 516104 | tf_op jit(solution)/shard_map/ppermute | solution.py:192
  9.7 7.2 %collective-permute-start.3 = (bf16[672,128]{1,0:T(8,128)(2,1)S(1)}, bf16[672,128]{1,0:T(8,128)(2,1)S(1)}, u32[]{:S(2)}, u32[]{:S(2)}) collective-permute-start(bf16[672,128]{1,0:T(8,128)(2,1)S(1)} %bitcast.57), channel_id=1, source_target_pairs={{0,4},{2,6},{4,0},{6,2},{8,12},{10,14},{12,8},{14,10},{16,20},{18,... | collective-permute-start | bytes 516104 | tf_op jit(solution)/shard_map/ppermute | solution.py:192
  11.3 5.7 %copy-start.3 = (bf16[1,128,2048]{2,1,0:T(8,128)(2,1)S(1)}, bf16[1,128,2048]{2,1,0:T(8,128)(2,1)}, u32[]{:S(2)}) copy-start(bf16[1,128,2048]{2,1,0:T(8,128)(2,1)} %param.10) | copy-start | bytes 1572868
  11.3 5.7 %copy-start.2 = (bf16[1,128,2048]{2,1,0:T(8,128)(2,1)S(1)}, bf16[1,128,2048]{2,1,0:T(8,128)(2,1)}, u32[]{:S(2)}) copy-start(bf16[1,128,2048]{2,1,0:T(8,128)(2,1)} %param.7) | copy-start | bytes 1572868
  11.4 10.5 %collective-permute-start.4 = (bf16[672,128]{1,0:T(8,128)(2,1)S(1)}, bf16[672,128]{1,0:T(8,128)(2,1)S(1)}, u32[]{:S(2)}, u32[]{:S(2)}) collective-permute-start(bf16[672,128]{1,0:T(8,128)(2,1)S(1)} %bitcast.56), channel_id=1, source_target_pairs={{0,6},{2,4},{4,2},{6,0},{8,14},{10,12},{12,10},{14,8},{16,22},{18,... | collective-permute-start | bytes 516104 | tf_op jit(solution)/shard_map/ppermute | solution.py:192
  18.9 5.7 %collective-permute-start.5 = (bf16[128,512]{1,0:T(8,128)(2,1)S(1)}, bf16[128,512]{1,0:T(8,128)(2,1)S(1)}, u32[]{:S(2)}, u32[]{:S(2)}) collective-permute-start(bf16[128,512]{1,0:T(8,128)(2,1)S(1)} %get-tuple-element.42), channel_id=1, source_target_pairs={{0,1},{1,0},{2,3},{3,2},{4,5},{5,4},{6,7},{7,6},{8,9},{9,8},{10,11... | collective-permute-start | bytes 393224 | tf_op jit(solution)/shard_map/ppermute | solution.py:256
  20.6 6.8 %collective-permute-start.6 = (bf16[128,512]{1,0:T(8,128)(2,1)S(1)}, bf16[128,512]{1,0:T(8,128)(2,1)S(1)}, u32[]{:S(2)}, u32[]{:S(2)}) collective-permute-start(bf16[128,512]{1,0:T(8,128)(2,1)S(1)} %get-tuple-element.46), channel_id=1, source_target_pairs={{1,0},{3,2},{5,4},{7,6},{9,8},{11,10},{13,12},{15,14},{17,16},{19,... | collective-permute-start | bytes 393224 | tf_op jit(solution)/shard_map/ppermute | solution.py:257
  27.4 6.8 %collective-permute-start.14 = (bf16[128,512]{1,0:T(8,128)(2,1)S(1)}, bf16[128,512]{1,0:T(8,128)(2,1)S(1)}, u32[]{:S(2)}, u32[]{:S(2)}) collective-permute-start(bf16[128,512]{1,0:T(8,128)(2,1)S(1)} %get-tuple-element.63), channel_id=1, source_target_pairs={{1,0},{3,2},{5,4},{7,6},{9,8},{11,10},{13,12},{15,14},{17,16},{19,... | collective-permute-start | bytes 393224 | tf_op jit(solution)/shard_map/ppermute | solution.py:257
  28.7 7.0 %collective-permute-start.8 = (bf16[128,512]{1,0:T(8,128)(2,1)S(1)}, bf16[128,512]{1,0:T(8,128)(2,1)S(1)}, u32[]{:S(2)}, u32[]{:S(2)}) collective-permute-start(bf16[128,512]{1,0:T(8,128)(2,1)S(1)} %get-tuple-element.55), channel_id=1, source_target_pairs={{0,1},{1,0},{2,3},{3,2},{4,5},{5,4},{6,7},{7,6},{8,9},{9,8},{10,11... | collective-permute-start | bytes 393224 | tf_op jit(solution)/shard_map/ppermute | solution.py:256
  31.5 8.0 %collective-permute-start.11 = (bf16[256,512]{1,0:T(8,128)(2,1)S(1)}, bf16[256,512]{1,0:T(8,128)(2,1)S(1)}, u32[]{:S(2)}, u32[]{:S(2)}) collective-permute-start(bf16[256,512]{1,0:T(8,128)(2,1)S(1)} %pad_maximum_fusion.2.refs_6_), channel_id=1, source_target_pairs={{0,4},{2,6},{4,0},{6,2},{8,12},{10,14},{12,8},{14,10},{16,20},{18,... | collective-permute-start | bytes 786440 | tf_op jit(solution)/shard_map/ppermute | solution.py:192
  33.1 10.5 %collective-permute-start.10 = (bf16[256,512]{1,0:T(8,128)(2,1)S(1)}, bf16[256,512]{1,0:T(8,128)(2,1)S(1)}, u32[]{:S(2)}, u32[]{:S(2)}) collective-permute-start(bf16[256,512]{1,0:T(8,128)(2,1)S(1)} %pad_maximum_fusion.2.refs_6_), channel_id=1, source_target_pairs={{0,2},{2,0},{4,6},{6,4},{8,10},{10,8},{12,14},{14,12},{16,18},{18,... | collective-permute-start | bytes 786440 | tf_op jit(solution)/shard_map/ppermute | solution.py:192
  33.1 8.6 %collective-permute-start.9 = (bf16[3,336,128]{2,1,0:T(8,128)(2,1)S(1)}, bf16[3,336,128]{2,1,0:T(8,128)(2,1)S(1)}, u32[]{:S(2)}, u32[]{:S(2)}) collective-permute-start(bf16[3,336,128]{2,1,0:T(8,128)(2,1)S(1)} %get-tuple-element.60), channel_id=1, source_target_pairs={{0,1},{1,0},{2,3},{3,2},{4,5},{5,4},{6,7},{7,6},{8,9},{9,8},{10,11... | collective-permute-start | bytes 774152 | tf_op jit(solution)/shard_map/ppermute | solution.py:270
  35.8 7.8 %collective-permute-start.16 = (bf16[256,512]{1,0:T(8,128)(2,1)S(1)}, bf16[256,512]{1,0:T(8,128)(2,1)S(1)}, u32[]{:S(2)}, u32[]{:S(2)}) collective-permute-start(bf16[256,512]{1,0:T(8,128)(2,1)S(1)} %pad_maximum_fusion.4.refs_6_), channel_id=1, source_target_pairs={{0,4},{2,6},{4,0},{6,2},{8,12},{10,14},{12,8},{14,10},{16,20},{18,... | collective-permute-start | bytes 786440 | tf_op jit(solution)/shard_map/ppermute | solution.py:192
  39.5 4.1 %collective-permute-start.12 = (bf16[256,512]{1,0:T(8,128)(2,1)S(1)}, bf16[256,512]{1,0:T(8,128)(2,1)S(1)}, u32[]{:S(2)}, u32[]{:S(2)}) collective-permute-start(bf16[256,512]{1,0:T(8,128)(2,1)S(1)} %collective-permute-done.11.refs_8_), channel_id=1, source_target_pairs={{0,2},{2,0},{4,6},{6,4},{8,10},{10,8},{12,14},{14,12},{16,18},{18,... | collective-permute-start | bytes 786440 | tf_op jit(solution)/shard_map/ppermute | solution.py:192
  40.4 8.6 %collective-permute-start.18 = (bf16[3,336,128]{2,1,0:T(8,128)(2,1)S(1)}, bf16[3,336,128]{2,1,0:T(8,128)(2,1)S(1)}, u32[]{:S(2)}, u32[]{:S(2)}) collective-permute-start(bf16[3,336,128]{2,1,0:T(8,128)(2,1)S(1)} %get-tuple-element.64), channel_id=1, source_target_pairs={{0,1},{1,0},{2,3},{3,2},{4,5},{5,4},{6,7},{7,6},{8,9},{9,8},{10,11... | collective-permute-start | bytes 774152 | tf_op jit(solution)/shard_map/ppermute | solution.py:270
  41.7 8.6 %collective-permute-start.15 = (bf16[256,512]{1,0:T(8,128)(2,1)S(1)}, bf16[256,512]{1,0:T(8,128)(2,1)S(1)}, u32[]{:S(2)}, u32[]{:S(2)}) collective-permute-start(bf16[256,512]{1,0:T(8,128)(2,1)S(1)} %pad_maximum_fusion.4.refs_6_), channel_id=1, source_target_pairs={{0,2},{2,0},{4,6},{6,4},{8,10},{10,8},{12,14},{14,12},{16,18},{18,... | collective-permute-start | bytes 786440 | tf_op jit(solution)/shard_map/ppermute | solution.py:192
  43.6 6.7 %collective-permute-start.17 = (bf16[256,512]{1,0:T(8,128)(2,1)S(1)}, bf16[256,512]{1,0:T(8,128)(2,1)S(1)}, u32[]{:S(2)}, u32[]{:S(2)}) collective-permute-start(bf16[256,512]{1,0:T(8,128)(2,1)S(1)} %collective-permute-done.16.refs_8_), channel_id=1, source_target_pairs={{0,2},{2,0},{4,6},{6,4},{8,10},{10,8},{12,14},{14,12},{16,18},{18,... | collective-permute-start | bytes 786440 | tf_op jit(solution)/shard_map/ppermute | solution.py:192
  44.1 9.9 %collective-permute-start.19 = (bf16[336,256]{1,0:T(8,128)(2,1)S(1)}, bf16[336,256]{1,0:T(8,128)(2,1)S(1)}, u32[]{:S(2)}, u32[]{:S(2)}) collective-permute-start(bf16[336,256]{1,0:T(8,128)(2,1)S(1)} %get-tuple-element.67), channel_id=1, source_target_pairs={{0,8},{2,10},{4,12},{6,14},{8,0},{10,2},{12,4},{14,6},{16,24},{18,... | collective-permute-start | bytes 516104 | tf_op jit(solution)/shard_map/ppermute | solution.py:192
  46.5 10.2 %collective-permute-start.21 = (bf16[336,256]{1,0:T(8,128)(2,1)S(1)}, bf16[336,256]{1,0:T(8,128)(2,1)S(1)}, u32[]{:S(2)}, u32[]{:S(2)}) collective-permute-start(bf16[336,256]{1,0:T(8,128)(2,1)S(1)} %get-tuple-element.69), channel_id=1, source_target_pairs={{0,8},{2,10},{4,12},{6,14},{8,0},{10,2},{12,4},{14,6},{16,24},{18,... | collective-permute-start | bytes 516104 | tf_op jit(solution)/shard_map/ppermute | solution.py:192
  49.0 15.8 %collective-permute-start.13 = (bf16[128,1024]{1,0:T(8,128)(2,1)S(1)}, bf16[128,1024]{1,0:T(8,128)(2,1)S(1)}, u32[]{:S(2)}, u32[]{:S(2)}) collective-permute-start(bf16[128,1024]{1,0:T(8,128)(2,1)S(1)} %pad_maximum_fusion.3), channel_id=1, source_target_pairs={{1,0},{3,2},{5,4},{7,6},{9,8},{11,10},{13,12},{15,14},{17,16},{19,... | collective-permute-start | bytes 786440 | tf_op jit(solution)/shard_map/ppermute | solution.py:319
  50.8 18.3 %collective-permute-start.25 = (bf16[336,256]{1,0:T(8,128)(2,1)S(1)}, bf16[336,256]{1,0:T(8,128)(2,1)S(1)}, u32[]{:S(2)}, u32[]{:S(2)}) collective-permute-start(bf16[336,256]{1,0:T(8,128)(2,1)S(1)} %get-tuple-element.77), channel_id=1, source_target_pairs={{0,8},{2,10},{4,12},{6,14},{8,0},{10,2},{12,4},{14,6},{16,24},{18,... | collective-permute-start | bytes 516104 | tf_op jit(solution)/shard_map/ppermute | solution.py:192
  52.5 13.2 %collective-permute-start.23 = (bf16[336,256]{1,0:T(8,128)(2,1)S(1)}, bf16[336,256]{1,0:T(8,128)(2,1)S(1)}, u32[]{:S(2)}, u32[]{:S(2)}) collective-permute-start(bf16[336,256]{1,0:T(8,128)(2,1)S(1)} %get-tuple-element.75), channel_id=1, source_target_pairs={{0,8},{2,10},{4,12},{6,14},{8,0},{10,2},{12,4},{14,6},{16,24},{18,... | collective-permute-start | bytes 516104 | tf_op jit(solution)/shard_map/ppermute | solution.py:192
  54.1 9.3 %collective-permute-start.20 = (bf16[168,256]{1,0:T(8,128)(2,1)S(1)}, bf16[168,256]{1,0:T(8,128)(2,1)S(1)}, u32[]{:S(2)}, u32[]{:S(2)}) collective-permute-start(bf16[168,256]{1,0:T(8,128)(2,1)S(1)} %slice.122), channel_id=1, source_target_pairs={{0,16},{2,18},{4,20},{6,22},{8,24},{10,26},{12,28},{14,30},{16,0},... | collective-permute-start | bytes 258056 | tf_op jit(solution)/shard_map/ppermute | solution.py:192
  56.8 8.0 %collective-permute-start.22 = (bf16[168,256]{1,0:T(8,128)(2,1)S(1)}, bf16[168,256]{1,0:T(8,128)(2,1)S(1)}, u32[]{:S(2)}, u32[]{:S(2)}) collective-permute-start(bf16[168,256]{1,0:T(8,128)(2,1)S(1)} %slice.121), channel_id=1, source_target_pairs={{0,16},{2,18},{4,20},{6,22},{8,24},{10,26},{12,28},{14,30},{16,0},... | collective-permute-start | bytes 258056 | tf_op jit(solution)/shard_map/ppermute | solution.py:192
  65.8 6.0 %collective-permute-start.24 = (bf16[168,256]{1,0:T(8,128)(2,1)S(1)}, bf16[168,256]{1,0:T(8,128)(2,1)S(1)}, u32[]{:S(2)}, u32[]{:S(2)}) collective-permute-start(bf16[168,256]{1,0:T(8,128)(2,1)S(1)} %slice.120), channel_id=1, source_target_pairs={{0,16},{2,18},{4,20},{6,22},{8,24},{10,26},{12,28},{14,30},{16,0},... | collective-permute-start | bytes 258056 | tf_op jit(solution)/shard_map/ppermute | solution.py:192
  69.2 8.2 %collective-permute-start.26 = (bf16[168,256]{1,0:T(8,128)(2,1)S(1)}, bf16[168,256]{1,0:T(8,128)(2,1)S(1)}, u32[]{:S(2)}, u32[]{:S(2)}) collective-permute-start(bf16[168,256]{1,0:T(8,128)(2,1)S(1)} %slice.119), channel_id=1, source_target_pairs={{0,16},{2,18},{4,20},{6,22},{8,24},{10,26},{12,28},{14,30},{16,0},... | collective-permute-start | bytes 258056 | tf_op jit(solution)/shard_map/ppermute | solution.py:192
  (1 other events, 0.9 us)

commit v4 on v3

--- a/solution.py
+++ b/solution.py
@@ -1,3 +1,4 @@
+import math
 from functools import partial
 
 import jax
@@ -10,7 +11,6 @@
 HD = 128
 WIN = 1024
 CHUNKS = 2
-SPLIT = 2
 SCORE_FLOOR = -1e30
 MIB = 1024 * 1024
 SEG_ROWS = 16
@@ -126,41 +126,39 @@
             out_specs=[whole(*shape) for shape in out_shapes],
         ),
         out_shape=[jax.ShapeDtypeStruct(shape, jnp.bfloat16) for shape in out_shapes],
-        compiler_params=pltpu.CompilerParams(vmem_limit_bytes=48 * MIB),
+        compiler_params=pltpu.CompilerParams(vmem_limit_bytes=24 * MIB),
         cost_estimate=SMALL,
     )(*operands)
 
 
-def product_kernel(traces, *refs):
-    own_refs, first_ref, rest_ref = refs[:traces], refs[traces], refs[traces + 1]
-    grad_refs = refs[traces + 2 : 2 * traces + 2]
-    outs = refs[2 * traces + 2 :]
-    away = [first_ref[...]] + [rest_ref[t] for t in range(traces - 1)]
-    features = jnp.concatenate(
-        [piece for t in range(traces) for piece in (own_refs[t][...], away[t])], axis=1
-    )
-    grads = jnp.concatenate([ref[...] for ref in grad_refs], axis=0)
-    width = outs[0].shape[1]
-    for n, out in enumerate(outs):
-        out[...] = dot_f32(features, grads[:, n * width : (n + 1) * width]).astype(out.dtype)
-
-
-def product(half, own, first_away, rest_away, grads, dtype):
-    traces, (rows, tok) = len(own), own[0].shape
-    rows //= 2
-    width = grads[0].shape[1] // SPLIT
-    half_of = lambda array: pl.BlockSpec((rows, array.shape[1]), lambda i: (half, 0))
-    whole = lambda array: pl.BlockSpec(array.shape, lambda i: (0,) * array.ndim)
+def product_kernel(*refs):
+    grad_refs, (send_ref, keep_ref) = refs[4:-2], refs[-2:]
+    grads = jnp.concatenate([ref[t] for ref in grad_refs for t in range(ref.shape[0])], axis=0)
+    rows = send_ref.shape[1]
+    for core in range(2):
+        near, far = refs[2 * core : 2 * core + 2]
+        features = jnp.concatenate(
+            [ref[t ^ core] for t in range(near.shape[0]) for ref in (near, far)], axis=1
+        )
+        total = dot_f32(features, grads)
+        send_ref[core] = total[:rows].astype(jnp.bfloat16)
+        keep_ref[core] = total[rows:]
+
+
+def product(mine, other, grads):
+    rows = mine[0].shape[1] // 2
+    width = grads[0].shape[2]
+    shape = (2, rows, width)
+    moved = sum(math.prod(array.shape) for array in (*mine, *other, *grads)) * 2
     return pl.pallas_call(
-        partial(product_kernel, traces),
-        grid=(1,),
-        in_specs=[half_of(piece) for piece in (*own, first_away)]
-        + [whole(piece) for piece in (rest_away, *grads)],
-        out_specs=[pl.BlockSpec((rows, width), lambda i: (0, 0))] * SPLIT,
-        out_shape=[jax.ShapeDtypeStruct((rows, width), dtype)] * SPLIT,
-        compiler_params=pltpu.CompilerParams(vmem_limit_bytes=48 * MIB),
+        product_kernel,
+        out_shape=[
+            jax.ShapeDtypeStruct(shape, jnp.bfloat16),
+            jax.ShapeDtypeStruct(shape, jnp.float32),
+        ],
+        compiler_params=pltpu.CompilerParams(vmem_limit_bytes=8 * MIB + 4 * moved),
         cost_estimate=SMALL,
-    )(*own, first_away, rest_away, *grads)
+    )(*mine, *other, *grads)
 
 
 def local(hidden_in, queries, key_states, value_states, out_grad, segment_ids):
@@ -201,32 +199,34 @@
     steps = range(hops, 0, -1)
     seg_rows = jnp.broadcast_to(segment_ids.astype(jnp.bfloat16), (SEG_ROWS, tok))
     seg_rows = jnp.pad(seg_rows, ((0, 0), (0, 2 * width - tok)))
-    rim_pairs = []
+    pairs = []
     for chunk in range(CHUNKS):
         cols = slice(chunk * width, (chunk + 1) * width)
         pair = jnp.concatenate([own_keys[:, cols], own_values[:, cols]], axis=1)
-        if chunk == 0:
-            pair = jnp.concatenate([pair, seg_rows], axis=0)
-        rim_pairs.append([shifted(pair, "ctx", step) for step in steps])
+        pairs.append(pair if chunk else jnp.concatenate([pair, seg_rows], axis=0))
+    pairs, hidden = lax.optimization_barrier((pairs, hidden_in[0]))
+    rim_pairs = [[shifted(pair, "ctx", step) for step in steps] for pair in pairs]
 
     rows = hidden_in.shape[2] // dp_count
-    by_feature = hidden_in[0].T.reshape(slow_count, mid_count, core_count, rows, tok)
-    pieces = []
+    by_feature = hidden.T.reshape(slow_count, mid_count, core_count, rows, tok)
+
+    def share_of(step, turn):
+        blocks = [
+            lax.dynamic_slice(
+                by_feature,
+                (slow_at ^ turn ^ further, (mid_at + step) % mid_count, 0, 0, 0),
+                (1, 1, core_count, rows, tok),
+            )
+            for further in (2, 0)
+        ]
+        return jnp.concatenate(blocks, axis=3).reshape(core_count, 2 * rows, tok)
+
+    shares = []
     for step in range(mid_count):
-        for flip in range(core_count):
-            share = lax.dynamic_slice(
-                by_feature,
-                (0, (mid_at + step) % mid_count, core_at ^ flip, 0, 0),
-                (slow_count, 1, 1, rows, tok),
-            )
-            share = jnp.concatenate(
-                [lax.dynamic_index_in_dim(share, slow_at ^ turn, 0) for turn in (3, 1, 2, 0)]
-            ).reshape(slow_count * rows, tok)
-            away = lambda slow, mid, core: (slow, (mid + step) % mid_count, core ^ flip)
-            pieces.append(share if step == flip == 0 else dp_send(share, away))
-
-    half_rows = slow_count // 2 * rows
-    low_high = [(0, half_rows), (half_rows, 2 * half_rows)]
+        for turn in (0, 1):
+            away = lambda slow, mid, core: (slow ^ turn, (mid + step) % mid_count, core)
+            share = share_of(step, turn)
+            shares.append(dp_send(share, away) if step or turn else share)
 
     attended = []
     for chunk in range(CHUNKS):
@@ -246,28 +246,29 @@
             )
         )
     query_grad = jnp.concatenate([outs[0] for outs in attended], axis=1)
+    shares = jnp.stack(shares)
+    of_core = lambda core: lax.dynamic_index_in_dim(shares, core, 1, False)
+    near = jnp.stack([of_core(core_at), dp_send(of_core(1 - core_at), swap_core)], axis=1)
+    near = near.reshape(-1, 2 * rows, tok)
 
     if ctx_count == 2:
-        first_away = lax.ppermute(pieces[0], "ctx", swap_ctx)
-        columns, rest_away = [], []
+        columns = []
         for chunk, (_, sent, addend, key_own, value_own, _) in enumerate(attended):
             if chunk > 0:
                 sent, key_own, _ = lax.optimization_barrier((sent, key_own, arrived))
             arrived = lax.ppermute(sent, "ctx", swap_ctx)
             late_keys = lax.ppermute(key_own, "ctx", [(1, 0)])
             if chunk == 0:
-                arrived, late_keys, first_away, *_ = lax.optimization_barrier(
-                    (arrived, late_keys, first_away, rim_pairs[1:])
+                arrived, late_keys, _ = lax.optimization_barrier(
+                    (arrived, late_keys, rim_pairs[1:])
                 )
             total = (addend.astype(jnp.float32) + arrived.astype(jnp.float32)).astype(jnp.bfloat16)
             block = jnp.concatenate(
                 [jnp.where(first, total, value_own), jnp.where(first, late_keys, total)], axis=0
             )
             if chunk == 0:
-                for low, high in low_high:
-                    rest = jnp.stack([piece[low:high] for piece in pieces[1:]])
-                    rest, block = lax.optimization_barrier((rest, block))
-                    rest_away.append(lax.ppermute(rest, "ctx", swap_ctx))
+                sent_near, block = lax.optimization_barrier((near, block))
+                far = lax.ppermute(sent_near, "ctx", swap_ctx)
             columns.append(block)
         key_grad = jnp.where(
             first,
@@ -293,26 +294,27 @@
             tiled=True,
         )
         columns = jnp.split(both, CHUNKS, axis=1)
-        every = lax.all_gather(jnp.stack(pieces), "ctx", axis=2, tiled=True)
-        near, away = jnp.split(every, 2, axis=2)
-        pieces, first_away = list(near), away[0]
-        rest_away = [away[1:, low:high] for low, high in low_high]
-
-    gathered = []
-    for block in columns:
-        near = [block] + [dp_send(block, mid_by(step)) for step in range(1, mid_count)]
-        gathered.append(
-            [piece for near_one in near for piece in (near_one, dp_send(near_one, swap_core))]
-        )
-    gathered[-1], rest_away[1] = lax.optimization_barrier((gathered[-1], rest_away[1]))
-    sent, kept = (
-        [
-            piece
-            for grads in gathered
-            for piece in product(half, pieces, first_away, rest_away[half], grads, dtype)
-        ]
-        for half, dtype in ((0, jnp.bfloat16), (1, jnp.float32))
-    )
+        every = lax.all_gather(near, "ctx", axis=2, tiled=True)
+        near, far = jnp.split(every, 2, axis=2)
+
+    mine = [near, far]
+    other = [dp_send(piece, swap_core) for piece in mine]
+    sent, kept = [], []
+    for chunk, block in enumerate(columns):
+        cols = block.shape[1] // core_count
+        of_core = lambda core: lax.dynamic_slice_in_dim(block, core * cols, cols, 1)
+        block = jnp.stack([of_core(core_at), dp_send(of_core(1 - core_at), swap_core)])
+        steps = range(1, mid_count)
+        turned = dp_send(block, flip_slow(1))
+        moved = [dp_send(block, mid_by(step)) for step in steps]
+        if chunk % 2 == 0:
+            both = [dp_send(turned, mid_by(step)) for step in steps]
+        else:
+            both = [dp_send(piece, flip_slow(1)) for piece in moved]
+        grads = [block, turned] + [piece for pair in zip(moved, both) for piece in pair]
+        for parts, part in zip((sent, kept), product(mine, other, grads)):
+            parts.append(part)
+
     if ctx_count == 2:
         value_rim = jnp.concatenate([outs[5] for outs in attended], axis=1)
         value_rim, sent[0] = lax.optimization_barrier((value_rim, sent[0]))
@@ -321,16 +323,18 @@
         value_grad = (value_own.astype(jnp.float32) + returned.astype(jnp.float32)).astype(
             jnp.bfloat16
         )
-    halves = [
-        near + dp_send(far, flip_slow(1)).astype(jnp.float32) for near, far in zip(kept, sent)
+    totals = [
+        near + dp_send(far, flip_slow(2)).astype(jnp.float32) for near, far in zip(kept, sent)
     ]
-    last = [dp_send(half[:rows].astype(jnp.bfloat16), flip_slow(2)) for half in halves]
-    piece_width = halves[0].shape[1]
-    weight_grad = jnp.zeros((rows, piece_width * len(halves)), jnp.float32)
-    for n, (half, final) in enumerate(zip(halves, last)):
-        weight_grad = lax.dynamic_update_slice(
-            weight_grad, half[rows:] + final.astype(jnp.float32), (0, n * piece_width)
-        )
+    finals = [(total[0], dp_send(total[1], swap_core)) for total in totals]
+    weight_grad = jnp.concatenate(
+        [
+            jnp.where(core_at == at, mine, theirs)
+            for mine, theirs in finals
+            for at in range(core_count)
+        ],
+        axis=1,
+    )
     return (query_grad[None], key_grad[None], value_grad[None], weight_grad)
 
 

time: 78.5 us -> 96.5 us (1.23)
  waiting for transfers between devices: 32.9 us -> 42.5 us
  other arithmetic: 3.04 us -> 9.43 us
  local copies, waits for them, and re-layouts: 2.6 us -> 4.69 us
    ppermute x3 -> x1, waiting for transfers between devices: 3.34 us -> 8.6 us  [local(): far = lax.ppermute(sent_near, 'ctx', swap_ctx)]
    ppermute x3 -> x1, starting transfers between devices: 3.05 us -> 0.08 us  [local(): far = lax.ppermute(sent_near, 'ctx', swap_ctx)]
    another operation x1 -> x6, other arithmetic: 0.06 us -> 2.34 us  [the longest x2 1.19 us: local(): shares = jnp.stack(shares)]
    ppermute x2, starting transfers between devices: 4.05 us -> 6.18 us  [shifted(): lax.ppermute(value, axis, [(source, source + steps) for source in range(l...]
    ppermute x17 -> x18, waiting for transfers between devices: 23.5 us -> 25.3 us  [dp_send(): return lax.ppermute(value, 'dp', pairs)]
    ppermute x2, waiting for transfers between devices: 3.91 us -> 5.56 us  [local(): late_keys = lax.ppermute(key_own, 'ctx', [(1, 0)])]
    unnamed x13 -> x39, local copies, waits for them, and re-layouts: 2.31 us -> 3.76 us
    reshape x0 -> x3, other arithmetic: none -> 1.38 us  [share_of(): return jnp.concatenate(blocks, axis=3).reshape(core_count, 2 * rows, tok)]
  transfers between devices with their start and end apart: 27 -> 26, of which waited for: 14 -> 13; matrix products, arithmetic and copies ran while one was open for 4% -> 8% of each run, Pallas kernels for 7% -> 7%
where the time goes in v4:
time: 96.5 us; the launch traced here: 96.2 us
  waiting for transfers between devices  42.5 us (44%)
  starting transfers between devices  31.9 us (33%)
  other arithmetic  9.43 us (10%)
  Pallas kernels  6.5 us (7%)
  local copies, waits for them, and re-layouts  4.69 us (5%)
  between operations  1.17 us (1%)
    ppermute x18, waiting for transfers between devices, dp_send(): return lax.ppermute(value, 'dp', pairs)  25.3 us
    ppermute x18, starting transfers between devices, dp_send(): return lax.ppermute(value, 'dp', pairs)  16.5 us
    ppermute x1, waiting for transfers between devices, local(): far = lax.ppermute(sent_near, 'ctx', swap_ctx)  8.6 us
    ppermute x2, starting transfers between devices, shifted(): lax.ppermute(value, axis, [(source, source + steps) for source in range(l...  6.18 us
    ppermute x2, waiting for transfers between devices, local(): late_keys = lax.ppermute(key_own, 'ctx', [(1, 0)])  5.56 us
    ppermute x2, starting transfers between devices, local(): arrived = lax.ppermute(sent, 'ctx', swap_ctx)  5.26 us
    pallas_call x2, Pallas kernels, attend(): pl.pallas_call(partial(attention_kernel, hops, group, len(out_shapes)), g...  3.77 us
    unnamed x39, local copies, waits for them, and re-layouts  3.76 us
  transfers between devices with their start and end apart: 26, of which 13 were waited for; matrix products, arithmetic and copies ran while one was open for 8% of the time, Pallas kernels for 7%

profile of v4, /device:TPU:0, one launch (start us, length us, event | category | flops | bytes accessed | tf_op | source)
XLA Modules:
  0.0 96.2 jit_solution(8311234914618719026)
XLA Ops:
  1.3 1.5 %copy.18 = bf16[1,128,2688]{1,2,0:T(8,128)(2,1)S(1)} copy(bf16[1,128,2688]{2,1,0:T(8,128)(2,1)} %param.6) | data formatting | bytes 1376256 | tf_op args[0]
  3.6 4.9 %collective-permute-start = (bf16[144,1024]{1,0:T(8,128)(2,1)S(1)}, bf16[144,1024]{1,0:T(8,128)(2,1)S(1)}, u32[]{:S(2)}, u32[]{:S(2)}) collective-permute-start(bf16[144,1024]{1,0:T(8,128)(2,1)S(1)} %pad_maximum_fusion.3), channel_id=1, source_target_pairs={{0,1},{2,3},{4,5},{6,7},{8,9},{10,11},{12,13},{14,15},{16,17},{18,... | collective-permute-start | bytes 884744 | tf_op jit(solution)/shard_map/ppermute | solution.py:30
  9.4 2.5 %collective-permute-start.4 = (bf16[2,336,128]{2,1,0:T(8,128)(2,1)}, bf16[2,336,128]{2,1,0:T(8,128)(2,1)}, u32[]{:S(2)}, u32[]{:S(2)}) collective-permute-start(bf16[2,336,128]{2,1,0:T(8,128)(2,1)} %maximum_bitcast_fusion.4), channel_id=1, source_target_pairs={{0,12},{2,14},{4,8},{6,10},{8,4},{10,6},{12,0},{14,2},{16,28},{18,... | collective-permute-start | bytes 516104 | tf_op jit(solution)/shard_map/ppermute | solution.py:190
  13.6 1.3 %collective-permute-start.1 = (bf16[128,1024]{1,0:T(8,128)(2,1)}, bf16[128,1024]{1,0:T(8,128)(2,1)S(1)}, u32[]{:S(2)}, u32[]{:S(2)}) collective-permute-start(bf16[128,1024]{1,0:T(8,128)(2,1)} %pad_maximum_fusion.4), channel_id=1, source_target_pairs={{0,1},{2,3},{4,5},{6,7},{8,9},{10,11},{12,13},{14,15},{16,17},{18,... | collective-permute-start | bytes 786440 | tf_op jit(solution)/shard_map/ppermute | solution.py:30
  15.9 1.9 %shard_map.93 = (bf16[128,1024]{1,0:T(8,128)(2,1)S(1)}, bf16[128,512]{1,0:T(8,128)(2,1)S(1)}, bf16[128,512]{1,0:T(8,128)(2,1)S(1)}, bf16[128,512]{1,0:T(8,128)(2...) custom-call(s32[1]{0:T(128)} %bitcast.place_ref, s32[1,128]{1,0:T(1,128)S(1)} %copy-done.14, ...), custom_call_target="tpu_custom_call" | custom-call | flops 1024 | bytes 1024 | tf_op jit(solution)/shard_map/pallas_call | solution.py:112
  17.8 2.5 %collective-permute-start.6 = (bf16[128,512]{1,0:T(8,128)(2,1)S(1)}, bf16[128,512]{1,0:T(8,128)(2,1)S(1)}, u32[]{:S(2)}, u32[]{:S(2)}) collective-permute-start(bf16[128,512]{1,0:T(8,128)(2,1)S(1)} %get-tuple-element.35), channel_id=1, source_target_pairs={{0,1},{1,0},{2,3},{3,2},{4,5},{5,4},{6,7},{7,6},{8,9},{9,8},{10,11... | collective-permute-start | bytes 393224 | tf_op jit(solution)/shard_map/ppermute | solution.py:259
  20.4 1.3 %collective-permute-start.7 = (bf16[128,512]{1,0:T(8,128)(2,1)S(1)}, bf16[128,512]{1,0:T(8,128)(2,1)S(1)}, u32[]{:S(2)}, u32[]{:S(2)}) collective-permute-start(bf16[128,512]{1,0:T(8,128)(2,1)S(1)} %get-tuple-element.40), channel_id=1, source_target_pairs={{1,0},{3,2},{5,4},{7,6},{9,8},{11,10},{13,12},{15,14},{17,16},{19,... | collective-permute-start | bytes 393224 | tf_op jit(solution)/shard_map/ppermute | solution.py:260
  21.7 1.2 %pad_maximum_fusion = bf16[4,2,336,128]{3,2,1,0:T(8,128)(2,1)S(1)} fusion(bf16[1,2,336,128]{3,2,1,0:T(8,128)(2,1)} %bitcast.17, bf16[1,2,336,128]{3,2,1,0:T(8,128)(2,1)} %bitcast.15, bf16[1,2,336,128]{3,2,1,0:T(8,128)(2,1)} %bitcast.13, bf16[1,2,336,128]{3,2,1,0:T(8,128)(2,1)S(1)} %maximum_bitcast_fusion.1), kind=kLoop, calls=%fused_computation | loop fusion | flops 1032192 | bytes 1376256 | tf_op jit(solution)/shard_map/stack | solution.py:249
  23.0 1.9 %shard_map.94 = (bf16[128,1024]{1,0:T(8,128)(2,1)S(1)}, bf16[128,512]{1,0:T(8,128)(2,1)S(1)}, bf16[128,512]{1,0:T(8,128)(2,1)S(1)}, bf16[128,512]{1,0:T(8,128)(2...) custom-call(s32[1]{0:T(128)} %bitcast.place_ref, s32[1,128]{1,0:T(1,128)S(1)} %copy-done.14, ...), custom_call_target="tpu_custom_call" | custom-call | flops 1024 | bytes 1024 | tf_op jit(solution)/shard_map/pallas_call | solution.py:112
  25.0 2.2 %collective-permute-done.7 = bf16[128,512]{1,0:T(8,128)(2,1)S(1)} collective-permute-done((bf16[128,512]{1,0:T(8,128)(2,1)S(1)}, bf16[128,512]{1,0:T(8,128)(2,1)S(1)}, u32[]{:S(2)}, u32[]{:S(2)}) %collective-permute-start.7) | collective-permute-done | bytes 131104 | tf_op jit(solution)/shard_map/ppermute | solution.py:260
  27.2 1.3 %collective-permute-start.19 = (bf16[128,512]{1,0:T(8,128)(2,1)S(1)}, bf16[128,512]{1,0:T(8,128)(2,1)S(1)}, u32[]{:S(2)}, u32[]{:S(2)}) collective-permute-start(bf16[128,512]{1,0:T(8,128)(2,1)S(1)} %get-tuple-element.57), channel_id=1, source_target_pairs={{1,0},{3,2},{5,4},{7,6},{9,8},{11,10},{13,12},{15,14},{17,16},{19,... | collective-permute-start | bytes 393224 | tf_op jit(solution)/shard_map/ppermute | solution.py:260
  28.5 2.7 %collective-permute-start.8 = (bf16[128,512]{1,0:T(8,128)(2,1)S(1)}, bf16[128,512]{1,0:T(8,128)(2,1)S(1)}, u32[]{:S(2)}, u32[]{:S(2)}) collective-permute-start(bf16[128,512]{1,0:T(8,128)(2,1)S(1)} %get-tuple-element.48), channel_id=1, source_target_pairs={{0,1},{1,0},{2,3},{3,2},{4,5},{5,4},{6,7},{7,6},{8,9},{9,8},{10,11... | collective-permute-start | bytes 393224 | tf_op jit(solution)/shard_map/ppermute | solution.py:259
  32.2 3.3 %collective-permute-done.19 = bf16[128,512]{1,0:T(8,128)(2,1)S(1)} collective-permute-done((bf16[128,512]{1,0:T(8,128)(2,1)S(1)}, bf16[128,512]{1,0:T(8,128)(2,1)S(1)}, u32[]{:S(2)}, u32[]{:S(2)}) %collective-permute-start.19) | collective-permute-done | bytes 131104 | tf_op jit(solution)/shard_map/ppermute | solution.py:260
  35.5 2.8 %collective-permute-done.8 = bf16[128,512]{1,0:T(8,128)(2,1)S(1)} collective-permute-done((bf16[128,512]{1,0:T(8,128)(2,1)S(1)}, bf16[128,512]{1,0:T(8,128)(2,1)S(1)}, u32[]{:S(2)}, u32[]{:S(2)}) %collective-permute-start.8) | collective-permute-done | bytes 131104 | tf_op jit(solution)/shard_map/ppermute | solution.py:259
  40.4 1.5 %collective-permute-start.22 = (bf16[2,256,256]{2,1,0:T(8,128)(2,1)S(1)}, bf16[2,256,256]{2,1,0:T(8,128)(2,1)}, u32[]{:S(2)}, u32[]{:S(2)}) collective-permute-start(bf16[2,256,256]{2,1,0:T(8,128)(2,1)S(1)} %pad_maximum_fusion.8.refs_4_), channel_id=1, source_target_pairs={{0,4},{2,6},{4,0},{6,2},{8,12},{10,14},{12,8},{14,10},{16,20},{18,... | collective-permute-start | bytes 786440 | tf_op jit(solution)/shard_map/ppermute | solution.py:190
  42.0 8.6 %collective-permute-done.9.refs_1_ = bf16[8,336,128]{2,1,0:T(8,128)(2,1)S(1)} collective-permute-done((bf16[8,336,128]{2,1,0:T(8,128)(2,1)S(1)}, bf16[8,336,128]{2,1,0:T(8,128)(2,1)S(1)}, u32[]{:S(2)}, u32[]{:S(2)}) %collective-permute-start.9) | collective-permute-done | bytes 688160 | tf_op jit(solution)/shard_map/ppermute | solution.py:271
  51.8 1.4 %collective-permute-done.12 = bf16[256,256]{1,0:T(8,128)(2,1)} collective-permute-done((bf16[256,256]{1,0:T(8,128)(2,1)}, bf16[256,256]{1,0:T(8,128)(2,1)}, u32[]{:S(2)}, u32[]{:S(2)}) %collective-permute-start.12) | collective-permute-done | bytes 131104 | tf_op jit(solution)/shard_map/ppermute | solution.py:190
  53.3 1.0 %pad_maximum_fusion.7.refs_4_ = bf16[2,256,256]{2,1,0:T(8,128)(2,1)S(1)} fusion(bf16[1,256,256]{2,1,0:T(8,128)(2,1)} %bitcast.26, bf16[1,256,256]{2,1,0:T(8,128)(2,1)} %get-tuple-element.78), kind=kLoop, calls=%fused_computation.18 | loop fusion | flops 131072 | bytes 524288 | tf_op jit(solution)/shard_map/stack | solution.py:306
  54.3 1.6 %collective-permute-start.13 = (bf16[2,256,256]{2,1,0:T(8,128)(2,1)S(1)}, bf16[2,256,256]{2,1,0:T(8,128)(2,1)S(1)}, u32[]{:S(2)}, u32[]{:S(2)}) collective-permute-start(bf16[2,256,256]{2,1,0:T(8,128)(2,1)S(1)} %pad_maximum_fusion.7.refs_4_), channel_id=1, source_target_pairs={{0,8},{2,10},{4,12},{6,14},{8,0},{10,2},{12,4},{14,6},{16,24},{18,... | collective-permute-start | bytes 786440 | tf_op jit(solution)/shard_map/ppermute | solution.py:190
  56.4 1.6 %collective-permute-start.23 = (bf16[2,256,256]{2,1,0:T(8,128)(2,1)}, bf16[2,256,256]{2,1,0:T(8,128)(2,1)S(1)}, u32[]{:S(2)}, u32[]{:S(2)}) collective-permute-start(bf16[2,256,256]{2,1,0:T(8,128)(2,1)} %collective-permute-done.22.refs_6_), channel_id=1, source_target_pairs={{0,8},{2,10},{4,12},{6,14},{8,0},{10,2},{12,4},{14,6},{16,24},{18,... | collective-permute-start | bytes 786440 | tf_op jit(solution)/shard_map/ppermute | solution.py:190
  58.0 0.9 copy-done.5
  59.8 3.7 %collective-permute-done.13.refs_5_ = bf16[2,256,256]{2,1,0:T(8,128)(2,1)S(1)} collective-permute-done((bf16[2,256,256]{2,1,0:T(8,128)(2,1)S(1)}, bf16[2,256,256]{2,1,0:T(8,128)(2,1)S(1)}, u32[]{:S(2)}, u32[]{:S(2)}) %collective-permute-start.13) | collective-permute-done | bytes 262176 | tf_op jit(solution)/shard_map/ppermute | solution.py:190
  63.5 1.5 %collective-permute-start.14 = (bf16[2,256,256]{2,1,0:T(8,128)(2,1)S(1)}, bf16[2,256,256]{2,1,0:T(8,128)(2,1)S(1)}, u32[]{:S(2)}, u32[]{:S(2)}) collective-permute-start(bf16[2,256,256]{2,1,0:T(8,128)(2,1)S(1)} %pad_maximum_fusion.7.refs_4_), channel_id=1, source_target_pairs={{0,4},{2,6},{4,0},{6,2},{8,12},{10,14},{12,8},{14,10},{16,20},{18,... | collective-permute-start | bytes 786440 | tf_op jit(solution)/shard_map/ppermute | solution.py:190
  65.0 4.1 %collective-permute-done.21.refs_5_ = bf16[2,256,256]{2,1,0:T(8,128)(2,1)S(1)} collective-permute-done((bf16[2,256,256]{2,1,0:T(8,128)(2,1)S(1)}, bf16[2,256,256]{2,1,0:T(8,128)(2,1)S(1)}, u32[]{:S(2)}, u32[]{:S(2)}) %collective-permute-start.21) | collective-permute-done | bytes 262176 | tf_op jit(solution)/shard_map/ppermute | solution.py:190
  69.1 1.5 %collective-permute-start.15 = (bf16[2,256,256]{2,1,0:T(8,128)(2,1)S(1)}, bf16[2,256,256]{2,1,0:T(8,128)(2,1)S(1)}, u32[]{:S(2)}, u32[]{:S(2)}) collective-permute-start(bf16[2,256,256]{2,1,0:T(8,128)(2,1)S(1)} %collective-permute-done.13.refs_5_), channel_id=1, source_target_pairs={{0,4},{2,6},{4,0},{6,2},{8,12},{10,14},{12,8},{14,10},{16,20},{18,... | collective-permute-start | bytes 786440 | tf_op jit(solution)/shard_map/ppermute | solution.py:190
  70.6 3.5 %collective-permute-done.23.refs_7_ = bf16[2,256,256]{2,1,0:T(8,128)(2,1)S(1)} collective-permute-done((bf16[2,256,256]{2,1,0:T(8,128)(2,1)}, bf16[2,256,256]{2,1,0:T(8,128)(2,1)S(1)}, u32[]{:S(2)}, u32[]{:S(2)}) %collective-permute-start.23) | collective-permute-done | bytes 262176 | tf_op jit(solution)/shard_map/ppermute | solution.py:190
  74.1 1.9 %shard_map.96 = (bf16[2,168,256]{2,1,0:T(8,128)(2,1)S(1)}, f32[2,168,256]{2,1,0:T(8,128)S(1)}) custom-call(bf16[8,336,128]{2,1,0:T(8,128)(2,1)S(1)} %bitcast.59, bf16[8,336,128]{2,1,0:T(8,128)(2,1)S(1)} %collective-permute-done.9.refs_1_, bf16[8,336,128]{2,1,0:T(8,128)(2,1)S(1)} %collective-permute-done.10.refs_2_, ...), custom_call_target="tpu_custom_call" | custom-call | flops 1024 | bytes 1024 | tf_op jit(solution)/shard_map/pallas_call | solution.py:153
  76.0 2.6 %collective-permute-start.24 = (bf16[2,168,256]{2,1,0:T(8,128)(2,1)S(1)}, bf16[2,168,256]{2,1,0:T(8,128)(2,1)S(1)}, u32[]{:S(2)}, u32[]{:S(2)}) collective-permute-start(bf16[2,168,256]{2,1,0:T(8,128)(2,1)S(1)} %get-tuple-element.59), channel_id=1, source_target_pairs={{0,16},{2,18},{4,20},{6,22},{8,24},{10,26},{12,28},{14,30},{16,0},... | collective-permute-start | bytes 516104 | tf_op jit(solution)/shard_map/ppermute | solution.py:190
  80.3 1.3 %collective-permute-start.16 = (bf16[128,1024]{1,0:T(8,128)(2,1)S(1)}, bf16[128,1024]{1,0:T(8,128)(2,1)S(1)}, u32[]{:S(2)}, u32[]{:S(2)}) collective-permute-start(bf16[128,1024]{1,0:T(8,128)(2,1)S(1)} %pad_maximum_fusion.6), channel_id=1, source_target_pairs={{1,0},{3,2},{5,4},{7,6},{9,8},{11,10},{13,12},{15,14},{17,16},{19,... | collective-permute-start | bytes 786440 | tf_op jit(solution)/shard_map/ppermute | solution.py:321
  82.5 8.7 %collective-permute-done.24 = bf16[2,168,256]{2,1,0:T(8,128)(2,1)S(1)} collective-permute-done((bf16[2,168,256]{2,1,0:T(8,128)(2,1)S(1)}, bf16[2,168,256]{2,1,0:T(8,128)(2,1)S(1)}, u32[]{:S(2)}, u32[]{:S(2)}) %collective-permute-start.24) | collective-permute-done | bytes 172064 | tf_op jit(solution)/shard_map/ppermute | solution.py:190
  91.3 2.4 %collective-permute-done.17 = bf16[2,168,256]{2,1,0:T(8,128)(2,1)S(1)} collective-permute-done((bf16[2,168,256]{2,1,0:T(8,128)(2,1)S(1)}, bf16[2,168,256]{2,1,0:T(8,128)(2,1)S(1)}, u32[]{:S(2)}, u32[]{:S(2)}) %collective-permute-start.17) | collective-permute-done | bytes 172064 | tf_op jit(solution)/shard_map/ppermute | solution.py:190
  95.3 0.9 pad_maximum_fusion.2
  (96 shorter events, 14.8 us)
Async XLA Ops:
  3.6 11.6 %collective-permute-start = (bf16[144,1024]{1,0:T(8,128)(2,1)S(1)}, bf16[144,1024]{1,0:T(8,128)(2,1)S(1)}, u32[]{:S(2)}, u32[]{:S(2)}) collective-permute-start(bf16[144,1024]{1,0:T(8,128)(2,1)S(1)} %pad_maximum_fusion.3), channel_id=1, source_target_pairs={{0,1},{2,3},{4,5},{6,7},{8,9},{10,11},{12,13},{14,15},{16,17},{18,... | collective-permute-start | bytes 884744 | tf_op jit(solution)/shard_map/ppermute | solution.py:30
  9.4 11.0 %collective-permute-start.4 = (bf16[2,336,128]{2,1,0:T(8,128)(2,1)}, bf16[2,336,128]{2,1,0:T(8,128)(2,1)}, u32[]{:S(2)}, u32[]{:S(2)}) collective-permute-start(bf16[2,336,128]{2,1,0:T(8,128)(2,1)} %maximum_bitcast_fusion.4), channel_id=1, source_target_pairs={{0,12},{2,14},{4,8},{6,10},{8,4},{10,6},{12,0},{14,2},{16,28},{18,... | collective-permute-start | bytes 516104 | tf_op jit(solution)/shard_map/ppermute | solution.py:190
  11.9 9.7 %collective-permute-start.3 = (bf16[2,336,128]{2,1,0:T(8,128)(2,1)S(1)}, bf16[2,336,128]{2,1,0:T(8,128)(2,1)}, u32[]{:S(2)}, u32[]{:S(2)}) collective-permute-start(bf16[2,336,128]{2,1,0:T(8,128)(2,1)S(1)} %maximum_bitcast_fusion.3), channel_id=1, source_target_pairs={{0,4},{2,6},{4,0},{6,2},{8,12},{10,14},{12,8},{14,10},{16,20},{18,... | collective-permute-start | bytes 516104 | tf_op jit(solution)/shard_map/ppermute | solution.py:190
  13.2 8.5 %collective-permute-start.2 = (bf16[2,336,128]{2,1,0:T(8,128)(2,1)}, bf16[2,336,128]{2,1,0:T(8,128)(2,1)}, u32[]{:S(2)}, u32[]{:S(2)}) collective-permute-start(bf16[2,336,128]{2,1,0:T(8,128)(2,1)} %maximum_bitcast_fusion.2), channel_id=1, source_target_pairs={{0,8},{2,10},{4,12},{6,14},{8,0},{10,2},{12,4},{14,6},{16,24},{18,... | collective-permute-start | bytes 516104 | tf_op jit(solution)/shard_map/ppermute | solution.py:190
  13.6 9.4 %collective-permute-start.1 = (bf16[128,1024]{1,0:T(8,128)(2,1)}, bf16[128,1024]{1,0:T(8,128)(2,1)S(1)}, u32[]{:S(2)}, u32[]{:S(2)}) collective-permute-start(bf16[128,1024]{1,0:T(8,128)(2,1)} %pad_maximum_fusion.4), channel_id=1, source_target_pairs={{0,1},{2,3},{4,5},{6,7},{8,9},{10,11},{12,13},{14,15},{16,17},{18,... | collective-permute-start | bytes 786440 | tf_op jit(solution)/shard_map/ppermute | solution.py:30
  17.8 5.1 %copy-start.6 = (bf16[128,512]{1,0:T(8,128)(2,1)}, bf16[128,512]{1,0:T(8,128)(2,1)S(1)}, u32[]{:S(2)}) copy-start(bf16[128,512]{1,0:T(8,128)(2,1)S(1)} %get-tuple-element.40) | copy-start | bytes 393220
  17.8 7.2 %collective-permute-start.6 = (bf16[128,512]{1,0:T(8,128)(2,1)S(1)}, bf16[128,512]{1,0:T(8,128)(2,1)S(1)}, u32[]{:S(2)}, u32[]{:S(2)}) collective-permute-start(bf16[128,512]{1,0:T(8,128)(2,1)S(1)} %get-tuple-element.35), channel_id=1, source_target_pairs={{0,1},{1,0},{2,3},{3,2},{4,5},{5,4},{6,7},{7,6},{8,9},{9,8},{10,11... | collective-permute-start | bytes 393224 | tf_op jit(solution)/shard_map/ppermute | solution.py:259
  20.4 6.9 %collective-permute-start.7 = (bf16[128,512]{1,0:T(8,128)(2,1)S(1)}, bf16[128,512]{1,0:T(8,128)(2,1)S(1)}, u32[]{:S(2)}, u32[]{:S(2)}) collective-permute-start(bf16[128,512]{1,0:T(8,128)(2,1)S(1)} %get-tuple-element.40), channel_id=1, source_target_pairs={{1,0},{3,2},{5,4},{7,6},{9,8},{11,10},{13,12},{15,14},{17,16},{19,... | collective-permute-start | bytes 393224 | tf_op jit(solution)/shard_map/ppermute | solution.py:260
  22.9 9.1 %collective-permute-start.5 = (bf16[4,336,128]{2,1,0:T(8,128)(2,1)S(1)}, bf16[4,336,128]{2,1,0:T(8,128)(2,1)S(1)}, u32[]{:S(2)}, u32[]{:S(2)}) collective-permute-start(bf16[4,336,128]{2,1,0:T(8,128)(2,1)S(1)} %get-tuple-element.61), channel_id=1, source_target_pairs={{0,2},{2,0},{4,6},{6,4},{8,10},{10,8},{12,14},{14,12},{16,18},{18,... | collective-permute-start | bytes 1032200 | tf_op jit(solution)/shard_map/ppermute | solution.py:190
  24.9 6.4 %copy-start.4 = (bf16[128,1024]{1,0:T(8,128)(2,1)}, bf16[128,1024]{1,0:T(8,128)(2,1)S(1)}, u32[]{:S(2)}) copy-start(bf16[128,1024]{1,0:T(8,128)(2,1)S(1)} %get-tuple-element.37) | copy-start | bytes 786436
  24.9 6.4 %copy-start.10 = (bf16[128,512]{1,0:T(8,128)(2,1)}, bf16[128,512]{1,0:T(8,128)(2,1)S(1)}, u32[]{:S(2)}) copy-start(bf16[128,512]{1,0:T(8,128)(2,1)S(1)} %get-tuple-element.57) | copy-start | bytes 393220
  24.9 6.4 %copy-start.12 = (bf16[128,512]{1,0:T(8,128)(2,1)}, bf16[128,512]{1,0:T(8,128)(2,1)S(1)}, u32[]{:S(2)}) copy-start(bf16[128,512]{1,0:T(8,128)(2,1)S(1)} %get-tuple-element.51) | copy-start | bytes 393220
  27.2 8.3 %collective-permute-start.19 = (bf16[128,512]{1,0:T(8,128)(2,1)S(1)}, bf16[128,512]{1,0:T(8,128)(2,1)S(1)}, u32[]{:S(2)}, u32[]{:S(2)}) collective-permute-start(bf16[128,512]{1,0:T(8,128)(2,1)S(1)} %get-tuple-element.57), channel_id=1, source_target_pairs={{1,0},{3,2},{5,4},{7,6},{9,8},{11,10},{13,12},{15,14},{17,16},{19,... | collective-permute-start | bytes 393224 | tf_op jit(solution)/shard_map/ppermute | solution.py:260
  28.5 9.8 %collective-permute-start.8 = (bf16[128,512]{1,0:T(8,128)(2,1)S(1)}, bf16[128,512]{1,0:T(8,128)(2,1)S(1)}, u32[]{:S(2)}, u32[]{:S(2)}) collective-permute-start(bf16[128,512]{1,0:T(8,128)(2,1)S(1)} %get-tuple-element.48), channel_id=1, source_target_pairs={{0,1},{1,0},{2,3},{3,2},{4,5},{5,4},{6,7},{7,6},{8,9},{9,8},{10,11... | collective-permute-start | bytes 393224 | tf_op jit(solution)/shard_map/ppermute | solution.py:259
  32.1 18.5 %collective-permute-start.9 = (bf16[8,336,128]{2,1,0:T(8,128)(2,1)S(1)}, bf16[8,336,128]{2,1,0:T(8,128)(2,1)S(1)}, u32[]{:S(2)}, u32[]{:S(2)}) collective-permute-start(bf16[8,336,128]{2,1,0:T(8,128)(2,1)S(1)} %bitcast.57), channel_id=1, source_target_pairs={{0,1},{1,0},{2,3},{3,2},{4,5},{5,4},{6,7},{7,6},{8,9},{9,8},{10,11... | collective-permute-start | bytes 2064392 | tf_op jit(solution)/shard_map/ppermute | solution.py:271
  39.1 1.3 %collective-permute-start.20 = (bf16[256,256]{1,0:T(8,128)(2,1)S(1)}, bf16[256,256]{1,0:T(8,128)(2,1)S(1)}, u32[]{:S(2)}, u32[]{:S(2)}) collective-permute-start(bf16[256,256]{1,0:T(8,128)(2,1)S(1)} %get-tuple-element.75), channel_id=1, source_target_pairs={{0,2},{2,0},{4,6},{6,4},{8,10},{10,8},{12,14},{14,12},{16,18},{18,... | collective-permute-start | bytes 393224 | tf_op jit(solution)/shard_map/ppermute | solution.py:190
  39.1 31.5 %collective-permute-start.10 = (bf16[8,336,128]{2,1,0:T(8,128)(2,1)S(1)}, bf16[8,336,128]{2,1,0:T(8,128)(2,1)S(1)}, u32[]{:S(2)}, u32[]{:S(2)}) collective-permute-start(bf16[8,336,128]{2,1,0:T(8,128)(2,1)S(1)} %bitcast.58), channel_id=1, source_target_pairs={{0,2},{2,0},{4,6},{6,4},{8,10},{10,8},{12,14},{14,12},{16,18},{18,... | collective-permute-start | bytes 2064392 | tf_op jit(solution)/shard_map/ppermute | solution.py:190
  40.4 10.2 %copy-start.15 = (bf16[256,512]{1,0:T(8,128)(2,1)S(1)}, bf16[256,512]{1,0:T(8,128)(2,1)}, u32[]{:S(2)}) copy-start(bf16[256,512]{1,0:T(8,128)(2,1)} %pad_maximum_fusion.5) | copy-start | bytes 786436
  40.4 16.0 %collective-permute-start.22 = (bf16[2,256,256]{2,1,0:T(8,128)(2,1)S(1)}, bf16[2,256,256]{2,1,0:T(8,128)(2,1)}, u32[]{:S(2)}, u32[]{:S(2)}) collective-permute-start(bf16[2,256,256]{2,1,0:T(8,128)(2,1)S(1)} %pad_maximum_fusion.8.refs_4_), channel_id=1, source_target_pairs={{0,4},{2,6},{4,0},{6,2},{8,12},{10,14},{12,8},{14,10},{16,20},{18,... | collective-permute-start | bytes 786440 | tf_op jit(solution)/shard_map/ppermute | solution.py:190
  50.6 23.5 %collective-permute-start.11 = (bf16[8,336,128]{2,1,0:T(8,128)(2,1)S(1)}, bf16[8,336,128]{2,1,0:T(8,128)(2,1)S(1)}, u32[]{:S(2)}, u32[]{:S(2)}) collective-permute-start(bf16[8,336,128]{2,1,0:T(8,128)(2,1)S(1)} %collective-permute-done.9.refs_1_), channel_id=1, source_target_pairs={{0,2},{2,0},{4,6},{6,4},{8,10},{10,8},{12,14},{14,12},{16,18},{18,... | collective-permute-start | bytes 2064392 | tf_op jit(solution)/shard_map/ppermute | solution.py:190
  51.3 2.0 %collective-permute-start.12 = (bf16[256,256]{1,0:T(8,128)(2,1)}, bf16[256,256]{1,0:T(8,128)(2,1)}, u32[]{:S(2)}, u32[]{:S(2)}) collective-permute-start(bf16[256,256]{1,0:T(8,128)(2,1)} %get-tuple-element.79), channel_id=1, source_target_pairs={{0,2},{2,0},{4,6},{6,4},{8,10},{10,8},{12,14},{14,12},{16,18},{18,... | collective-permute-start | bytes 393224 | tf_op jit(solution)/shard_map/ppermute | solution.py:190
  54.3 9.2 %collective-permute-start.13 = (bf16[2,256,256]{2,1,0:T(8,128)(2,1)S(1)}, bf16[2,256,256]{2,1,0:T(8,128)(2,1)S(1)}, u32[]{:S(2)}, u32[]{:S(2)}) collective-permute-start(bf16[2,256,256]{2,1,0:T(8,128)(2,1)S(1)} %pad_maximum_fusion.7.refs_4_), channel_id=1, source_target_pairs={{0,8},{2,10},{4,12},{6,14},{8,0},{10,2},{12,4},{14,6},{16,24},{18,... | collective-permute-start | bytes 786440 | tf_op jit(solution)/shard_map/ppermute | solution.py:190
  56.0 13.2 %collective-permute-start.21 = (bf16[2,256,256]{2,1,0:T(8,128)(2,1)S(1)}, bf16[2,256,256]{2,1,0:T(8,128)(2,1)S(1)}, u32[]{:S(2)}, u32[]{:S(2)}) collective-permute-start(bf16[2,256,256]{2,1,0:T(8,128)(2,1)S(1)} %pad_maximum_fusion.8.refs_4_), channel_id=1, source_target_pairs={{0,8},{2,10},{4,12},{6,14},{8,0},{10,2},{12,4},{14,6},{16,24},{18,... | collective-permute-start | bytes 786440 | tf_op jit(solution)/shard_map/ppermute | solution.py:190
  56.4 17.7 %collective-permute-start.23 = (bf16[2,256,256]{2,1,0:T(8,128)(2,1)}, bf16[2,256,256]{2,1,0:T(8,128)(2,1)S(1)}, u32[]{:S(2)}, u32[]{:S(2)}) collective-permute-start(bf16[2,256,256]{2,1,0:T(8,128)(2,1)} %collective-permute-done.22.refs_6_), channel_id=1, source_target_pairs={{0,8},{2,10},{4,12},{6,14},{8,0},{10,2},{12,4},{14,6},{16,24},{18,... | collective-permute-start | bytes 786440 | tf_op jit(solution)/shard_map/ppermute | solution.py:190
  59.8 18.8 %copy-start.16 = (bf16[256,512]{1,0:T(8,128)(2,1)S(1)}, bf16[256,512]{1,0:T(8,128)(2,1)}, u32[]{:S(2)}) copy-start(bf16[256,512]{1,0:T(8,128)(2,1)} %pad_maximum_fusion.5) | copy-start | bytes 786436
  63.5 15.9 %collective-permute-start.14 = (bf16[2,256,256]{2,1,0:T(8,128)(2,1)S(1)}, bf16[2,256,256]{2,1,0:T(8,128)(2,1)S(1)}, u32[]{:S(2)}, u32[]{:S(2)}) collective-permute-start(bf16[2,256,256]{2,1,0:T(8,128)(2,1)S(1)} %pad_maximum_fusion.7.refs_4_), channel_id=1, source_target_pairs={{0,4},{2,6},{4,0},{6,2},{8,12},{10,14},{12,8},{14,10},{16,20},{18,... | collective-permute-start | bytes 786440 | tf_op jit(solution)/shard_map/ppermute | solution.py:190
  69.1 10.3 %collective-permute-start.15 = (bf16[2,256,256]{2,1,0:T(8,128)(2,1)S(1)}, bf16[2,256,256]{2,1,0:T(8,128)(2,1)S(1)}, u32[]{:S(2)}, u32[]{:S(2)}) collective-permute-start(bf16[2,256,256]{2,1,0:T(8,128)(2,1)S(1)} %collective-permute-done.13.refs_5_), channel_id=1, source_target_pairs={{0,4},{2,6},{4,0},{6,2},{8,12},{10,14},{12,8},{14,10},{16,20},{18,... | collective-permute-start | bytes 786440 | tf_op jit(solution)/shard_map/ppermute | solution.py:190
  76.0 15.2 %collective-permute-start.24 = (bf16[2,168,256]{2,1,0:T(8,128)(2,1)S(1)}, bf16[2,168,256]{2,1,0:T(8,128)(2,1)S(1)}, u32[]{:S(2)}, u32[]{:S(2)}) collective-permute-start(bf16[2,168,256]{2,1,0:T(8,128)(2,1)S(1)} %get-tuple-element.59), channel_id=1, source_target_pairs={{0,16},{2,18},{4,20},{6,22},{8,24},{10,26},{12,28},{14,30},{16,0},... | collective-permute-start | bytes 516104 | tf_op jit(solution)/shard_map/ppermute | solution.py:190
  80.3 13.5 %collective-permute-start.16 = (bf16[128,1024]{1,0:T(8,128)(2,1)S(1)}, bf16[128,1024]{1,0:T(8,128)(2,1)S(1)}, u32[]{:S(2)}, u32[]{:S(2)}) collective-permute-start(bf16[128,1024]{1,0:T(8,128)(2,1)S(1)} %pad_maximum_fusion.6), channel_id=1, source_target_pairs={{1,0},{3,2},{5,4},{7,6},{9,8},{11,10},{13,12},{15,14},{17,16},{19,... | collective-permute-start | bytes 786440 | tf_op jit(solution)/shard_map/ppermute | solution.py:321
  81.6 12.1 %collective-permute-start.17 = (bf16[2,168,256]{2,1,0:T(8,128)(2,1)S(1)}, bf16[2,168,256]{2,1,0:T(8,128)(2,1)S(1)}, u32[]{:S(2)}, u32[]{:S(2)}) collective-permute-start(bf16[2,168,256]{2,1,0:T(8,128)(2,1)S(1)} %get-tuple-element.56), channel_id=1, source_target_pairs={{0,16},{2,18},{4,20},{6,22},{8,24},{10,26},{12,28},{14,30},{16,0},... | collective-permute-start | bytes 516104 | tf_op jit(solution)/shard_map/ppermute | solution.py:190
  91.2 3.4 %collective-permute-start.25 = (f32[168,256]{1,0:T(8,128)S(1)}, f32[168,256]{1,0:T(8,128)S(1)}, u32[]{:S(2)}, u32[]{:S(2)}) collective-permute-start(f32[168,256]{1,0:T(8,128)S(1)} %slice_bitcast_fusion), channel_id=1, source_target_pairs={{0,2},{2,0},{4,6},{6,4},{8,10},{10,8},{12,14},{14,12},{16,18},{18,... | collective-permute-start | bytes 516104 | tf_op jit(solution)/shard_map/ppermute | solution.py:190
  93.8 1.5 %collective-permute-start.18 = (f32[168,256]{1,0:T(8,128)S(1)}, f32[168,256]{1,0:T(8,128)S(1)}, u32[]{:S(2)}, u32[]{:S(2)}) collective-permute-start(f32[168,256]{1,0:T(8,128)S(1)} %slice_bitcast_fusion.2), channel_id=1, source_target_pairs={{0,2},{2,0},{4,6},{6,4},{8,10},{10,8},{12,14},{14,12},{16,18},{18,... | collective-permute-start | bytes 516104 | tf_op jit(solution)/shard_map/ppermute | solution.py:190
  (13 other events, 36.4 us)

commit v5 on v3

--- a/solution.py
+++ b/solution.py
@@ -105,7 +105,7 @@
     span = (hops + 1) * tok
     whole = lambda *shape: pl.BlockSpec(shape, lambda i, *_: (0,) * len(shape))
     part = lambda *shape: pl.BlockSpec(shape, lambda i, *_: (0, chunk))
-    seg_row = pl.BlockSpec((SEG_ROWS, tok), lambda i, *_: (tok // SEG_ROWS, 0))
+    seg_row = pl.BlockSpec((SEG_ROWS, tok), lambda i, *_: (0, 2 * width // tok))
     out_shapes = [(tok, group * width)]
     out_shapes += [(tok, width)] * 5 if hops == 1 else [(span, width)] * 2
     operands = [place, segs, queries, out_grad, keys, values, *rim_pairs, *rim_segs]
@@ -121,46 +121,53 @@
                 part(tok, width),
                 part(tok, width),
             ]
-            + [whole(tok, 2 * width)] * hops
+            + [pl.BlockSpec((tok, 2 * width), lambda i, *_: (0, 0))] * hops
             + [seg_row] * hops,
             out_specs=[whole(*shape) for shape in out_shapes],
         ),
         out_shape=[jax.ShapeDtypeStruct(shape, jnp.bfloat16) for shape in out_shapes],
-        compiler_params=pltpu.CompilerParams(vmem_limit_bytes=48 * MIB),
+        compiler_params=pltpu.CompilerParams(vmem_limit_bytes=24 * MIB),
         cost_estimate=SMALL,
     )(*operands)
 
 
-def product_kernel(traces, *refs):
-    own_refs, first_ref, rest_ref = refs[:traces], refs[traces], refs[traces + 1]
-    grad_refs = refs[traces + 2 : 2 * traces + 2]
-    outs = refs[2 * traces + 2 :]
-    away = [first_ref[...]] + [rest_ref[t] for t in range(traces - 1)]
+def product_kernel(traces, place_ref, *refs):
+    own_refs, grad_refs, rest = refs[:traces], refs[traces : 2 * traces], refs[2 * traces :]
+    away_ref, rest = rest[0], rest[1:]
+    away = [away_ref[t] for t in range(traces)]
+    if len(rest) > SPLIT:
+        first = place_ref[0] == 0
+        away = [jnp.where(first, rest[t][...], away[t]) for t in range(traces)]
     features = jnp.concatenate(
         [piece for t in range(traces) for piece in (own_refs[t][...], away[t])], axis=1
     )
     grads = jnp.concatenate([ref[...] for ref in grad_refs], axis=0)
+    outs = rest[-SPLIT:]
     width = outs[0].shape[1]
     for n, out in enumerate(outs):
         out[...] = dot_f32(features, grads[:, n * width : (n + 1) * width]).astype(out.dtype)
 
 
-def product(half, own, first_away, rest_away, grads, dtype):
+def product(half, place, own, away, first_away, grads, dtype):
     traces, (rows, tok) = len(own), own[0].shape
     rows //= 2
     width = grads[0].shape[1] // SPLIT
-    half_of = lambda array: pl.BlockSpec((rows, array.shape[1]), lambda i: (half, 0))
-    whole = lambda array: pl.BlockSpec(array.shape, lambda i: (0,) * array.ndim)
+    half_of = lambda array: pl.BlockSpec((rows, array.shape[1]), lambda i, *_: (half, 0))
+    whole = lambda array: pl.BlockSpec(array.shape, lambda i, *_: (0,) * array.ndim)
     return pl.pallas_call(
         partial(product_kernel, traces),
-        grid=(1,),
-        in_specs=[half_of(piece) for piece in (*own, first_away)]
-        + [whole(piece) for piece in (rest_away, *grads)],
-        out_specs=[pl.BlockSpec((rows, width), lambda i: (0, 0))] * SPLIT,
+        grid_spec=pltpu.PrefetchScalarGridSpec(
+            num_scalar_prefetch=1,
+            grid=(1,),
+            in_specs=[half_of(piece) for piece in own]
+            + [whole(piece) for piece in (*grads, away)]
+            + [half_of(piece) for piece in first_away],
+            out_specs=[pl.BlockSpec((rows, width), lambda i, *_: (0, 0))] * SPLIT,
+        ),
         out_shape=[jax.ShapeDtypeStruct((rows, width), dtype)] * SPLIT,
-        compiler_params=pltpu.CompilerParams(vmem_limit_bytes=48 * MIB),
+        compiler_params=pltpu.CompilerParams(vmem_limit_bytes=24 * MIB),
         cost_estimate=SMALL,
-    )(*own, first_away, rest_away, *grads)
+    )(place, *own, *grads, away, *first_away)
 
 
 def local(hidden_in, queries, key_states, value_states, out_grad, segment_ids):
@@ -181,7 +188,7 @@
     mid_at = dp_place // core_count % mid_count
     slow_at = dp_place // (core_count * mid_count)
 
-    def dp_send(value, move):
+    def dp_send(value, move, only_first=False):
         pairs = []
         for source in range(dp_count):
             core = source % core_count
@@ -189,6 +196,9 @@
             slow = source // (core_count * mid_count)
             slow, mid, core = move(slow, mid, core)
             pairs.append((source, (slow * mid_count + mid) * core_count + core))
+        if only_first:
+            pairs = [(source * ctx_count, target * ctx_count) for source, target in pairs]
+            return lax.ppermute(value, ("dp", "ctx"), pairs)
         return lax.ppermute(value, "dp", pairs)
 
     swap_core = lambda slow, mid, core: (slow, mid, core ^ 1)
@@ -199,31 +209,49 @@
     own_keys, own_values = key_states[0], value_states[0]
 
     steps = range(hops, 0, -1)
-    seg_rows = jnp.broadcast_to(segment_ids.astype(jnp.bfloat16), (SEG_ROWS, tok))
-    seg_rows = jnp.pad(seg_rows, ((0, 0), (0, 2 * width - tok)))
+    hidden = hidden_in[0]
     rim_pairs = []
+    late_hidden = []
     for chunk in range(CHUNKS):
         cols = slice(chunk * width, (chunk + 1) * width)
-        pair = jnp.concatenate([own_keys[:, cols], own_values[:, cols]], axis=1)
+        parts = [own_keys[:, cols], own_values[:, cols]]
         if chunk == 0:
-            pair = jnp.concatenate([pair, seg_rows], axis=0)
-        rim_pairs.append([shifted(pair, "ctx", step) for step in steps])
+            parts.append(jnp.broadcast_to(segment_ids.astype(jnp.bfloat16), (tok, tok)))
+        pair = jnp.concatenate(parts, axis=1)
+        if ctx_count == 2:
+            low = sum(array.shape[1] for array in late_hidden)
+            wide = hidden.shape[1] - low if chunk == CHUNKS - 1 else pair.shape[1]
+            pair = jnp.pad(pair, ((0, 0), (0, wide - pair.shape[1])))
+            pair = jnp.where(first, pair, hidden[:, low : low + wide])
+            arrived = lax.ppermute(pair, "ctx", swap_ctx)
+            late_hidden.append(arrived)
+            rim_pairs.append([arrived])
+        else:
+            rim_pairs.append([shifted(pair, "ctx", step) for step in steps])
 
     rows = hidden_in.shape[2] // dp_count
-    by_feature = hidden_in[0].T.reshape(slow_count, mid_count, core_count, rows, tok)
-    pieces = []
-    for step in range(mid_count):
-        for flip in range(core_count):
-            share = lax.dynamic_slice(
-                by_feature,
-                (0, (mid_at + step) % mid_count, core_at ^ flip, 0, 0),
-                (slow_count, 1, 1, rows, tok),
-            )
-            share = jnp.concatenate(
-                [lax.dynamic_index_in_dim(share, slow_at ^ turn, 0) for turn in (3, 1, 2, 0)]
-            ).reshape(slow_count * rows, tok)
-            away = lambda slow, mid, core: (slow, (mid + step) % mid_count, core ^ flip)
-            pieces.append(share if step == flip == 0 else dp_send(share, away))
+
+    def by_feature(array):
+        array = array.T.reshape(slow_count, mid_count, core_count, rows, tok)
+        turns = [lax.dynamic_index_in_dim(array, slow_at ^ turn, 0, False) for turn in (3, 1, 2, 0)]
+        return jnp.stack(turns)
+
+    def spread(array, only_first):
+        found = []
+        for step in range(mid_count):
+            for flip in range(core_count):
+                share = lax.dynamic_slice(
+                    array,
+                    (0, (mid_at + step) % mid_count, core_at ^ flip, 0, 0),
+                    (array.shape[0], 1, 1, rows, tok),
+                ).reshape(-1, tok)
+                away = lambda slow, mid, core: (slow, (mid + step) % mid_count, core ^ flip)
+                if step or flip:
+                    share = dp_send(share, away, only_first)
+                found.append(share)
+        return found
+
+    pieces = spread(by_feature(hidden), False)
 
     half_rows = slow_count // 2 * rows
     low_high = [(0, half_rows), (half_rows, 2 * half_rows)]
@@ -248,26 +276,31 @@
     query_grad = jnp.concatenate([outs[0] for outs in attended], axis=1)
 
     if ctx_count == 2:
-        first_away = lax.ppermute(pieces[0], "ctx", swap_ctx)
-        columns, rest_away = [], []
+        late_hidden, pieces, _ = lax.optimization_barrier((late_hidden, pieces, attended[0][1]))
+        first_away = spread(by_feature(jnp.concatenate(late_hidden, axis=1)), True)
+        columns = []
+        half_stack = lambda low, high: jnp.stack([piece[low:high] for piece in pieces])
         for chunk, (_, sent, addend, key_own, value_own, _) in enumerate(attended):
             if chunk > 0:
                 sent, key_own, _ = lax.optimization_barrier((sent, key_own, arrived))
             arrived = lax.ppermute(sent, "ctx", swap_ctx)
             late_keys = lax.ppermute(key_own, "ctx", [(1, 0)])
             if chunk == 0:
-                arrived, late_keys, first_away, *_ = lax.optimization_barrier(
-                    (arrived, late_keys, first_away, rim_pairs[1:])
+                arrived, late_keys, _ = lax.optimization_barrier(
+                    (arrived, late_keys, rim_pairs[1:])
+                )
+                sent_away = lax.ppermute(half_stack(*low_high[0]), "ctx", [(0, 1)])
+            elif chunk == 1:
+                arrived, late_keys, sent_away, first_away = lax.optimization_barrier(
+                    (arrived, late_keys, sent_away, first_away)
                 )
             total = (addend.astype(jnp.float32) + arrived.astype(jnp.float32)).astype(jnp.bfloat16)
             block = jnp.concatenate(
                 [jnp.where(first, total, value_own), jnp.where(first, late_keys, total)], axis=0
             )
             if chunk == 0:
-                for low, high in low_high:
-                    rest = jnp.stack([piece[low:high] for piece in pieces[1:]])
-                    rest, block = lax.optimization_barrier((rest, block))
-                    rest_away.append(lax.ppermute(rest, "ctx", swap_ctx))
+                rest, block = lax.optimization_barrier((half_stack(*low_high[1]), block))
+                kept_away = lax.ppermute(rest, "ctx", [(0, 1)])
             columns.append(block)
         key_grad = jnp.where(
             first,
@@ -295,8 +328,8 @@
         columns = jnp.split(both, CHUNKS, axis=1)
         every = lax.all_gather(jnp.stack(pieces), "ctx", axis=2, tiled=True)
         near, away = jnp.split(every, 2, axis=2)
-        pieces, first_away = list(near), away[0]
-        rest_away = [away[1:, low:high] for low, high in low_high]
+        pieces, first_away = list(near), []
+        sent_away, kept_away = (away[:, low:high] for low, high in low_high)
 
     gathered = []
     for block in columns:
@@ -304,18 +337,20 @@
         gathered.append(
             [piece for near_one in near for piece in (near_one, dp_send(near_one, swap_core))]
         )
-    gathered[-1], rest_away[1] = lax.optimization_barrier((gathered[-1], rest_away[1]))
-    sent, kept = (
-        [
-            piece
-            for grads in gathered
-            for piece in product(half, pieces, first_away, rest_away[half], grads, dtype)
-        ]
-        for half, dtype in ((0, jnp.bfloat16), (1, jnp.float32))
-    )
+    gathered[-1], kept_away = lax.optimization_barrier((gathered[-1], kept_away))
+    sent = [
+        piece
+        for grads in gathered
+        for piece in product(0, place_arg, pieces, sent_away, first_away, grads, jnp.bfloat16)
+    ]
+    kept = [
+        piece
+        for grads in gathered
+        for piece in product(1, place_arg, pieces, kept_away, first_away, grads, jnp.float32)
+    ]
     if ctx_count == 2:
         value_rim = jnp.concatenate([outs[5] for outs in attended], axis=1)
-        value_rim, sent[0] = lax.optimization_barrier((value_rim, sent[0]))
+        value_rim, sent[-1] = lax.optimization_barrier((value_rim, sent[-1]))
         returned = lax.ppermute(value_rim, "ctx", [(1, 0)])
         value_own = jnp.concatenate([outs[4] for outs in attended], axis=1)
         value_grad = (value_own.astype(jnp.float32) + returned.astype(jnp.float32)).astype(

time: 78.5 us -> 91.2 us (1.16)
  starting transfers between devices: 32.7 us -> 40 us
  other arithmetic: 3.04 us -> 7.37 us
  local copies, waits for them, and re-layouts: 2.6 us -> 6.75 us
  waiting for transfers between devices: 32.9 us -> 28.9 us
    ppermute x5 -> x7, starting transfers between devices: 7.1 us -> 16 us  [the longest x3 7.72 us: dp_send(): return lax.ppermute(value, ('dp', 'ctx'), pairs)]
    ppermute x5 -> x7, waiting for transfers between devices: 3.35 us -> 11.1 us  [the longest x3 5.68 us: dp_send(): return lax.ppermute(value, ('dp', 'ctx'), pairs)]
    ppermute x17, waiting for transfers between devices: 23.5 us -> 17.8 us  [dp_send(): return lax.ppermute(value, 'dp', pairs)]
    ppermute x2, waiting for transfers between devices: 3.91 us -> 0.01 us  [local(): late_keys = lax.ppermute(key_own, 'ctx', [(1, 0)])]
    transpose x0 -> x2, local copies, waits for them, and re-layouts: none -> 2.59 us  [by_feature(): array = array.T.reshape(slow_count, mid_count, core_count, rows, tok)]
    ppermute x2, starting transfers between devices: 4.34 us -> 2.13 us  [local(): arrived = lax.ppermute(sent, 'ctx', swap_ctx)]
    ppermute x2, waiting for transfers between devices: 2.18 us -> 0.01 us  [local(): arrived = lax.ppermute(sent, 'ctx', swap_ctx)]
    select_n x0 -> x2, other arithmetic: none -> 1.63 us  [local(): pair = jnp.where(first, pair, hidden[:, low:low + wide])]
  transfers between devices with their start and end apart: 27 -> 29, of which waited for: 14 -> 10; matrix products, arithmetic and copies ran while one was open for 4% -> 10% of each run, Pallas kernels for 7% -> 7%
where the time goes in v5:
time: 91.2 us; the launch traced here: 90.8 us
  starting transfers between devices  40 us (44%)
  waiting for transfers between devices  28.9 us (32%)
  other arithmetic  7.37 us (8%)
  local copies, waits for them, and re-layouts  6.75 us (7%)
  Pallas kernels  6.55 us (7%)
  between operations  1.23 us (1%)
    ppermute x17, starting transfers between devices, dp_send(): return lax.ppermute(value, 'dp', pairs)  17.9 us
    ppermute x17, waiting for transfers between devices, dp_send(): return lax.ppermute(value, 'dp', pairs)  17.8 us
    ppermute x3, starting transfers between devices, dp_send(): return lax.ppermute(value, ('dp', 'ctx'), pairs)  7.72 us
    ppermute x3, waiting for transfers between devices, dp_send(): return lax.ppermute(value, ('dp', 'ctx'), pairs)  5.68 us
    ppermute x2, waiting for transfers between devices, local(): arrived = lax.ppermute(pair, 'ctx', swap_ctx)  5.47 us
    pallas_call x2, Pallas kernels, attend(): pl.pallas_call(partial(attention_kernel, hops, group, len(out_shapes)), g...  4.47 us
    ppermute x1, starting transfers between devices, local(): sent_away = lax.ppermute(half_stack(*low_high[0]), 'ctx', [(0, 1)])  4.05 us
    ppermute x2, starting transfers between devices, local(): arrived = lax.ppermute(pair, 'ctx', swap_ctx)  2.97 us
  transfers between devices with their start and end apart: 29, of which 10 were waited for; matrix products, arithmetic and copies ran while one was open for 10% of the time, Pallas kernels for 7%

profile of v5, /device:TPU:0, one launch (start us, length us, event | category | flops | bytes accessed | tf_op | source)
XLA Modules:
  0.0 90.8 jit_solution(17383283511931442340)
XLA Ops:
  1.4 1.1 %fusion.8 = (bf16[128,512]{1,0:T(8,128)(2,1)S(1)}, bf16[128,512]{1,0:T(8,128)(2,1)S(1)}, bf16[128,512]{1,0:T(8,128)(2,1)S(1)}, bf16[128,512]{1,0:T(8,128)(2,1)S(1)}) fusion(bf16[128,1024]{1,0:T(8,128)(2,1)} %bitcast.56, bf16[128,1024]{1,0:T(8,128)(2,1)} %bitcast.59), kind=kLoop, calls=%fused_computation.65 | loop fusion | bytes 1048576 | tf_op jit(solution)/shard_map/slice | solution.py:217
  3.3 3.0 %collective-permute-start = (bf16[128,1152]{1,0:T(8,128)(2,1)}, bf16[128,1152]{1,0:T(8,128)(2,1)S(1)}, u32[]{:S(2)}, u32[]{:S(2)}) collective-permute-start(bf16[128,1152]{1,0:T(8,128)(2,1)} %slice_select_fusion), channel_id=1, source_target_pairs={{0,1},{1,0},{2,3},{3,2},{4,5},{5,4},{6,7},{7,6},{8,9},{9,8},{10,11... | collective-permute-start | bytes 884744 | tf_op jit(solution)/shard_map/ppermute | solution.py:226
  7.9 2.1 %collective-permute-start.3 = (bf16[672,128]{1,0:T(8,128)(2,1)S(1)}, bf16[672,128]{1,0:T(8,128)(2,1)S(1)}, u32[]{:S(2)}, u32[]{:S(2)}) collective-permute-start(bf16[672,128]{1,0:T(8,128)(2,1)S(1)} %bitcast.77), channel_id=1, source_target_pairs={{0,4},{2,6},{4,0},{6,2},{8,12},{10,14},{12,8},{14,10},{16,20},{18,... | collective-permute-start | bytes 516104 | tf_op jit(solution)/shard_map/ppermute | solution.py:202
  10.0 4.3 %collective-permute-done.refs_5_.refs_6_ = bf16[128,1152]{1,0:T(8,128)(2,1)S(1)} collective-permute-done((bf16[128,1152]{1,0:T(8,128)(2,1)}, bf16[128,1152]{1,0:T(8,128)(2,1)S(1)}, u32[]{:S(2)}, u32[]{:S(2)}) %collective-permute-start) | collective-permute-done | bytes 294944 | tf_op jit(solution)/shard_map/ppermute | solution.py:226
  14.4 2.6 %shard_map.93 = (bf16[128,1024]{1,0:T(8,128)(2,1)S(1)}, bf16[128,512]{1,0:T(8,128)(2,1)}, bf16[128,512]{1,0:T(8,128)(2,1)S(1)}, bf16[128,512]{1,0:T(8,128)(2,1)S...) custom-call(s32[1]{0:T(128)} %bitcast.place_ref, s32[1,128]{1,0:T(1,128)S(1)} %copy-done.8, ...), custom_call_target="tpu_custom_call" | custom-call | flops 1024 | bytes 1024 | tf_op jit(solution)/shard_map/pallas_call | solution.py:112
  18.2 2.1 %collective-permute-start.5 = (bf16[128,512]{1,0:T(8,128)(2,1)}, bf16[128,512]{1,0:T(8,128)(2,1)}, u32[]{:S(2)}, u32[]{:S(2)}) collective-permute-start(bf16[128,512]{1,0:T(8,128)(2,1)} %get-tuple-element.52), channel_id=1, source_target_pairs={{0,1},{1,0},{2,3},{3,2},{4,5},{5,4},{6,7},{7,6},{8,9},{9,8},{10,11... | collective-permute-start | bytes 393224 | tf_op jit(solution)/shard_map/ppermute | solution.py:286
  20.3 1.3 %collective-permute-start.6 = (bf16[128,512]{1,0:T(8,128)(2,1)S(1)}, bf16[128,512]{1,0:T(8,128)(2,1)}, u32[]{:S(2)}, u32[]{:S(2)}) collective-permute-start(bf16[128,512]{1,0:T(8,128)(2,1)S(1)} %get-tuple-element.60), channel_id=1, source_target_pairs={{1,0},{3,2},{5,4},{7,6},{9,8},{11,10},{13,12},{15,14},{17,16},{19,... | collective-permute-start | bytes 393224 | tf_op jit(solution)/shard_map/ppermute | solution.py:287
  21.6 1.2 %collective-permute-done.1.refs_5_ = bf16[128,1536]{1,0:T(8,128)(2,1)S(1)} collective-permute-done((bf16[128,1536]{1,0:T(8,128)(2,1)}, bf16[128,1536]{1,0:T(8,128)(2,1)S(1)}, u32[]{:S(2)}, u32[]{:S(2)}) %collective-permute-start.1) | collective-permute-done | bytes 393248 | tf_op jit(solution)/shard_map/ppermute | solution.py:226
  23.7 2.2 %copy.19 = bf16[2688,128]{1,0:T(8,128)(2,1)} copy(bf16[2688,128]{0,1:T(8,128)(2,1)} %maximum_bitcast_fusion) | data formatting | bytes 1376256 | tf_op jit(solution)/shard_map/transpose | solution.py:235
  25.9 1.2 %constant_dynamic-slice_fusion.7 = (bf16[1,2,2,168,128]{4,3,2,1,0:T(8,128)(2,1)S(1)}, bf16[1,2,2,168,128]{4,3,2,1,0:T(8,128)(2,1)S(1)}, bf16[1,2,2,168,128]{4,3,...) fusion(bf16[4,2,2,168,128]{4,3,2,1,0:T(8,128)(2,1)} %bitcast.69, s32[]{:T(128)S(6)} %select_n.136, s32[]{:T(128)S(6)} %select_n.139, ...), kind=kLoop, calls=%fused_computation.55 | loop fusion | bytes 1376272 | tf_op jit(solution)/shard_map/jit(dynamic_index_in_dim)/dynamic_slice | solution.py:236
  27.3 4.1 %collective-permute-start.9 = (bf16[4,336,128]{2,1,0:T(8,128)(2,1)S(1)}, bf16[4,336,128]{2,1,0:T(8,128)(2,1)S(1)}, u32[]{:S(2)}, u32[]{:S(2)}) collective-permute-start(bf16[4,336,128]{2,1,0:T(8,128)(2,1)S(1)} %pad_maximum_fusion.3), channel_id=1, source_target_pairs={{0,1},{2,3},{4,5},{6,7},{8,9},{10,11},{12,13},{14,15},{16,17},{18,... | collective-permute-start | bytes 1032200 | tf_op jit(solution)/shard_map/ppermute | solution.py:292
  31.4 1.9 %shard_map.94 = (bf16[128,1024]{1,0:T(8,128)(2,1)S(1)}, bf16[128,512]{1,0:T(8,128)(2,1)S(1)}, bf16[128,512]{1,0:T(8,128)(2,1)S(1)}, bf16[128,512]{1,0:T(8,128)(2...) custom-call(s32[1]{0:T(128)} %bitcast.place_ref, s32[1,128]{1,0:T(1,128)S(1)} %copy-done.8, ...), custom_call_target="tpu_custom_call" | custom-call | flops 1024 | bytes 1024 | tf_op jit(solution)/shard_map/pallas_call | solution.py:112
  33.5 1.3 %collective-permute-start.8 = (bf16[128,512]{1,0:T(8,128)(2,1)S(1)}, bf16[128,512]{1,0:T(8,128)(2,1)S(1)}, u32[]{:S(2)}, u32[]{:S(2)}) collective-permute-start(bf16[128,512]{1,0:T(8,128)(2,1)S(1)} %get-tuple-element.69), channel_id=1, source_target_pairs={{1,0},{3,2},{5,4},{7,6},{9,8},{11,10},{13,12},{15,14},{17,16},{19,... | collective-permute-start | bytes 393224 | tf_op jit(solution)/shard_map/ppermute | solution.py:287
  35.9 1.6 %collective-permute-start.19 = (bf16[256,512]{1,0:T(8,128)(2,1)S(1)}, bf16[256,512]{1,0:T(8,128)(2,1)S(1)}, u32[]{:S(2)}, u32[]{:S(2)}) collective-permute-start(bf16[256,512]{1,0:T(8,128)(2,1)S(1)} %pad_maximum_fusion.4.refs_4_), channel_id=1, source_target_pairs={{0,4},{2,6},{4,0},{6,2},{8,12},{10,14},{12,8},{14,10},{16,20},{18,... | collective-permute-start | bytes 786440 | tf_op jit(solution)/shard_map/ppermute | solution.py:202
  37.5 2.1 %collective-permute-start.10 = (bf16[672,128]{1,0:T(8,128)(2,1)S(1)}, bf16[672,128]{1,0:T(8,128)(2,1)S(1)}, u32[]{:S(2)}, u32[]{:S(2)}) collective-permute-start(bf16[672,128]{1,0:T(8,128)(2,1)S(1)} %bitcast.79), channel_id=1, source_target_pairs={{0,2},{2,0},{4,6},{6,4},{8,10},{10,8},{12,14},{14,12},{16,18},{18,... | collective-permute-start | bytes 516104 | tf_op jit(solution)/shard_map/ppermute | solution.py:201
  39.6 3.1 %collective-permute-start.11 = (bf16[672,128]{1,0:T(8,128)(2,1)S(1)}, bf16[672,128]{1,0:T(8,128)(2,1)S(1)}, u32[]{:S(2)}, u32[]{:S(2)}) collective-permute-start(bf16[672,128]{1,0:T(8,128)(2,1)S(1)} %bitcast.76), channel_id=1, source_target_pairs={{0,4},{2,6},{4,0},{6,2},{8,12},{10,14},{12,8},{14,10},{16,20},{18,... | collective-permute-start | bytes 516104 | tf_op jit(solution)/shard_map/ppermute | solution.py:201
  42.7 2.5 %collective-permute-start.12 = (bf16[672,128]{1,0:T(8,128)(2,1)S(1)}, bf16[672,128]{1,0:T(8,128)(2,1)S(1)}, u32[]{:S(2)}, u32[]{:S(2)}) collective-permute-start(bf16[672,128]{1,0:T(8,128)(2,1)S(1)} %bitcast.74), channel_id=1, source_target_pairs={{0,6},{2,4},{4,2},{6,0},{8,14},{10,12},{12,10},{14,8},{16,22},{18,... | collective-permute-start | bytes 516104 | tf_op jit(solution)/shard_map/ppermute | solution.py:201
  45.9 2.8 %collective-permute-done.11.refs_11_ = bf16[672,128]{1,0:T(8,128)(2,1)S(1)} collective-permute-done((bf16[672,128]{1,0:T(8,128)(2,1)S(1)}, bf16[672,128]{1,0:T(8,128)(2,1)S(1)}, u32[]{:S(2)}, u32[]{:S(2)}) %collective-permute-start.11) | collective-permute-done | bytes 172064 | tf_op jit(solution)/shard_map/ppermute | solution.py:201
  48.7 2.9 %collective-permute-done.12.refs_12_ = bf16[672,128]{1,0:T(8,128)(2,1)S(1)} collective-permute-done((bf16[672,128]{1,0:T(8,128)(2,1)S(1)}, bf16[672,128]{1,0:T(8,128)(2,1)S(1)}, u32[]{:S(2)}, u32[]{:S(2)}) %collective-permute-start.12) | collective-permute-done | bytes 172064 | tf_op jit(solution)/shard_map/ppermute | solution.py:201
  53.2 1.3 %collective-permute-start.16 = (bf16[4,336,128]{2,1,0:T(8,128)(2,1)S(1)}, bf16[4,336,128]{2,1,0:T(8,128)(2,1)S(1)}, u32[]{:S(2)}, u32[]{:S(2)}) collective-permute-start(bf16[4,336,128]{2,1,0:T(8,128)(2,1)S(1)} %pad_maximum_fusion.2), channel_id=1, source_target_pairs={{0,1},{2,3},{4,5},{6,7},{8,9},{10,11},{12,13},{14,15},{16,17},{18,... | collective-permute-start | bytes 1032200 | tf_op jit(solution)/shard_map/ppermute | solution.py:303
  55.2 1.6 %collective-permute-start.21 = (bf16[336,256]{1,0:T(8,128)(2,1)S(1)}, bf16[336,256]{1,0:T(8,128)(2,1)S(1)}, u32[]{:S(2)}, u32[]{:S(2)}) collective-permute-start(bf16[336,256]{1,0:T(8,128)(2,1)S(1)} %get-tuple-element.91), channel_id=1, source_target_pairs={{0,8},{2,10},{4,12},{6,14},{8,0},{10,2},{12,4},{14,6},{16,24},{18,... | collective-permute-start | bytes 516104 | tf_op jit(solution)/shard_map/ppermute | solution.py:202
  56.8 3.4 %collective-permute-done.14.refs_6_ = bf16[256,512]{1,0:T(8,128)(2,1)S(1)} collective-permute-done((bf16[256,512]{1,0:T(8,128)(2,1)S(1)}, bf16[256,512]{1,0:T(8,128)(2,1)S(1)}, u32[]{:S(2)}, u32[]{:S(2)}) %collective-permute-start.14) | collective-permute-done | bytes 262176 | tf_op jit(solution)/shard_map/ppermute | solution.py:202
  61.0 1.6 %collective-permute-start.23 = (bf16[336,256]{1,0:T(8,128)(2,1)S(1)}, bf16[336,256]{1,0:T(8,128)(2,1)S(1)}, u32[]{:S(2)}, u32[]{:S(2)}) collective-permute-start(bf16[336,256]{1,0:T(8,128)(2,1)S(1)} %get-tuple-element.93), channel_id=1, source_target_pairs={{0,8},{2,10},{4,12},{6,14},{8,0},{10,2},{12,4},{14,6},{16,24},{18,... | collective-permute-start | bytes 516104 | tf_op jit(solution)/shard_map/ppermute | solution.py:202
  63.6 1.2 %collective-permute-start.27 = (bf16[336,256]{1,0:T(8,128)(2,1)S(1)}, bf16[336,256]{1,0:T(8,128)(2,1)S(1)}, u32[]{:S(2)}, u32[]{:S(2)}) collective-permute-start(bf16[336,256]{1,0:T(8,128)(2,1)S(1)} %get-tuple-element.97), channel_id=1, source_target_pairs={{0,8},{2,10},{4,12},{6,14},{8,0},{10,2},{12,4},{14,6},{16,24},{18,... | collective-permute-start | bytes 516104 | tf_op jit(solution)/shard_map/ppermute | solution.py:202
  66.3 2.7 %collective-permute-start.22 = (bf16[168,256]{1,0:T(8,128)(2,1)S(1)}, bf16[168,256]{1,0:T(8,128)(2,1)S(1)}, u32[]{:S(2)}, u32[]{:S(2)}) collective-permute-start(bf16[168,256]{1,0:T(8,128)(2,1)S(1)} %slice.138), channel_id=1, source_target_pairs={{0,16},{2,18},{4,20},{6,22},{8,24},{10,26},{12,28},{14,30},{16,0},... | collective-permute-start | bytes 258056 | tf_op jit(solution)/shard_map/ppermute | solution.py:202
  69.0 1.8 %collective-permute-start.24 = (bf16[168,256]{1,0:T(8,128)(2,1)S(1)}, bf16[168,256]{1,0:T(8,128)(2,1)S(1)}, u32[]{:S(2)}, u32[]{:S(2)}) collective-permute-start(bf16[168,256]{1,0:T(8,128)(2,1)S(1)} %slice.137), channel_id=1, source_target_pairs={{0,16},{2,18},{4,20},{6,22},{8,24},{10,26},{12,28},{14,30},{16,0},... | collective-permute-start | bytes 258056 | tf_op jit(solution)/shard_map/ppermute | solution.py:202
  70.8 1.3 %collective-permute-start.17 = (bf16[128,1024]{1,0:T(8,128)(2,1)S(1)}, bf16[128,1024]{1,0:T(8,128)(2,1)S(1)}, u32[]{:S(2)}, u32[]{:S(2)}) collective-permute-start(bf16[128,1024]{1,0:T(8,128)(2,1)S(1)} %pad_maximum_fusion.5), channel_id=1, source_target_pairs={{1,0},{3,2},{5,4},{7,6},{9,8},{11,10},{13,12},{15,14},{17,16},{19,... | collective-permute-start | bytes 786440 | tf_op jit(solution)/shard_map/ppermute | solution.py:354
  72.1 4.3 %collective-permute-done.22 = bf16[168,256]{1,0:T(8,128)(2,1)S(1)} collective-permute-done((bf16[168,256]{1,0:T(8,128)(2,1)S(1)}, bf16[168,256]{1,0:T(8,128)(2,1)S(1)}, u32[]{:S(2)}, u32[]{:S(2)}) %collective-permute-start.22) | collective-permute-done | bytes 86048 | tf_op jit(solution)/shard_map/ppermute | solution.py:202
  76.5 1.4 %collective-permute-done.24 = bf16[168,256]{1,0:T(8,128)(2,1)S(1)} collective-permute-done((bf16[168,256]{1,0:T(8,128)(2,1)S(1)}, bf16[168,256]{1,0:T(8,128)(2,1)S(1)}, u32[]{:S(2)}, u32[]{:S(2)}) %collective-permute-start.24) | collective-permute-done | bytes 86048 | tf_op jit(solution)/shard_map/ppermute | solution.py:202
  78.9 2.6 %collective-permute-start.26 = (bf16[168,256]{1,0:T(8,128)(2,1)S(1)}, bf16[168,256]{1,0:T(8,128)(2,1)S(1)}, u32[]{:S(2)}, u32[]{:S(2)}) collective-permute-start(bf16[168,256]{1,0:T(8,128)(2,1)S(1)} %slice.136), channel_id=1, source_target_pairs={{0,16},{2,18},{4,20},{6,22},{8,24},{10,26},{12,28},{14,30},{16,0},... | collective-permute-start | bytes 258056 | tf_op jit(solution)/shard_map/ppermute | solution.py:202
  82.0 2.3 %collective-permute-done.26 = bf16[168,256]{1,0:T(8,128)(2,1)S(1)} collective-permute-done((bf16[168,256]{1,0:T(8,128)(2,1)S(1)}, bf16[168,256]{1,0:T(8,128)(2,1)S(1)}, u32[]{:S(2)}, u32[]{:S(2)}) %collective-permute-start.26) | collective-permute-done | bytes 86048 | tf_op jit(solution)/shard_map/ppermute | solution.py:202
  84.3 5.5 %collective-permute-done.28 = bf16[168,256]{1,0:T(8,128)(2,1)S(1)} collective-permute-done((bf16[168,256]{1,0:T(8,128)(2,1)S(1)}, bf16[168,256]{1,0:T(8,128)(2,1)S(1)}, u32[]{:S(2)}, u32[]{:S(2)}) %collective-permute-start.28) | collective-permute-done | bytes 86048 | tf_op jit(solution)/shard_map/ppermute | solution.py:202
  (96 shorter events, 15.5 us)
Async XLA Ops:
  3.3 11.0 %collective-permute-start = (bf16[128,1152]{1,0:T(8,128)(2,1)}, bf16[128,1152]{1,0:T(8,128)(2,1)S(1)}, u32[]{:S(2)}, u32[]{:S(2)}) collective-permute-start(bf16[128,1152]{1,0:T(8,128)(2,1)} %slice_select_fusion), channel_id=1, source_target_pairs={{0,1},{1,0},{2,3},{3,2},{4,5},{5,4},{6,7},{7,6},{8,9},{9,8},{10,11... | collective-permute-start | bytes 884744 | tf_op jit(solution)/shard_map/ppermute | solution.py:226
  7.1 15.6 %collective-permute-start.1 = (bf16[128,1536]{1,0:T(8,128)(2,1)}, bf16[128,1536]{1,0:T(8,128)(2,1)S(1)}, u32[]{:S(2)}, u32[]{:S(2)}) collective-permute-start(bf16[128,1536]{1,0:T(8,128)(2,1)} %fusion.3), channel_id=1, source_target_pairs={{0,1},{1,0},{2,3},{3,2},{4,5},{5,4},{6,7},{7,6},{8,9},{9,8},{10,11... | collective-permute-start | bytes 1179656 | tf_op jit(solution)/shard_map/ppermute | solution.py:226
  7.6 6.8 %copy-start.3 = (bf16[1,128,2048]{2,1,0:T(8,128)(2,1)S(1)}, bf16[1,128,2048]{2,1,0:T(8,128)(2,1)}, u32[]{:S(2)}) copy-start(bf16[1,128,2048]{2,1,0:T(8,128)(2,1)} %param.10) | copy-start | bytes 1572868
  7.7 6.6 %copy-start = (bf16[1,128,1024]{2,1,0:T(8,128)(2,1)S(1)}, bf16[1,128,1024]{2,1,0:T(8,128)(2,1)}, u32[]{:S(2)}) copy-start(bf16[1,128,1024]{2,1,0:T(8,128)(2,1)} %param.8) | copy-start | bytes 786436
  7.8 12.5 %collective-permute-start.2 = (bf16[672,128]{1,0:T(8,128)(2,1)S(1)}, bf16[672,128]{1,0:T(8,128)(2,1)S(1)}, u32[]{:S(2)}, u32[]{:S(2)}) collective-permute-start(bf16[672,128]{1,0:T(8,128)(2,1)S(1)} %bitcast.78), channel_id=1, source_target_pairs={{0,2},{2,0},{4,6},{6,4},{8,10},{10,8},{12,14},{14,12},{16,18},{18,... | collective-permute-start | bytes 516104 | tf_op jit(solution)/shard_map/ppermute | solution.py:202
  7.9 13.7 %collective-permute-start.3 = (bf16[672,128]{1,0:T(8,128)(2,1)S(1)}, bf16[672,128]{1,0:T(8,128)(2,1)S(1)}, u32[]{:S(2)}, u32[]{:S(2)}) collective-permute-start(bf16[672,128]{1,0:T(8,128)(2,1)S(1)} %bitcast.77), channel_id=1, source_target_pairs={{0,4},{2,6},{4,0},{6,2},{8,12},{10,14},{12,8},{14,10},{16,20},{18,... | collective-permute-start | bytes 516104 | tf_op jit(solution)/shard_map/ppermute | solution.py:202
  10.0 11.6 %collective-permute-start.4 = (bf16[672,128]{1,0:T(8,128)(2,1)S(1)}, bf16[672,128]{1,0:T(8,128)(2,1)S(1)}, u32[]{:S(2)}, u32[]{:S(2)}) collective-permute-start(bf16[672,128]{1,0:T(8,128)(2,1)S(1)} %bitcast.75), channel_id=1, source_target_pairs={{0,6},{2,4},{4,2},{6,0},{8,14},{10,12},{12,10},{14,8},{16,22},{18,... | collective-permute-start | bytes 516104 | tf_op jit(solution)/shard_map/ppermute | solution.py:202
  18.2 15.2 %collective-permute-start.5 = (bf16[128,512]{1,0:T(8,128)(2,1)}, bf16[128,512]{1,0:T(8,128)(2,1)}, u32[]{:S(2)}, u32[]{:S(2)}) collective-permute-start(bf16[128,512]{1,0:T(8,128)(2,1)} %get-tuple-element.52), channel_id=1, source_target_pairs={{0,1},{1,0},{2,3},{3,2},{4,5},{5,4},{6,7},{7,6},{8,9},{9,8},{10,11... | collective-permute-start | bytes 393224 | tf_op jit(solution)/shard_map/ppermute | solution.py:286
  20.3 13.1 %collective-permute-start.6 = (bf16[128,512]{1,0:T(8,128)(2,1)S(1)}, bf16[128,512]{1,0:T(8,128)(2,1)}, u32[]{:S(2)}, u32[]{:S(2)}) collective-permute-start(bf16[128,512]{1,0:T(8,128)(2,1)S(1)} %get-tuple-element.60), channel_id=1, source_target_pairs={{1,0},{3,2},{5,4},{7,6},{9,8},{11,10},{13,12},{15,14},{17,16},{19,... | collective-permute-start | bytes 393224 | tf_op jit(solution)/shard_map/ppermute | solution.py:287
  27.3 24.3 %collective-permute-start.9 = (bf16[4,336,128]{2,1,0:T(8,128)(2,1)S(1)}, bf16[4,336,128]{2,1,0:T(8,128)(2,1)S(1)}, u32[]{:S(2)}, u32[]{:S(2)}) collective-permute-start(bf16[4,336,128]{2,1,0:T(8,128)(2,1)S(1)} %pad_maximum_fusion.3), channel_id=1, source_target_pairs={{0,1},{2,3},{4,5},{6,7},{8,9},{10,11},{12,13},{14,15},{16,17},{18,... | collective-permute-start | bytes 1032200 | tf_op jit(solution)/shard_map/ppermute | solution.py:292
  33.4 6.2 %collective-permute-start.7 = (bf16[128,512]{1,0:T(8,128)(2,1)S(1)}, bf16[128,512]{1,0:T(8,128)(2,1)S(1)}, u32[]{:S(2)}, u32[]{:S(2)}) collective-permute-start(bf16[128,512]{1,0:T(8,128)(2,1)S(1)} %get-tuple-element.68), channel_id=1, source_target_pairs={{0,1},{1,0},{2,3},{3,2},{4,5},{5,4},{6,7},{7,6},{8,9},{9,8},{10,11... | collective-permute-start | bytes 393224 | tf_op jit(solution)/shard_map/ppermute | solution.py:286
  33.5 9.2 %collective-permute-start.8 = (bf16[128,512]{1,0:T(8,128)(2,1)S(1)}, bf16[128,512]{1,0:T(8,128)(2,1)S(1)}, u32[]{:S(2)}, u32[]{:S(2)}) collective-permute-start(bf16[128,512]{1,0:T(8,128)(2,1)S(1)} %get-tuple-element.69), channel_id=1, source_target_pairs={{1,0},{3,2},{5,4},{7,6},{9,8},{11,10},{13,12},{15,14},{17,16},{19,... | collective-permute-start | bytes 393224 | tf_op jit(solution)/shard_map/ppermute | solution.py:287
  35.9 9.8 %collective-permute-start.19 = (bf16[256,512]{1,0:T(8,128)(2,1)S(1)}, bf16[256,512]{1,0:T(8,128)(2,1)S(1)}, u32[]{:S(2)}, u32[]{:S(2)}) collective-permute-start(bf16[256,512]{1,0:T(8,128)(2,1)S(1)} %pad_maximum_fusion.4.refs_4_), channel_id=1, source_target_pairs={{0,4},{2,6},{4,0},{6,2},{8,12},{10,14},{12,8},{14,10},{16,20},{18,... | collective-permute-start | bytes 786440 | tf_op jit(solution)/shard_map/ppermute | solution.py:202
  37.5 14.8 %copy-start.5 = (bf16[128,512]{1,0:T(8,128)(2,1)S(1)}, bf16[128,512]{1,0:T(8,128)(2,1)}, u32[]{:S(2)}) copy-start(bf16[128,512]{1,0:T(8,128)(2,1)} %copy-done.4) | copy-start | bytes 393220
  37.5 7.8 %collective-permute-start.10 = (bf16[672,128]{1,0:T(8,128)(2,1)S(1)}, bf16[672,128]{1,0:T(8,128)(2,1)S(1)}, u32[]{:S(2)}, u32[]{:S(2)}) collective-permute-start(bf16[672,128]{1,0:T(8,128)(2,1)S(1)} %bitcast.79), channel_id=1, source_target_pairs={{0,2},{2,0},{4,6},{6,4},{8,10},{10,8},{12,14},{14,12},{16,18},{18,... | collective-permute-start | bytes 516104 | tf_op jit(solution)/shard_map/ppermute | solution.py:201
  39.6 9.1 %collective-permute-start.11 = (bf16[672,128]{1,0:T(8,128)(2,1)S(1)}, bf16[672,128]{1,0:T(8,128)(2,1)S(1)}, u32[]{:S(2)}, u32[]{:S(2)}) collective-permute-start(bf16[672,128]{1,0:T(8,128)(2,1)S(1)} %bitcast.76), channel_id=1, source_target_pairs={{0,4},{2,6},{4,0},{6,2},{8,12},{10,14},{12,8},{14,10},{16,20},{18,... | collective-permute-start | bytes 516104 | tf_op jit(solution)/shard_map/ppermute | solution.py:201
  42.7 8.8 %collective-permute-start.12 = (bf16[672,128]{1,0:T(8,128)(2,1)S(1)}, bf16[672,128]{1,0:T(8,128)(2,1)S(1)}, u32[]{:S(2)}, u32[]{:S(2)}) collective-permute-start(bf16[672,128]{1,0:T(8,128)(2,1)S(1)} %bitcast.74), channel_id=1, source_target_pairs={{0,6},{2,4},{4,2},{6,0},{8,14},{10,12},{12,10},{14,8},{16,22},{18,... | collective-permute-start | bytes 516104 | tf_op jit(solution)/shard_map/ppermute | solution.py:201
  45.3 9.3 %collective-permute-start.18 = (bf16[256,512]{1,0:T(8,128)(2,1)S(1)}, bf16[256,512]{1,0:T(8,128)(2,1)S(1)}, u32[]{:S(2)}, u32[]{:S(2)}) collective-permute-start(bf16[256,512]{1,0:T(8,128)(2,1)S(1)} %pad_maximum_fusion.4.refs_4_), channel_id=1, source_target_pairs={{0,2},{2,0},{4,6},{6,4},{8,10},{10,8},{12,14},{14,12},{16,18},{18,... | collective-permute-start | bytes 786440 | tf_op jit(solution)/shard_map/ppermute | solution.py:202
  45.7 9.0 %collective-permute-start.20 = (bf16[256,512]{1,0:T(8,128)(2,1)S(1)}, bf16[256,512]{1,0:T(8,128)(2,1)S(1)}, u32[]{:S(2)}, u32[]{:S(2)}) collective-permute-start(bf16[256,512]{1,0:T(8,128)(2,1)S(1)} %collective-permute-done.19.refs_6_), channel_id=1, source_target_pairs={{0,2},{2,0},{4,6},{6,4},{8,10},{10,8},{12,14},{14,12},{16,18},{18,... | collective-permute-start | bytes 786440 | tf_op jit(solution)/shard_map/ppermute | solution.py:202
  51.7 8.5 %collective-permute-start.14 = (bf16[256,512]{1,0:T(8,128)(2,1)S(1)}, bf16[256,512]{1,0:T(8,128)(2,1)S(1)}, u32[]{:S(2)}, u32[]{:S(2)}) collective-permute-start(bf16[256,512]{1,0:T(8,128)(2,1)S(1)} %pad_maximum_fusion.6.refs_4_), channel_id=1, source_target_pairs={{0,4},{2,6},{4,0},{6,2},{8,12},{10,14},{12,8},{14,10},{16,20},{18,... | collective-permute-start | bytes 786440 | tf_op jit(solution)/shard_map/ppermute | solution.py:202
  53.2 9.3 %collective-permute-start.16 = (bf16[4,336,128]{2,1,0:T(8,128)(2,1)S(1)}, bf16[4,336,128]{2,1,0:T(8,128)(2,1)S(1)}, u32[]{:S(2)}, u32[]{:S(2)}) collective-permute-start(bf16[4,336,128]{2,1,0:T(8,128)(2,1)S(1)} %pad_maximum_fusion.2), channel_id=1, source_target_pairs={{0,1},{2,3},{4,5},{6,7},{8,9},{10,11},{12,13},{14,15},{16,17},{18,... | collective-permute-start | bytes 1032200 | tf_op jit(solution)/shard_map/ppermute | solution.py:303
  54.5 8.0 %collective-permute-start.13 = (bf16[256,512]{1,0:T(8,128)(2,1)S(1)}, bf16[256,512]{1,0:T(8,128)(2,1)S(1)}, u32[]{:S(2)}, u32[]{:S(2)}) collective-permute-start(bf16[256,512]{1,0:T(8,128)(2,1)S(1)} %pad_maximum_fusion.6.refs_4_), channel_id=1, source_target_pairs={{0,2},{2,0},{4,6},{6,4},{8,10},{10,8},{12,14},{14,12},{16,18},{18,... | collective-permute-start | bytes 786440 | tf_op jit(solution)/shard_map/ppermute | solution.py:202
  55.2 11.1 %collective-permute-start.21 = (bf16[336,256]{1,0:T(8,128)(2,1)S(1)}, bf16[336,256]{1,0:T(8,128)(2,1)S(1)}, u32[]{:S(2)}, u32[]{:S(2)}) collective-permute-start(bf16[336,256]{1,0:T(8,128)(2,1)S(1)} %get-tuple-element.91), channel_id=1, source_target_pairs={{0,8},{2,10},{4,12},{6,14},{8,0},{10,2},{12,4},{14,6},{16,24},{18,... | collective-permute-start | bytes 516104 | tf_op jit(solution)/shard_map/ppermute | solution.py:202
  60.2 2.4 %collective-permute-start.15 = (bf16[256,512]{1,0:T(8,128)(2,1)S(1)}, bf16[256,512]{1,0:T(8,128)(2,1)S(1)}, u32[]{:S(2)}, u32[]{:S(2)}) collective-permute-start(bf16[256,512]{1,0:T(8,128)(2,1)S(1)} %collective-permute-done.14.refs_6_), channel_id=1, source_target_pairs={{0,2},{2,0},{4,6},{6,4},{8,10},{10,8},{12,14},{14,12},{16,18},{18,... | collective-permute-start | bytes 786440 | tf_op jit(solution)/shard_map/ppermute | solution.py:202
  61.0 8.0 %collective-permute-start.23 = (bf16[336,256]{1,0:T(8,128)(2,1)S(1)}, bf16[336,256]{1,0:T(8,128)(2,1)S(1)}, u32[]{:S(2)}, u32[]{:S(2)}) collective-permute-start(bf16[336,256]{1,0:T(8,128)(2,1)S(1)} %get-tuple-element.93), channel_id=1, source_target_pairs={{0,8},{2,10},{4,12},{6,14},{8,0},{10,2},{12,4},{14,6},{16,24},{18,... | collective-permute-start | bytes 516104 | tf_op jit(solution)/shard_map/ppermute | solution.py:202
  63.6 17.8 %collective-permute-start.27 = (bf16[336,256]{1,0:T(8,128)(2,1)S(1)}, bf16[336,256]{1,0:T(8,128)(2,1)S(1)}, u32[]{:S(2)}, u32[]{:S(2)}) collective-permute-start(bf16[336,256]{1,0:T(8,128)(2,1)S(1)} %get-tuple-element.97), channel_id=1, source_target_pairs={{0,8},{2,10},{4,12},{6,14},{8,0},{10,2},{12,4},{14,6},{16,24},{18,... | collective-permute-start | bytes 516104 | tf_op jit(solution)/shard_map/ppermute | solution.py:202
  64.8 14.0 %collective-permute-start.25 = (bf16[336,256]{1,0:T(8,128)(2,1)S(1)}, bf16[336,256]{1,0:T(8,128)(2,1)S(1)}, u32[]{:S(2)}, u32[]{:S(2)}) collective-permute-start(bf16[336,256]{1,0:T(8,128)(2,1)S(1)} %get-tuple-element.95), channel_id=1, source_target_pairs={{0,8},{2,10},{4,12},{6,14},{8,0},{10,2},{12,4},{14,6},{16,24},{18,... | collective-permute-start | bytes 516104 | tf_op jit(solution)/shard_map/ppermute | solution.py:202
  66.3 10.2 %collective-permute-start.22 = (bf16[168,256]{1,0:T(8,128)(2,1)S(1)}, bf16[168,256]{1,0:T(8,128)(2,1)S(1)}, u32[]{:S(2)}, u32[]{:S(2)}) collective-permute-start(bf16[168,256]{1,0:T(8,128)(2,1)S(1)} %slice.138), channel_id=1, source_target_pairs={{0,16},{2,18},{4,20},{6,22},{8,24},{10,26},{12,28},{14,30},{16,0},... | collective-permute-start | bytes 258056 | tf_op jit(solution)/shard_map/ppermute | solution.py:202
  69.0 8.9 %collective-permute-start.24 = (bf16[168,256]{1,0:T(8,128)(2,1)S(1)}, bf16[168,256]{1,0:T(8,128)(2,1)S(1)}, u32[]{:S(2)}, u32[]{:S(2)}) collective-permute-start(bf16[168,256]{1,0:T(8,128)(2,1)S(1)} %slice.137), channel_id=1, source_target_pairs={{0,16},{2,18},{4,20},{6,22},{8,24},{10,26},{12,28},{14,30},{16,0},... | collective-permute-start | bytes 258056 | tf_op jit(solution)/shard_map/ppermute | solution.py:202
  70.8 19.0 %collective-permute-start.17 = (bf16[128,1024]{1,0:T(8,128)(2,1)S(1)}, bf16[128,1024]{1,0:T(8,128)(2,1)S(1)}, u32[]{:S(2)}, u32[]{:S(2)}) collective-permute-start(bf16[128,1024]{1,0:T(8,128)(2,1)S(1)} %pad_maximum_fusion.5), channel_id=1, source_target_pairs={{1,0},{3,2},{5,4},{7,6},{9,8},{11,10},{13,12},{15,14},{17,16},{19,... | collective-permute-start | bytes 786440 | tf_op jit(solution)/shard_map/ppermute | solution.py:354
  78.9 5.5 %collective-permute-start.26 = (bf16[168,256]{1,0:T(8,128)(2,1)S(1)}, bf16[168,256]{1,0:T(8,128)(2,1)S(1)}, u32[]{:S(2)}, u32[]{:S(2)}) collective-permute-start(bf16[168,256]{1,0:T(8,128)(2,1)S(1)} %slice.136), channel_id=1, source_target_pairs={{0,16},{2,18},{4,20},{6,22},{8,24},{10,26},{12,28},{14,30},{16,0},... | collective-permute-start | bytes 258056 | tf_op jit(solution)/shard_map/ppermute | solution.py:202
  81.5 8.3 %collective-permute-start.28 = (bf16[168,256]{1,0:T(8,128)(2,1)S(1)}, bf16[168,256]{1,0:T(8,128)(2,1)S(1)}, u32[]{:S(2)}, u32[]{:S(2)}) collective-permute-start(bf16[168,256]{1,0:T(8,128)(2,1)S(1)} %slice.135), channel_id=1, source_target_pairs={{0,16},{2,18},{4,20},{6,22},{8,24},{10,26},{12,28},{14,30},{16,0},... | collective-permute-start | bytes 258056 | tf_op jit(solution)/shard_map/ppermute | solution.py:202
  (8 other events, 25.5 us)

commit v6 on v3

v6 whole, which is shorter than its diff:
```python
from functools import partial

import jax
import jax.numpy as jnp
from jax import lax
from jax.experimental import pallas as pl
from jax.experimental.pallas import tpu as pltpu
from jax.sharding import PartitionSpec as P

HD = 128
WIN = 1024
CHUNKS = 2
SCORE_FLOOR = -1e30
MIB = 1024 * 1024
SEG_ROWS = 16
SMALL = pl.CostEstimate(flops=1024, bytes_accessed=1024, transcendentals=0)

NT = (((1,), (1,)), ((), ()))
TN = (((0,), (0,)), ((), ()))


def dot_f32(left, right, dims=(((1,), (0,)), ((), ()))):
    return lax.dot_general(left, right, dims, preferred_element_type=jnp.float32)


def shifted(value, axis, steps):
    count = lax.axis_size(axis)
    leading, last = (max(0, -steps), min(count, count - steps))
    return lax.ppermute(value, axis, [(source, source + steps) for source in range(leading, last)])


def attention_kernel(chunk, hops, group, place_ref, *refs):
    segs_ref, query_ref, grad_ref, key_ref, value_ref = refs[:5]
    rim_pairs, rim_segs, refs = refs[5 : 5 + hops], refs[5 + hops : 5 + 2 * hops], refs[5 + 2 * hops :]
    tok = query_ref.shape[0]
    heads = key_ref.shape[1] // HD
    rim = hops * tok
    span = rim + tok
    place = place_ref[0]
    scale = HD**-0.5

    query_segs = segs_ref[...].astype(jnp.float32)
    key_cols = [
        jnp.transpose(jnp.broadcast_to(ref[...].astype(jnp.float32)[:1], (tok, tok)))
        for ref in (*rim_segs, segs_ref)
    ]
    key_segs = jnp.concatenate(key_cols, axis=0)
    key_at = lax.broadcasted_iota(jnp.int32, (span, tok), 0)
    distance = rim + lax.broadcasted_iota(jnp.int32, (span, tok), 1) - key_at
    allowed = (
        (key_at >= rim - place * tok)
        & (distance >= 0)
        & (distance < WIN)
        & (key_segs == query_segs)
    )
    floor = jnp.where(allowed, 0.0, SCORE_FLOOR)
    floor = jnp.concatenate([floor] * group, axis=1)
    keep = floor == 0.0

    for head in range(heads):
        cols = slice(head * HD, (head + 1) * HD)
        value_cols = slice((heads + head) * HD, (heads + head + 1) * HD)
        q_cols = [slice((head * group + g) * HD, (head * group + g + 1) * HD) for g in range(group)]
        query = jnp.concatenate([query_ref[:, c] for c in q_cols], axis=0)
        grad = jnp.concatenate([grad_ref[:, c] for c in q_cols], axis=0)
        keys = jnp.concatenate([ref[:tok, cols] for ref in rim_pairs] + [key_ref[:, cols]], axis=0)
        values = jnp.concatenate(
            [ref[:tok, value_cols] for ref in rim_pairs] + [value_ref[:, cols]], axis=0
        )
        scores = jnp.where(keep, dot_f32(keys, query, NT) * scale, SCORE_FLOOR)
        weights = jnp.exp(scores - jnp.max(scores, axis=0, keepdims=True))
        probs = weights * (1.0 / jnp.sum(weights, axis=0, keepdims=True))
        probs_low = probs.astype(jnp.bfloat16)
        dprobs = dot_f32(values, grad, NT)
        delta = jnp.sum(probs_low.astype(jnp.float32) * dprobs, axis=0, keepdims=True)
        dscores = (probs * (dprobs - delta)).astype(jnp.bfloat16)
        query_part = (dot_f32(dscores, keys, TN) * scale).astype(jnp.bfloat16)
        key_part = dot_f32(dscores, query) * scale
        value_part = dot_f32(probs_low, grad)
        if hops == 1:
            piece_ref, query_out, sent, addend, key_out, value_out, rim_out = refs
            first = place == 0
            key_rim, key_own = key_part[:tok], key_part[tok:]
            value_rim, value_own = value_part[:tok], value_part[tok:]
            sent[:tok, cols] = jnp.where(first, value_own, key_rim).astype(jnp.bfloat16)
            low = (chunk * heads + head) * tok
            high = min(low + tok, piece_ref.shape[0])
            late = key_own.astype(jnp.bfloat16)
            if low < high:
                part = piece_ref[low:high]
                if high - low < tok:
                    part = jnp.concatenate([part, late[: tok - (high - low)]], axis=0)
                late = jnp.where(first, part, late)
            sent[tok:, cols] = late
            addend[:, cols] = jnp.where(first, key_own, value_rim).astype(jnp.bfloat16)
            key_out[:, cols] = key_own.astype(jnp.bfloat16)
            value_out[:, cols] = value_own.astype(jnp.bfloat16)
            rim_out[:, cols] = value_rim.astype(jnp.bfloat16)
        else:
            query_out = refs[0]
            refs[1][:, cols] = key_part.astype(jnp.bfloat16)
            refs[2][:, cols] = value_part.astype(jnp.bfloat16)
        for g, c in enumerate(q_cols):
            query_out[:, c] = query_part[g * tok : (g + 1) * tok]


def attend(chunk, place, segs, queries, out_grad, keys, values, rim_pairs, rim_segs, piece):
    hops = len(rim_pairs)
    tok = queries.shape[0]
    group = queries.shape[1] // keys.shape[1]
    width = keys.shape[1] // CHUNKS
    span = (hops + 1) * tok
    whole = lambda *shape: pl.BlockSpec(shape, lambda i, *_: (0,) * len(shape))
    part = lambda *shape: pl.BlockSpec(shape, lambda i, *_: (0, chunk))
    seg_row = pl.BlockSpec((SEG_ROWS, tok), lambda i, *_: (tok // SEG_ROWS, 0))
    out_shapes = [(tok, group * width)]
    if hops == 1:
        out_shapes += [(2 * tok, width)] + [(tok, width)] * 4
    else:
        out_shapes += [(span, width)] * 2
    operands = [place, segs, queries, out_grad, keys, values, *rim_pairs, *rim_segs, *piece]
    return pl.pallas_call(
        partial(attention_kernel, chunk, hops, group),
        grid_spec=pltpu.PrefetchScalarGridSpec(
            num_scalar_prefetch=1,
            grid=(1,),
            in_specs=[
                whole(1, tok),
                part(tok, group * width),
                part(tok, group * width),
                part(tok, width),
                part(tok, width),
            ]
            + [whole(tok, 2 * width)] * hops
            + [seg_row] * hops
            + [whole(*array.shape) for array in piece],
            out_specs=[whole(*shape) for shape in out_shapes],
        ),
        out_shape=[jax.ShapeDtypeStruct(shape, jnp.bfloat16) for shape in out_shapes],
        compiler_params=pltpu.CompilerParams(vmem_limit_bytes=48 * MIB),
        cost_estimate=SMALL,
    )(*operands)


def product_kernel(own_ref, others_ref, own_away_ref, others_away_ref, *refs):
    grads = jnp.concatenate([ref[...] for ref in refs[:-1]], axis=0)
    others = range(others_ref.shape[0])
    near = [own_ref[...]] + [others_ref[t] for t in others]
    away = [own_away_ref[...]] + [others_away_ref[t] for t in others]
    features = jnp.concatenate([piece for pair in zip(near, away) for piece in pair], axis=1)
    refs[-1][...] = dot_f32(features, grads).astype(refs[-1].dtype)


def product(half, own, others, own_away, others_away, grads, dtype):
    traces, rows, tok = others.shape
    rows //= 2
    width = grads[0].shape[1]
    of_half = lambda array: pl.BlockSpec((rows, array.shape[1]), lambda i: (half, 0))
    whole = lambda array: pl.BlockSpec(array.shape, lambda i: (0,) * array.ndim)
    return pl.pallas_call(
        product_kernel,
        grid=(1,),
        in_specs=[
            of_half(own),
            pl.BlockSpec((traces, rows, tok), lambda i: (0, half, 0)),
            of_half(own_away),
            whole(others_away),
        ]
        + [whole(piece) for piece in grads],
        out_specs=pl.BlockSpec((rows, width), lambda i: (0, 0)),
        out_shape=jax.ShapeDtypeStruct((rows, width), dtype),
        compiler_params=pltpu.CompilerParams(vmem_limit_bytes=48 * MIB),
        cost_estimate=SMALL,
    )(own, others, own_away, others_away, *grads)


def local(hidden_in, queries, key_states, value_states, out_grad, segment_ids):
    tok = queries.shape[1]
    key_width = key_states.shape[2]
    width = key_width // CHUNKS
    ctx_count = lax.axis_size("ctx")
    hops = min(WIN // tok, ctx_count - 1)
    place = lax.axis_index("ctx")
    first = place == 0
    place_arg = place.astype(jnp.int32).reshape(1)

    dp_count = lax.axis_size("dp")
    slow_count, core_count = 4, 2
    mid_count = dp_count // (slow_count * core_count)
    dp_place = lax.axis_index("dp")
    core_at = dp_place % core_count
    mid_at = dp_place // core_count % mid_count
    slow_at = dp_place // (core_count * mid_count)

    def dp_send(value, move):
        pairs = []
        for source in range(dp_count):
            core = source % core_count
            mid = source // core_count % mid_count
            slow = source // (core_count * mid_count)
            slow, mid, core = move(slow, mid, core)
            pairs.append((source, (slow * mid_count + mid) * core_count + core))
        return lax.ppermute(value, "dp", pairs)

    swap_core = lambda slow, mid, core: (slow, mid, core ^ 1)
    mid_by = lambda step: lambda slow, mid, core: (slow, (mid + step) % mid_count, core)
    flip_slow = lambda bit: lambda slow, mid, core: (slow ^ bit, mid, core)
    swap_ctx = [(c, c ^ 1) for c in range(ctx_count)]

    own_keys, own_values = key_states[0], value_states[0]

    rows = hidden_in.shape[2] // dp_count
    by_feature = hidden_in[0].T.reshape(slow_count, mid_count, core_count, rows, tok)
    by_feature = jnp.stack(
        [lax.dynamic_index_in_dim(by_feature, slow_at ^ turn, 0, False) for turn in (3, 1, 2, 0)]
    )
    of_mid = lambda at: lax.dynamic_index_in_dim(by_feature, at % mid_count, 1, False)
    mids = [of_mid(mid_at)]
    mids += [dp_send(of_mid(mid_at + step), mid_by(step)) for step in range(1, mid_count)]
    share_of = lambda array, core: lax.dynamic_index_in_dim(array, core, -3, False).reshape(
        array.shape[:-4] + (slow_count * rows, tok)
    )
    own_piece = share_of(mids[0], core_at)

    steps = range(hops, 0, -1)
    seg_rows = jnp.broadcast_to(segment_ids.astype(jnp.bfloat16), (SEG_ROWS, tok))
    seg_rows = jnp.pad(seg_rows, ((0, 0), (0, 2 * width - tok)))
    to_rows = lambda array: array.reshape(tok, -1, HD).transpose(1, 0, 2).reshape(-1, HD)
    rim_pairs = []
    for chunk in range(CHUNKS):
        cols = slice(chunk * width, (chunk + 1) * width)
        pair = jnp.concatenate([own_keys[:, cols], own_values[:, cols]], axis=1)
        if chunk == 0:
            pair = jnp.concatenate([pair, seg_rows], axis=0)
        if ctx_count == 2 and chunk == CHUNKS - 1:
            back = jnp.pad(own_piece, ((0, 2 * width - own_piece.shape[0]), (0, 0)))
            back = back.reshape(-1, tok, HD).transpose(1, 0, 2).reshape(tok, -1)
            rim_pairs.append([lax.ppermute(jnp.where(first, pair, back), "ctx", swap_ctx)])
        else:
            rim_pairs.append([shifted(pair, "ctx", step) for step in steps])

    half_rows = slow_count // 2 * rows
    low_high = [(0, half_rows), (half_rows, 2 * half_rows)]

    attended = []
    for chunk in range(CHUNKS):
        if chunk > 0:
            rim_pairs[chunk], _ = lax.optimization_barrier((rim_pairs[chunk], attended[-1][1]))
        attended.append(
            attend(
                chunk,
                place_arg,
                segment_ids,
                queries[0],
                out_grad[0],
                own_keys,
                own_values,
                rim_pairs[chunk],
                rim_pairs[0],
                [own_piece] if hops == 1 else [],
            )
        )
    query_grad = jnp.concatenate([outs[0] for outs in attended], axis=1)

    mids = jnp.stack(mids)
    kept_core, sent_core = share_of(mids, core_at), share_of(mids, 1 - core_at)
    other_core = dp_send(sent_core, swap_core)
    others = jnp.concatenate([kept_core[1:], other_core])

    if ctx_count == 2:
        columns, held_back, others_away = [], [], []
        for chunk, (_, sent, addend, key_own, value_own, _) in enumerate(attended):
            arrived = lax.ppermute(sent, "ctx", swap_ctx)
            held_back.append(to_rows(arrived[tok:]))
            if chunk == 0:
                arrived, _ = lax.optimization_barrier((arrived, rim_pairs[1:]))
            else:
                arrived, _ = lax.optimization_barrier((arrived, columns[-1]))
            total = (addend.astype(jnp.float32) + arrived[:tok].astype(jnp.float32)).astype(
                jnp.bfloat16
            )
            block = jnp.concatenate(
                [jnp.where(first, total, value_own), jnp.where(first, arrived[tok:], total)], axis=0
            )
            if chunk == 0:
                for low, high in low_high:
                    rest, block = lax.optimization_barrier((others[:, low:high], block))
                    others_away.append(lax.ppermute(rest, "ctx", swap_ctx))
            columns.append(block)
        piece_rows = own_piece.shape[0]
        own_away = jnp.where(
            first, to_rows(rim_pairs[-1][0])[:piece_rows], jnp.concatenate(held_back)[:piece_rows]
        )
        key_grad = jnp.where(
            first,
            jnp.concatenate([block[:tok] for block in columns], axis=1),
            jnp.concatenate([outs[3] for outs in attended], axis=1),
        )
    else:
        key_rows = jnp.concatenate([outs[1] for outs in attended], axis=1)
        value_rows = jnp.concatenate([outs[2] for outs in attended], axis=1)
        totals = [part[hops * tok :].astype(jnp.float32) for part in (key_rows, value_rows)]
        for step in range(1, hops + 1):
            low = (hops - step) * tok
            totals = [
                total + shifted(part[low : low + tok], "ctx", -step).astype(jnp.float32)
                for total, part in zip(totals, (key_rows, value_rows))
            ]
        key_grad, value_grad = (total.astype(jnp.bfloat16) for total in totals)
        both = lax.all_to_all(
            jnp.concatenate([key_grad, value_grad], axis=1),
            "ctx",
            split_axis=1,
            concat_axis=0,
            tiled=True,
        )
        columns = jnp.split(both, CHUNKS, axis=1)
        every = jnp.concatenate([own_piece[None], others])
        near, away = jnp.split(lax.all_gather(every, "ctx", axis=2, tiled=True), 2, axis=2)
        own_piece, others, own_away = near[0], near[1:], away[0]
        others_away = [away[1:, low:high] for low, high in low_high]

    gathered = []
    for block in columns:
        near = [block] + [dp_send(block, mid_by(step)) for step in range(1, mid_count)]
        gathered.append(near + [dp_send(near_one, swap_core) for near_one in near])
    together = lambda half, dtype: [
        product(half, own_piece, others, own_away, others_away[half], grads, dtype)
        for grads in gathered
    ]
    sent = together(0, jnp.bfloat16)
    others_away[1], _ = lax.optimization_barrier((others_away[1], sent))
    kept = together(1, jnp.float32)
    halves = [
        near + dp_send(far, flip_slow(1)).astype(jnp.float32) for near, far in zip(kept, sent)
    ]
    if ctx_count == 2:
        value_rim = jnp.concatenate([outs[5] for outs in attended], axis=1)
        value_rim, _ = lax.optimization_barrier((value_rim, halves[0]))
        returned = lax.ppermute(value_rim, "ctx", [(1, 0)])
        value_own = jnp.concatenate([outs[4] for outs in attended], axis=1)
        value_grad = (value_own.astype(jnp.float32) + returned.astype(jnp.float32)).astype(
            jnp.bfloat16
        )
    last = [dp_send(half[:rows].astype(jnp.bfloat16), flip_slow(2)) for half in halves]
    piece_width = halves[0].shape[1]
    weight_grad = jnp.zeros((rows, piece_width * len(halves)), jnp.float32)
    for n, (half, final) in enumerate(zip(halves, last)):
        weight_grad = lax.dynamic_update_slice(
            weight_grad, half[rows:] + final.astype(jnp.float32), (0, n * piece_width)
        )
    return (query_grad[None], key_grad[None], value_grad[None], weight_grad)


def solution(mesh):
    placed = (
        P("dp", "ctx", None),
        P("dp", "ctx", None),
        P("dp", "ctx", None),
        P("dp", "ctx", None),
        P("dp", "ctx", None),
        P("dp", "ctx"),
    )
    return jax.shard_map(
        local,
        mesh=mesh,
        in_specs=placed,
        out_specs=(
            P("dp", "ctx", None),
            P("dp", "ctx", None),
            P("dp", "ctx", None),
            P("dp", "ctx"),
        ),
        check_vma=False,
    )
```

time: 78.5 us -> 79.9 us (1.018)
  starting transfers between devices: 32.7 us -> 24.7 us
  other arithmetic: 3.04 us -> 8.87 us
  local copies, waits for them, and re-layouts: 2.6 us -> 4.96 us
  waiting for transfers between devices: 32.9 us -> 34.1 us
    ppermute x17 -> x12, starting transfers between devices: 17.4 us -> 11.1 us  [dp_send(): return lax.ppermute(value, 'dp', pairs)]
    ppermute x2 -> x1, waiting for transfers between devices: 0.01 us -> 3.9 us  [shifted(): lax.ppermute(value, axis, [(source, source + steps) for source in range(l...]
    ppermute x5 -> x3, starting transfers between devices: 5.61 us -> 2.56 us  [the longest x2 2.56 us: local(): others_away.append(lax.ppermute(rest, 'ctx', swap_ctx))]
    ppermute x5 -> x3, waiting for transfers between devices: 7.26 us -> 4.92 us  [the longest x2 4.29 us: local(): others_away.append(lax.ppermute(rest, 'ctx', swap_ctx))]
    ppermute x2, waiting for transfers between devices: 2.18 us -> 0.01 us  [local(): arrived = lax.ppermute(sent, 'ctx', swap_ctx)]
    another operation x1 -> x3, other arithmetic: 0.06 us -> 2.05 us  [the longest x2 1.96 us: local(): mids = jnp.stack(mids)]
    ppermute x17 -> x12, waiting for transfers between devices: 23.5 us -> 25.2 us  [dp_send(): return lax.ppermute(value, 'dp', pairs)]
    slice x1, local copies, waits for them, and re-layouts: 0.04 us -> 1.2 us  [local(): pair = jnp.concatenate([own_keys[:, cols], own_values[:, cols]], axis=1)]
  transfers between devices with their start and end apart: 27 -> 19, of which waited for: 14 -> 9; matrix products, arithmetic and copies ran while one was open for 4% -> 11% of each run, Pallas kernels for 7% -> 7%
where the time goes in v6:
time: 79.9 us; the launch traced here: 79.7 us
  waiting for transfers between devices  34.1 us (43%)
  starting transfers between devices  24.7 us (31%)
  other arithmetic  8.87 us (11%)
  Pallas kernels  5.91 us (7%)
  local copies, waits for them, and re-layouts  4.96 us (6%)
  between operations  1.14 us (1%)
    ppermute x12, waiting for transfers between devices, dp_send(): return lax.ppermute(value, 'dp', pairs)  25.2 us
    ppermute x12, starting transfers between devices, dp_send(): return lax.ppermute(value, 'dp', pairs)  11.1 us
    ppermute x2, starting transfers between devices, local(): arrived = lax.ppermute(sent, 'ctx', swap_ctx)  4.88 us
    ppermute x1, starting transfers between devices, shifted(): lax.ppermute(value, axis, [(source, source + steps) for source in range(l...  4.88 us
    ppermute x2, waiting for transfers between devices, local(): others_away.append(lax.ppermute(rest, 'ctx', swap_ctx))  4.29 us
    ppermute x1, waiting for transfers between devices, shifted(): lax.ppermute(value, axis, [(source, source + steps) for source in range(l...  3.9 us
    pallas_call x2, Pallas kernels, attend(): pl.pallas_call(partial(attention_kernel, chunk, hops, group), grid_spec=p...  3.78 us
    ppermute x2, starting transfers between devices, local(): others_away.append(lax.ppermute(rest, 'ctx', swap_ctx))  2.56 us
  transfers between devices with their start and end apart: 19, of which 9 were waited for; matrix products, arithmetic and copies ran while one was open for 11% of the time, Pallas kernels for 7%

profile of v6, /device:TPU:0, one launch (start us, length us, event | category | flops | bytes accessed | tf_op | source)
XLA Modules:
  0.0 79.7 jit_solution(4049726704782385025)
XLA Ops:
  1.3 1.2 %fusion.6 = (bf16[128,512]{1,0:T(8,128)(2,1)S(1)}, bf16[128,512]{1,0:T(8,128)(2,1)S(1)}, bf16[128,512]{1,0:T(8,128)(2,1)S(1)}, bf16[128,512]{1,0:T(8,128)(2,1)S(1)}) fusion(bf16[128,1024]{1,0:T(8,128)(2,1)} %bitcast.54, bf16[128,1024]{1,0:T(8,128)(2,1)} %bitcast.57), kind=kLoop, calls=%fused_computation.48 | loop fusion | bytes 1048576 | tf_op jit(solution)/shard_map/slice | solution.py:232
  3.3 4.9 %collective-permute-start = (bf16[144,1024]{1,0:T(8,128)(2,1)}, bf16[144,1024]{1,0:T(8,128)(2,1)S(1)}, u32[]{:S(2)}, u32[]{:S(2)}) collective-permute-start(bf16[144,1024]{1,0:T(8,128)(2,1)} %pad_maximum_fusion.3), channel_id=1, source_target_pairs={{0,1},{2,3},{4,5},{6,7},{8,9},{10,11},{12,13},{14,15},{16,17},{18,... | collective-permute-start | bytes 884744 | tf_op jit(solution)/shard_map/ppermute | solution.py:29
  8.9 0.8 bitcast_select_fusion
  9.7 0.8 dynamic-slice_bitcast_fusion
  10.5 1.5 %collective-permute-start.2 = (bf16[4,2,168,128]{3,2,1,0:T(8,128)(2,1)}, bf16[4,2,168,128]{3,2,1,0:T(8,128)(2,1)}, u32[]{:S(2)}, u32[]{:S(2)}) collective-permute-start(bf16[4,2,168,128]{3,2,1,0:T(8,128)(2,1)} %get-tuple-element.46), channel_id=1, source_target_pairs={{0,4},{2,6},{4,0},{6,2},{8,12},{10,14},{12,8},{14,10},{16,20},{18,... | collective-permute-start | bytes 1032200 | tf_op jit(solution)/shard_map/ppermute | solution.py:203
  11.9 3.9 %collective-permute-done.refs_5_.refs_6_ = bf16[144,1024]{1,0:T(8,128)(2,1)S(1)} collective-permute-done((bf16[144,1024]{1,0:T(8,128)(2,1)}, bf16[144,1024]{1,0:T(8,128)(2,1)S(1)}, u32[]{:S(2)}, u32[]{:S(2)}) %collective-permute-start) | collective-permute-done | bytes 294944 | tf_op jit(solution)/shard_map/ppermute | solution.py:29
  16.5 1.9 %shard_map.93 = (bf16[128,1024]{1,0:T(8,128)(2,1)S(1)}, bf16[256,512]{1,0:T(8,128)(2,1)S(1)}, bf16[128,512]{1,0:T(8,128)(2,1)S(1)}, bf16[128,512]{1,0:T(8,128)(2...) custom-call(s32[1]{0:T(128)} %bitcast.place_ref, s32[1,128]{1,0:T(1,128)S(1)} %copy-done.4, ...), custom_call_target="tpu_custom_call" | custom-call | flops 1024 | bytes 1024 | tf_op jit(solution)/shard_map/pallas_call | solution.py:122
  18.4 2.4 %collective-permute-start.4 = (bf16[256,512]{1,0:T(8,128)(2,1)S(1)}, bf16[256,512]{1,0:T(8,128)(2,1)S(1)}, u32[]{:S(2)}, u32[]{:S(2)}) collective-permute-start(bf16[256,512]{1,0:T(8,128)(2,1)S(1)} %get-tuple-element.26), channel_id=1, source_target_pairs={{0,1},{1,0},{2,3},{3,2},{4,5},{5,4},{6,7},{7,6},{8,9},{9,8},{10,11... | collective-permute-start | bytes 786440 | tf_op jit(solution)/shard_map/ppermute | solution.py:273
  21.5 0.8 copy_bitcast_fusion
  22.2 1.9 %shard_map.94 = (bf16[128,1024]{1,0:T(8,128)(2,1)S(1)}, bf16[256,512]{1,0:T(8,128)(2,1)S(1)}, bf16[128,512]{1,0:T(8,128)(2,1)S(1)}, bf16[128,512]{1,0:T(8,128)(2...) custom-call(s32[1]{0:T(128)} %bitcast.place_ref, s32[1,128]{1,0:T(1,128)S(1)} %copy-done.4, ...), custom_call_target="tpu_custom_call" | custom-call | flops 1024 | bytes 1024 | tf_op jit(solution)/shard_map/pallas_call | solution.py:122
  24.1 2.4 %collective-permute-start.5 = (bf16[256,512]{1,0:T(8,128)(2,1)S(1)}, bf16[256,512]{1,0:T(8,128)(2,1)S(1)}, u32[]{:S(2)}, u32[]{:S(2)}) collective-permute-start(bf16[256,512]{1,0:T(8,128)(2,1)S(1)} %get-tuple-element.35), channel_id=1, source_target_pairs={{0,1},{1,0},{2,3},{3,2},{4,5},{5,4},{6,7},{7,6},{8,9},{9,8},{10,11... | collective-permute-start | bytes 786440 | tf_op jit(solution)/shard_map/ppermute | solution.py:273
  26.6 0.8 %maximum_bitcast_fusion = bf16[1,128,2048]{2,1,0:T(8,128)(2,1)} fusion(bf16[128,1024]{1,0:T(8,128)(2,1)S(1)} %get-tuple-element.28, bf16[128,1024]{1,0:T(8,128)(2,1)S(1)} %get-tuple-element.25), kind=kLoop, calls=%fused_computation.13 | loop fusion | flops 1048576 | bytes 1048576 | tf_op jit(solution)/shard_map/broadcast_in_dim | solution.py:352
  27.4 1.0 %fusion = bf16[2,4,1,168,128]{4,3,2,1,0:T(8,128)(2,1)S(1)} fusion(s32[]{:T(128)S(6)} %select_n.126, bf16[1,4,2,168,128]{4,3,2,1,0:T(8,128)(2,1)S(1)} %get-tuple-element.47, bf16[1,4,2,168,128]{4,3,2,1,0:T(8,128)(2,1)} %bitcast.17), kind=kLoop, calls=%fused_computation.15 | loop fusion | flops 172032 | bytes 1032196 | tf_op jit(solution)/shard_map/stack | solution.py:265
  28.4 1.0 %fusion.4 = bf16[1,4,1,168,128]{4,3,2,1,0:T(8,128)(2,1)S(1)} fusion(s32[]{:T(128)S(6)} %add.98, s32[]{:T(128)S(6)} %select_n.119, bf16[1,4,2,168,128]{4,3,2,1,0:T(8,128)(2,1)S(1)} %get-tuple-element.47, bf16[1,4,2,168,128]{4,3,2,1,0:T(8,128)(2,1)} %bitcast.17), kind=kLoop, calls=%fused_computation.34 | loop fusion | flops 86016 | bytes 860168 | tf_op jit(solution)/shard_map/stack | solution.py:265
  30.1 0.8 %fusion.3 = (bf16[3,336,128]{2,1,0:T(8,128)(2,1)}, bf16[3,336,128]{2,1,0:T(8,128)(2,1)}) fusion(bf16[2,672,128]{2,1,0:T(8,128)(2,1)S(1)} %collective-permute-done.3, bf16[1,672,128]{2,1,0:T(8,128)(2,1)S(1)} %bitcast.67), kind=kLoop, calls=%fused_computation.33 | loop fusion | flops 258048 | bytes 1032192 | tf_op jit(solution)/shard_map/concatenate | solution.py:268
  30.9 1.5 %collective-permute-start.8 = (bf16[256,512]{1,0:T(8,128)(2,1)S(1)}, bf16[256,512]{1,0:T(8,128)(2,1)S(1)}, u32[]{:S(2)}, u32[]{:S(2)}) collective-permute-start(bf16[256,512]{1,0:T(8,128)(2,1)S(1)} %pad_maximum_fusion.4.refs_0_), channel_id=1, source_target_pairs={{0,4},{2,6},{4,0},{6,2},{8,12},{10,14},{12,8},{14,10},{16,20},{18,... | collective-permute-start | bytes 786440 | tf_op jit(solution)/shard_map/ppermute | solution.py:203
  33.4 0.9 %copy-done.8 = bf16[3,336,128]{2,1,0:T(8,128)(2,1)S(1)} copy-done((bf16[3,336,128]{2,1,0:T(8,128)(2,1)S(1)}, bf16[3,336,128]{2,1,0:T(8,128)(2,1)}, u32[]{:S(2)}) %copy-start.8) | copy-done | bytes 258072
  34.3 2.5 %collective-permute-start.7 = (bf16[3,336,128]{2,1,0:T(8,128)(2,1)S(1)}, bf16[3,336,128]{2,1,0:T(8,128)(2,1)S(1)}, u32[]{:S(2)}, u32[]{:S(2)}) collective-permute-start(bf16[3,336,128]{2,1,0:T(8,128)(2,1)S(1)} %copy-done.8), channel_id=1, source_target_pairs={{0,1},{1,0},{2,3},{3,2},{4,5},{5,4},{6,7},{7,6},{8,9},{9,8},{10,11... | collective-permute-start | bytes 774152 | tf_op jit(solution)/shard_map/ppermute | solution.py:288
  36.8 3.3 %collective-permute-done.8.refs_1_ = bf16[256,512]{1,0:T(8,128)(2,1)S(1)} collective-permute-done((bf16[256,512]{1,0:T(8,128)(2,1)S(1)}, bf16[256,512]{1,0:T(8,128)(2,1)S(1)}, u32[]{:S(2)}, u32[]{:S(2)}) %collective-permute-start.8) | collective-permute-done | bytes 262176 | tf_op jit(solution)/shard_map/ppermute | solution.py:203
  40.7 4.2 %collective-permute-done.11.refs_1_ = bf16[256,512]{1,0:T(8,128)(2,1)S(1)} collective-permute-done((bf16[256,512]{1,0:T(8,128)(2,1)S(1)}, bf16[256,512]{1,0:T(8,128)(2,1)S(1)}, u32[]{:S(2)}, u32[]{:S(2)}) %collective-permute-start.11) | collective-permute-done | bytes 262176 | tf_op jit(solution)/shard_map/ppermute | solution.py:203
  45.6 1.6 %collective-permute-start.14 = (bf16[336,512]{1,0:T(8,128)(2,1)S(1)}, bf16[336,512]{1,0:T(8,128)(2,1)S(1)}, u32[]{:S(2)}, u32[]{:S(2)}) collective-permute-start(bf16[336,512]{1,0:T(8,128)(2,1)S(1)} %shard_map.95), channel_id=1, source_target_pairs={{0,8},{2,10},{4,12},{6,14},{8,0},{10,2},{12,4},{14,6},{16,24},{18,... | collective-permute-start | bytes 1032200 | tf_op jit(solution)/shard_map/ppermute | solution.py:203
  47.8 0.8 collective-permute-start.17
  48.6 0.8 maximum_select_fusion
  49.3 4.3 %collective-permute-done.6.others_away_ref = bf16[3,336,128]{2,1,0:T(8,128)(2,1)S(1)} collective-permute-done((bf16[3,336,128]{2,1,0:T(8,128)(2,1)S(1)}, bf16[3,336,128]{2,1,0:T(8,128)(2,1)S(1)}, u32[]{:S(2)}, u32[]{:S(2)}) %collective-permute-start.6) | collective-permute-done | bytes 258080 | tf_op jit(solution)/shard_map/ppermute | solution.py:288
  54.7 1.8 %collective-permute-done.14 = bf16[336,512]{1,0:T(8,128)(2,1)S(1)} collective-permute-done((bf16[336,512]{1,0:T(8,128)(2,1)S(1)}, bf16[336,512]{1,0:T(8,128)(2,1)S(1)}, u32[]{:S(2)}, u32[]{:S(2)}) %collective-permute-start.14) | collective-permute-done | bytes 344096 | tf_op jit(solution)/shard_map/ppermute | solution.py:203
  56.6 2.6 %collective-permute-start.16 = (bf16[168,512]{1,0:T(8,128)(2,1)S(1)}, bf16[168,512]{1,0:T(8,128)(2,1)S(1)}, u32[]{:S(2)}, u32[]{:S(2)}) collective-permute-start(bf16[168,512]{1,0:T(8,128)(2,1)S(1)} %slice.132), channel_id=1, source_target_pairs={{0,16},{2,18},{4,20},{6,22},{8,24},{10,26},{12,28},{14,30},{16,0},... | collective-permute-start | bytes 516104 | tf_op jit(solution)/shard_map/ppermute | solution.py:203
  59.3 1.3 %collective-permute-start.15 = (bf16[128,1024]{1,0:T(8,128)(2,1)S(1)}, bf16[128,1024]{1,0:T(8,128)(2,1)S(1)}, u32[]{:S(2)}, u32[]{:S(2)}) collective-permute-start(bf16[128,1024]{1,0:T(8,128)(2,1)S(1)} %pad_maximum_fusion.5), channel_id=1, source_target_pairs={{1,0},{3,2},{5,4},{7,6},{9,8},{11,10},{13,12},{15,14},{17,16},{19,... | collective-permute-start | bytes 786440 | tf_op jit(solution)/shard_map/ppermute | solution.py:340
  60.6 6.6 %collective-permute-done.17 = bf16[336,512]{1,0:T(8,128)(2,1)S(1)} collective-permute-done((bf16[336,512]{1,0:T(8,128)(2,1)S(1)}, bf16[336,512]{1,0:T(8,128)(2,1)S(1)}, u32[]{:S(2)}, u32[]{:S(2)}) %collective-permute-start.17) | collective-permute-done | bytes 344096 | tf_op jit(solution)/shard_map/ppermute | solution.py:203
  67.3 1.8 %collective-permute-start.18 = (bf16[168,512]{1,0:T(8,128)(2,1)S(1)}, bf16[168,512]{1,0:T(8,128)(2,1)S(1)}, u32[]{:S(2)}, u32[]{:S(2)}) collective-permute-start(bf16[168,512]{1,0:T(8,128)(2,1)S(1)} %slice.131), channel_id=1, source_target_pairs={{0,16},{2,18},{4,20},{6,22},{8,24},{10,26},{12,28},{14,30},{16,0},... | collective-permute-start | bytes 516104 | tf_op jit(solution)/shard_map/ppermute | solution.py:203
  69.1 8.8 %collective-permute-done.18 = bf16[168,512]{1,0:T(8,128)(2,1)S(1)} collective-permute-done((bf16[168,512]{1,0:T(8,128)(2,1)S(1)}, bf16[168,512]{1,0:T(8,128)(2,1)S(1)}, u32[]{:S(2)}, u32[]{:S(2)}) %collective-permute-start.18) | collective-permute-done | bytes 172064 | tf_op jit(solution)/shard_map/ppermute | solution.py:203
  78.0 0.9 %pad_maximum_fusion.2 = f32[168,1024]{1,0:T(8,128)} fusion(f32[168,512]{1,0:T(8,128)S(1)} %slice_add_fusion, f32[168,512]{1,0:T(8,128)S(1)} %slice_add_fusion.1), kind=kLoop, calls=%fused_computation.8 | loop fusion | flops 172032 | bytes 1376256 | tf_op jit(solution)/shard_map/dynamic_update_slice | solution.py:349
  78.9 0.8 fusion.1
  (70 shorter events, 8.1 us)
Async XLA Ops:
  1.3 6.9 %copy-start.6 = (bf16[1,128,2688]{2,1,0:T(8,128)(2,1)S(1)}, bf16[1,128,2688]{2,1,0:T(8,128)(2,1)}, u32[]{:S(2)}) copy-start(bf16[1,128,2688]{2,1,0:T(8,128)(2,1)} %param.6) | copy-start | bytes 2064388
  3.3 12.6 %collective-permute-start = (bf16[144,1024]{1,0:T(8,128)(2,1)}, bf16[144,1024]{1,0:T(8,128)(2,1)S(1)}, u32[]{:S(2)}, u32[]{:S(2)}) collective-permute-start(bf16[144,1024]{1,0:T(8,128)(2,1)} %pad_maximum_fusion.3), channel_id=1, source_target_pairs={{0,1},{2,3},{4,5},{6,7},{8,9},{10,11},{12,13},{14,15},{16,17},{18,... | collective-permute-start | bytes 884744 | tf_op jit(solution)/shard_map/ppermute | solution.py:29
  8.9 7.0 %copy-start.3 = (bf16[1,128,2048]{2,1,0:T(8,128)(2,1)S(1)}, bf16[1,128,2048]{2,1,0:T(8,128)(2,1)}, u32[]{:S(2)}) copy-start(bf16[1,128,2048]{2,1,0:T(8,128)(2,1)} %param.10) | copy-start | bytes 1572868
  9.6 11.8 %collective-permute-start.1 = (bf16[128,1024]{1,0:T(8,128)(2,1)}, bf16[128,1024]{1,0:T(8,128)(2,1)S(1)}, u32[]{:S(2)}, u32[]{:S(2)}) collective-permute-start(bf16[128,1024]{1,0:T(8,128)(2,1)} %bitcast_select_fusion), channel_id=1, source_target_pairs={{0,1},{1,0},{2,3},{3,2},{4,5},{5,4},{6,7},{7,6},{8,9},{9,8},{10,11... | collective-permute-start | bytes 786440 | tf_op jit(solution)/shard_map/ppermute | solution.py:238
  9.6 6.2 %copy-start = (bf16[1,128,1024]{2,1,0:T(8,128)(2,1)S(1)}, bf16[1,128,1024]{2,1,0:T(8,128)(2,1)}, u32[]{:S(2)}) copy-start(bf16[1,128,1024]{2,1,0:T(8,128)(2,1)} %param.8) | copy-start | bytes 786436
  9.6 6.2 %copy-start.1 = (bf16[1,128,1024]{2,1,0:T(8,128)(2,1)S(1)}, bf16[1,128,1024]{2,1,0:T(8,128)(2,1)}, u32[]{:S(2)}) copy-start(bf16[1,128,1024]{2,1,0:T(8,128)(2,1)} %param.9) | copy-start | bytes 786436
  9.6 6.2 %copy-start.2 = (bf16[1,128,2048]{2,1,0:T(8,128)(2,1)S(1)}, bf16[1,128,2048]{2,1,0:T(8,128)(2,1)}, u32[]{:S(2)}) copy-start(bf16[1,128,2048]{2,1,0:T(8,128)(2,1)} %param.7) | copy-start | bytes 1572868
  10.5 16.9 %collective-permute-start.2 = (bf16[4,2,168,128]{3,2,1,0:T(8,128)(2,1)}, bf16[4,2,168,128]{3,2,1,0:T(8,128)(2,1)}, u32[]{:S(2)}, u32[]{:S(2)}) collective-permute-start(bf16[4,2,168,128]{3,2,1,0:T(8,128)(2,1)} %get-tuple-element.46), channel_id=1, source_target_pairs={{0,4},{2,6},{4,0},{6,2},{8,12},{10,14},{12,8},{14,10},{16,20},{18,... | collective-permute-start | bytes 1032200 | tf_op jit(solution)/shard_map/ppermute | solution.py:203
  15.8 0.7 copy-start.4
  18.4 11.0 %collective-permute-start.4 = (bf16[256,512]{1,0:T(8,128)(2,1)S(1)}, bf16[256,512]{1,0:T(8,128)(2,1)S(1)}, u32[]{:S(2)}, u32[]{:S(2)}) collective-permute-start(bf16[256,512]{1,0:T(8,128)(2,1)S(1)} %get-tuple-element.26), channel_id=1, source_target_pairs={{0,1},{1,0},{2,3},{3,2},{4,5},{5,4},{6,7},{7,6},{8,9},{9,8},{10,11... | collective-permute-start | bytes 786440 | tf_op jit(solution)/shard_map/ppermute | solution.py:273
  24.1 8.3 %collective-permute-start.5 = (bf16[256,512]{1,0:T(8,128)(2,1)S(1)}, bf16[256,512]{1,0:T(8,128)(2,1)S(1)}, u32[]{:S(2)}, u32[]{:S(2)}) collective-permute-start(bf16[256,512]{1,0:T(8,128)(2,1)S(1)} %get-tuple-element.35), channel_id=1, source_target_pairs={{0,1},{1,0},{2,3},{3,2},{4,5},{5,4},{6,7},{7,6},{8,9},{9,8},{10,11... | collective-permute-start | bytes 786440 | tf_op jit(solution)/shard_map/ppermute | solution.py:273
  28.3 1.7 %collective-permute-start.3 = (bf16[2,672,128]{2,1,0:T(8,128)(2,1)S(1)}, bf16[2,672,128]{2,1,0:T(8,128)(2,1)S(1)}, u32[]{:S(2)}, u32[]{:S(2)}) collective-permute-start(bf16[2,672,128]{2,1,0:T(8,128)(2,1)S(1)} %bitcast.76), channel_id=1, source_target_pairs={{0,2},{2,0},{4,6},{6,4},{8,10},{10,8},{12,14},{14,12},{16,18},{18,... | collective-permute-start | bytes 1032200 | tf_op jit(solution)/shard_map/ppermute | solution.py:203
  30.9 9.1 %collective-permute-start.8 = (bf16[256,512]{1,0:T(8,128)(2,1)S(1)}, bf16[256,512]{1,0:T(8,128)(2,1)S(1)}, u32[]{:S(2)}, u32[]{:S(2)}) collective-permute-start(bf16[256,512]{1,0:T(8,128)(2,1)S(1)} %pad_maximum_fusion.4.refs_0_), channel_id=1, source_target_pairs={{0,4},{2,6},{4,0},{6,2},{8,12},{10,14},{12,8},{14,10},{16,20},{18,... | collective-permute-start | bytes 786440 | tf_op jit(solution)/shard_map/ppermute | solution.py:203
  32.5 12.4 %collective-permute-start.11 = (bf16[256,512]{1,0:T(8,128)(2,1)S(1)}, bf16[256,512]{1,0:T(8,128)(2,1)S(1)}, u32[]{:S(2)}, u32[]{:S(2)}) collective-permute-start(bf16[256,512]{1,0:T(8,128)(2,1)S(1)} %pad_maximum_fusion.6.refs_0_), channel_id=1, source_target_pairs={{0,4},{2,6},{4,0},{6,2},{8,12},{10,14},{12,8},{14,10},{16,20},{18,... | collective-permute-start | bytes 786440 | tf_op jit(solution)/shard_map/ppermute | solution.py:203
  33.2 6.8 %copy-start.5 = (bf16[128,8,128]{2,0,1:T(8,128)(2,1)S(1)}, bf16[128,8,128]{2,0,1:T(8,128)(2,1)}, u32[]{:S(2)}) copy-start(bf16[128,8,128]{2,0,1:T(8,128)(2,1)} %copy_bitcast_fusion) | copy-start | bytes 786436
  33.3 1.0 %copy-start.8 = (bf16[3,336,128]{2,1,0:T(8,128)(2,1)S(1)}, bf16[3,336,128]{2,1,0:T(8,128)(2,1)}, u32[]{:S(2)}) copy-start(bf16[3,336,128]{2,1,0:T(8,128)(2,1)} %get-tuple-element.43) | copy-start | bytes 774148
  33.3 11.7 %collective-permute-start.9 = (bf16[256,512]{1,0:T(8,128)(2,1)S(1)}, bf16[256,512]{1,0:T(8,128)(2,1)S(1)}, u32[]{:S(2)}, u32[]{:S(2)}) collective-permute-start(bf16[256,512]{1,0:T(8,128)(2,1)S(1)} %pad_maximum_fusion.4.refs_0_), channel_id=1, source_target_pairs={{0,2},{2,0},{4,6},{6,4},{8,10},{10,8},{12,14},{14,12},{16,18},{18,... | collective-permute-start | bytes 786440 | tf_op jit(solution)/shard_map/ppermute | solution.py:203
  34.3 10.6 %collective-permute-start.7 = (bf16[3,336,128]{2,1,0:T(8,128)(2,1)S(1)}, bf16[3,336,128]{2,1,0:T(8,128)(2,1)S(1)}, u32[]{:S(2)}, u32[]{:S(2)}) collective-permute-start(bf16[3,336,128]{2,1,0:T(8,128)(2,1)S(1)} %copy-done.8), channel_id=1, source_target_pairs={{0,1},{1,0},{2,3},{3,2},{4,5},{5,4},{6,7},{7,6},{8,9},{9,8},{10,11... | collective-permute-start | bytes 774152 | tf_op jit(solution)/shard_map/ppermute | solution.py:288
  40.0 5.0 %collective-permute-start.10 = (bf16[256,512]{1,0:T(8,128)(2,1)S(1)}, bf16[256,512]{1,0:T(8,128)(2,1)S(1)}, u32[]{:S(2)}, u32[]{:S(2)}) collective-permute-start(bf16[256,512]{1,0:T(8,128)(2,1)S(1)} %collective-permute-done.8.refs_1_), channel_id=1, source_target_pairs={{0,2},{2,0},{4,6},{6,4},{8,10},{10,8},{12,14},{14,12},{16,18},{18,... | collective-permute-start | bytes 786440 | tf_op jit(solution)/shard_map/ppermute | solution.py:203
  40.1 4.8 %copy-start.7 = (bf16[3,336,128]{2,1,0:T(8,128)(2,1)S(1)}, bf16[3,336,128]{2,1,0:T(8,128)(2,1)}, u32[]{:S(2)}) copy-start(bf16[3,336,128]{2,1,0:T(8,128)(2,1)} %get-tuple-element.42) | copy-start | bytes 774148
  40.1 7.1 %collective-permute-start.12 = (bf16[256,512]{1,0:T(8,128)(2,1)S(1)}, bf16[256,512]{1,0:T(8,128)(2,1)S(1)}, u32[]{:S(2)}, u32[]{:S(2)}) collective-permute-start(bf16[256,512]{1,0:T(8,128)(2,1)S(1)} %pad_maximum_fusion.6.refs_0_), channel_id=1, source_target_pairs={{0,2},{2,0},{4,6},{6,4},{8,10},{10,8},{12,14},{14,12},{16,18},{18,... | collective-permute-start | bytes 786440 | tf_op jit(solution)/shard_map/ppermute | solution.py:203
  44.9 2.4 %collective-permute-start.13 = (bf16[256,512]{1,0:T(8,128)(2,1)S(1)}, bf16[256,512]{1,0:T(8,128)(2,1)S(1)}, u32[]{:S(2)}, u32[]{:S(2)}) collective-permute-start(bf16[256,512]{1,0:T(8,128)(2,1)S(1)} %collective-permute-done.11.refs_1_), channel_id=1, source_target_pairs={{0,2},{2,0},{4,6},{6,4},{8,10},{10,8},{12,14},{14,12},{16,18},{18,... | collective-permute-start | bytes 786440 | tf_op jit(solution)/shard_map/ppermute | solution.py:203
  44.9 8.7 %collective-permute-start.6 = (bf16[3,336,128]{2,1,0:T(8,128)(2,1)S(1)}, bf16[3,336,128]{2,1,0:T(8,128)(2,1)S(1)}, u32[]{:S(2)}, u32[]{:S(2)}) collective-permute-start(bf16[3,336,128]{2,1,0:T(8,128)(2,1)S(1)} %copy-done.7), channel_id=1, source_target_pairs={{0,1},{1,0},{2,3},{3,2},{4,5},{5,4},{6,7},{7,6},{8,9},{9,8},{10,11... | collective-permute-start | bytes 774152 | tf_op jit(solution)/shard_map/ppermute | solution.py:288
  45.6 10.9 %collective-permute-start.14 = (bf16[336,512]{1,0:T(8,128)(2,1)S(1)}, bf16[336,512]{1,0:T(8,128)(2,1)S(1)}, u32[]{:S(2)}, u32[]{:S(2)}) collective-permute-start(bf16[336,512]{1,0:T(8,128)(2,1)S(1)} %shard_map.95), channel_id=1, source_target_pairs={{0,8},{2,10},{4,12},{6,14},{8,0},{10,2},{12,4},{14,6},{16,24},{18,... | collective-permute-start | bytes 1032200 | tf_op jit(solution)/shard_map/ppermute | solution.py:203
  47.8 19.4 %collective-permute-start.17 = (bf16[336,512]{1,0:T(8,128)(2,1)S(1)}, bf16[336,512]{1,0:T(8,128)(2,1)S(1)}, u32[]{:S(2)}, u32[]{:S(2)}) collective-permute-start(bf16[336,512]{1,0:T(8,128)(2,1)S(1)} %shard_map.96), channel_id=1, source_target_pairs={{0,8},{2,10},{4,12},{6,14},{8,0},{10,2},{12,4},{14,6},{16,24},{18,... | collective-permute-start | bytes 1032200 | tf_op jit(solution)/shard_map/ppermute | solution.py:203
  56.6 12.4 %collective-permute-start.16 = (bf16[168,512]{1,0:T(8,128)(2,1)S(1)}, bf16[168,512]{1,0:T(8,128)(2,1)S(1)}, u32[]{:S(2)}, u32[]{:S(2)}) collective-permute-start(bf16[168,512]{1,0:T(8,128)(2,1)S(1)} %slice.132), channel_id=1, source_target_pairs={{0,16},{2,18},{4,20},{6,22},{8,24},{10,26},{12,28},{14,30},{16,0},... | collective-permute-start | bytes 516104 | tf_op jit(solution)/shard_map/ppermute | solution.py:203
  59.3 19.6 %collective-permute-start.15 = (bf16[128,1024]{1,0:T(8,128)(2,1)S(1)}, bf16[128,1024]{1,0:T(8,128)(2,1)S(1)}, u32[]{:S(2)}, u32[]{:S(2)}) collective-permute-start(bf16[128,1024]{1,0:T(8,128)(2,1)S(1)} %pad_maximum_fusion.5), channel_id=1, source_target_pairs={{1,0},{3,2},{5,4},{7,6},{9,8},{11,10},{13,12},{15,14},{17,16},{19,... | collective-permute-start | bytes 786440 | tf_op jit(solution)/shard_map/ppermute | solution.py:340
  67.3 10.7 %collective-permute-start.18 = (bf16[168,512]{1,0:T(8,128)(2,1)S(1)}, bf16[168,512]{1,0:T(8,128)(2,1)S(1)}, u32[]{:S(2)}, u32[]{:S(2)}) collective-permute-start(bf16[168,512]{1,0:T(8,128)(2,1)S(1)} %slice.131), channel_id=1, source_target_pairs={{0,16},{2,18},{4,20},{6,22},{8,24},{10,26},{12,28},{14,30},{16,0},... | collective-permute-start | bytes 516104 | tf_op jit(solution)/shard_map/ppermute | solution.py:203

commit v7 on v6

--- a/solution.py
+++ b/solution.py
@@ -39,7 +39,7 @@
     place = place_ref[0]
     scale = HD**-0.5
 
-    query_segs = segs_ref[...].astype(jnp.float32)
+    query_segs = segs_ref[:1].astype(jnp.float32)
     key_cols = [
         jnp.transpose(jnp.broadcast_to(ref[...].astype(jnp.float32)[:1], (tok, tok)))
         for ref in (*rim_segs, segs_ref)
@@ -125,7 +125,7 @@
             num_scalar_prefetch=1,
             grid=(1,),
             in_specs=[
-                whole(1, tok),
+                whole(SEG_ROWS, tok),
                 part(tok, group * width),
                 part(tok, group * width),
                 part(tok, width),
@@ -224,14 +224,14 @@
 
     steps = range(hops, 0, -1)
     seg_rows = jnp.broadcast_to(segment_ids.astype(jnp.bfloat16), (SEG_ROWS, tok))
-    seg_rows = jnp.pad(seg_rows, ((0, 0), (0, 2 * width - tok)))
+    wide_rows = jnp.pad(seg_rows, ((0, 0), (0, 2 * width - tok)))
     to_rows = lambda array: array.reshape(tok, -1, HD).transpose(1, 0, 2).reshape(-1, HD)
     rim_pairs = []
     for chunk in range(CHUNKS):
         cols = slice(chunk * width, (chunk + 1) * width)
         pair = jnp.concatenate([own_keys[:, cols], own_values[:, cols]], axis=1)
         if chunk == 0:
-            pair = jnp.concatenate([pair, seg_rows], axis=0)
+            pair = jnp.concatenate([pair, wide_rows], axis=0)
         if ctx_count == 2 and chunk == CHUNKS - 1:
             back = jnp.pad(own_piece, ((0, 2 * width - own_piece.shape[0]), (0, 0)))
             back = back.reshape(-1, tok, HD).transpose(1, 0, 2).reshape(tok, -1)
@@ -242,15 +242,19 @@
     half_rows = slow_count // 2 * rows
     low_high = [(0, half_rows), (half_rows, 2 * half_rows)]
 
+    mids = jnp.stack(mids)
+    sent_core = share_of(mids, 1 - core_at)
     attended = []
     for chunk in range(CHUNKS):
-        if chunk > 0:
-            rim_pairs[chunk], _ = lax.optimization_barrier((rim_pairs[chunk], attended[-1][1]))
+        if chunk == 1:
+            rim_pairs[1], sent_core, _ = lax.optimization_barrier(
+                (rim_pairs[1], sent_core, attended[0][1])
+            )
         attended.append(
             attend(
                 chunk,
                 place_arg,
-                segment_ids,
+                seg_rows,
                 queries[0],
                 out_grad[0],
                 own_keys,
@@ -260,10 +264,7 @@
                 [own_piece] if hops == 1 else [],
             )
         )
-    query_grad = jnp.concatenate([outs[0] for outs in attended], axis=1)
-
-    mids = jnp.stack(mids)
-    kept_core, sent_core = share_of(mids, core_at), share_of(mids, 1 - core_at)
+    kept_core = share_of(mids, core_at)
     other_core = dp_send(sent_core, swap_core)
     others = jnp.concatenate([kept_core[1:], other_core])
 
@@ -334,6 +335,10 @@
     halves = [
         near + dp_send(far, flip_slow(1)).astype(jnp.float32) for near, far in zip(kept, sent)
     ]
+    last = [dp_send(half[:rows].astype(jnp.bfloat16), flip_slow(2)) for half in halves]
+    parts = [half[rows:] + final.astype(jnp.float32) for half, final in zip(halves, last)]
+    query_parts, _ = lax.optimization_barrier(([outs[0] for outs in attended], kept[0]))
+    query_grad = jnp.concatenate(query_parts, axis=1)
     if ctx_count == 2:
         value_rim = jnp.concatenate([outs[5] for outs in attended], axis=1)
         value_rim, _ = lax.optimization_barrier((value_rim, halves[0]))
@@ -342,13 +347,9 @@
         value_grad = (value_own.astype(jnp.float32) + returned.astype(jnp.float32)).astype(
             jnp.bfloat16
         )
-    last = [dp_send(half[:rows].astype(jnp.bfloat16), flip_slow(2)) for half in halves]
-    piece_width = halves[0].shape[1]
-    weight_grad = jnp.zeros((rows, piece_width * len(halves)), jnp.float32)
-    for n, (half, final) in enumerate(zip(halves, last)):
-        weight_grad = lax.dynamic_update_slice(
-            weight_grad, half[rows:] + final.astype(jnp.float32), (0, n * piece_width)
-        )
+    if ctx_count == 2:
+        parts[-1], value_grad = lax.optimization_barrier((parts[-1], value_grad))
+    weight_grad = jnp.concatenate(parts, axis=1)
     return (query_grad[None], key_grad[None], value_grad[None], weight_grad)
 
 

time: 79.9 us -> 76.2 us (0.954)
  waiting for transfers between devices: 34.1 us -> 27.6 us
  starting transfers between devices: 24.7 us -> 26.1 us
  local copies, waits for them, and re-layouts: 4.96 us -> 6.2 us
    ppermute x12, waiting for transfers between devices: 25.2 us -> 20.8 us  [dp_send(): return lax.ppermute(value, 'dp', pairs)]
    ppermute x2, waiting for transfers between devices: 4.29 us -> 0.78 us  [local(): others_away.append(lax.ppermute(rest, 'ctx', swap_ctx))]
    ppermute x2, waiting for transfers between devices: 0.01 us -> 2.54 us  [local(): arrived = lax.ppermute(sent, 'ctx', swap_ctx)]
    ppermute x2, starting transfers between devices: 2.56 us -> 3.99 us  [local(): others_away.append(lax.ppermute(rest, 'ctx', swap_ctx))]
    dynamic_update_slice x1 -> x0, other arithmetic: 0.89 us -> none  [local(): lax.dynamic_update_slice(weight_grad, half[rows:] + final.astype(jnp.floa...]
    slice x2 -> x3, local copies, waits for them, and re-layouts: 0.02 us -> 0.91 us  [local(): held_back.append(to_rows(arrived[tok:]))]
    unnamed x19 -> x25, local copies, waits for them, and re-layouts: 1.9 us -> 2.21 us
  transfers between devices with their start and end apart: 19 -> 19, of which waited for: 9 -> 8; matrix products, arithmetic and copies ran while one was open for 11% -> 12% of each run, Pallas kernels for 7% -> 8%
where the time goes in v7:
time: 76.2 us; the launch traced here: 75.9 us
  waiting for transfers between devices  27.6 us (36%)
  starting transfers between devices  26.1 us (34%)
  other arithmetic  8.92 us (12%)
  local copies, waits for them, and re-layouts  6.2 us (8%)
  Pallas kernels  5.91 us (8%)
  between operations  1.12 us (1%)
    ppermute x12, waiting for transfers between devices, dp_send(): return lax.ppermute(value, 'dp', pairs)  20.8 us
    ppermute x12, starting transfers between devices, dp_send(): return lax.ppermute(value, 'dp', pairs)  11.8 us
    ppermute x1, starting transfers between devices, shifted(): lax.ppermute(value, axis, [(source, source + steps) for source in range(l...  4.89 us
    ppermute x2, starting transfers between devices, local(): arrived = lax.ppermute(sent, 'ctx', swap_ctx)  4.18 us
    ppermute x2, starting transfers between devices, local(): others_away.append(lax.ppermute(rest, 'ctx', swap_ctx))  3.99 us
    pallas_call x2, Pallas kernels, attend(): pl.pallas_call(partial(attention_kernel, chunk, hops, group), grid_spec=p...  3.79 us
    ppermute x1, waiting for transfers between devices, shifted(): lax.ppermute(value, axis, [(source, source + steps) for source in range(l...  3.47 us
    ppermute x2, waiting for transfers between devices, local(): arrived = lax.ppermute(sent, 'ctx', swap_ctx)  2.54 us
  transfers between devices with their start and end apart: 19, of which 8 were waited for; matrix products, arithmetic and copies ran while one was open for 12% of the time, Pallas kernels for 8%

profile of v7, /device:TPU:0, one launch (start us, length us, event | category | flops | bytes accessed | tf_op | source)
XLA Modules:
  0.0 75.9 jit_solution(9432722462629537091)
XLA Ops:
  1.3 1.2 %fusion.7 = (bf16[128,512]{1,0:T(8,128)(2,1)S(1)}, bf16[128,512]{1,0:T(8,128)(2,1)S(1)}, bf16[128,512]{1,0:T(8,128)(2,1)S(1)}, bf16[128,512]{1,0:T(8,128)(2,1)S(1)}) fusion(bf16[128,1024]{1,0:T(8,128)(2,1)} %bitcast.53, bf16[128,1024]{1,0:T(8,128)(2,1)} %bitcast.56), kind=kLoop, calls=%fused_computation.49 | loop fusion | bytes 1048576 | tf_op jit(solution)/shard_map/slice | solution.py:232
  2.5 4.9 %collective-permute-start = (bf16[144,1024]{1,0:T(8,128)(2,1)S(1)}, bf16[144,1024]{1,0:T(8,128)(2,1)S(1)}, u32[]{:S(2)}, u32[]{:S(2)}) collective-permute-start(bf16[144,1024]{1,0:T(8,128)(2,1)S(1)} %fusion.2), channel_id=1, source_target_pairs={{0,1},{2,3},{4,5},{6,7},{8,9},{10,11},{12,13},{14,15},{16,17},{18,... | collective-permute-start | bytes 884744 | tf_op jit(solution)/shard_map/ppermute | solution.py:29
  8.1 0.9 %dynamic-slice_bitcast_fusion = (bf16[4,2,168,128]{3,2,1,0:T(8,128)(2,1)}, bf16[1,4,2,168,128]{4,3,2,1,0:T(8,128)(2,1)}) fusion(bf16[4,2,2,168,128]{4,3,2,1,0:T(8,128)(2,1)S(1)} %pad_maximum_fusion.1, s32[]{:T(128)S(6)} %select_n.124, s32[]{:T(128)S(6)} %select_n.116), kind=kLoop, calls=%fused_computation.22 | loop fusion | bytes 1376264 | tf_op jit(solution)/shard_map/jit(dynamic_index_in_dim)/squeeze | solution.py:217
  9.0 1.5 %collective-permute-start.2 = (bf16[4,2,168,128]{3,2,1,0:T(8,128)(2,1)}, bf16[4,2,168,128]{3,2,1,0:T(8,128)(2,1)}, u32[]{:S(2)}, u32[]{:S(2)}) collective-permute-start(bf16[4,2,168,128]{3,2,1,0:T(8,128)(2,1)} %get-tuple-element.56), channel_id=1, source_target_pairs={{0,4},{2,6},{4,0},{6,2},{8,12},{10,14},{12,8},{14,10},{16,20},{18,... | collective-permute-start | bytes 1032200 | tf_op jit(solution)/shard_map/ppermute | solution.py:203
  10.6 0.8 %bitcast_select_fusion = bf16[128,1024]{1,0:T(8,128)(2,1)} fusion(bf16[8,16,8,128]{3,2,1,0:T(8,128)(2,1)S(1)} %bitcast.69, bf16[128,512]{1,0:T(8,128)(2,1)S(1)} %get-tuple-element.73, bf16[128,512]{1,0:T(8,128)(2,1)S(1)} %get-tuple-element.68, pred[]{:T(512)S(6)} %eq.8), kind=kLoop, calls=%fused_computation.25 | loop fusion | flops 655360 | bytes 786433 | tf_op jit(solution)/shard_map/jit(_where)/select_n | solution.py:238
  11.3 3.5 %collective-permute-done.refs_5_.refs_6_ = bf16[144,1024]{1,0:T(8,128)(2,1)S(1)} collective-permute-done((bf16[144,1024]{1,0:T(8,128)(2,1)S(1)}, bf16[144,1024]{1,0:T(8,128)(2,1)S(1)}, u32[]{:S(2)}, u32[]{:S(2)}) %collective-permute-start) | collective-permute-done | bytes 294944 | tf_op jit(solution)/shard_map/ppermute | solution.py:29
  14.8 1.9 %shard_map.93 = (bf16[128,1024]{1,0:T(8,128)(2,1)S(1)}, bf16[256,512]{1,0:T(8,128)(2,1)S(1)}, bf16[128,512]{1,0:T(8,128)(2,1)S(1)}, bf16[128,512]{1,0:T(8,128)(2...) custom-call(s32[1]{0:T(128)} %bitcast.place_ref, bf16[16,128]{1,0:T(8,128)(2,1)S(1)} %broadcast_in_dim.15.refs_0_, ...), custom_call_target="tpu_custom_call" | custom-call | flops 1024 | bytes 1024 | tf_op jit(solution)/shard_map/pallas_call | solution.py:122
  16.7 2.6 %collective-permute-start.4 = (bf16[256,512]{1,0:T(8,128)(2,1)S(1)}, bf16[256,512]{1,0:T(8,128)(2,1)S(1)}, u32[]{:S(2)}, u32[]{:S(2)}) collective-permute-start(bf16[256,512]{1,0:T(8,128)(2,1)S(1)} %get-tuple-element.31), channel_id=1, source_target_pairs={{0,1},{1,0},{2,3},{3,2},{4,5},{5,4},{6,7},{7,6},{8,9},{9,8},{10,11... | collective-permute-start | bytes 786440 | tf_op jit(solution)/shard_map/ppermute | solution.py:274
  19.3 1.0 %fusion.1 = bf16[2,4,1,168,128]{4,3,2,1,0:T(8,128)(2,1)S(1)} fusion(s32[]{:T(128)S(6)} %select_n.125, bf16[1,4,2,168,128]{4,3,2,1,0:T(8,128)(2,1)S(1)} %copy-done.4, bf16[1,4,2,168,128]{4,3,2,1,0:T(8,128)(2,1)} %bitcast.16), kind=kLoop, calls=%fused_computation.17 | loop fusion | flops 172032 | bytes 1032196 | tf_op jit(solution)/shard_map/stack | solution.py:245
  20.2 1.0 %fusion.5 = bf16[1,4,1,168,128]{4,3,2,1,0:T(8,128)(2,1)S(1)} fusion(s32[]{:T(128)S(6)} %add.98, s32[]{:T(128)S(6)} %select_n.119, bf16[1,4,2,168,128]{4,3,2,1,0:T(8,128)(2,1)S(1)} %copy-done.4, bf16[1,4,2,168,128]{4,3,2,1,0:T(8,128)(2,1)} %bitcast.16), kind=kLoop, calls=%fused_computation.35 | loop fusion | flops 86016 | bytes 860168 | tf_op jit(solution)/shard_map/stack | solution.py:245
  21.3 1.9 %shard_map.94 = (bf16[128,1024]{1,0:T(8,128)(2,1)S(1)}, bf16[256,512]{1,0:T(8,128)(2,1)S(1)}, bf16[128,512]{1,0:T(8,128)(2,1)S(1)}, bf16[128,512]{1,0:T(8,128)(2...) custom-call(s32[1]{0:T(128)} %bitcast.place_ref, bf16[16,128]{1,0:T(8,128)(2,1)S(1)} %broadcast_in_dim.15.refs_0_, ...), custom_call_target="tpu_custom_call" | custom-call | flops 1024 | bytes 1024 | tf_op jit(solution)/shard_map/pallas_call | solution.py:122
  23.3 1.6 %collective-permute-start.5 = (bf16[256,512]{1,0:T(8,128)(2,1)S(1)}, bf16[256,512]{1,0:T(8,128)(2,1)S(1)}, u32[]{:S(2)}, u32[]{:S(2)}) collective-permute-start(bf16[256,512]{1,0:T(8,128)(2,1)S(1)} %get-tuple-element.35), channel_id=1, source_target_pairs={{0,1},{1,0},{2,3},{3,2},{4,5},{5,4},{6,7},{7,6},{8,9},{9,8},{10,11... | collective-permute-start | bytes 786440 | tf_op jit(solution)/shard_map/ppermute | solution.py:274
  25.1 0.9 %fusion.4 = (bf16[3,336,128]{2,1,0:T(8,128)(2,1)}, bf16[3,336,128]{2,1,0:T(8,128)(2,1)}) fusion(bf16[2,672,128]{2,1,0:T(8,128)(2,1)S(1)} %collective-permute-done.3, bf16[1,672,128]{2,1,0:T(8,128)(2,1)S(1)} %bitcast.66), kind=kLoop, calls=%fused_computation.34 | loop fusion | flops 258048 | bytes 1032192 | tf_op jit(solution)/shard_map/concatenate | solution.py:269
  26.0 2.4 %collective-permute-start.7 = (bf16[3,336,128]{2,1,0:T(8,128)(2,1)}, bf16[3,336,128]{2,1,0:T(8,128)(2,1)S(1)}, u32[]{:S(2)}, u32[]{:S(2)}) collective-permute-start(bf16[3,336,128]{2,1,0:T(8,128)(2,1)} %get-tuple-element.41), channel_id=1, source_target_pairs={{0,1},{1,0},{2,3},{3,2},{4,5},{5,4},{6,7},{7,6},{8,9},{9,8},{10,11... | collective-permute-start | bytes 774152 | tf_op jit(solution)/shard_map/ppermute | solution.py:289
  28.4 1.5 %collective-permute-start.8 = (bf16[256,512]{1,0:T(8,128)(2,1)S(1)}, bf16[256,512]{1,0:T(8,128)(2,1)S(1)}, u32[]{:S(2)}, u32[]{:S(2)}) collective-permute-start(bf16[256,512]{1,0:T(8,128)(2,1)S(1)} %pad_maximum_fusion.3.refs_0_), channel_id=1, source_target_pairs={{0,4},{2,6},{4,0},{6,2},{8,12},{10,14},{12,8},{14,10},{16,20},{18,... | collective-permute-start | bytes 786440 | tf_op jit(solution)/shard_map/ppermute | solution.py:203
  29.9 2.5 %collective-permute-done.5 = bf16[256,512]{1,0:T(8,128)(2,1)S(1)} collective-permute-done((bf16[256,512]{1,0:T(8,128)(2,1)S(1)}, bf16[256,512]{1,0:T(8,128)(2,1)S(1)}, u32[]{:S(2)}, u32[]{:S(2)}) %collective-permute-start.5) | collective-permute-done | bytes 262176 | tf_op jit(solution)/shard_map/ppermute | solution.py:274
  33.1 1.6 %collective-permute-start.11 = (bf16[256,512]{1,0:T(8,128)(2,1)S(1)}, bf16[256,512]{1,0:T(8,128)(2,1)S(1)}, u32[]{:S(2)}, u32[]{:S(2)}) collective-permute-start(bf16[256,512]{1,0:T(8,128)(2,1)S(1)} %pad_maximum_fusion.4.refs_0_), channel_id=1, source_target_pairs={{0,4},{2,6},{4,0},{6,2},{8,12},{10,14},{12,8},{14,10},{16,20},{18,... | collective-permute-start | bytes 786440 | tf_op jit(solution)/shard_map/ppermute | solution.py:203
  36.2 0.9 %slice-done = bf16[128,512]{1,0:T(8,128)(2,1)S(1)} async-done(((bf16[256,512]{1,0:T(8,128)(2,1)}), bf16[128,512]{1,0:T(8,128)(2,1)S(1)}, s32[]{:S(2)}) %slice-start) | async-done | bytes 131096 | tf_op jit(solution)/shard_map/slice | solution.py:275
  37.1 0.9 %copy-done.9 = bf16[4,128,128]{2,1,0:T(8,128)(2,1)S(1)} copy-done((bf16[4,128,128]{2,1,0:T(8,128)(2,1)S(1)}, bf16[4,128,128]{2,1,0:T(8,128)(2,1)}, u32[]{:S(2)}) %copy-start.9) | copy-done | bytes 131096
  39.0 1.6 %collective-permute-start.6 = (bf16[3,336,128]{2,1,0:T(8,128)(2,1)S(1)}, bf16[3,336,128]{2,1,0:T(8,128)(2,1)S(1)}, u32[]{:S(2)}, u32[]{:S(2)}) collective-permute-start(bf16[3,336,128]{2,1,0:T(8,128)(2,1)S(1)} %copy-done.11), channel_id=1, source_target_pairs={{0,1},{1,0},{2,3},{3,2},{4,5},{5,4},{6,7},{7,6},{8,9},{9,8},{10,11... | collective-permute-start | bytes 774152 | tf_op jit(solution)/shard_map/ppermute | solution.py:289
  41.1 0.9 %collective-permute-done.10.refs_3_ = bf16[256,512]{1,0:T(8,128)(2,1)S(1)} collective-permute-done((bf16[256,512]{1,0:T(8,128)(2,1)S(1)}, bf16[256,512]{1,0:T(8,128)(2,1)S(1)}, u32[]{:S(2)}, u32[]{:S(2)}) %collective-permute-start.10) | collective-permute-done | bytes 262176 | tf_op jit(solution)/shard_map/ppermute | solution.py:203
  42.6 1.6 %collective-permute-start.16 = (bf16[336,512]{1,0:T(8,128)(2,1)S(1)}, bf16[336,512]{1,0:T(8,128)(2,1)S(1)}, u32[]{:S(2)}, u32[]{:S(2)}) collective-permute-start(bf16[336,512]{1,0:T(8,128)(2,1)S(1)} %shard_map.95), channel_id=1, source_target_pairs={{0,8},{2,10},{4,12},{6,14},{8,0},{10,2},{12,4},{14,6},{16,24},{18,... | collective-permute-start | bytes 1032200 | tf_op jit(solution)/shard_map/ppermute | solution.py:203
  46.1 0.8 %collective-permute-done.6.others_away_ref = bf16[3,336,128]{2,1,0:T(8,128)(2,1)S(1)} collective-permute-done((bf16[3,336,128]{2,1,0:T(8,128)(2,1)S(1)}, bf16[3,336,128]{2,1,0:T(8,128)(2,1)S(1)}, u32[]{:S(2)}, u32[]{:S(2)}) %collective-permute-start.6) | collective-permute-done | bytes 258080 | tf_op jit(solution)/shard_map/ppermute | solution.py:289
  47.4 0.8 %maximum_bitcast_fusion = bf16[1,128,2048]{2,1,0:T(8,128)(2,1)} fusion(bf16[128,1024]{1,0:T(8,128)(2,1)S(1)} %get-tuple-element.48, bf16[128,1024]{1,0:T(8,128)(2,1)S(1)} %get-tuple-element.47), kind=kLoop, calls=%fused_computation.15 | loop fusion | flops 1048576 | bytes 1048576 | tf_op jit(solution)/shard_map/broadcast_in_dim | solution.py:353
  48.7 4.8 %collective-permute-done.16 = bf16[336,512]{1,0:T(8,128)(2,1)S(1)} collective-permute-done((bf16[336,512]{1,0:T(8,128)(2,1)S(1)}, bf16[336,512]{1,0:T(8,128)(2,1)S(1)}, u32[]{:S(2)}, u32[]{:S(2)}) %collective-permute-start.16) | collective-permute-done | bytes 344096 | tf_op jit(solution)/shard_map/ppermute | solution.py:203
  53.7 2.7 %collective-permute-start.18 = (bf16[168,512]{1,0:T(8,128)(2,1)S(1)}, bf16[168,512]{1,0:T(8,128)(2,1)S(1)}, u32[]{:S(2)}, u32[]{:S(2)}) collective-permute-start(bf16[168,512]{1,0:T(8,128)(2,1)S(1)} %slice.131), channel_id=1, source_target_pairs={{0,16},{2,18},{4,20},{6,22},{8,24},{10,26},{12,28},{14,30},{16,0},... | collective-permute-start | bytes 516104 | tf_op jit(solution)/shard_map/ppermute | solution.py:203
  56.4 1.3 %collective-permute-start.17 = (bf16[128,1024]{1,0:T(8,128)(2,1)S(1)}, bf16[128,1024]{1,0:T(8,128)(2,1)S(1)}, u32[]{:S(2)}, u32[]{:S(2)}) collective-permute-start(bf16[128,1024]{1,0:T(8,128)(2,1)S(1)} %copy-done.10), channel_id=1, source_target_pairs={{1,0},{3,2},{5,4},{7,6},{9,8},{11,10},{13,12},{15,14},{17,16},{19,... | collective-permute-start | bytes 786440 | tf_op jit(solution)/shard_map/ppermute | solution.py:345
  57.7 6.2 %collective-permute-done.14 = bf16[336,512]{1,0:T(8,128)(2,1)S(1)} collective-permute-done((bf16[336,512]{1,0:T(8,128)(2,1)S(1)}, bf16[336,512]{1,0:T(8,128)(2,1)S(1)}, u32[]{:S(2)}, u32[]{:S(2)}) %collective-permute-start.14) | collective-permute-done | bytes 344096 | tf_op jit(solution)/shard_map/ppermute | solution.py:203
  64.0 1.7 %collective-permute-start.15 = (bf16[168,512]{1,0:T(8,128)(2,1)S(1)}, bf16[168,512]{1,0:T(8,128)(2,1)S(1)}, u32[]{:S(2)}, u32[]{:S(2)}) collective-permute-start(bf16[168,512]{1,0:T(8,128)(2,1)S(1)} %slice.132), channel_id=1, source_target_pairs={{0,16},{2,18},{4,20},{6,22},{8,24},{10,26},{12,28},{14,30},{16,0},... | collective-permute-start | bytes 516104 | tf_op jit(solution)/shard_map/ppermute | solution.py:203
  65.7 8.5 %collective-permute-done.15 = bf16[168,512]{1,0:T(8,128)(2,1)S(1)} collective-permute-done((bf16[168,512]{1,0:T(8,128)(2,1)S(1)}, bf16[168,512]{1,0:T(8,128)(2,1)S(1)}, u32[]{:S(2)}, u32[]{:S(2)}) %collective-permute-start.15) | collective-permute-done | bytes 172064 | tf_op jit(solution)/shard_map/ppermute | solution.py:203
  74.3 0.8 %add_convert_fusion = bf16[128,1024]{1,0:T(8,128)(2,1)} fusion(bf16[128,1024]{1,0:T(8,128)(2,1)S(1)} %collective-permute-done.17, bf16[128,512]{1,0:T(8,128)(2,1)S(1)} %get-tuple-element.45, bf16[128,512]{1,0:T(8,128)(2,1)S(1)} %get-tuple-element.38), kind=kLoop, calls=%fused_computation.16 | loop fusion | flops 917504 | bytes 786432 | tf_op jit(solution)/shard_map/convert_element_type | solution.py:347
  75.0 0.9 %pad_maximum_fusion.2 = f32[168,1024]{1,0:T(8,128)} fusion(f32[168,512]{1,0:T(8,128)S(1)} %slice_add_fusion.1, f32[168,512]{1,0:T(8,128)S(1)} %slice_add_fusion), kind=kLoop, calls=%fused_computation.8 | loop fusion | flops 172032 | bytes 1376256 | tf_op jit(solution)/shard_map/concatenate | solution.py:352
  (76 shorter events, 9.0 us)
Async XLA Ops:
  1.3 6.2 %copy-start.7 = (bf16[1,128,2688]{2,1,0:T(8,128)(2,1)S(1)}, bf16[1,128,2688]{2,1,0:T(8,128)(2,1)}, u32[]{:S(2)}) copy-start(bf16[1,128,2688]{2,1,0:T(8,128)(2,1)} %param.6) | copy-start | bytes 2064388
  2.5 12.3 %collective-permute-start = (bf16[144,1024]{1,0:T(8,128)(2,1)S(1)}, bf16[144,1024]{1,0:T(8,128)(2,1)S(1)}, u32[]{:S(2)}, u32[]{:S(2)}) collective-permute-start(bf16[144,1024]{1,0:T(8,128)(2,1)S(1)} %fusion.2), channel_id=1, source_target_pairs={{0,1},{2,3},{4,5},{6,7},{8,9},{10,11},{12,13},{14,15},{16,17},{18,... | collective-permute-start | bytes 884744 | tf_op jit(solution)/shard_map/ppermute | solution.py:29
  9.0 10.3 %collective-permute-start.2 = (bf16[4,2,168,128]{3,2,1,0:T(8,128)(2,1)}, bf16[4,2,168,128]{3,2,1,0:T(8,128)(2,1)}, u32[]{:S(2)}, u32[]{:S(2)}) collective-permute-start(bf16[4,2,168,128]{3,2,1,0:T(8,128)(2,1)} %get-tuple-element.56), channel_id=1, source_target_pairs={{0,4},{2,6},{4,0},{6,2},{8,12},{10,14},{12,8},{14,10},{16,20},{18,... | collective-permute-start | bytes 1032200 | tf_op jit(solution)/shard_map/ppermute | solution.py:203
  10.5 4.3 %copy-start.3 = (bf16[1,128,2048]{2,1,0:T(8,128)(2,1)S(1)}, bf16[1,128,2048]{2,1,0:T(8,128)(2,1)}, u32[]{:S(2)}) copy-start(bf16[1,128,2048]{2,1,0:T(8,128)(2,1)} %param.10) | copy-start | bytes 1572868
  10.5 4.3 %copy-start.2 = (bf16[1,128,2048]{2,1,0:T(8,128)(2,1)S(1)}, bf16[1,128,2048]{2,1,0:T(8,128)(2,1)}, u32[]{:S(2)}) copy-start(bf16[1,128,2048]{2,1,0:T(8,128)(2,1)} %param.7) | copy-start | bytes 1572868
  10.5 4.3 %copy-start = (bf16[1,128,1024]{2,1,0:T(8,128)(2,1)S(1)}, bf16[1,128,1024]{2,1,0:T(8,128)(2,1)}, u32[]{:S(2)}) copy-start(bf16[1,128,1024]{2,1,0:T(8,128)(2,1)} %param.8) | copy-start | bytes 786436
  10.6 4.3 %copy-start.1 = (bf16[1,128,1024]{2,1,0:T(8,128)(2,1)S(1)}, bf16[1,128,1024]{2,1,0:T(8,128)(2,1)}, u32[]{:S(2)}) copy-start(bf16[1,128,1024]{2,1,0:T(8,128)(2,1)} %param.9) | copy-start | bytes 786436
  11.3 9.9 %collective-permute-start.1 = (bf16[128,1024]{1,0:T(8,128)(2,1)}, bf16[128,1024]{1,0:T(8,128)(2,1)S(1)}, u32[]{:S(2)}, u32[]{:S(2)}) collective-permute-start(bf16[128,1024]{1,0:T(8,128)(2,1)} %bitcast_select_fusion), channel_id=1, source_target_pairs={{0,1},{1,0},{2,3},{3,2},{4,5},{5,4},{6,7},{7,6},{8,9},{9,8},{10,11... | collective-permute-start | bytes 786440 | tf_op jit(solution)/shard_map/ppermute | solution.py:238
  14.8 4.5 %copy-start.4 = (bf16[1,4,2,168,128]{4,3,2,1,0:T(8,128)(2,1)S(1)}, bf16[1,4,2,168,128]{4,3,2,1,0:T(8,128)(2,1)}, u32[]{:S(2)}) copy-start(bf16[1,4,2,168,128]{4,3,2,1,0:T(8,128)(2,1)} %get-tuple-element.57) | copy-start | bytes 1032196
  16.7 8.2 %collective-permute-start.4 = (bf16[256,512]{1,0:T(8,128)(2,1)S(1)}, bf16[256,512]{1,0:T(8,128)(2,1)S(1)}, u32[]{:S(2)}, u32[]{:S(2)}) collective-permute-start(bf16[256,512]{1,0:T(8,128)(2,1)S(1)} %get-tuple-element.31), channel_id=1, source_target_pairs={{0,1},{1,0},{2,3},{3,2},{4,5},{5,4},{6,7},{7,6},{8,9},{9,8},{10,11... | collective-permute-start | bytes 786440 | tf_op jit(solution)/shard_map/ppermute | solution.py:274
  21.3 3.8 %collective-permute-start.3 = (bf16[2,672,128]{2,1,0:T(8,128)(2,1)S(1)}, bf16[2,672,128]{2,1,0:T(8,128)(2,1)S(1)}, u32[]{:S(2)}, u32[]{:S(2)}) collective-permute-start(bf16[2,672,128]{2,1,0:T(8,128)(2,1)S(1)} %bitcast.75), channel_id=1, source_target_pairs={{0,2},{2,0},{4,6},{6,4},{8,10},{10,8},{12,14},{14,12},{16,18},{18,... | collective-permute-start | bytes 1032200 | tf_op jit(solution)/shard_map/ppermute | solution.py:203
  23.3 9.2 %collective-permute-start.5 = (bf16[256,512]{1,0:T(8,128)(2,1)S(1)}, bf16[256,512]{1,0:T(8,128)(2,1)S(1)}, u32[]{:S(2)}, u32[]{:S(2)}) collective-permute-start(bf16[256,512]{1,0:T(8,128)(2,1)S(1)} %get-tuple-element.35), channel_id=1, source_target_pairs={{0,1},{1,0},{2,3},{3,2},{4,5},{5,4},{6,7},{7,6},{8,9},{9,8},{10,11... | collective-permute-start | bytes 786440 | tf_op jit(solution)/shard_map/ppermute | solution.py:274
  25.1 0.9 %copy-start.5 = (bf16[2,672,128]{2,1,0:T(8,128)(2,1)}, bf16[2,672,128]{2,1,0:T(8,128)(2,1)S(1)}, u32[]{:S(2)}) copy-start(bf16[2,672,128]{2,1,0:T(8,128)(2,1)S(1)} %collective-permute-done.3) | copy-start | bytes 1032196
  26.0 12.7 %collective-permute-start.7 = (bf16[3,336,128]{2,1,0:T(8,128)(2,1)}, bf16[3,336,128]{2,1,0:T(8,128)(2,1)S(1)}, u32[]{:S(2)}, u32[]{:S(2)}) collective-permute-start(bf16[3,336,128]{2,1,0:T(8,128)(2,1)} %get-tuple-element.41), channel_id=1, source_target_pairs={{0,1},{1,0},{2,3},{3,2},{4,5},{5,4},{6,7},{7,6},{8,9},{9,8},{10,11... | collective-permute-start | bytes 774152 | tf_op jit(solution)/shard_map/ppermute | solution.py:289
  28.4 12.1 %collective-permute-start.8 = (bf16[256,512]{1,0:T(8,128)(2,1)S(1)}, bf16[256,512]{1,0:T(8,128)(2,1)S(1)}, u32[]{:S(2)}, u32[]{:S(2)}) collective-permute-start(bf16[256,512]{1,0:T(8,128)(2,1)S(1)} %pad_maximum_fusion.3.refs_0_), channel_id=1, source_target_pairs={{0,4},{2,6},{4,0},{6,2},{8,12},{10,14},{12,8},{14,10},{16,20},{18,... | collective-permute-start | bytes 786440 | tf_op jit(solution)/shard_map/ppermute | solution.py:203
  32.4 0.7 copy-start.8
  33.1 7.8 %collective-permute-start.11 = (bf16[256,512]{1,0:T(8,128)(2,1)S(1)}, bf16[256,512]{1,0:T(8,128)(2,1)S(1)}, u32[]{:S(2)}, u32[]{:S(2)}) collective-permute-start(bf16[256,512]{1,0:T(8,128)(2,1)S(1)} %pad_maximum_fusion.4.refs_0_), channel_id=1, source_target_pairs={{0,4},{2,6},{4,0},{6,2},{8,12},{10,14},{12,8},{14,10},{16,20},{18,... | collective-permute-start | bytes 786440 | tf_op jit(solution)/shard_map/ppermute | solution.py:203
  36.2 0.9 %slice-start = ((bf16[256,512]{1,0:T(8,128)(2,1)}), bf16[128,512]{1,0:T(8,128)(2,1)S(1)}, s32[]{:S(2)}) async-start(bf16[256,512]{1,0:T(8,128)(2,1)} %copy-done.8), calls=%async_computation | async-start | bytes 262144 | tf_op jit(solution)/shard_map/slice | solution.py:275
  37.1 0.9 %copy-start.9 = (bf16[4,128,128]{2,1,0:T(8,128)(2,1)S(1)}, bf16[4,128,128]{2,1,0:T(8,128)(2,1)}, u32[]{:S(2)}) copy-start(bf16[4,128,128]{2,1,0:T(8,128)(2,1)} %copy.26) | copy-start | bytes 393220
  38.0 0.9 %copy-start.11 = (bf16[3,336,128]{2,1,0:T(8,128)(2,1)S(1)}, bf16[3,336,128]{2,1,0:T(8,128)(2,1)}, u32[]{:S(2)}) copy-start(bf16[3,336,128]{2,1,0:T(8,128)(2,1)} %get-tuple-element.40) | copy-start | bytes 774148
  38.0 3.0 %copy-start.6 = (bf16[2,672,128]{2,1,0:T(8,128)(2,1)S(1)}, bf16[2,672,128]{2,1,0:T(8,128)(2,1)}, u32[]{:S(2)}) copy-start(bf16[2,672,128]{2,1,0:T(8,128)(2,1)} %copy-done.5) | copy-start | bytes 1032196
  38.1 3.1 %collective-permute-start.9 = (bf16[256,512]{1,0:T(8,128)(2,1)S(1)}, bf16[256,512]{1,0:T(8,128)(2,1)S(1)}, u32[]{:S(2)}, u32[]{:S(2)}) collective-permute-start(bf16[256,512]{1,0:T(8,128)(2,1)S(1)} %pad_maximum_fusion.3.refs_0_), channel_id=1, source_target_pairs={{0,2},{2,0},{4,6},{6,4},{8,10},{10,8},{12,14},{14,12},{16,18},{18,... | collective-permute-start | bytes 786440 | tf_op jit(solution)/shard_map/ppermute | solution.py:203
  38.1 6.9 %collective-permute-start.12 = (bf16[256,512]{1,0:T(8,128)(2,1)S(1)}, bf16[256,512]{1,0:T(8,128)(2,1)S(1)}, u32[]{:S(2)}, u32[]{:S(2)}) collective-permute-start(bf16[256,512]{1,0:T(8,128)(2,1)S(1)} %pad_maximum_fusion.4.refs_0_), channel_id=1, source_target_pairs={{0,2},{2,0},{4,6},{6,4},{8,10},{10,8},{12,14},{14,12},{16,18},{18,... | collective-permute-start | bytes 786440 | tf_op jit(solution)/shard_map/ppermute | solution.py:203
  39.0 7.9 %collective-permute-start.6 = (bf16[3,336,128]{2,1,0:T(8,128)(2,1)S(1)}, bf16[3,336,128]{2,1,0:T(8,128)(2,1)S(1)}, u32[]{:S(2)}, u32[]{:S(2)}) collective-permute-start(bf16[3,336,128]{2,1,0:T(8,128)(2,1)S(1)} %copy-done.11), channel_id=1, source_target_pairs={{0,1},{1,0},{2,3},{3,2},{4,5},{5,4},{6,7},{7,6},{8,9},{9,8},{10,11... | collective-permute-start | bytes 774152 | tf_op jit(solution)/shard_map/ppermute | solution.py:289
  40.5 1.5 %collective-permute-start.10 = (bf16[256,512]{1,0:T(8,128)(2,1)S(1)}, bf16[256,512]{1,0:T(8,128)(2,1)S(1)}, u32[]{:S(2)}, u32[]{:S(2)}) collective-permute-start(bf16[256,512]{1,0:T(8,128)(2,1)S(1)} %collective-permute-done.8.refs_1_), channel_id=1, source_target_pairs={{0,2},{2,0},{4,6},{6,4},{8,10},{10,8},{12,14},{14,12},{16,18},{18,... | collective-permute-start | bytes 786440 | tf_op jit(solution)/shard_map/ppermute | solution.py:203
  40.9 4.1 %collective-permute-start.13 = (bf16[256,512]{1,0:T(8,128)(2,1)S(1)}, bf16[256,512]{1,0:T(8,128)(2,1)S(1)}, u32[]{:S(2)}, u32[]{:S(2)}) collective-permute-start(bf16[256,512]{1,0:T(8,128)(2,1)S(1)} %collective-permute-done.11.refs_1_), channel_id=1, source_target_pairs={{0,2},{2,0},{4,6},{6,4},{8,10},{10,8},{12,14},{14,12},{16,18},{18,... | collective-permute-start | bytes 786440 | tf_op jit(solution)/shard_map/ppermute | solution.py:203
  42.6 11.0 %collective-permute-start.16 = (bf16[336,512]{1,0:T(8,128)(2,1)S(1)}, bf16[336,512]{1,0:T(8,128)(2,1)S(1)}, u32[]{:S(2)}, u32[]{:S(2)}) collective-permute-start(bf16[336,512]{1,0:T(8,128)(2,1)S(1)} %shard_map.95), channel_id=1, source_target_pairs={{0,8},{2,10},{4,12},{6,14},{8,0},{10,2},{12,4},{14,6},{16,24},{18,... | collective-permute-start | bytes 1032200 | tf_op jit(solution)/shard_map/ppermute | solution.py:203
  45.6 18.3 %collective-permute-start.14 = (bf16[336,512]{1,0:T(8,128)(2,1)S(1)}, bf16[336,512]{1,0:T(8,128)(2,1)S(1)}, u32[]{:S(2)}, u32[]{:S(2)}) collective-permute-start(bf16[336,512]{1,0:T(8,128)(2,1)S(1)} %shard_map.96), channel_id=1, source_target_pairs={{0,8},{2,10},{4,12},{6,14},{8,0},{10,2},{12,4},{14,6},{16,24},{18,... | collective-permute-start | bytes 1032200 | tf_op jit(solution)/shard_map/ppermute | solution.py:203
  53.7 2.7 %copy-start.10 = (bf16[128,1024]{1,0:T(8,128)(2,1)S(1)}, bf16[128,1024]{1,0:T(8,128)(2,1)}, u32[]{:S(2)}) copy-start(bf16[128,1024]{1,0:T(8,128)(2,1)} %pad_maximum_fusion.5) | copy-start | bytes 786436
  53.7 11.9 %collective-permute-start.18 = (bf16[168,512]{1,0:T(8,128)(2,1)S(1)}, bf16[168,512]{1,0:T(8,128)(2,1)S(1)}, u32[]{:S(2)}, u32[]{:S(2)}) collective-permute-start(bf16[168,512]{1,0:T(8,128)(2,1)S(1)} %slice.131), channel_id=1, source_target_pairs={{0,16},{2,18},{4,20},{6,22},{8,24},{10,26},{12,28},{14,30},{16,0},... | collective-permute-start | bytes 516104 | tf_op jit(solution)/shard_map/ppermute | solution.py:203
  56.4 17.9 %collective-permute-start.17 = (bf16[128,1024]{1,0:T(8,128)(2,1)S(1)}, bf16[128,1024]{1,0:T(8,128)(2,1)S(1)}, u32[]{:S(2)}, u32[]{:S(2)}) collective-permute-start(bf16[128,1024]{1,0:T(8,128)(2,1)S(1)} %copy-done.10), channel_id=1, source_target_pairs={{1,0},{3,2},{5,4},{7,6},{9,8},{11,10},{13,12},{15,14},{17,16},{19,... | collective-permute-start | bytes 786440 | tf_op jit(solution)/shard_map/ppermute | solution.py:345
  64.0 10.2 %collective-permute-start.15 = (bf16[168,512]{1,0:T(8,128)(2,1)S(1)}, bf16[168,512]{1,0:T(8,128)(2,1)S(1)}, u32[]{:S(2)}, u32[]{:S(2)}) collective-permute-start(bf16[168,512]{1,0:T(8,128)(2,1)S(1)} %slice.132), channel_id=1, source_target_pairs={{0,16},{2,18},{4,20},{6,22},{8,24},{10,26},{12,28},{14,30},{16,0},... | collective-permute-start | bytes 516104 | tf_op jit(solution)/shard_map/ppermute | solution.py:203

commit v8 on v7

--- a/solution.py
+++ b/solution.py
@@ -142,36 +142,52 @@
     )(*operands)
 
 
-def product_kernel(own_ref, others_ref, own_away_ref, others_away_ref, *refs):
-    grads = jnp.concatenate([ref[...] for ref in refs[:-1]], axis=0)
+def product_kernel(half, traces, place_ref, own_ref, others_ref, others_away_ref, *refs):
+    grad_refs, refs = refs[:traces], refs[traces:]
     others = range(others_ref.shape[0])
+    rows, tok = others_away_ref.shape[1:]
+    if len(refs) > 2:
+        rim_ref, *back_refs = refs[: 1 + CHUNKS]
+        refs = refs[1 + CHUNKS :]
+        backs = jnp.concatenate([ref[tok:] for ref in back_refs], axis=1)
+        blocks = jnp.where(place_ref[0] == 0, rim_ref[...], backs)
+        own_away = jnp.concatenate(
+            [blocks[:, low : low + HD] for low in range(0, 2 * rows, HD)], axis=0
+        )[half * rows : (half + 1) * rows]
+    else:
+        own_away, refs = refs[0][...], refs[1:]
+    (out_ref,) = refs
+    grads = jnp.concatenate([ref[...] for ref in grad_refs], axis=0)
     near = [own_ref[...]] + [others_ref[t] for t in others]
-    away = [own_away_ref[...]] + [others_away_ref[t] for t in others]
+    away = [own_away] + [others_away_ref[t] for t in others]
     features = jnp.concatenate([piece for pair in zip(near, away) for piece in pair], axis=1)
-    refs[-1][...] = dot_f32(features, grads).astype(refs[-1].dtype)
-
-
-def product(half, own, others, own_away, others_away, grads, dtype):
+    out_ref[...] = dot_f32(features, grads).astype(out_ref.dtype)
+
+
+def product(half, place, own, others, own_away, others_away, grads, dtype):
     traces, rows, tok = others.shape
     rows //= 2
     width = grads[0].shape[1]
-    of_half = lambda array: pl.BlockSpec((rows, array.shape[1]), lambda i: (half, 0))
-    whole = lambda array: pl.BlockSpec(array.shape, lambda i: (0,) * array.ndim)
+    of_half = lambda array: pl.BlockSpec((rows, array.shape[1]), lambda i, *_: (half, 0))
+    whole = lambda array: pl.BlockSpec(array.shape, lambda i, *_: (0,) * array.ndim)
     return pl.pallas_call(
-        product_kernel,
-        grid=(1,),
-        in_specs=[
-            of_half(own),
-            pl.BlockSpec((traces, rows, tok), lambda i: (0, half, 0)),
-            of_half(own_away),
-            whole(others_away),
-        ]
-        + [whole(piece) for piece in grads],
-        out_specs=pl.BlockSpec((rows, width), lambda i: (0, 0)),
+        partial(product_kernel, half, len(grads)),
+        grid_spec=pltpu.PrefetchScalarGridSpec(
+            num_scalar_prefetch=1,
+            grid=(1,),
+            in_specs=[
+                of_half(own),
+                pl.BlockSpec((traces, rows, tok), lambda i, *_: (0, half, 0)),
+                whole(others_away),
+            ]
+            + [whole(piece) for piece in grads]
+            + [(whole if len(own_away) > 1 else of_half)(piece) for piece in own_away],
+            out_specs=pl.BlockSpec((rows, width), lambda i, *_: (0, 0)),
+        ),
         out_shape=jax.ShapeDtypeStruct((rows, width), dtype),
         compiler_params=pltpu.CompilerParams(vmem_limit_bytes=48 * MIB),
         cost_estimate=SMALL,
-    )(own, others, own_away, others_away, *grads)
+    )(place, own, others, others_away, *grads, *own_away)
 
 
 def local(hidden_in, queries, key_states, value_states, out_grad, segment_ids):
@@ -225,7 +241,6 @@
     steps = range(hops, 0, -1)
     seg_rows = jnp.broadcast_to(segment_ids.astype(jnp.bfloat16), (SEG_ROWS, tok))
     wide_rows = jnp.pad(seg_rows, ((0, 0), (0, 2 * width - tok)))
-    to_rows = lambda array: array.reshape(tok, -1, HD).transpose(1, 0, 2).reshape(-1, HD)
     rim_pairs = []
     for chunk in range(CHUNKS):
         cols = slice(chunk * width, (chunk + 1) * width)
@@ -272,7 +287,7 @@
         columns, held_back, others_away = [], [], []
         for chunk, (_, sent, addend, key_own, value_own, _) in enumerate(attended):
             arrived = lax.ppermute(sent, "ctx", swap_ctx)
-            held_back.append(to_rows(arrived[tok:]))
+            held_back.append(arrived)
             if chunk == 0:
                 arrived, _ = lax.optimization_barrier((arrived, rim_pairs[1:]))
             else:
@@ -288,10 +303,7 @@
                     rest, block = lax.optimization_barrier((others[:, low:high], block))
                     others_away.append(lax.ppermute(rest, "ctx", swap_ctx))
             columns.append(block)
-        piece_rows = own_piece.shape[0]
-        own_away = jnp.where(
-            first, to_rows(rim_pairs[-1][0])[:piece_rows], jnp.concatenate(held_back)[:piece_rows]
-        )
+        own_away = [rim_pairs[-1][0], *held_back]
         key_grad = jnp.where(
             first,
             jnp.concatenate([block[:tok] for block in columns], axis=1),
@@ -318,17 +330,17 @@
         columns = jnp.split(both, CHUNKS, axis=1)
         every = jnp.concatenate([own_piece[None], others])
         near, away = jnp.split(lax.all_gather(every, "ctx", axis=2, tiled=True), 2, axis=2)
-        own_piece, others, own_away = near[0], near[1:], away[0]
+        own_piece, others, own_away = near[0], near[1:], [away[0]]
         others_away = [away[1:, low:high] for low, high in low_high]
 
     gathered = []
     for block in columns:
         near = [block] + [dp_send(block, mid_by(step)) for step in range(1, mid_count)]
         gathered.append(near + [dp_send(near_one, swap_core) for near_one in near])
-    together = lambda half, dtype: [
-        product(half, own_piece, others, own_away, others_away[half], grads, dtype)
-        for grads in gathered
-    ]
+    def together(half, dtype):
+        ends = (place_arg, own_piece, others, own_away, others_away[half])
+        return [product(half, *ends, grads, dtype) for grads in gathered]
+
     sent = together(0, jnp.bfloat16)
     others_away[1], _ = lax.optimization_barrier((others_away[1], sent))
     kept = together(1, jnp.float32)
@@ -340,15 +352,13 @@
     query_parts, _ = lax.optimization_barrier(([outs[0] for outs in attended], kept[0]))
     query_grad = jnp.concatenate(query_parts, axis=1)
     if ctx_count == 2:
-        value_rim = jnp.concatenate([outs[5] for outs in attended], axis=1)
-        value_rim, _ = lax.optimization_barrier((value_rim, halves[0]))
+        value_rims, _ = lax.optimization_barrier(([outs[5] for outs in attended], halves[0]))
+        value_rim = jnp.concatenate(value_rims, axis=1)
         returned = lax.ppermute(value_rim, "ctx", [(1, 0)])
         value_own = jnp.concatenate([outs[4] for outs in attended], axis=1)
         value_grad = (value_own.astype(jnp.float32) + returned.astype(jnp.float32)).astype(
             jnp.bfloat16
         )
-    if ctx_count == 2:
-        parts[-1], value_grad = lax.optimization_barrier((parts[-1], value_grad))
     weight_grad = jnp.concatenate(parts, axis=1)
     return (query_grad[None], key_grad[None], value_grad[None], weight_grad)
 

time: 76.2 us -> 79.3 us (1.041)
  waiting for transfers between devices: 27.6 us -> 34.3 us
  local copies, waits for them, and re-layouts: 6.2 us -> 2.88 us
  other arithmetic: 8.92 us -> 8.1 us
    ppermute x2, waiting for transfers between devices: 0.78 us -> 5.36 us  [local(): others_away.append(lax.ppermute(rest, 'ctx', swap_ctx))]
    unnamed x25 -> x13, local copies, waits for them, and re-layouts: 2.21 us -> 0.44 us
    ppermute x2, waiting for transfers between devices: 2.54 us -> 4.24 us  [local(): arrived = lax.ppermute(sent, 'ctx', swap_ctx)]
    slice x3 -> x0, local copies, waits for them, and re-layouts: 0.91 us -> none  [local(): held_back.append(to_rows(arrived[tok:]))]
    concatenate x2, other arithmetic: 0.93 us -> 0.1 us  [local(): others = jnp.concatenate([kept_core[1:], other_core])]
    broadcast_in_dim x1 -> x2, other arithmetic: 0.83 us -> 1.6 us  [local(): return (query_grad[None], key_grad[None], value_grad[None], weight_grad)]
  transfers between devices with their start and end apart: 19 -> 19, of which waited for: 8 -> 7; matrix products, arithmetic and copies ran while one was open for 12% -> 10% of each run, Pallas kernels for 8% -> 8%
where the time goes in v8:
time: 79.3 us; the launch traced here: 79 us
  waiting for transfers between devices  34.3 us (43%)
  starting transfers between devices  26 us (33%)
  other arithmetic  8.1 us (10%)
  Pallas kernels  6.64 us (8%)
  local copies, waits for them, and re-layouts  2.88 us (4%)
  between operations  1.06 us (1%)
    ppermute x12, waiting for transfers between devices, dp_send(): return lax.ppermute(value, 'dp', pairs)  21.2 us
    ppermute x12, starting transfers between devices, dp_send(): return lax.ppermute(value, 'dp', pairs)  12.2 us
    ppermute x2, waiting for transfers between devices, local(): others_away.append(lax.ppermute(rest, 'ctx', swap_ctx))  5.36 us
    ppermute x1, starting transfers between devices, shifted(): lax.ppermute(value, axis, [(source, source + steps) for source in range(l...  4.88 us
    pallas_call x2, Pallas kernels, attend(): pl.pallas_call(partial(attention_kernel, chunk, hops, group), grid_spec=p...  4.49 us
    ppermute x2, waiting for transfers between devices, local(): arrived = lax.ppermute(sent, 'ctx', swap_ctx)  4.24 us
    ppermute x2, starting transfers between devices, local(): arrived = lax.ppermute(sent, 'ctx', swap_ctx)  4.22 us
    ppermute x1, waiting for transfers between devices, shifted(): lax.ppermute(value, axis, [(source, source + steps) for source in range(l...  3.55 us
  transfers between devices with their start and end apart: 19, of which 7 were waited for; matrix products, arithmetic and copies ran while one was open for 10% of the time, Pallas kernels for 8%

profile of v8, /device:TPU:0, one launch (start us, length us, event | category | flops | bytes accessed | tf_op | source)
XLA Modules:
  0.0 79.0 jit_solution(16790919612565912537)
XLA Ops:
  0.6 0.7 convert_bitcast_fusion
  1.3 1.2 %fusion.7 = (bf16[128,512]{1,0:T(8,128)(2,1)S(1)}, bf16[128,512]{1,0:T(8,128)(2,1)S(1)}, bf16[128,512]{1,0:T(8,128)(2,1)S(1)}, bf16[128,512]{1,0:T(8,128)(2,1)S(1)}) fusion(bf16[128,1024]{1,0:T(8,128)(2,1)} %bitcast.41, bf16[128,1024]{1,0:T(8,128)(2,1)} %bitcast.44), kind=kLoop, calls=%fused_computation.47 | loop fusion | bytes 1048576 | tf_op jit(solution)/shard_map/slice | solution.py:247
  2.5 0.7 fusion.2
  3.2 4.9 %collective-permute-start = (bf16[144,1024]{1,0:T(8,128)(2,1)}, bf16[144,1024]{1,0:T(8,128)(2,1)S(1)}, u32[]{:S(2)}, u32[]{:S(2)}) collective-permute-start(bf16[144,1024]{1,0:T(8,128)(2,1)} %fusion.2), channel_id=1, source_target_pairs={{0,1},{2,3},{4,5},{6,7},{8,9},{10,11},{12,13},{14,15},{16,17},{18,... | collective-permute-start | bytes 884744 | tf_op jit(solution)/shard_map/ppermute | solution.py:29
  8.8 0.9 %dynamic-slice_bitcast_fusion = (bf16[4,2,168,128]{3,2,1,0:T(8,128)(2,1)}, bf16[1,4,2,168,128]{4,3,2,1,0:T(8,128)(2,1)}) fusion(bf16[4,2,2,168,128]{4,3,2,1,0:T(8,128)(2,1)S(1)} %pad_maximum_fusion.1, s32[]{:T(128)S(6)} %select_n.116, s32[]{:T(128)S(6)} %select_n.108), kind=kLoop, calls=%fused_computation.22 | loop fusion | bytes 1376264 | tf_op jit(solution)/shard_map/jit(dynamic_index_in_dim)/squeeze | solution.py:233
  9.7 1.5 %collective-permute-start.2 = (bf16[4,2,168,128]{3,2,1,0:T(8,128)(2,1)}, bf16[4,2,168,128]{3,2,1,0:T(8,128)(2,1)}, u32[]{:S(2)}, u32[]{:S(2)}) collective-permute-start(bf16[4,2,168,128]{3,2,1,0:T(8,128)(2,1)} %get-tuple-element.54), channel_id=1, source_target_pairs={{0,4},{2,6},{4,0},{6,2},{8,12},{10,14},{12,8},{14,10},{16,20},{18,... | collective-permute-start | bytes 1032200 | tf_op jit(solution)/shard_map/ppermute | solution.py:219
  11.5 0.8 bitcast_select_fusion
  12.3 3.6 %collective-permute-done.refs_5_.refs_6_ = bf16[144,1024]{1,0:T(8,128)(2,1)S(1)} collective-permute-done((bf16[144,1024]{1,0:T(8,128)(2,1)}, bf16[144,1024]{1,0:T(8,128)(2,1)S(1)}, u32[]{:S(2)}, u32[]{:S(2)}) %collective-permute-start) | collective-permute-done | bytes 294944 | tf_op jit(solution)/shard_map/ppermute | solution.py:29
  15.8 2.6 %shard_map.93 = (bf16[128,1024]{1,0:T(8,128)(2,1)S(1)}, bf16[256,512]{1,0:T(8,128)(2,1)}, bf16[128,512]{1,0:T(8,128)(2,1)S(1)}, bf16[128,512]{1,0:T(8,128)(2,1)S...) custom-call(s32[1]{0:T(128)} %bitcast.place_ref, bf16[16,128]{1,0:T(8,128)(2,1)S(1)} %broadcast_in_dim.15.refs_0_, ...), custom_call_target="tpu_custom_call" | custom-call | flops 1024 | bytes 1024 | tf_op jit(solution)/shard_map/pallas_call | solution.py:122
  18.4 2.4 %collective-permute-start.4 = (bf16[256,512]{1,0:T(8,128)(2,1)}, bf16[256,512]{1,0:T(8,128)(2,1)S(1)}, u32[]{:S(2)}, u32[]{:S(2)}) collective-permute-start(bf16[256,512]{1,0:T(8,128)(2,1)} %get-tuple-element.30), channel_id=1, source_target_pairs={{0,1},{1,0},{2,3},{3,2},{4,5},{5,4},{6,7},{7,6},{8,9},{9,8},{10,11... | collective-permute-start | bytes 786440 | tf_op jit(solution)/shard_map/ppermute | solution.py:289
  20.8 1.0 %fusion.1 = bf16[2,4,1,168,128]{4,3,2,1,0:T(8,128)(2,1)S(1)} fusion(s32[]{:T(128)S(6)} %select_n.117, bf16[1,4,2,168,128]{4,3,2,1,0:T(8,128)(2,1)} %get-tuple-element.55, bf16[1,4,2,168,128]{4,3,2,1,0:T(8,128)(2,1)} %bitcast.16), kind=kLoop, calls=%fused_computation.17 | loop fusion | flops 172032 | bytes 1032196 | tf_op jit(solution)/shard_map/stack | solution.py:260
  21.9 1.9 %shard_map.94 = (bf16[128,1024]{1,0:T(8,128)(2,1)S(1)}, bf16[256,512]{1,0:T(8,128)(2,1)S(1)}, bf16[128,512]{1,0:T(8,128)(2,1)S(1)}, bf16[128,512]{1,0:T(8,128)(2...) custom-call(s32[1]{0:T(128)} %bitcast.place_ref, bf16[16,128]{1,0:T(8,128)(2,1)S(1)} %broadcast_in_dim.15.refs_0_, ...), custom_call_target="tpu_custom_call" | custom-call | flops 1024 | bytes 1024 | tf_op jit(solution)/shard_map/pallas_call | solution.py:122
  23.9 1.8 %collective-permute-start.10 = (bf16[256,512]{1,0:T(8,128)(2,1)S(1)}, bf16[256,512]{1,0:T(8,128)(2,1)S(1)}, u32[]{:S(2)}, u32[]{:S(2)}) collective-permute-start(bf16[256,512]{1,0:T(8,128)(2,1)S(1)} %get-tuple-element.41), channel_id=1, source_target_pairs={{0,1},{1,0},{2,3},{3,2},{4,5},{5,4},{6,7},{7,6},{8,9},{9,8},{10,11... | collective-permute-start | bytes 786440 | tf_op jit(solution)/shard_map/ppermute | solution.py:289
  25.7 1.0 %fusion.6 = bf16[1,4,1,168,128]{4,3,2,1,0:T(8,128)(2,1)S(1)} fusion(s32[]{:T(128)S(6)} %add.98, s32[]{:T(128)S(6)} %select_n.111, bf16[1,4,2,168,128]{4,3,2,1,0:T(8,128)(2,1)S(1)} %copy-done.4, bf16[1,4,2,168,128]{4,3,2,1,0:T(8,128)(2,1)} %bitcast.16), kind=kLoop, calls=%fused_computation.35 | loop fusion | flops 86016 | bytes 860168 | tf_op jit(solution)/shard_map/stack | solution.py:260
  26.9 1.6 %collective-permute-start.7 = (bf16[256,512]{1,0:T(8,128)(2,1)S(1)}, bf16[256,512]{1,0:T(8,128)(2,1)S(1)}, u32[]{:S(2)}, u32[]{:S(2)}) collective-permute-start(bf16[256,512]{1,0:T(8,128)(2,1)S(1)} %pad_maximum_fusion.3.refs_0_), channel_id=1, source_target_pairs={{0,4},{2,6},{4,0},{6,2},{8,12},{10,14},{12,8},{14,10},{16,20},{18,... | collective-permute-start | bytes 786440 | tf_op jit(solution)/shard_map/ppermute | solution.py:219
  28.4 4.2 %collective-permute-done.10.refs_6_ = bf16[256,512]{1,0:T(8,128)(2,1)S(1)} collective-permute-done((bf16[256,512]{1,0:T(8,128)(2,1)S(1)}, bf16[256,512]{1,0:T(8,128)(2,1)S(1)}, u32[]{:S(2)}, u32[]{:S(2)}) %collective-permute-start.10) | collective-permute-done | bytes 262176 | tf_op jit(solution)/shard_map/ppermute | solution.py:289
  32.8 1.6 %collective-permute-start.11 = (bf16[256,512]{1,0:T(8,128)(2,1)S(1)}, bf16[256,512]{1,0:T(8,128)(2,1)S(1)}, u32[]{:S(2)}, u32[]{:S(2)}) collective-permute-start(bf16[256,512]{1,0:T(8,128)(2,1)S(1)} %pad_maximum_fusion.4.refs_0_), channel_id=1, source_target_pairs={{0,4},{2,6},{4,0},{6,2},{8,12},{10,14},{12,8},{14,10},{16,20},{18,... | collective-permute-start | bytes 786440 | tf_op jit(solution)/shard_map/ppermute | solution.py:219
  34.3 1.7 %collective-permute-start.6 = (bf16[3,336,128]{2,1,0:T(8,128)(2,1)S(1)}, bf16[3,336,128]{2,1,0:T(8,128)(2,1)S(1)}, u32[]{:S(2)}, u32[]{:S(2)}) collective-permute-start(bf16[3,336,128]{2,1,0:T(8,128)(2,1)S(1)} %get-tuple-element.39), channel_id=1, source_target_pairs={{0,1},{1,0},{2,3},{3,2},{4,5},{5,4},{6,7},{7,6},{8,9},{9,8},{10,11... | collective-permute-start | bytes 774152 | tf_op jit(solution)/shard_map/ppermute | solution.py:304
  36.6 5.4 %collective-permute-done.6.others_away_ref = bf16[3,336,128]{2,1,0:T(8,128)(2,1)S(1)} collective-permute-done((bf16[3,336,128]{2,1,0:T(8,128)(2,1)S(1)}, bf16[3,336,128]{2,1,0:T(8,128)(2,1)S(1)}, u32[]{:S(2)}, u32[]{:S(2)}) %collective-permute-start.6) | collective-permute-done | bytes 258080 | tf_op jit(solution)/shard_map/ppermute | solution.py:304
  41.9 1.7 %collective-permute-start.5 = (bf16[3,336,128]{2,1,0:T(8,128)(2,1)S(1)}, bf16[3,336,128]{2,1,0:T(8,128)(2,1)S(1)}, u32[]{:S(2)}, u32[]{:S(2)}) collective-permute-start(bf16[3,336,128]{2,1,0:T(8,128)(2,1)S(1)} %get-tuple-element.38), channel_id=1, source_target_pairs={{0,1},{1,0},{2,3},{3,2},{4,5},{5,4},{6,7},{7,6},{8,9},{9,8},{10,11... | collective-permute-start | bytes 774152 | tf_op jit(solution)/shard_map/ppermute | solution.py:304
  44.2 0.9 %collective-permute-done.9.refs_3_ = bf16[256,512]{1,0:T(8,128)(2,1)S(1)} collective-permute-done((bf16[256,512]{1,0:T(8,128)(2,1)S(1)}, bf16[256,512]{1,0:T(8,128)(2,1)S(1)}, u32[]{:S(2)}, u32[]{:S(2)}) %collective-permute-start.9) | collective-permute-done | bytes 262176 | tf_op jit(solution)/shard_map/ppermute | solution.py:219
  45.7 1.6 %collective-permute-start.14 = (bf16[336,512]{1,0:T(8,128)(2,1)S(1)}, bf16[336,512]{1,0:T(8,128)(2,1)S(1)}, u32[]{:S(2)}, u32[]{:S(2)}) collective-permute-start(bf16[336,512]{1,0:T(8,128)(2,1)S(1)} %shard_map.95), channel_id=1, source_target_pairs={{0,8},{2,10},{4,12},{6,14},{8,0},{10,2},{12,4},{14,6},{16,24},{18,... | collective-permute-start | bytes 1032200 | tf_op jit(solution)/shard_map/ppermute | solution.py:219
  47.4 0.8 maximum_select_fusion
  50.3 0.8 %maximum_bitcast_fusion = bf16[1,128,2048]{2,1,0:T(8,128)(2,1)} fusion(bf16[128,1024]{1,0:T(8,128)(2,1)S(1)} %get-tuple-element.47, bf16[128,1024]{1,0:T(8,128)(2,1)S(1)} %get-tuple-element.46), kind=kLoop, calls=%fused_computation.15 | loop fusion | flops 1048576 | bytes 1048576 | tf_op jit(solution)/shard_map/broadcast_in_dim | solution.py:363
  51.1 5.6 %collective-permute-done.14 = bf16[336,512]{1,0:T(8,128)(2,1)S(1)} collective-permute-done((bf16[336,512]{1,0:T(8,128)(2,1)S(1)}, bf16[336,512]{1,0:T(8,128)(2,1)S(1)}, u32[]{:S(2)}, u32[]{:S(2)}) %collective-permute-start.14) | collective-permute-done | bytes 344096 | tf_op jit(solution)/shard_map/ppermute | solution.py:219
  56.8 2.7 %collective-permute-start.16 = (bf16[168,512]{1,0:T(8,128)(2,1)S(1)}, bf16[168,512]{1,0:T(8,128)(2,1)S(1)}, u32[]{:S(2)}, u32[]{:S(2)}) collective-permute-start(bf16[168,512]{1,0:T(8,128)(2,1)S(1)} %slice.112), channel_id=1, source_target_pairs={{0,16},{2,18},{4,20},{6,22},{8,24},{10,26},{12,28},{14,30},{16,0},... | collective-permute-start | bytes 516104 | tf_op jit(solution)/shard_map/ppermute | solution.py:219
  59.5 1.3 %collective-permute-start.15 = (bf16[128,1024]{1,0:T(8,128)(2,1)S(1)}, bf16[128,1024]{1,0:T(8,128)(2,1)S(1)}, u32[]{:S(2)}, u32[]{:S(2)}) collective-permute-start(bf16[128,1024]{1,0:T(8,128)(2,1)S(1)} %pad_maximum_fusion.5), channel_id=1, source_target_pairs={{1,0},{3,2},{5,4},{7,6},{9,8},{11,10},{13,12},{15,14},{17,16},{19,... | collective-permute-start | bytes 786440 | tf_op jit(solution)/shard_map/ppermute | solution.py:357
  60.8 6.2 %collective-permute-done.17 = bf16[336,512]{1,0:T(8,128)(2,1)S(1)} collective-permute-done((bf16[336,512]{1,0:T(8,128)(2,1)S(1)}, bf16[336,512]{1,0:T(8,128)(2,1)S(1)}, u32[]{:S(2)}, u32[]{:S(2)}) %collective-permute-start.17) | collective-permute-done | bytes 344096 | tf_op jit(solution)/shard_map/ppermute | solution.py:219
  67.1 1.7 %collective-permute-start.18 = (bf16[168,512]{1,0:T(8,128)(2,1)S(1)}, bf16[168,512]{1,0:T(8,128)(2,1)S(1)}, u32[]{:S(2)}, u32[]{:S(2)}) collective-permute-start(bf16[168,512]{1,0:T(8,128)(2,1)S(1)} %slice.111), channel_id=1, source_target_pairs={{0,16},{2,18},{4,20},{6,22},{8,24},{10,26},{12,28},{14,30},{16,0},... | collective-permute-start | bytes 516104 | tf_op jit(solution)/shard_map/ppermute | solution.py:219
  68.8 8.5 %collective-permute-done.18 = bf16[168,512]{1,0:T(8,128)(2,1)S(1)} collective-permute-done((bf16[168,512]{1,0:T(8,128)(2,1)S(1)}, bf16[168,512]{1,0:T(8,128)(2,1)S(1)}, u32[]{:S(2)}, u32[]{:S(2)}) %collective-permute-start.18) | collective-permute-done | bytes 172064 | tf_op jit(solution)/shard_map/ppermute | solution.py:219
  77.4 0.9 %pad_maximum_fusion.2 = f32[168,1024]{1,0:T(8,128)} fusion(f32[168,512]{1,0:T(8,128)S(1)} %slice_add_fusion, f32[168,512]{1,0:T(8,128)S(1)} %slice_add_fusion.1), kind=kLoop, calls=%fused_computation.8 | loop fusion | flops 172032 | bytes 1376256 | tf_op jit(solution)/shard_map/concatenate | solution.py:362
  78.3 0.8 fusion.3
  (56 shorter events, 5.2 us)
Async XLA Ops:
  1.3 6.9 %copy-start.5 = (bf16[1,128,2688]{2,1,0:T(8,128)(2,1)S(1)}, bf16[1,128,2688]{2,1,0:T(8,128)(2,1)}, u32[]{:S(2)}) copy-start(bf16[1,128,2688]{2,1,0:T(8,128)(2,1)} %param.6) | copy-start | bytes 2064388
  3.2 12.6 %collective-permute-start = (bf16[144,1024]{1,0:T(8,128)(2,1)}, bf16[144,1024]{1,0:T(8,128)(2,1)S(1)}, u32[]{:S(2)}, u32[]{:S(2)}) collective-permute-start(bf16[144,1024]{1,0:T(8,128)(2,1)} %fusion.2), channel_id=1, source_target_pairs={{0,1},{2,3},{4,5},{6,7},{8,9},{10,11},{12,13},{14,15},{16,17},{18,... | collective-permute-start | bytes 884744 | tf_op jit(solution)/shard_map/ppermute | solution.py:29
  9.7 11.1 %collective-permute-start.2 = (bf16[4,2,168,128]{3,2,1,0:T(8,128)(2,1)}, bf16[4,2,168,128]{3,2,1,0:T(8,128)(2,1)}, u32[]{:S(2)}, u32[]{:S(2)}) collective-permute-start(bf16[4,2,168,128]{3,2,1,0:T(8,128)(2,1)} %get-tuple-element.54), channel_id=1, source_target_pairs={{0,4},{2,6},{4,0},{6,2},{8,12},{10,14},{12,8},{14,10},{16,20},{18,... | collective-permute-start | bytes 1032200 | tf_op jit(solution)/shard_map/ppermute | solution.py:219
  11.2 4.6 %copy-start.3 = (bf16[1,128,2048]{2,1,0:T(8,128)(2,1)S(1)}, bf16[1,128,2048]{2,1,0:T(8,128)(2,1)}, u32[]{:S(2)}) copy-start(bf16[1,128,2048]{2,1,0:T(8,128)(2,1)} %param.10) | copy-start | bytes 1572868
  11.3 4.5 %copy-start.2 = (bf16[1,128,2048]{2,1,0:T(8,128)(2,1)S(1)}, bf16[1,128,2048]{2,1,0:T(8,128)(2,1)}, u32[]{:S(2)}) copy-start(bf16[1,128,2048]{2,1,0:T(8,128)(2,1)} %param.7) | copy-start | bytes 1572868
  11.5 4.4 %copy-start = (bf16[1,128,1024]{2,1,0:T(8,128)(2,1)S(1)}, bf16[1,128,1024]{2,1,0:T(8,128)(2,1)}, u32[]{:S(2)}) copy-start(bf16[1,128,1024]{2,1,0:T(8,128)(2,1)} %param.8) | copy-start | bytes 786436
  11.5 4.3 %copy-start.1 = (bf16[1,128,1024]{2,1,0:T(8,128)(2,1)S(1)}, bf16[1,128,1024]{2,1,0:T(8,128)(2,1)}, u32[]{:S(2)}) copy-start(bf16[1,128,1024]{2,1,0:T(8,128)(2,1)} %param.9) | copy-start | bytes 786436
  12.3 9.6 %collective-permute-start.1 = (bf16[128,1024]{1,0:T(8,128)(2,1)}, bf16[128,1024]{1,0:T(8,128)(2,1)S(1)}, u32[]{:S(2)}, u32[]{:S(2)}) collective-permute-start(bf16[128,1024]{1,0:T(8,128)(2,1)} %bitcast_select_fusion), channel_id=1, source_target_pairs={{0,1},{1,0},{2,3},{3,2},{4,5},{5,4},{6,7},{7,6},{8,9},{9,8},{10,11... | collective-permute-start | bytes 786440 | tf_op jit(solution)/shard_map/ppermute | solution.py:253
  18.4 8.3 %collective-permute-start.4 = (bf16[256,512]{1,0:T(8,128)(2,1)}, bf16[256,512]{1,0:T(8,128)(2,1)S(1)}, u32[]{:S(2)}, u32[]{:S(2)}) collective-permute-start(bf16[256,512]{1,0:T(8,128)(2,1)} %get-tuple-element.30), channel_id=1, source_target_pairs={{0,1},{1,0},{2,3},{3,2},{4,5},{5,4},{6,7},{7,6},{8,9},{9,8},{10,11... | collective-permute-start | bytes 786440 | tf_op jit(solution)/shard_map/ppermute | solution.py:289
  21.9 3.8 %copy-start.4 = (bf16[1,4,2,168,128]{4,3,2,1,0:T(8,128)(2,1)S(1)}, bf16[1,4,2,168,128]{4,3,2,1,0:T(8,128)(2,1)}, u32[]{:S(2)}) copy-start(bf16[1,4,2,168,128]{4,3,2,1,0:T(8,128)(2,1)} %get-tuple-element.55) | copy-start | bytes 1032196
  21.9 4.9 %collective-permute-start.3 = (bf16[2,672,128]{2,1,0:T(8,128)(2,1)S(1)}, bf16[2,672,128]{2,1,0:T(8,128)(2,1)S(1)}, u32[]{:S(2)}, u32[]{:S(2)}) collective-permute-start(bf16[2,672,128]{2,1,0:T(8,128)(2,1)S(1)} %bitcast.59), channel_id=1, source_target_pairs={{0,2},{2,0},{4,6},{6,4},{8,10},{10,8},{12,14},{14,12},{16,18},{18,... | collective-permute-start | bytes 1032200 | tf_op jit(solution)/shard_map/ppermute | solution.py:219
  23.9 8.8 %collective-permute-start.10 = (bf16[256,512]{1,0:T(8,128)(2,1)S(1)}, bf16[256,512]{1,0:T(8,128)(2,1)S(1)}, u32[]{:S(2)}, u32[]{:S(2)}) collective-permute-start(bf16[256,512]{1,0:T(8,128)(2,1)S(1)} %get-tuple-element.41), channel_id=1, source_target_pairs={{0,1},{1,0},{2,3},{3,2},{4,5},{5,4},{6,7},{7,6},{8,9},{9,8},{10,11... | collective-permute-start | bytes 786440 | tf_op jit(solution)/shard_map/ppermute | solution.py:289
  26.9 16.8 %collective-permute-start.7 = (bf16[256,512]{1,0:T(8,128)(2,1)S(1)}, bf16[256,512]{1,0:T(8,128)(2,1)S(1)}, u32[]{:S(2)}, u32[]{:S(2)}) collective-permute-start(bf16[256,512]{1,0:T(8,128)(2,1)S(1)} %pad_maximum_fusion.3.refs_0_), channel_id=1, source_target_pairs={{0,4},{2,6},{4,0},{6,2},{8,12},{10,14},{12,8},{14,10},{16,20},{18,... | collective-permute-start | bytes 786440 | tf_op jit(solution)/shard_map/ppermute | solution.py:219
  32.8 10.9 %collective-permute-start.11 = (bf16[256,512]{1,0:T(8,128)(2,1)S(1)}, bf16[256,512]{1,0:T(8,128)(2,1)S(1)}, u32[]{:S(2)}, u32[]{:S(2)}) collective-permute-start(bf16[256,512]{1,0:T(8,128)(2,1)S(1)} %pad_maximum_fusion.4.refs_0_), channel_id=1, source_target_pairs={{0,4},{2,6},{4,0},{6,2},{8,12},{10,14},{12,8},{14,10},{16,20},{18,... | collective-permute-start | bytes 786440 | tf_op jit(solution)/shard_map/ppermute | solution.py:219
  34.3 7.6 %collective-permute-start.6 = (bf16[3,336,128]{2,1,0:T(8,128)(2,1)S(1)}, bf16[3,336,128]{2,1,0:T(8,128)(2,1)S(1)}, u32[]{:S(2)}, u32[]{:S(2)}) collective-permute-start(bf16[3,336,128]{2,1,0:T(8,128)(2,1)S(1)} %get-tuple-element.39), channel_id=1, source_target_pairs={{0,1},{1,0},{2,3},{3,2},{4,5},{5,4},{6,7},{7,6},{8,9},{9,8},{10,11... | collective-permute-start | bytes 774152 | tf_op jit(solution)/shard_map/ppermute | solution.py:304
  36.1 8.2 %collective-permute-start.8 = (bf16[256,512]{1,0:T(8,128)(2,1)S(1)}, bf16[256,512]{1,0:T(8,128)(2,1)S(1)}, u32[]{:S(2)}, u32[]{:S(2)}) collective-permute-start(bf16[256,512]{1,0:T(8,128)(2,1)S(1)} %pad_maximum_fusion.3.refs_0_), channel_id=1, source_target_pairs={{0,2},{2,0},{4,6},{6,4},{8,10},{10,8},{12,14},{14,12},{16,18},{18,... | collective-permute-start | bytes 786440 | tf_op jit(solution)/shard_map/ppermute | solution.py:219
  36.1 12.1 %collective-permute-start.12 = (bf16[256,512]{1,0:T(8,128)(2,1)S(1)}, bf16[256,512]{1,0:T(8,128)(2,1)S(1)}, u32[]{:S(2)}, u32[]{:S(2)}) collective-permute-start(bf16[256,512]{1,0:T(8,128)(2,1)S(1)} %pad_maximum_fusion.4.refs_0_), channel_id=1, source_target_pairs={{0,2},{2,0},{4,6},{6,4},{8,10},{10,8},{12,14},{14,12},{16,18},{18,... | collective-permute-start | bytes 786440 | tf_op jit(solution)/shard_map/ppermute | solution.py:219
  41.9 7.3 %collective-permute-start.5 = (bf16[3,336,128]{2,1,0:T(8,128)(2,1)S(1)}, bf16[3,336,128]{2,1,0:T(8,128)(2,1)S(1)}, u32[]{:S(2)}, u32[]{:S(2)}) collective-permute-start(bf16[3,336,128]{2,1,0:T(8,128)(2,1)S(1)} %get-tuple-element.38), channel_id=1, source_target_pairs={{0,1},{1,0},{2,3},{3,2},{4,5},{5,4},{6,7},{7,6},{8,9},{9,8},{10,11... | collective-permute-start | bytes 774152 | tf_op jit(solution)/shard_map/ppermute | solution.py:304
  43.6 1.5 %collective-permute-start.9 = (bf16[256,512]{1,0:T(8,128)(2,1)S(1)}, bf16[256,512]{1,0:T(8,128)(2,1)S(1)}, u32[]{:S(2)}, u32[]{:S(2)}) collective-permute-start(bf16[256,512]{1,0:T(8,128)(2,1)S(1)} %collective-permute-done.7.refs_1_), channel_id=1, source_target_pairs={{0,2},{2,0},{4,6},{6,4},{8,10},{10,8},{12,14},{14,12},{16,18},{18,... | collective-permute-start | bytes 786440 | tf_op jit(solution)/shard_map/ppermute | solution.py:219
  43.7 4.5 %collective-permute-start.13 = (bf16[256,512]{1,0:T(8,128)(2,1)S(1)}, bf16[256,512]{1,0:T(8,128)(2,1)S(1)}, u32[]{:S(2)}, u32[]{:S(2)}) collective-permute-start(bf16[256,512]{1,0:T(8,128)(2,1)S(1)} %collective-permute-done.11.refs_1_), channel_id=1, source_target_pairs={{0,2},{2,0},{4,6},{6,4},{8,10},{10,8},{12,14},{14,12},{16,18},{18,... | collective-permute-start | bytes 786440 | tf_op jit(solution)/shard_map/ppermute | solution.py:219
  45.7 11.0 %collective-permute-start.14 = (bf16[336,512]{1,0:T(8,128)(2,1)S(1)}, bf16[336,512]{1,0:T(8,128)(2,1)S(1)}, u32[]{:S(2)}, u32[]{:S(2)}) collective-permute-start(bf16[336,512]{1,0:T(8,128)(2,1)S(1)} %shard_map.95), channel_id=1, source_target_pairs={{0,8},{2,10},{4,12},{6,14},{8,0},{10,2},{12,4},{14,6},{16,24},{18,... | collective-permute-start | bytes 1032200 | tf_op jit(solution)/shard_map/ppermute | solution.py:219
  48.7 18.3 %collective-permute-start.17 = (bf16[336,512]{1,0:T(8,128)(2,1)S(1)}, bf16[336,512]{1,0:T(8,128)(2,1)S(1)}, u32[]{:S(2)}, u32[]{:S(2)}) collective-permute-start(bf16[336,512]{1,0:T(8,128)(2,1)S(1)} %shard_map.96), channel_id=1, source_target_pairs={{0,8},{2,10},{4,12},{6,14},{8,0},{10,2},{12,4},{14,6},{16,24},{18,... | collective-permute-start | bytes 1032200 | tf_op jit(solution)/shard_map/ppermute | solution.py:219
  56.8 12.0 %collective-permute-start.16 = (bf16[168,512]{1,0:T(8,128)(2,1)S(1)}, bf16[168,512]{1,0:T(8,128)(2,1)S(1)}, u32[]{:S(2)}, u32[]{:S(2)}) collective-permute-start(bf16[168,512]{1,0:T(8,128)(2,1)S(1)} %slice.112), channel_id=1, source_target_pairs={{0,16},{2,18},{4,20},{6,22},{8,24},{10,26},{12,28},{14,30},{16,0},... | collective-permute-start | bytes 516104 | tf_op jit(solution)/shard_map/ppermute | solution.py:219
  59.5 18.8 %collective-permute-start.15 = (bf16[128,1024]{1,0:T(8,128)(2,1)S(1)}, bf16[128,1024]{1,0:T(8,128)(2,1)S(1)}, u32[]{:S(2)}, u32[]{:S(2)}) collective-permute-start(bf16[128,1024]{1,0:T(8,128)(2,1)S(1)} %pad_maximum_fusion.5), channel_id=1, source_target_pairs={{1,0},{3,2},{5,4},{7,6},{9,8},{11,10},{13,12},{15,14},{17,16},{19,... | collective-permute-start | bytes 786440 | tf_op jit(solution)/shard_map/ppermute | solution.py:357
  67.1 10.2 %collective-permute-start.18 = (bf16[168,512]{1,0:T(8,128)(2,1)S(1)}, bf16[168,512]{1,0:T(8,128)(2,1)S(1)}, u32[]{:S(2)}, u32[]{:S(2)}) collective-permute-start(bf16[168,512]{1,0:T(8,128)(2,1)S(1)} %slice.111), channel_id=1, source_target_pairs={{0,16},{2,18},{4,20},{6,22},{8,24},{10,26},{12,28},{14,30},{16,0},... | collective-permute-start | bytes 516104 | tf_op jit(solution)/shard_map/ppermute | solution.py:219

commit v9 on v8

--- a/solution.py
+++ b/solution.py
@@ -178,7 +178,7 @@
             in_specs=[
                 of_half(own),
                 pl.BlockSpec((traces, rows, tok), lambda i, *_: (0, half, 0)),
-                whole(others_away),
+                pl.BlockSpec((traces, rows, tok), lambda i, *_: (0, half, 0)),
             ]
             + [whole(piece) for piece in grads]
             + [(whole if len(own_away) > 1 else of_half)(piece) for piece in own_away],
@@ -254,8 +254,6 @@
         else:
             rim_pairs.append([shifted(pair, "ctx", step) for step in steps])
 
-    half_rows = slow_count // 2 * rows
-    low_high = [(0, half_rows), (half_rows, 2 * half_rows)]
 
     mids = jnp.stack(mids)
     sent_core = share_of(mids, 1 - core_at)
@@ -284,7 +282,7 @@
     others = jnp.concatenate([kept_core[1:], other_core])
 
     if ctx_count == 2:
-        columns, held_back, others_away = [], [], []
+        columns, held_back = [], []
         for chunk, (_, sent, addend, key_own, value_own, _) in enumerate(attended):
             arrived = lax.ppermute(sent, "ctx", swap_ctx)
             held_back.append(arrived)
@@ -299,9 +297,8 @@
                 [jnp.where(first, total, value_own), jnp.where(first, arrived[tok:], total)], axis=0
             )
             if chunk == 0:
-                for low, high in low_high:
-                    rest, block = lax.optimization_barrier((others[:, low:high], block))
-                    others_away.append(lax.ppermute(rest, "ctx", swap_ctx))
+                rest, block = lax.optimization_barrier((others, block))
+                others_away = lax.ppermute(rest, "ctx", swap_ctx)
             columns.append(block)
         own_away = [rim_pairs[-1][0], *held_back]
         key_grad = jnp.where(
@@ -331,18 +328,18 @@
         every = jnp.concatenate([own_piece[None], others])
         near, away = jnp.split(lax.all_gather(every, "ctx", axis=2, tiled=True), 2, axis=2)
         own_piece, others, own_away = near[0], near[1:], [away[0]]
-        others_away = [away[1:, low:high] for low, high in low_high]
+        others_away = away[1:]
 
     gathered = []
     for block in columns:
         near = [block] + [dp_send(block, mid_by(step)) for step in range(1, mid_count)]
         gathered.append(near + [dp_send(near_one, swap_core) for near_one in near])
     def together(half, dtype):
-        ends = (place_arg, own_piece, others, own_away, others_away[half])
+        ends = (place_arg, own_piece, others, own_away, others_away)
         return [product(half, *ends, grads, dtype) for grads in gathered]
 
     sent = together(0, jnp.bfloat16)
-    others_away[1], _ = lax.optimization_barrier((others_away[1], sent))
+    others_away, _ = lax.optimization_barrier((others_away, sent))
     kept = together(1, jnp.float32)
     halves = [
         near + dp_send(far, flip_slow(1)).astype(jnp.float32) for near, far in zip(kept, sent)

time: 79.3 us -> 77 us (0.971)
  starting transfers between devices: 26 us -> 23.2 us
    ppermute x12, waiting for transfers between devices: 21.2 us -> 25.6 us  [dp_send(): return lax.ppermute(value, 'dp', pairs)]
    ppermute x2 -> x1, waiting for transfers between devices: 5.36 us -> 2.71 us  [local(): others_away = lax.ppermute(rest, 'ctx', swap_ctx)]
    ppermute x2 -> x1, starting transfers between devices: 3.44 us -> 1.57 us  [local(): others_away = lax.ppermute(rest, 'ctx', swap_ctx)]
    ppermute x2, waiting for transfers between devices: 4.24 us -> 3.03 us  [local(): arrived = lax.ppermute(sent, 'ctx', swap_ctx)]
    ppermute x12, starting transfers between devices: 12.2 us -> 11.3 us  [dp_send(): return lax.ppermute(value, 'dp', pairs)]
  transfers between devices with their start and end apart: 19 -> 18, of which waited for: 7 -> 8; matrix products, arithmetic and copies ran while one was open for 10% -> 10% of each run, Pallas kernels for 8% -> 9%
where the time goes in v9:
time: 77 us; the launch traced here: 76.8 us
  waiting for transfers between devices  35 us (45%)
  starting transfers between devices  23.2 us (30%)
  other arithmetic  8.05 us (10%)
  Pallas kernels  6.67 us (9%)
  local copies, waits for them, and re-layouts  2.84 us (4%)
  between operations  1.05 us (1%)
    ppermute x12, waiting for transfers between devices, dp_send(): return lax.ppermute(value, 'dp', pairs)  25.6 us
    ppermute x12, starting transfers between devices, dp_send(): return lax.ppermute(value, 'dp', pairs)  11.3 us
    ppermute x1, starting transfers between devices, shifted(): lax.ppermute(value, axis, [(source, source + steps) for source in range(l...  4.88 us
    pallas_call x2, Pallas kernels, attend(): pl.pallas_call(partial(attention_kernel, chunk, hops, group), grid_spec=p...  4.51 us
    ppermute x2, starting transfers between devices, local(): arrived = lax.ppermute(sent, 'ctx', swap_ctx)  4.21 us
    ppermute x1, waiting for transfers between devices, shifted(): lax.ppermute(value, axis, [(source, source + steps) for source in range(l...  3.6 us
    ppermute x2, waiting for transfers between devices, local(): arrived = lax.ppermute(sent, 'ctx', swap_ctx)  3.03 us
    ppermute x1, waiting for transfers between devices, local(): others_away = lax.ppermute(rest, 'ctx', swap_ctx)  2.71 us
  transfers between devices with their start and end apart: 18, of which 8 were waited for; matrix products, arithmetic and copies ran while one was open for 10% of the time, Pallas kernels for 9%

profile of v9, /device:TPU:0, one launch (start us, length us, event | category | flops | bytes accessed | tf_op | source)
XLA Modules:
  0.0 76.8 jit_solution(18163879028475755967)
XLA Ops:
  0.6 0.7 convert_bitcast_fusion
  1.3 1.2 %fusion.5 = (bf16[128,512]{1,0:T(8,128)(2,1)S(1)}, bf16[128,512]{1,0:T(8,128)(2,1)S(1)}, bf16[128,512]{1,0:T(8,128)(2,1)S(1)}, bf16[128,512]{1,0:T(8,128)(2,1)S(1)}) fusion(bf16[128,1024]{1,0:T(8,128)(2,1)} %bitcast.41, bf16[128,1024]{1,0:T(8,128)(2,1)} %bitcast.44), kind=kLoop, calls=%fused_computation.41 | loop fusion | bytes 1048576 | tf_op jit(solution)/shard_map/slice | solution.py:247
  2.5 0.7 fusion.2
  3.2 4.9 %collective-permute-start = (bf16[144,1024]{1,0:T(8,128)(2,1)}, bf16[144,1024]{1,0:T(8,128)(2,1)S(1)}, u32[]{:S(2)}, u32[]{:S(2)}) collective-permute-start(bf16[144,1024]{1,0:T(8,128)(2,1)} %fusion.2), channel_id=1, source_target_pairs={{0,1},{2,3},{4,5},{6,7},{8,9},{10,11},{12,13},{14,15},{16,17},{18,... | collective-permute-start | bytes 884744 | tf_op jit(solution)/shard_map/ppermute | solution.py:29
  8.8 0.9 %dynamic-slice_bitcast_fusion = (bf16[4,2,168,128]{3,2,1,0:T(8,128)(2,1)}, bf16[1,4,2,168,128]{4,3,2,1,0:T(8,128)(2,1)}) fusion(bf16[4,2,2,168,128]{4,3,2,1,0:T(8,128)(2,1)S(1)} %pad_maximum_fusion, s32[]{:T(128)S(6)} %select_n.116, s32[]{:T(128)S(6)} %select_n.108), kind=kLoop, calls=%fused_computation.18 | loop fusion | bytes 1376264 | tf_op jit(solution)/shard_map/jit(dynamic_index_in_dim)/squeeze | solution.py:233
  9.7 1.5 %collective-permute-start.2 = (bf16[4,2,168,128]{3,2,1,0:T(8,128)(2,1)}, bf16[4,2,168,128]{3,2,1,0:T(8,128)(2,1)}, u32[]{:S(2)}, u32[]{:S(2)}) collective-permute-start(bf16[4,2,168,128]{3,2,1,0:T(8,128)(2,1)} %get-tuple-element.50), channel_id=1, source_target_pairs={{0,4},{2,6},{4,0},{6,2},{8,12},{10,14},{12,8},{14,10},{16,20},{18,... | collective-permute-start | bytes 1032200 | tf_op jit(solution)/shard_map/ppermute | solution.py:219
  11.5 0.8 bitcast_select_fusion
  12.2 3.6 %collective-permute-done.refs_5_.refs_6_ = bf16[144,1024]{1,0:T(8,128)(2,1)S(1)} collective-permute-done((bf16[144,1024]{1,0:T(8,128)(2,1)}, bf16[144,1024]{1,0:T(8,128)(2,1)S(1)}, u32[]{:S(2)}, u32[]{:S(2)}) %collective-permute-start) | collective-permute-done | bytes 294944 | tf_op jit(solution)/shard_map/ppermute | solution.py:29
  15.8 2.6 %shard_map.93 = (bf16[128,1024]{1,0:T(8,128)(2,1)S(1)}, bf16[256,512]{1,0:T(8,128)(2,1)}, bf16[128,512]{1,0:T(8,128)(2,1)S(1)}, bf16[128,512]{1,0:T(8,128)(2,1)S...) custom-call(s32[1]{0:T(128)} %bitcast.place_ref, bf16[16,128]{1,0:T(8,128)(2,1)S(1)} %broadcast_in_dim.15.refs_0_, ...), custom_call_target="tpu_custom_call" | custom-call | flops 1024 | bytes 1024 | tf_op jit(solution)/shard_map/pallas_call | solution.py:122
  18.4 2.4 %collective-permute-start.4 = (bf16[256,512]{1,0:T(8,128)(2,1)}, bf16[256,512]{1,0:T(8,128)(2,1)S(1)}, u32[]{:S(2)}, u32[]{:S(2)}) collective-permute-start(bf16[256,512]{1,0:T(8,128)(2,1)} %get-tuple-element.28), channel_id=1, source_target_pairs={{0,1},{1,0},{2,3},{3,2},{4,5},{5,4},{6,7},{7,6},{8,9},{9,8},{10,11... | collective-permute-start | bytes 786440 | tf_op jit(solution)/shard_map/ppermute | solution.py:287
  20.8 1.0 %fusion.1 = bf16[2,4,1,168,128]{4,3,2,1,0:T(8,128)(2,1)S(1)} fusion(s32[]{:T(128)S(6)} %select_n.117, bf16[1,4,2,168,128]{4,3,2,1,0:T(8,128)(2,1)} %get-tuple-element.51, bf16[1,4,2,168,128]{4,3,2,1,0:T(8,128)(2,1)} %bitcast.16), kind=kLoop, calls=%fused_computation.13 | loop fusion | flops 172032 | bytes 1032196 | tf_op jit(solution)/shard_map/stack | solution.py:258
  22.0 1.9 %shard_map.94 = (bf16[128,1024]{1,0:T(8,128)(2,1)S(1)}, bf16[256,512]{1,0:T(8,128)(2,1)S(1)}, bf16[128,512]{1,0:T(8,128)(2,1)S(1)}, bf16[128,512]{1,0:T(8,128)(2...) custom-call(s32[1]{0:T(128)} %bitcast.place_ref, bf16[16,128]{1,0:T(8,128)(2,1)S(1)} %broadcast_in_dim.15.refs_0_, ...), custom_call_target="tpu_custom_call" | custom-call | flops 1024 | bytes 1024 | tf_op jit(solution)/shard_map/pallas_call | solution.py:122
  23.9 1.8 %collective-permute-start.9 = (bf16[256,512]{1,0:T(8,128)(2,1)S(1)}, bf16[256,512]{1,0:T(8,128)(2,1)S(1)}, u32[]{:S(2)}, u32[]{:S(2)}) collective-permute-start(bf16[256,512]{1,0:T(8,128)(2,1)S(1)} %get-tuple-element.37), channel_id=1, source_target_pairs={{0,1},{1,0},{2,3},{3,2},{4,5},{5,4},{6,7},{7,6},{8,9},{9,8},{10,11... | collective-permute-start | bytes 786440 | tf_op jit(solution)/shard_map/ppermute | solution.py:287
  25.7 1.0 %fusion.4 = bf16[1,4,1,168,128]{4,3,2,1,0:T(8,128)(2,1)S(1)} fusion(s32[]{:T(128)S(6)} %add.98, s32[]{:T(128)S(6)} %select_n.111, bf16[1,4,2,168,128]{4,3,2,1,0:T(8,128)(2,1)S(1)} %copy-done.4, bf16[1,4,2,168,128]{4,3,2,1,0:T(8,128)(2,1)} %bitcast.16), kind=kLoop, calls=%fused_computation.29 | loop fusion | flops 86016 | bytes 860168 | tf_op jit(solution)/shard_map/stack | solution.py:258
  26.9 1.6 %collective-permute-start.6 = (bf16[256,512]{1,0:T(8,128)(2,1)S(1)}, bf16[256,512]{1,0:T(8,128)(2,1)S(1)}, u32[]{:S(2)}, u32[]{:S(2)}) collective-permute-start(bf16[256,512]{1,0:T(8,128)(2,1)S(1)} %pad_maximum_fusion.3.refs_0_), channel_id=1, source_target_pairs={{0,4},{2,6},{4,0},{6,2},{8,12},{10,14},{12,8},{14,10},{16,20},{18,... | collective-permute-start | bytes 786440 | tf_op jit(solution)/shard_map/ppermute | solution.py:219
  28.4 1.6 %collective-permute-start.5 = (bf16[3,672,128]{2,1,0:T(8,128)(2,1)S(1)}, bf16[3,672,128]{2,1,0:T(8,128)(2,1)S(1)}, u32[]{:S(2)}, u32[]{:S(2)}) collective-permute-start(bf16[3,672,128]{2,1,0:T(8,128)(2,1)S(1)} %pad_maximum_fusion.2.others_ref), channel_id=1, source_target_pairs={{0,1},{1,0},{2,3},{3,2},{4,5},{5,4},{6,7},{7,6},{8,9},{9,8},{10,11... | collective-permute-start | bytes 1548296 | tf_op jit(solution)/shard_map/ppermute | solution.py:301
  30.0 3.0 %collective-permute-done.9.refs_6_ = bf16[256,512]{1,0:T(8,128)(2,1)S(1)} collective-permute-done((bf16[256,512]{1,0:T(8,128)(2,1)S(1)}, bf16[256,512]{1,0:T(8,128)(2,1)S(1)}, u32[]{:S(2)}, u32[]{:S(2)}) %collective-permute-start.9) | collective-permute-done | bytes 262176 | tf_op jit(solution)/shard_map/ppermute | solution.py:287
  33.1 1.6 %collective-permute-start.10 = (bf16[256,512]{1,0:T(8,128)(2,1)S(1)}, bf16[256,512]{1,0:T(8,128)(2,1)S(1)}, u32[]{:S(2)}, u32[]{:S(2)}) collective-permute-start(bf16[256,512]{1,0:T(8,128)(2,1)S(1)} %pad_maximum_fusion.4.refs_0_), channel_id=1, source_target_pairs={{0,4},{2,6},{4,0},{6,2},{8,12},{10,14},{12,8},{14,10},{16,20},{18,... | collective-permute-start | bytes 786440 | tf_op jit(solution)/shard_map/ppermute | solution.py:219
  34.7 0.8 %collective-permute-done.6.refs_1_ = bf16[256,512]{1,0:T(8,128)(2,1)S(1)} collective-permute-done((bf16[256,512]{1,0:T(8,128)(2,1)S(1)}, bf16[256,512]{1,0:T(8,128)(2,1)S(1)}, u32[]{:S(2)}, u32[]{:S(2)}) %collective-permute-start.6) | collective-permute-done | bytes 262176 | tf_op jit(solution)/shard_map/ppermute | solution.py:219
  36.0 5.0 %collective-permute-done.10.refs_1_ = bf16[256,512]{1,0:T(8,128)(2,1)S(1)} collective-permute-done((bf16[256,512]{1,0:T(8,128)(2,1)S(1)}, bf16[256,512]{1,0:T(8,128)(2,1)S(1)}, u32[]{:S(2)}, u32[]{:S(2)}) %collective-permute-start.10) | collective-permute-done | bytes 262176 | tf_op jit(solution)/shard_map/ppermute | solution.py:219
  41.0 2.7 %collective-permute-done.5.others_away_ref = bf16[3,672,128]{2,1,0:T(8,128)(2,1)S(1)} collective-permute-done((bf16[3,672,128]{2,1,0:T(8,128)(2,1)S(1)}, bf16[3,672,128]{2,1,0:T(8,128)(2,1)S(1)}, u32[]{:S(2)}, u32[]{:S(2)}) %collective-permute-start.5) | collective-permute-done | bytes 516128 | tf_op jit(solution)/shard_map/ppermute | solution.py:301
  44.3 1.6 %collective-permute-start.13 = (bf16[336,512]{1,0:T(8,128)(2,1)S(1)}, bf16[336,512]{1,0:T(8,128)(2,1)S(1)}, u32[]{:S(2)}, u32[]{:S(2)}) collective-permute-start(bf16[336,512]{1,0:T(8,128)(2,1)S(1)} %shard_map.95), channel_id=1, source_target_pairs={{0,8},{2,10},{4,12},{6,14},{8,0},{10,2},{12,4},{14,6},{16,24},{18,... | collective-permute-start | bytes 1032200 | tf_op jit(solution)/shard_map/ppermute | solution.py:219
  45.9 0.8 maximum_select_fusion
  48.9 0.8 %maximum_bitcast_fusion = bf16[1,128,2048]{2,1,0:T(8,128)(2,1)} fusion(bf16[128,1024]{1,0:T(8,128)(2,1)S(1)} %get-tuple-element.43, bf16[128,1024]{1,0:T(8,128)(2,1)S(1)} %get-tuple-element.42), kind=kLoop, calls=%fused_computation.10 | loop fusion | flops 1048576 | bytes 1048576 | tf_op jit(solution)/shard_map/broadcast_in_dim | solution.py:360
  49.7 5.6 %collective-permute-done.13 = bf16[336,512]{1,0:T(8,128)(2,1)S(1)} collective-permute-done((bf16[336,512]{1,0:T(8,128)(2,1)S(1)}, bf16[336,512]{1,0:T(8,128)(2,1)S(1)}, u32[]{:S(2)}, u32[]{:S(2)}) %collective-permute-start.13) | collective-permute-done | bytes 344096 | tf_op jit(solution)/shard_map/ppermute | solution.py:219
  55.5 2.7 %collective-permute-start.15 = (bf16[168,512]{1,0:T(8,128)(2,1)S(1)}, bf16[168,512]{1,0:T(8,128)(2,1)S(1)}, u32[]{:S(2)}, u32[]{:S(2)}) collective-permute-start(bf16[168,512]{1,0:T(8,128)(2,1)S(1)} %slice.88), channel_id=1, source_target_pairs={{0,16},{2,18},{4,20},{6,22},{8,24},{10,26},{12,28},{14,30},{16,0},... | collective-permute-start | bytes 516104 | tf_op jit(solution)/shard_map/ppermute | solution.py:219
  58.1 1.3 %collective-permute-start.14 = (bf16[128,1024]{1,0:T(8,128)(2,1)S(1)}, bf16[128,1024]{1,0:T(8,128)(2,1)S(1)}, u32[]{:S(2)}, u32[]{:S(2)}) collective-permute-start(bf16[128,1024]{1,0:T(8,128)(2,1)S(1)} %pad_maximum_fusion.5), channel_id=1, source_target_pairs={{1,0},{3,2},{5,4},{7,6},{9,8},{11,10},{13,12},{15,14},{17,16},{19,... | collective-permute-start | bytes 786440 | tf_op jit(solution)/shard_map/ppermute | solution.py:354
  59.4 5.7 %collective-permute-done.16 = bf16[336,512]{1,0:T(8,128)(2,1)S(1)} collective-permute-done((bf16[336,512]{1,0:T(8,128)(2,1)S(1)}, bf16[336,512]{1,0:T(8,128)(2,1)S(1)}, u32[]{:S(2)}, u32[]{:S(2)}) %collective-permute-start.16) | collective-permute-done | bytes 344096 | tf_op jit(solution)/shard_map/ppermute | solution.py:219
  65.3 1.3 %collective-permute-start.17 = (bf16[168,512]{1,0:T(8,128)(2,1)S(1)}, bf16[168,512]{1,0:T(8,128)(2,1)S(1)}, u32[]{:S(2)}, u32[]{:S(2)}) collective-permute-start(bf16[168,512]{1,0:T(8,128)(2,1)S(1)} %slice.87), channel_id=1, source_target_pairs={{0,16},{2,18},{4,20},{6,22},{8,24},{10,26},{12,28},{14,30},{16,0},... | collective-permute-start | bytes 516104 | tf_op jit(solution)/shard_map/ppermute | solution.py:219
  66.6 8.5 %collective-permute-done.17 = bf16[168,512]{1,0:T(8,128)(2,1)S(1)} collective-permute-done((bf16[168,512]{1,0:T(8,128)(2,1)S(1)}, bf16[168,512]{1,0:T(8,128)(2,1)S(1)}, u32[]{:S(2)}, u32[]{:S(2)}) %collective-permute-start.17) | collective-permute-done | bytes 172064 | tf_op jit(solution)/shard_map/ppermute | solution.py:219
  75.1 0.9 %pad_maximum_fusion.1 = f32[168,1024]{1,0:T(8,128)} fusion(f32[168,512]{1,0:T(8,128)S(1)} %slice_add_fusion, f32[168,512]{1,0:T(8,128)S(1)} %slice_add_fusion.1), kind=kLoop, calls=%fused_computation.5 | loop fusion | flops 172032 | bytes 1376256 | tf_op jit(solution)/shard_map/concatenate | solution.py:359
  76.0 0.8 %fusion.3 = bf16[1,128,1024]{2,1,0:T(8,128)(2,1)} fusion(bf16[128,1024]{1,0:T(8,128)(2,1)S(1)} %collective-permute-done.14, bf16[128,512]{1,0:T(8,128)(2,1)S(1)} %get-tuple-element.40, bf16[128,512]{1,0:T(8,128)(2,1)S(1)} %get-tuple-element.34), kind=kLoop, calls=%fused_computation.21 | loop fusion | flops 917504 | bytes 786432 | tf_op jit(solution)/shard_map/broadcast_in_dim | solution.py:360
  (53 shorter events, 4.6 us)
Async XLA Ops:
  1.3 6.9 %copy-start.5 = (bf16[1,128,2688]{2,1,0:T(8,128)(2,1)S(1)}, bf16[1,128,2688]{2,1,0:T(8,128)(2,1)}, u32[]{:S(2)}) copy-start(bf16[1,128,2688]{2,1,0:T(8,128)(2,1)} %param.6) | copy-start | bytes 2064388
  3.2 12.6 %collective-permute-start = (bf16[144,1024]{1,0:T(8,128)(2,1)}, bf16[144,1024]{1,0:T(8,128)(2,1)S(1)}, u32[]{:S(2)}, u32[]{:S(2)}) collective-permute-start(bf16[144,1024]{1,0:T(8,128)(2,1)} %fusion.2), channel_id=1, source_target_pairs={{0,1},{2,3},{4,5},{6,7},{8,9},{10,11},{12,13},{14,15},{16,17},{18,... | collective-permute-start | bytes 884744 | tf_op jit(solution)/shard_map/ppermute | solution.py:29
  9.7 11.1 %collective-permute-start.2 = (bf16[4,2,168,128]{3,2,1,0:T(8,128)(2,1)}, bf16[4,2,168,128]{3,2,1,0:T(8,128)(2,1)}, u32[]{:S(2)}, u32[]{:S(2)}) collective-permute-start(bf16[4,2,168,128]{3,2,1,0:T(8,128)(2,1)} %get-tuple-element.50), channel_id=1, source_target_pairs={{0,4},{2,6},{4,0},{6,2},{8,12},{10,14},{12,8},{14,10},{16,20},{18,... | collective-permute-start | bytes 1032200 | tf_op jit(solution)/shard_map/ppermute | solution.py:219
  11.2 4.6 %copy-start.3 = (bf16[1,128,2048]{2,1,0:T(8,128)(2,1)S(1)}, bf16[1,128,2048]{2,1,0:T(8,128)(2,1)}, u32[]{:S(2)}) copy-start(bf16[1,128,2048]{2,1,0:T(8,128)(2,1)} %param.10) | copy-start | bytes 1572868
  11.2 4.6 %copy-start.2 = (bf16[1,128,2048]{2,1,0:T(8,128)(2,1)S(1)}, bf16[1,128,2048]{2,1,0:T(8,128)(2,1)}, u32[]{:S(2)}) copy-start(bf16[1,128,2048]{2,1,0:T(8,128)(2,1)} %param.7) | copy-start | bytes 1572868
  11.4 4.4 %copy-start = (bf16[1,128,1024]{2,1,0:T(8,128)(2,1)S(1)}, bf16[1,128,1024]{2,1,0:T(8,128)(2,1)}, u32[]{:S(2)}) copy-start(bf16[1,128,1024]{2,1,0:T(8,128)(2,1)} %param.8) | copy-start | bytes 786436
  11.4 4.4 %copy-start.1 = (bf16[1,128,1024]{2,1,0:T(8,128)(2,1)S(1)}, bf16[1,128,1024]{2,1,0:T(8,128)(2,1)}, u32[]{:S(2)}) copy-start(bf16[1,128,1024]{2,1,0:T(8,128)(2,1)} %param.9) | copy-start | bytes 786436
  12.2 9.6 %collective-permute-start.1 = (bf16[128,1024]{1,0:T(8,128)(2,1)}, bf16[128,1024]{1,0:T(8,128)(2,1)S(1)}, u32[]{:S(2)}, u32[]{:S(2)}) collective-permute-start(bf16[128,1024]{1,0:T(8,128)(2,1)} %bitcast_select_fusion), channel_id=1, source_target_pairs={{0,1},{1,0},{2,3},{3,2},{4,5},{5,4},{6,7},{7,6},{8,9},{9,8},{10,11... | collective-permute-start | bytes 786440 | tf_op jit(solution)/shard_map/ppermute | solution.py:253
  18.4 8.3 %collective-permute-start.4 = (bf16[256,512]{1,0:T(8,128)(2,1)}, bf16[256,512]{1,0:T(8,128)(2,1)S(1)}, u32[]{:S(2)}, u32[]{:S(2)}) collective-permute-start(bf16[256,512]{1,0:T(8,128)(2,1)} %get-tuple-element.28), channel_id=1, source_target_pairs={{0,1},{1,0},{2,3},{3,2},{4,5},{5,4},{6,7},{7,6},{8,9},{9,8},{10,11... | collective-permute-start | bytes 786440 | tf_op jit(solution)/shard_map/ppermute | solution.py:287
  21.9 3.8 %copy-start.4 = (bf16[1,4,2,168,128]{4,3,2,1,0:T(8,128)(2,1)S(1)}, bf16[1,4,2,168,128]{4,3,2,1,0:T(8,128)(2,1)}, u32[]{:S(2)}) copy-start(bf16[1,4,2,168,128]{4,3,2,1,0:T(8,128)(2,1)} %get-tuple-element.51) | copy-start | bytes 1032196
  21.9 4.9 %collective-permute-start.3 = (bf16[2,672,128]{2,1,0:T(8,128)(2,1)S(1)}, bf16[2,672,128]{2,1,0:T(8,128)(2,1)S(1)}, u32[]{:S(2)}, u32[]{:S(2)}) collective-permute-start(bf16[2,672,128]{2,1,0:T(8,128)(2,1)S(1)} %bitcast.58), channel_id=1, source_target_pairs={{0,2},{2,0},{4,6},{6,4},{8,10},{10,8},{12,14},{14,12},{16,18},{18,... | collective-permute-start | bytes 1032200 | tf_op jit(solution)/shard_map/ppermute | solution.py:219
  23.9 9.2 %collective-permute-start.9 = (bf16[256,512]{1,0:T(8,128)(2,1)S(1)}, bf16[256,512]{1,0:T(8,128)(2,1)S(1)}, u32[]{:S(2)}, u32[]{:S(2)}) collective-permute-start(bf16[256,512]{1,0:T(8,128)(2,1)S(1)} %get-tuple-element.37), channel_id=1, source_target_pairs={{0,1},{1,0},{2,3},{3,2},{4,5},{5,4},{6,7},{7,6},{8,9},{9,8},{10,11... | collective-permute-start | bytes 786440 | tf_op jit(solution)/shard_map/ppermute | solution.py:287
  26.9 8.6 %collective-permute-start.6 = (bf16[256,512]{1,0:T(8,128)(2,1)S(1)}, bf16[256,512]{1,0:T(8,128)(2,1)S(1)}, u32[]{:S(2)}, u32[]{:S(2)}) collective-permute-start(bf16[256,512]{1,0:T(8,128)(2,1)S(1)} %pad_maximum_fusion.3.refs_0_), channel_id=1, source_target_pairs={{0,4},{2,6},{4,0},{6,2},{8,12},{10,14},{12,8},{14,10},{16,20},{18,... | collective-permute-start | bytes 786440 | tf_op jit(solution)/shard_map/ppermute | solution.py:219
  28.4 15.3 %collective-permute-start.5 = (bf16[3,672,128]{2,1,0:T(8,128)(2,1)S(1)}, bf16[3,672,128]{2,1,0:T(8,128)(2,1)S(1)}, u32[]{:S(2)}, u32[]{:S(2)}) collective-permute-start(bf16[3,672,128]{2,1,0:T(8,128)(2,1)S(1)} %pad_maximum_fusion.2.others_ref), channel_id=1, source_target_pairs={{0,1},{1,0},{2,3},{3,2},{4,5},{5,4},{6,7},{7,6},{8,9},{9,8},{10,11... | collective-permute-start | bytes 1548296 | tf_op jit(solution)/shard_map/ppermute | solution.py:301
  33.1 7.9 %collective-permute-start.10 = (bf16[256,512]{1,0:T(8,128)(2,1)S(1)}, bf16[256,512]{1,0:T(8,128)(2,1)S(1)}, u32[]{:S(2)}, u32[]{:S(2)}) collective-permute-start(bf16[256,512]{1,0:T(8,128)(2,1)S(1)} %pad_maximum_fusion.4.refs_0_), channel_id=1, source_target_pairs={{0,4},{2,6},{4,0},{6,2},{8,12},{10,14},{12,8},{14,10},{16,20},{18,... | collective-permute-start | bytes 786440 | tf_op jit(solution)/shard_map/ppermute | solution.py:219
  34.7 6.3 %collective-permute-start.7 = (bf16[256,512]{1,0:T(8,128)(2,1)S(1)}, bf16[256,512]{1,0:T(8,128)(2,1)S(1)}, u32[]{:S(2)}, u32[]{:S(2)}) collective-permute-start(bf16[256,512]{1,0:T(8,128)(2,1)S(1)} %pad_maximum_fusion.3.refs_0_), channel_id=1, source_target_pairs={{0,2},{2,0},{4,6},{6,4},{8,10},{10,8},{12,14},{14,12},{16,18},{18,... | collective-permute-start | bytes 786440 | tf_op jit(solution)/shard_map/ppermute | solution.py:219
  35.5 8.2 %collective-permute-start.8 = (bf16[256,512]{1,0:T(8,128)(2,1)S(1)}, bf16[256,512]{1,0:T(8,128)(2,1)S(1)}, u32[]{:S(2)}, u32[]{:S(2)}) collective-permute-start(bf16[256,512]{1,0:T(8,128)(2,1)S(1)} %collective-permute-done.6.refs_1_), channel_id=1, source_target_pairs={{0,2},{2,0},{4,6},{6,4},{8,10},{10,8},{12,14},{14,12},{16,18},{18,... | collective-permute-start | bytes 786440 | tf_op jit(solution)/shard_map/ppermute | solution.py:219
  35.5 11.2 %collective-permute-start.11 = (bf16[256,512]{1,0:T(8,128)(2,1)S(1)}, bf16[256,512]{1,0:T(8,128)(2,1)S(1)}, u32[]{:S(2)}, u32[]{:S(2)}) collective-permute-start(bf16[256,512]{1,0:T(8,128)(2,1)S(1)} %pad_maximum_fusion.4.refs_0_), channel_id=1, source_target_pairs={{0,2},{2,0},{4,6},{6,4},{8,10},{10,8},{12,14},{14,12},{16,18},{18,... | collective-permute-start | bytes 786440 | tf_op jit(solution)/shard_map/ppermute | solution.py:219
  41.0 5.7 %collective-permute-start.12 = (bf16[256,512]{1,0:T(8,128)(2,1)S(1)}, bf16[256,512]{1,0:T(8,128)(2,1)S(1)}, u32[]{:S(2)}, u32[]{:S(2)}) collective-permute-start(bf16[256,512]{1,0:T(8,128)(2,1)S(1)} %collective-permute-done.10.refs_1_), channel_id=1, source_target_pairs={{0,2},{2,0},{4,6},{6,4},{8,10},{10,8},{12,14},{14,12},{16,18},{18,... | collective-permute-start | bytes 786440 | tf_op jit(solution)/shard_map/ppermute | solution.py:219
  44.3 11.0 %collective-permute-start.13 = (bf16[336,512]{1,0:T(8,128)(2,1)S(1)}, bf16[336,512]{1,0:T(8,128)(2,1)S(1)}, u32[]{:S(2)}, u32[]{:S(2)}) collective-permute-start(bf16[336,512]{1,0:T(8,128)(2,1)S(1)} %shard_map.95), channel_id=1, source_target_pairs={{0,8},{2,10},{4,12},{6,14},{8,0},{10,2},{12,4},{14,6},{16,24},{18,... | collective-permute-start | bytes 1032200 | tf_op jit(solution)/shard_map/ppermute | solution.py:219
  47.3 17.9 %collective-permute-start.16 = (bf16[336,512]{1,0:T(8,128)(2,1)S(1)}, bf16[336,512]{1,0:T(8,128)(2,1)S(1)}, u32[]{:S(2)}, u32[]{:S(2)}) collective-permute-start(bf16[336,512]{1,0:T(8,128)(2,1)S(1)} %shard_map.96), channel_id=1, source_target_pairs={{0,8},{2,10},{4,12},{6,14},{8,0},{10,2},{12,4},{14,6},{16,24},{18,... | collective-permute-start | bytes 1032200 | tf_op jit(solution)/shard_map/ppermute | solution.py:219
  55.5 11.1 %collective-permute-start.15 = (bf16[168,512]{1,0:T(8,128)(2,1)S(1)}, bf16[168,512]{1,0:T(8,128)(2,1)S(1)}, u32[]{:S(2)}, u32[]{:S(2)}) collective-permute-start(bf16[168,512]{1,0:T(8,128)(2,1)S(1)} %slice.88), channel_id=1, source_target_pairs={{0,16},{2,18},{4,20},{6,22},{8,24},{10,26},{12,28},{14,30},{16,0},... | collective-permute-start | bytes 516104 | tf_op jit(solution)/shard_map/ppermute | solution.py:219
  58.1 17.9 %collective-permute-start.14 = (bf16[128,1024]{1,0:T(8,128)(2,1)S(1)}, bf16[128,1024]{1,0:T(8,128)(2,1)S(1)}, u32[]{:S(2)}, u32[]{:S(2)}) collective-permute-start(bf16[128,1024]{1,0:T(8,128)(2,1)S(1)} %pad_maximum_fusion.5), channel_id=1, source_target_pairs={{1,0},{3,2},{5,4},{7,6},{9,8},{11,10},{13,12},{15,14},{17,16},{19,... | collective-permute-start | bytes 786440 | tf_op jit(solution)/shard_map/ppermute | solution.py:354
  65.3 9.8 %collective-permute-start.17 = (bf16[168,512]{1,0:T(8,128)(2,1)S(1)}, bf16[168,512]{1,0:T(8,128)(2,1)S(1)}, u32[]{:S(2)}, u32[]{:S(2)}) collective-permute-start(bf16[168,512]{1,0:T(8,128)(2,1)S(1)} %slice.87), channel_id=1, source_target_pairs={{0,16},{2,18},{4,20},{6,22},{8,24},{10,26},{12,28},{14,30},{16,0},... | collective-permute-start | bytes 516104 | tf_op jit(solution)/shard_map/ppermute | solution.py:219

commit v10 on v9

--- a/solution.py
+++ b/solution.py
@@ -137,7 +137,7 @@
             out_specs=[whole(*shape) for shape in out_shapes],
         ),
         out_shape=[jax.ShapeDtypeStruct(shape, jnp.bfloat16) for shape in out_shapes],
-        compiler_params=pltpu.CompilerParams(vmem_limit_bytes=48 * MIB),
+        compiler_params=pltpu.CompilerParams(vmem_limit_bytes=24 * MIB),
         cost_estimate=SMALL,
     )(*operands)
 
@@ -185,7 +185,7 @@
             out_specs=pl.BlockSpec((rows, width), lambda i, *_: (0, 0)),
         ),
         out_shape=jax.ShapeDtypeStruct((rows, width), dtype),
-        compiler_params=pltpu.CompilerParams(vmem_limit_bytes=48 * MIB),
+        compiler_params=pltpu.CompilerParams(vmem_limit_bytes=20 * MIB),
         cost_estimate=SMALL,
     )(place, own, others, others_away, *grads, *own_away)
 

time: 77 us -> 77 us (level)
  no operation moved by 1% of the time
where the time goes in v10:
time: 77 us; the launch traced here: 76.8 us
  waiting for transfers between devices  35 us (45%)
  starting transfers between devices  23.2 us (30%)
  other arithmetic  8.06 us (10%)
  Pallas kernels  6.67 us (9%)
  local copies, waits for them, and re-layouts  2.84 us (4%)
  between operations  1.05 us (1%)
    ppermute x12, waiting for transfers between devices, dp_send(): return lax.ppermute(value, 'dp', pairs)  25.6 us
    ppermute x12, starting transfers between devices, dp_send(): return lax.ppermute(value, 'dp', pairs)  11.3 us
    ppermute x1, starting transfers between devices, shifted(): lax.ppermute(value, axis, [(source, source + steps) for source in range(l...  4.88 us
    pallas_call x2, Pallas kernels, attend(): pl.pallas_call(partial(attention_kernel, chunk, hops, group), grid_spec=p...  4.51 us
    ppermute x2, starting transfers between devices, local(): arrived = lax.ppermute(sent, 'ctx', swap_ctx)  4.21 us
    ppermute x1, waiting for transfers between devices, shifted(): lax.ppermute(value, axis, [(source, source + steps) for source in range(l...  3.6 us
    ppermute x2, waiting for transfers between devices, local(): arrived = lax.ppermute(sent, 'ctx', swap_ctx)  3.03 us
    ppermute x1, waiting for transfers between devices, local(): others_away = lax.ppermute(rest, 'ctx', swap_ctx)  2.71 us
  transfers between devices with their start and end apart: 18, of which 8 were waited for; matrix products, arithmetic and copies ran while one was open for 10% of the time, Pallas kernels for 9%

profile of v10, /device:TPU:0, one launch (start us, length us, event | category | flops | bytes accessed | tf_op | source)
XLA Modules:
  0.0 76.8 jit_solution(14644976918606026829)
XLA Ops:
  0.6 0.7 convert_bitcast_fusion
  1.3 1.2 %fusion.5 = (bf16[128,512]{1,0:T(8,128)(2,1)S(1)}, bf16[128,512]{1,0:T(8,128)(2,1)S(1)}, bf16[128,512]{1,0:T(8,128)(2,1)S(1)}, bf16[128,512]{1,0:T(8,128)(2,1)S(1)}) fusion(bf16[128,1024]{1,0:T(8,128)(2,1)} %bitcast.41, bf16[128,1024]{1,0:T(8,128)(2,1)} %bitcast.44), kind=kLoop, calls=%fused_computation.41 | loop fusion | bytes 1048576 | tf_op jit(solution)/shard_map/slice | solution.py:247
  2.5 0.7 fusion.2
  3.2 4.9 %collective-permute-start = (bf16[144,1024]{1,0:T(8,128)(2,1)}, bf16[144,1024]{1,0:T(8,128)(2,1)S(1)}, u32[]{:S(2)}, u32[]{:S(2)}) collective-permute-start(bf16[144,1024]{1,0:T(8,128)(2,1)} %fusion.2), channel_id=1, source_target_pairs={{0,1},{2,3},{4,5},{6,7},{8,9},{10,11},{12,13},{14,15},{16,17},{18,... | collective-permute-start | bytes 884744 | tf_op jit(solution)/shard_map/ppermute | solution.py:29
  8.8 0.9 %dynamic-slice_bitcast_fusion = (bf16[4,2,168,128]{3,2,1,0:T(8,128)(2,1)}, bf16[1,4,2,168,128]{4,3,2,1,0:T(8,128)(2,1)}) fusion(bf16[4,2,2,168,128]{4,3,2,1,0:T(8,128)(2,1)S(1)} %pad_maximum_fusion, s32[]{:T(128)S(6)} %select_n.116, s32[]{:T(128)S(6)} %select_n.108), kind=kLoop, calls=%fused_computation.18 | loop fusion | bytes 1376264 | tf_op jit(solution)/shard_map/jit(dynamic_index_in_dim)/squeeze | solution.py:233
  9.7 1.5 %collective-permute-start.2 = (bf16[4,2,168,128]{3,2,1,0:T(8,128)(2,1)}, bf16[4,2,168,128]{3,2,1,0:T(8,128)(2,1)}, u32[]{:S(2)}, u32[]{:S(2)}) collective-permute-start(bf16[4,2,168,128]{3,2,1,0:T(8,128)(2,1)} %get-tuple-element.50), channel_id=1, source_target_pairs={{0,4},{2,6},{4,0},{6,2},{8,12},{10,14},{12,8},{14,10},{16,20},{18,... | collective-permute-start | bytes 1032200 | tf_op jit(solution)/shard_map/ppermute | solution.py:219
  11.5 0.8 bitcast_select_fusion
  12.2 3.6 %collective-permute-done.refs_5_.refs_6_ = bf16[144,1024]{1,0:T(8,128)(2,1)S(1)} collective-permute-done((bf16[144,1024]{1,0:T(8,128)(2,1)}, bf16[144,1024]{1,0:T(8,128)(2,1)S(1)}, u32[]{:S(2)}, u32[]{:S(2)}) %collective-permute-start) | collective-permute-done | bytes 294944 | tf_op jit(solution)/shard_map/ppermute | solution.py:29
  15.8 2.6 %shard_map.93 = (bf16[128,1024]{1,0:T(8,128)(2,1)S(1)}, bf16[256,512]{1,0:T(8,128)(2,1)}, bf16[128,512]{1,0:T(8,128)(2,1)S(1)}, bf16[128,512]{1,0:T(8,128)(2,1)S...) custom-call(s32[1]{0:T(128)} %bitcast.place_ref, bf16[16,128]{1,0:T(8,128)(2,1)S(1)} %broadcast_in_dim.15.refs_0_, ...), custom_call_target="tpu_custom_call" | custom-call | flops 1024 | bytes 1024 | tf_op jit(solution)/shard_map/pallas_call | solution.py:122
  18.4 2.4 %collective-permute-start.4 = (bf16[256,512]{1,0:T(8,128)(2,1)}, bf16[256,512]{1,0:T(8,128)(2,1)S(1)}, u32[]{:S(2)}, u32[]{:S(2)}) collective-permute-start(bf16[256,512]{1,0:T(8,128)(2,1)} %get-tuple-element.28), channel_id=1, source_target_pairs={{0,1},{1,0},{2,3},{3,2},{4,5},{5,4},{6,7},{7,6},{8,9},{9,8},{10,11... | collective-permute-start | bytes 786440 | tf_op jit(solution)/shard_map/ppermute | solution.py:287
  20.8 1.0 %fusion.1 = bf16[2,4,1,168,128]{4,3,2,1,0:T(8,128)(2,1)S(1)} fusion(s32[]{:T(128)S(6)} %select_n.117, bf16[1,4,2,168,128]{4,3,2,1,0:T(8,128)(2,1)} %get-tuple-element.51, bf16[1,4,2,168,128]{4,3,2,1,0:T(8,128)(2,1)} %bitcast.16), kind=kLoop, calls=%fused_computation.13 | loop fusion | flops 172032 | bytes 1032196 | tf_op jit(solution)/shard_map/stack | solution.py:258
  22.0 1.9 %shard_map.94 = (bf16[128,1024]{1,0:T(8,128)(2,1)S(1)}, bf16[256,512]{1,0:T(8,128)(2,1)S(1)}, bf16[128,512]{1,0:T(8,128)(2,1)S(1)}, bf16[128,512]{1,0:T(8,128)(2...) custom-call(s32[1]{0:T(128)} %bitcast.place_ref, bf16[16,128]{1,0:T(8,128)(2,1)S(1)} %broadcast_in_dim.15.refs_0_, ...), custom_call_target="tpu_custom_call" | custom-call | flops 1024 | bytes 1024 | tf_op jit(solution)/shard_map/pallas_call | solution.py:122
  23.9 1.8 %collective-permute-start.9 = (bf16[256,512]{1,0:T(8,128)(2,1)S(1)}, bf16[256,512]{1,0:T(8,128)(2,1)S(1)}, u32[]{:S(2)}, u32[]{:S(2)}) collective-permute-start(bf16[256,512]{1,0:T(8,128)(2,1)S(1)} %get-tuple-element.37), channel_id=1, source_target_pairs={{0,1},{1,0},{2,3},{3,2},{4,5},{5,4},{6,7},{7,6},{8,9},{9,8},{10,11... | collective-permute-start | bytes 786440 | tf_op jit(solution)/shard_map/ppermute | solution.py:287
  25.7 1.0 %fusion.4 = bf16[1,4,1,168,128]{4,3,2,1,0:T(8,128)(2,1)S(1)} fusion(s32[]{:T(128)S(6)} %add.98, s32[]{:T(128)S(6)} %select_n.111, bf16[1,4,2,168,128]{4,3,2,1,0:T(8,128)(2,1)S(1)} %copy-done.4, bf16[1,4,2,168,128]{4,3,2,1,0:T(8,128)(2,1)} %bitcast.16), kind=kLoop, calls=%fused_computation.29 | loop fusion | flops 86016 | bytes 860168 | tf_op jit(solution)/shard_map/stack | solution.py:258
  26.9 1.6 %collective-permute-start.6 = (bf16[256,512]{1,0:T(8,128)(2,1)S(1)}, bf16[256,512]{1,0:T(8,128)(2,1)S(1)}, u32[]{:S(2)}, u32[]{:S(2)}) collective-permute-start(bf16[256,512]{1,0:T(8,128)(2,1)S(1)} %pad_maximum_fusion.3.refs_0_), channel_id=1, source_target_pairs={{0,4},{2,6},{4,0},{6,2},{8,12},{10,14},{12,8},{14,10},{16,20},{18,... | collective-permute-start | bytes 786440 | tf_op jit(solution)/shard_map/ppermute | solution.py:219
  28.4 1.6 %collective-permute-start.5 = (bf16[3,672,128]{2,1,0:T(8,128)(2,1)S(1)}, bf16[3,672,128]{2,1,0:T(8,128)(2,1)S(1)}, u32[]{:S(2)}, u32[]{:S(2)}) collective-permute-start(bf16[3,672,128]{2,1,0:T(8,128)(2,1)S(1)} %pad_maximum_fusion.2.others_ref), channel_id=1, source_target_pairs={{0,1},{1,0},{2,3},{3,2},{4,5},{5,4},{6,7},{7,6},{8,9},{9,8},{10,11... | collective-permute-start | bytes 1548296 | tf_op jit(solution)/shard_map/ppermute | solution.py:301
  30.0 3.0 %collective-permute-done.9.refs_6_ = bf16[256,512]{1,0:T(8,128)(2,1)S(1)} collective-permute-done((bf16[256,512]{1,0:T(8,128)(2,1)S(1)}, bf16[256,512]{1,0:T(8,128)(2,1)S(1)}, u32[]{:S(2)}, u32[]{:S(2)}) %collective-permute-start.9) | collective-permute-done | bytes 262176 | tf_op jit(solution)/shard_map/ppermute | solution.py:287
  33.1 1.6 %collective-permute-start.10 = (bf16[256,512]{1,0:T(8,128)(2,1)S(1)}, bf16[256,512]{1,0:T(8,128)(2,1)S(1)}, u32[]{:S(2)}, u32[]{:S(2)}) collective-permute-start(bf16[256,512]{1,0:T(8,128)(2,1)S(1)} %pad_maximum_fusion.4.refs_0_), channel_id=1, source_target_pairs={{0,4},{2,6},{4,0},{6,2},{8,12},{10,14},{12,8},{14,10},{16,20},{18,... | collective-permute-start | bytes 786440 | tf_op jit(solution)/shard_map/ppermute | solution.py:219
  34.7 0.8 %collective-permute-done.6.refs_1_ = bf16[256,512]{1,0:T(8,128)(2,1)S(1)} collective-permute-done((bf16[256,512]{1,0:T(8,128)(2,1)S(1)}, bf16[256,512]{1,0:T(8,128)(2,1)S(1)}, u32[]{:S(2)}, u32[]{:S(2)}) %collective-permute-start.6) | collective-permute-done | bytes 262176 | tf_op jit(solution)/shard_map/ppermute | solution.py:219
  36.0 5.0 %collective-permute-done.10.refs_1_ = bf16[256,512]{1,0:T(8,128)(2,1)S(1)} collective-permute-done((bf16[256,512]{1,0:T(8,128)(2,1)S(1)}, bf16[256,512]{1,0:T(8,128)(2,1)S(1)}, u32[]{:S(2)}, u32[]{:S(2)}) %collective-permute-start.10) | collective-permute-done | bytes 262176 | tf_op jit(solution)/shard_map/ppermute | solution.py:219
  41.0 2.7 %collective-permute-done.5.others_away_ref = bf16[3,672,128]{2,1,0:T(8,128)(2,1)S(1)} collective-permute-done((bf16[3,672,128]{2,1,0:T(8,128)(2,1)S(1)}, bf16[3,672,128]{2,1,0:T(8,128)(2,1)S(1)}, u32[]{:S(2)}, u32[]{:S(2)}) %collective-permute-start.5) | collective-permute-done | bytes 516128 | tf_op jit(solution)/shard_map/ppermute | solution.py:301
  44.3 1.6 %collective-permute-start.13 = (bf16[336,512]{1,0:T(8,128)(2,1)S(1)}, bf16[336,512]{1,0:T(8,128)(2,1)S(1)}, u32[]{:S(2)}, u32[]{:S(2)}) collective-permute-start(bf16[336,512]{1,0:T(8,128)(2,1)S(1)} %shard_map.95), channel_id=1, source_target_pairs={{0,8},{2,10},{4,12},{6,14},{8,0},{10,2},{12,4},{14,6},{16,24},{18,... | collective-permute-start | bytes 1032200 | tf_op jit(solution)/shard_map/ppermute | solution.py:219
  45.9 0.8 maximum_select_fusion
  48.9 0.8 %maximum_bitcast_fusion = bf16[1,128,2048]{2,1,0:T(8,128)(2,1)} fusion(bf16[128,1024]{1,0:T(8,128)(2,1)S(1)} %get-tuple-element.43, bf16[128,1024]{1,0:T(8,128)(2,1)S(1)} %get-tuple-element.42), kind=kLoop, calls=%fused_computation.10 | loop fusion | flops 1048576 | bytes 1048576 | tf_op jit(solution)/shard_map/broadcast_in_dim | solution.py:360
  49.7 5.6 %collective-permute-done.13 = bf16[336,512]{1,0:T(8,128)(2,1)S(1)} collective-permute-done((bf16[336,512]{1,0:T(8,128)(2,1)S(1)}, bf16[336,512]{1,0:T(8,128)(2,1)S(1)}, u32[]{:S(2)}, u32[]{:S(2)}) %collective-permute-start.13) | collective-permute-done | bytes 344096 | tf_op jit(solution)/shard_map/ppermute | solution.py:219
  55.5 2.7 %collective-permute-start.15 = (bf16[168,512]{1,0:T(8,128)(2,1)S(1)}, bf16[168,512]{1,0:T(8,128)(2,1)S(1)}, u32[]{:S(2)}, u32[]{:S(2)}) collective-permute-start(bf16[168,512]{1,0:T(8,128)(2,1)S(1)} %slice.88), channel_id=1, source_target_pairs={{0,16},{2,18},{4,20},{6,22},{8,24},{10,26},{12,28},{14,30},{16,0},... | collective-permute-start | bytes 516104 | tf_op jit(solution)/shard_map/ppermute | solution.py:219
  58.1 1.3 %collective-permute-start.14 = (bf16[128,1024]{1,0:T(8,128)(2,1)S(1)}, bf16[128,1024]{1,0:T(8,128)(2,1)S(1)}, u32[]{:S(2)}, u32[]{:S(2)}) collective-permute-start(bf16[128,1024]{1,0:T(8,128)(2,1)S(1)} %pad_maximum_fusion.5), channel_id=1, source_target_pairs={{1,0},{3,2},{5,4},{7,6},{9,8},{11,10},{13,12},{15,14},{17,16},{19,... | collective-permute-start | bytes 786440 | tf_op jit(solution)/shard_map/ppermute | solution.py:354
  59.4 5.7 %collective-permute-done.16 = bf16[336,512]{1,0:T(8,128)(2,1)S(1)} collective-permute-done((bf16[336,512]{1,0:T(8,128)(2,1)S(1)}, bf16[336,512]{1,0:T(8,128)(2,1)S(1)}, u32[]{:S(2)}, u32[]{:S(2)}) %collective-permute-start.16) | collective-permute-done | bytes 344096 | tf_op jit(solution)/shard_map/ppermute | solution.py:219
  65.3 1.3 %collective-permute-start.17 = (bf16[168,512]{1,0:T(8,128)(2,1)S(1)}, bf16[168,512]{1,0:T(8,128)(2,1)S(1)}, u32[]{:S(2)}, u32[]{:S(2)}) collective-permute-start(bf16[168,512]{1,0:T(8,128)(2,1)S(1)} %slice.87), channel_id=1, source_target_pairs={{0,16},{2,18},{4,20},{6,22},{8,24},{10,26},{12,28},{14,30},{16,0},... | collective-permute-start | bytes 516104 | tf_op jit(solution)/shard_map/ppermute | solution.py:219
  66.6 8.5 %collective-permute-done.17 = bf16[168,512]{1,0:T(8,128)(2,1)S(1)} collective-permute-done((bf16[168,512]{1,0:T(8,128)(2,1)S(1)}, bf16[168,512]{1,0:T(8,128)(2,1)S(1)}, u32[]{:S(2)}, u32[]{:S(2)}) %collective-permute-start.17) | collective-permute-done | bytes 172064 | tf_op jit(solution)/shard_map/ppermute | solution.py:219
  75.1 0.9 %pad_maximum_fusion.1 = f32[168,1024]{1,0:T(8,128)} fusion(f32[168,512]{1,0:T(8,128)S(1)} %slice_add_fusion, f32[168,512]{1,0:T(8,128)S(1)} %slice_add_fusion.1), kind=kLoop, calls=%fused_computation.5 | loop fusion | flops 172032 | bytes 1376256 | tf_op jit(solution)/shard_map/concatenate | solution.py:359
  76.0 0.8 %fusion.3 = bf16[1,128,1024]{2,1,0:T(8,128)(2,1)} fusion(bf16[128,1024]{1,0:T(8,128)(2,1)S(1)} %collective-permute-done.14, bf16[128,512]{1,0:T(8,128)(2,1)S(1)} %get-tuple-element.40, bf16[128,512]{1,0:T(8,128)(2,1)S(1)} %get-tuple-element.34), kind=kLoop, calls=%fused_computation.21 | loop fusion | flops 917504 | bytes 786432 | tf_op jit(solution)/shard_map/broadcast_in_dim | solution.py:360
  (53 shorter events, 4.6 us)
Async XLA Ops:
  1.3 6.9 %copy-start.5 = (bf16[1,128,2688]{2,1,0:T(8,128)(2,1)S(1)}, bf16[1,128,2688]{2,1,0:T(8,128)(2,1)}, u32[]{:S(2)}) copy-start(bf16[1,128,2688]{2,1,0:T(8,128)(2,1)} %param.6) | copy-start | bytes 2064388
  3.2 12.6 %collective-permute-start = (bf16[144,1024]{1,0:T(8,128)(2,1)}, bf16[144,1024]{1,0:T(8,128)(2,1)S(1)}, u32[]{:S(2)}, u32[]{:S(2)}) collective-permute-start(bf16[144,1024]{1,0:T(8,128)(2,1)} %fusion.2), channel_id=1, source_target_pairs={{0,1},{2,3},{4,5},{6,7},{8,9},{10,11},{12,13},{14,15},{16,17},{18,... | collective-permute-start | bytes 884744 | tf_op jit(solution)/shard_map/ppermute | solution.py:29
  9.7 11.1 %collective-permute-start.2 = (bf16[4,2,168,128]{3,2,1,0:T(8,128)(2,1)}, bf16[4,2,168,128]{3,2,1,0:T(8,128)(2,1)}, u32[]{:S(2)}, u32[]{:S(2)}) collective-permute-start(bf16[4,2,168,128]{3,2,1,0:T(8,128)(2,1)} %get-tuple-element.50), channel_id=1, source_target_pairs={{0,4},{2,6},{4,0},{6,2},{8,12},{10,14},{12,8},{14,10},{16,20},{18,... | collective-permute-start | bytes 1032200 | tf_op jit(solution)/shard_map/ppermute | solution.py:219
  11.2 4.6 %copy-start.3 = (bf16[1,128,2048]{2,1,0:T(8,128)(2,1)S(1)}, bf16[1,128,2048]{2,1,0:T(8,128)(2,1)}, u32[]{:S(2)}) copy-start(bf16[1,128,2048]{2,1,0:T(8,128)(2,1)} %param.10) | copy-start | bytes 1572868
  11.2 4.6 %copy-start.2 = (bf16[1,128,2048]{2,1,0:T(8,128)(2,1)S(1)}, bf16[1,128,2048]{2,1,0:T(8,128)(2,1)}, u32[]{:S(2)}) copy-start(bf16[1,128,2048]{2,1,0:T(8,128)(2,1)} %param.7) | copy-start | bytes 1572868
  11.4 4.4 %copy-start = (bf16[1,128,1024]{2,1,0:T(8,128)(2,1)S(1)}, bf16[1,128,1024]{2,1,0:T(8,128)(2,1)}, u32[]{:S(2)}) copy-start(bf16[1,128,1024]{2,1,0:T(8,128)(2,1)} %param.8) | copy-start | bytes 786436
  11.4 4.4 %copy-start.1 = (bf16[1,128,1024]{2,1,0:T(8,128)(2,1)S(1)}, bf16[1,128,1024]{2,1,0:T(8,128)(2,1)}, u32[]{:S(2)}) copy-start(bf16[1,128,1024]{2,1,0:T(8,128)(2,1)} %param.9) | copy-start | bytes 786436
  12.2 9.6 %collective-permute-start.1 = (bf16[128,1024]{1,0:T(8,128)(2,1)}, bf16[128,1024]{1,0:T(8,128)(2,1)S(1)}, u32[]{:S(2)}, u32[]{:S(2)}) collective-permute-start(bf16[128,1024]{1,0:T(8,128)(2,1)} %bitcast_select_fusion), channel_id=1, source_target_pairs={{0,1},{1,0},{2,3},{3,2},{4,5},{5,4},{6,7},{7,6},{8,9},{9,8},{10,11... | collective-permute-start | bytes 786440 | tf_op jit(solution)/shard_map/ppermute | solution.py:253
  18.4 8.3 %collective-permute-start.4 = (bf16[256,512]{1,0:T(8,128)(2,1)}, bf16[256,512]{1,0:T(8,128)(2,1)S(1)}, u32[]{:S(2)}, u32[]{:S(2)}) collective-permute-start(bf16[256,512]{1,0:T(8,128)(2,1)} %get-tuple-element.28), channel_id=1, source_target_pairs={{0,1},{1,0},{2,3},{3,2},{4,5},{5,4},{6,7},{7,6},{8,9},{9,8},{10,11... | collective-permute-start | bytes 786440 | tf_op jit(solution)/shard_map/ppermute | solution.py:287
  21.9 3.8 %copy-start.4 = (bf16[1,4,2,168,128]{4,3,2,1,0:T(8,128)(2,1)S(1)}, bf16[1,4,2,168,128]{4,3,2,1,0:T(8,128)(2,1)}, u32[]{:S(2)}) copy-start(bf16[1,4,2,168,128]{4,3,2,1,0:T(8,128)(2,1)} %get-tuple-element.51) | copy-start | bytes 1032196
  21.9 4.9 %collective-permute-start.3 = (bf16[2,672,128]{2,1,0:T(8,128)(2,1)S(1)}, bf16[2,672,128]{2,1,0:T(8,128)(2,1)S(1)}, u32[]{:S(2)}, u32[]{:S(2)}) collective-permute-start(bf16[2,672,128]{2,1,0:T(8,128)(2,1)S(1)} %bitcast.58), channel_id=1, source_target_pairs={{0,2},{2,0},{4,6},{6,4},{8,10},{10,8},{12,14},{14,12},{16,18},{18,... | collective-permute-start | bytes 1032200 | tf_op jit(solution)/shard_map/ppermute | solution.py:219
  23.9 9.2 %collective-permute-start.9 = (bf16[256,512]{1,0:T(8,128)(2,1)S(1)}, bf16[256,512]{1,0:T(8,128)(2,1)S(1)}, u32[]{:S(2)}, u32[]{:S(2)}) collective-permute-start(bf16[256,512]{1,0:T(8,128)(2,1)S(1)} %get-tuple-element.37), channel_id=1, source_target_pairs={{0,1},{1,0},{2,3},{3,2},{4,5},{5,4},{6,7},{7,6},{8,9},{9,8},{10,11... | collective-permute-start | bytes 786440 | tf_op jit(solution)/shard_map/ppermute | solution.py:287
  26.9 8.6 %collective-permute-start.6 = (bf16[256,512]{1,0:T(8,128)(2,1)S(1)}, bf16[256,512]{1,0:T(8,128)(2,1)S(1)}, u32[]{:S(2)}, u32[]{:S(2)}) collective-permute-start(bf16[256,512]{1,0:T(8,128)(2,1)S(1)} %pad_maximum_fusion.3.refs_0_), channel_id=1, source_target_pairs={{0,4},{2,6},{4,0},{6,2},{8,12},{10,14},{12,8},{14,10},{16,20},{18,... | collective-permute-start | bytes 786440 | tf_op jit(solution)/shard_map/ppermute | solution.py:219
  28.4 15.3 %collective-permute-start.5 = (bf16[3,672,128]{2,1,0:T(8,128)(2,1)S(1)}, bf16[3,672,128]{2,1,0:T(8,128)(2,1)S(1)}, u32[]{:S(2)}, u32[]{:S(2)}) collective-permute-start(bf16[3,672,128]{2,1,0:T(8,128)(2,1)S(1)} %pad_maximum_fusion.2.others_ref), channel_id=1, source_target_pairs={{0,1},{1,0},{2,3},{3,2},{4,5},{5,4},{6,7},{7,6},{8,9},{9,8},{10,11... | collective-permute-start | bytes 1548296 | tf_op jit(solution)/shard_map/ppermute | solution.py:301
  33.1 7.9 %collective-permute-start.10 = (bf16[256,512]{1,0:T(8,128)(2,1)S(1)}, bf16[256,512]{1,0:T(8,128)(2,1)S(1)}, u32[]{:S(2)}, u32[]{:S(2)}) collective-permute-start(bf16[256,512]{1,0:T(8,128)(2,1)S(1)} %pad_maximum_fusion.4.refs_0_), channel_id=1, source_target_pairs={{0,4},{2,6},{4,0},{6,2},{8,12},{10,14},{12,8},{14,10},{16,20},{18,... | collective-permute-start | bytes 786440 | tf_op jit(solution)/shard_map/ppermute | solution.py:219
  34.7 6.3 %collective-permute-start.7 = (bf16[256,512]{1,0:T(8,128)(2,1)S(1)}, bf16[256,512]{1,0:T(8,128)(2,1)S(1)}, u32[]{:S(2)}, u32[]{:S(2)}) collective-permute-start(bf16[256,512]{1,0:T(8,128)(2,1)S(1)} %pad_maximum_fusion.3.refs_0_), channel_id=1, source_target_pairs={{0,2},{2,0},{4,6},{6,4},{8,10},{10,8},{12,14},{14,12},{16,18},{18,... | collective-permute-start | bytes 786440 | tf_op jit(solution)/shard_map/ppermute | solution.py:219
  35.5 8.2 %collective-permute-start.8 = (bf16[256,512]{1,0:T(8,128)(2,1)S(1)}, bf16[256,512]{1,0:T(8,128)(2,1)S(1)}, u32[]{:S(2)}, u32[]{:S(2)}) collective-permute-start(bf16[256,512]{1,0:T(8,128)(2,1)S(1)} %collective-permute-done.6.refs_1_), channel_id=1, source_target_pairs={{0,2},{2,0},{4,6},{6,4},{8,10},{10,8},{12,14},{14,12},{16,18},{18,... | collective-permute-start | bytes 786440 | tf_op jit(solution)/shard_map/ppermute | solution.py:219
  35.5 11.2 %collective-permute-start.11 = (bf16[256,512]{1,0:T(8,128)(2,1)S(1)}, bf16[256,512]{1,0:T(8,128)(2,1)S(1)}, u32[]{:S(2)}, u32[]{:S(2)}) collective-permute-start(bf16[256,512]{1,0:T(8,128)(2,1)S(1)} %pad_maximum_fusion.4.refs_0_), channel_id=1, source_target_pairs={{0,2},{2,0},{4,6},{6,4},{8,10},{10,8},{12,14},{14,12},{16,18},{18,... | collective-permute-start | bytes 786440 | tf_op jit(solution)/shard_map/ppermute | solution.py:219
  41.0 5.7 %collective-permute-start.12 = (bf16[256,512]{1,0:T(8,128)(2,1)S(1)}, bf16[256,512]{1,0:T(8,128)(2,1)S(1)}, u32[]{:S(2)}, u32[]{:S(2)}) collective-permute-start(bf16[256,512]{1,0:T(8,128)(2,1)S(1)} %collective-permute-done.10.refs_1_), channel_id=1, source_target_pairs={{0,2},{2,0},{4,6},{6,4},{8,10},{10,8},{12,14},{14,12},{16,18},{18,... | collective-permute-start | bytes 786440 | tf_op jit(solution)/shard_map/ppermute | solution.py:219
  44.3 11.0 %collective-permute-start.13 = (bf16[336,512]{1,0:T(8,128)(2,1)S(1)}, bf16[336,512]{1,0:T(8,128)(2,1)S(1)}, u32[]{:S(2)}, u32[]{:S(2)}) collective-permute-start(bf16[336,512]{1,0:T(8,128)(2,1)S(1)} %shard_map.95), channel_id=1, source_target_pairs={{0,8},{2,10},{4,12},{6,14},{8,0},{10,2},{12,4},{14,6},{16,24},{18,... | collective-permute-start | bytes 1032200 | tf_op jit(solution)/shard_map/ppermute | solution.py:219
  47.3 17.9 %collective-permute-start.16 = (bf16[336,512]{1,0:T(8,128)(2,1)S(1)}, bf16[336,512]{1,0:T(8,128)(2,1)S(1)}, u32[]{:S(2)}, u32[]{:S(2)}) collective-permute-start(bf16[336,512]{1,0:T(8,128)(2,1)S(1)} %shard_map.96), channel_id=1, source_target_pairs={{0,8},{2,10},{4,12},{6,14},{8,0},{10,2},{12,4},{14,6},{16,24},{18,... | collective-permute-start | bytes 1032200 | tf_op jit(solution)/shard_map/ppermute | solution.py:219
  55.5 11.1 %collective-permute-start.15 = (bf16[168,512]{1,0:T(8,128)(2,1)S(1)}, bf16[168,512]{1,0:T(8,128)(2,1)S(1)}, u32[]{:S(2)}, u32[]{:S(2)}) collective-permute-start(bf16[168,512]{1,0:T(8,128)(2,1)S(1)} %slice.88), channel_id=1, source_target_pairs={{0,16},{2,18},{4,20},{6,22},{8,24},{10,26},{12,28},{14,30},{16,0},... | collective-permute-start | bytes 516104 | tf_op jit(solution)/shard_map/ppermute | solution.py:219
  58.1 17.9 %collective-permute-start.14 = (bf16[128,1024]{1,0:T(8,128)(2,1)S(1)}, bf16[128,1024]{1,0:T(8,128)(2,1)S(1)}, u32[]{:S(2)}, u32[]{:S(2)}) collective-permute-start(bf16[128,1024]{1,0:T(8,128)(2,1)S(1)} %pad_maximum_fusion.5), channel_id=1, source_target_pairs={{1,0},{3,2},{5,4},{7,6},{9,8},{11,10},{13,12},{15,14},{17,16},{19,... | collective-permute-start | bytes 786440 | tf_op jit(solution)/shard_map/ppermute | solution.py:354
  65.3 9.8 %collective-permute-start.17 = (bf16[168,512]{1,0:T(8,128)(2,1)S(1)}, bf16[168,512]{1,0:T(8,128)(2,1)S(1)}, u32[]{:S(2)}, u32[]{:S(2)}) collective-permute-start(bf16[168,512]{1,0:T(8,128)(2,1)S(1)} %slice.87), channel_id=1, source_target_pairs={{0,16},{2,18},{4,20},{6,22},{8,24},{10,26},{12,28},{14,30},{16,0},... | collective-permute-start | bytes 516104 | tf_op jit(solution)/shard_map/ppermute | solution.py:219
